TPU v7x, 32 devices: a whole 2x2x4 slice. The times are simulated.
32 devices in a mesh: fsdp: 4 (over y, x), ctx: 4 (over z), tp: 2 (over core).
Axes of the slice: x: 2, y: 2, z: 4, core: 2. Of those that a mesh axis runs over, the one named last changes fastest.
Arguments:
- hidden_in: bfloat16 [4096, 2048], P(('fsdp', 'ctx')), may hold values from -6 to 6
- out_cotangent: bfloat16 [4096, 2048], P(('fsdp', 'ctx')), may hold values from -6 to 6
- norm1_gain: bfloat16 [2048], P('fsdp'), may hold values from 0.25 to 1.75
- q_weight: bfloat16 [2048, 2048], P('fsdp', 'tp'), may hold values from -0.125 to 0.125
- key_projection_weight: bfloat16 [2048, 512], P('fsdp', 'tp'), may hold values from -0.125 to 0.125
- value_projection_weight: bfloat16 [2048, 512], P('fsdp', 'tp'), may hold values from -0.125 to 0.125
- o_weight: bfloat16 [2048, 2048], P('fsdp', 'tp'), may hold values from -1 to 1
- norm2_gain: bfloat16 [2048], P('fsdp'), may hold values from 0.25 to 1.75
- gate_weight: bfloat16 [2048, 8192], P('fsdp', 'tp'), may hold values from -0.125 to 0.125
- up_weight: bfloat16 [2048, 8192], P('fsdp', 'tp'), may hold values from -0.125 to 0.125
- down_weight: bfloat16 [2048, 8192], P('fsdp', 'tp'), may hold values from -0.0625 to 0.0625
- seq_lengths: int32 [4, 4], P('fsdp'), may hold values from 1 to 768, as said below
- span_order: int32 [4, 4], P('fsdp'), may hold values from 0 to 3, each once within a row
Outputs:
- out_hidden: bfloat16 [4096, 2048], P(('fsdp', 'ctx'))
- in_grad: bfloat16 [4096, 2048], P(('fsdp', 'ctx'))
- norm1_grad: float32 [2048], P('fsdp')
- q_grad: float32 [2048, 2048], P('fsdp', 'tp')
- k_grad: float32 [2048, 512], P('fsdp', 'tp')
- v_grad: float32 [2048, 512], P('fsdp', 'tp')
- o_grad: float32 [2048, 2048], P('fsdp', 'tp')
- norm2_grad: float32 [2048], P('fsdp')
- gate_grad: float32 [2048, 8192], P('fsdp', 'tp')
- up_grad: float32 [2048, 8192], P('fsdp', 'tp')
- down_grad: float32 [2048, 8192], P('fsdp', 'tp')
Inputs may be any that keep to these rules, and one draw needn't show every extreme that they name: `seq_lengths`: each row holds 4 positive lengths that sum to 1024; exactly one of them is 768. `span_order`: each row is a permutation.
All inputs are finite; a program needn't handle non-finite values.
Results may differ from a plain program's by a relative error of at most 0.02.
Values may be sent and summed in bfloat16 or wider, within the bound.
No kernel may reach another device: no remote copies, remote signals or barrier semaphores. Data moves between devices by JAX's collectives and lax.ppermute only.
A program may use at most 320 MiB of HBM per device.

v0:
```python
import math

import jax
import jax.numpy as jnp
from jax import lax
from jax.sharding import PartitionSpec as P

QUERY_HEADS = 32
KEY_VALUE_HEADS = 8
HEAD_SIZE = 64


def stream_place(row_ids, order_row, length_row, tok_dev):
    cycle_size = order_row.shape[0]
    half_len = tok_dev // 2
    cycle_rank = row_ids // tok_dev
    within = row_ids % tok_dev
    first_section = jnp.sum(
        jnp.where(
            cycle_rank[:, None] == jnp.arange(cycle_size, dtype=jnp.int32)[None, :],
            order_row[None, :],
            0,
        ),
        axis=1,
        dtype=jnp.int32,
    )
    section = jnp.where(within >= half_len, 2 * cycle_size - 1 - first_section, first_section)
    places = section * half_len + within % half_len
    seq_ends = jnp.cumsum(length_row, dtype=jnp.int32)
    passed = places[:, None] >= seq_ends[None, :]
    segment = jnp.sum(passed.astype(jnp.int32), axis=1, dtype=jnp.int32)
    offset = places - jnp.sum(jnp.where(passed, length_row[None, :], 0), axis=1, dtype=jnp.int32)
    return (places, segment, offset)


def rotary_embedding(values, positions):
    half_len = values.shape[-1] // 2
    frequency = jnp.exp(
        -math.log(500000.0) * jnp.arange(half_len, dtype=jnp.float32) * 2.0 / values.shape[-1]
    )
    angles = positions.astype(jnp.float32)[:, None] * frequency[None, :]
    cosine = jnp.cos(angles)[:, None, :]
    sine = jnp.sin(angles)[:, None, :]
    lower_half = values[..., :half_len]
    upper_half = values[..., half_len:]
    return jnp.concatenate(
        [lower_half * cosine - upper_half * sine, upper_half * cosine + lower_half * sine], axis=-1
    )


def normalize(values, gain_vec):
    return values * lax.rsqrt(jnp.mean(values * values, axis=-1, keepdims=True) + 1e-05) * gain_vec


def swiglu(gate_val, up_val):
    return jax.nn.silu(gate_val) * up_val


def contract_last(left, right):
    return lax.dot_general(
        left, right, (((1,), (1,)), ((), ())), preferred_element_type=jnp.float32
    )


def contract_first(left, right):
    return lax.dot_general(
        left, right, (((0,), (0,)), ((), ())), preferred_element_type=jnp.float32
    )


def shards(
    hidden_in,
    out_cotangent,
    norm1_gain,
    q_weight,
    key_projection_weight,
    value_projection_weight,
    o_weight,
    norm2_gain,
    gate_weight,
    up_weight,
    down_weight,
    seq_lengths,
    span_order,
):
    rows_here = hidden_in.shape[0]
    order_row = span_order[0]
    length_row = seq_lengths[0]
    kv_heads = key_projection_weight.shape[1] // HEAD_SIZE
    query_groups = QUERY_HEADS // KEY_VALUE_HEADS
    score_scale = 1.0 / math.sqrt(HEAD_SIZE)
    whole_rows = rows_here * lax.axis_size("ctx")
    local_rows = lax.axis_index("ctx") * rows_here + jnp.arange(rows_here, dtype=jnp.int32)
    q_place, q_segment, q_offset = stream_place(local_rows, order_row, length_row, rows_here)
    inputs = hidden_in.astype(jnp.float32)
    gain_one, wq_full, wk_full, wv_full, wo_full = (
        lax.all_gather(norm1_gain, "fsdp", axis=0, tiled=True),
        lax.all_gather(q_weight, "fsdp", axis=0, tiled=True),
        lax.all_gather(key_projection_weight, "fsdp", axis=0, tiled=True),
        lax.all_gather(value_projection_weight, "fsdp", axis=0, tiled=True),
        lax.all_gather(o_weight, "fsdp", axis=0, tiled=True),
    )
    gain_one = gain_one.astype(jnp.float32)
    first_normalized = normalize(inputs, gain_one)
    normed_low = first_normalized.astype(jnp.bfloat16)
    q_linear = jnp.dot(normed_low, wq_full, preferred_element_type=jnp.float32).reshape(
        rows_here, kv_heads * query_groups, HEAD_SIZE
    )
    k_linear = jnp.dot(normed_low, wk_full, preferred_element_type=jnp.float32).reshape(
        rows_here, kv_heads, HEAD_SIZE
    )
    q_rotated = (
        rotary_embedding(q_linear, q_offset)
        .astype(jnp.bfloat16)
        .reshape(rows_here, kv_heads, query_groups, HEAD_SIZE)
    )
    k_rotated = (
        rotary_embedding(k_linear, q_offset)
        .astype(jnp.bfloat16)
        .reshape(rows_here, kv_heads * HEAD_SIZE)
    )
    v_low = jnp.dot(normed_low, wv_full, preferred_element_type=jnp.float32).astype(jnp.bfloat16)

    def key_blocks(shard_rows):
        row_count = shard_rows.shape[0]
        key_total_width = math.gcd(row_count, 512)
        number = row_count // key_total_width
        k_place, k_segment, _ = stream_place(
            jnp.arange(row_count, dtype=jnp.int32), order_row, length_row, rows_here
        )
        return (
            key_total_width,
            number,
            k_place.reshape(number, key_total_width),
            k_segment.reshape(number, key_total_width),
        )

    def scores_of(key_block, place_block, segment_block):
        scores = (
            jnp.einsum("qkgd,skd->kgqs", q_rotated, key_block, preferred_element_type=jnp.float32)
            * score_scale
        )
        visible = (
            (q_place[:, None] >= place_block[None, :])
            & (q_segment[:, None] == segment_block[None, :])
        )[None, None]
        return (jnp.where(visible, scores, -1e30), visible)

    start_state = (
        jnp.full((kv_heads, query_groups, rows_here), -1e30, jnp.float32),
        jnp.zeros((kv_heads, query_groups, rows_here), jnp.float32),
        jnp.zeros((kv_heads, query_groups, rows_here, HEAD_SIZE), jnp.float32),
    )
    folded = start_state
    key_row_block = lax.all_gather(k_rotated, "ctx", axis=0, tiled=True)
    value_row_block = lax.all_gather(v_low, "ctx", axis=0, tiled=True)
    key_total_width, number, k_place, k_segment = key_blocks(key_row_block)

    def one_step(carried, pieces):
        running_max, totals, accumulated = carried
        key_block, value_block, place_block, segment_block = pieces
        scores, visible = scores_of(key_block, place_block, segment_block)
        new_max = jnp.maximum(running_max, jnp.max(scores, axis=-1))
        weights = jnp.where(visible, jnp.exp(scores - new_max[..., None]), 0.0)
        factor = jnp.exp(running_max - new_max)
        totals = totals * factor + jnp.sum(weights, axis=-1)
        accumulated = accumulated * factor[..., None] + jnp.einsum(
            "kgqs,skd->kgqd",
            weights.astype(jnp.bfloat16),
            value_block,
            preferred_element_type=jnp.float32,
        )
        return ((new_max, totals, accumulated), None)

    pieces = (
        key_row_block.reshape(number, key_total_width, kv_heads, HEAD_SIZE),
        value_row_block.reshape(number, key_total_width, kv_heads, HEAD_SIZE),
        k_place,
        k_segment,
    )
    folded, _ = lax.scan(one_step, folded, pieces)
    running_max, totals, accumulated = folded
    mixed_out = jnp.transpose(accumulated / totals[..., None], (2, 0, 1, 3))
    log_sum = running_max + jnp.log(totals)
    attn_low = mixed_out.reshape(rows_here, kv_heads * query_groups * HEAD_SIZE).astype(
        jnp.bfloat16
    )
    branch = lax.psum(contract_last(attn_low, wo_full).astype(jnp.bfloat16), "tp").astype(
        jnp.float32
    )
    middle = inputs + branch
    gain_two, wg_full, wu_full, wd_full = (
        lax.all_gather(norm2_gain, "fsdp", axis=0, tiled=True),
        lax.all_gather(gate_weight, "fsdp", axis=0, tiled=True),
        lax.all_gather(up_weight, "fsdp", axis=0, tiled=True),
        lax.all_gather(down_weight, "fsdp", axis=0, tiled=True),
    )
    gain_two = gain_two.astype(jnp.float32)
    normed_two = normalize(middle, gain_two)
    normed_two_low = normed_two.astype(jnp.bfloat16)
    gate_val = jnp.dot(normed_two_low, wg_full, preferred_element_type=jnp.float32)
    up_val = jnp.dot(normed_two_low, wu_full, preferred_element_type=jnp.float32)
    hidden = swiglu(gate_val, up_val).astype(jnp.bfloat16)
    ffn_out = lax.psum(contract_last(hidden, wd_full).astype(jnp.bfloat16), "tp").astype(
        jnp.float32
    )
    result = (middle + ffn_out).astype(jnp.bfloat16)
    grad_out = out_cotangent.astype(jnp.float32)
    d_wd = contract_first(out_cotangent, hidden)
    d_hidden = jnp.dot(out_cotangent, wd_full, preferred_element_type=jnp.float32)
    _, swiglu_back = jax.vjp(swiglu, gate_val, up_val)
    d_gate, d_up = swiglu_back(d_hidden)
    d_gate_low = d_gate.astype(jnp.bfloat16)
    d_up_low = d_up.astype(jnp.bfloat16)
    d_wg = contract_first(normed_two_low, d_gate_low)
    d_wu = contract_first(normed_two_low, d_up_low)
    d_normed_two = lax.psum(
        (contract_last(d_gate_low, wg_full) + contract_last(d_up_low, wu_full)).astype(
            jnp.bfloat16
        ),
        "tp",
    ).astype(jnp.float32)
    _, norm_two_back = jax.vjp(normalize, middle, gain_two)
    d_middle_norm, d_gain_two = norm_two_back(d_normed_two)
    d_middle = grad_out + d_middle_norm
    d_branch_low = d_middle.astype(jnp.bfloat16)
    d_wo = contract_first(d_branch_low, attn_low)
    d_attn = jnp.dot(d_branch_low, wo_full, preferred_element_type=jnp.float32).astype(jnp.bfloat16)
    d_attn_heads = d_attn.reshape(rows_here, kv_heads, query_groups, HEAD_SIZE)
    row_delta = jnp.einsum("qkgd,qkgd->kgq", d_attn_heads.astype(jnp.float32), mixed_out)
    back_state = (
        jnp.zeros((rows_here, kv_heads, query_groups, HEAD_SIZE), jnp.float32),
        jnp.zeros((whole_rows, kv_heads, HEAD_SIZE), jnp.float32),
        jnp.zeros((whole_rows, kv_heads, HEAD_SIZE), jnp.float32),
    )
    folded = back_state
    key_row_block = lax.all_gather(k_rotated, "ctx", axis=0, tiled=True)
    value_row_block = lax.all_gather(v_low, "ctx", axis=0, tiled=True)
    key_total_width, number, k_place, k_segment = key_blocks(key_row_block)

    def one_step(carried, pieces):
        d_query, d_keys, d_values = carried
        key_block, value_block, place_block, segment_block, step_index = pieces
        scores, visible = scores_of(key_block, place_block, segment_block)
        prob_rows = jnp.where(visible, jnp.exp(scores - log_sum[..., None]), 0.0)
        d_values_block = jnp.einsum(
            "kgqs,qkgd->skd",
            prob_rows.astype(jnp.bfloat16),
            d_attn_heads,
            preferred_element_type=jnp.float32,
        )
        d_probs = jnp.einsum(
            "qkgd,skd->kgqs", d_attn_heads, value_block, preferred_element_type=jnp.float32
        )
        d_scores = (prob_rows * (d_probs - row_delta[..., None])).astype(jnp.bfloat16)
        d_query = (
            d_query
            + jnp.einsum("kgqs,skd->qkgd", d_scores, key_block, preferred_element_type=jnp.float32)
            * score_scale
        )
        d_keys_block = (
            jnp.einsum("kgqs,qkgd->skd", d_scores, q_rotated, preferred_element_type=jnp.float32)
            * score_scale
        )
        row_first = step_index * key_total_width
        d_keys = lax.dynamic_update_slice_in_dim(
            d_keys,
            lax.dynamic_slice_in_dim(d_keys, row_first, key_total_width, 0) + d_keys_block,
            row_first,
            0,
        )
        d_values = lax.dynamic_update_slice_in_dim(
            d_values,
            lax.dynamic_slice_in_dim(d_values, row_first, key_total_width, 0) + d_values_block,
            row_first,
            0,
        )
        return ((d_query, d_keys, d_values), None)

    pieces = (
        key_row_block.reshape(number, key_total_width, kv_heads, HEAD_SIZE),
        value_row_block.reshape(number, key_total_width, kv_heads, HEAD_SIZE),
        k_place,
        k_segment,
        jnp.arange(number, dtype=jnp.int32),
    )
    folded, _ = lax.scan(one_step, folded, pieces)
    d_query, d_keys_all, d_values_all = folded
    d_key_own, d_value_own = (
        lax.psum_scatter(
            d_keys_all.astype(jnp.bfloat16), "ctx", scatter_dimension=0, tiled=True
        ).astype(jnp.float32),
        lax.psum_scatter(
            d_values_all.astype(jnp.bfloat16), "ctx", scatter_dimension=0, tiled=True
        ).astype(jnp.float32),
    )
    _, rope_q_back = jax.vjp(lambda rotated_in: rotary_embedding(rotated_in, q_offset), q_linear)
    _, rope_k_back = jax.vjp(lambda rotated_in: rotary_embedding(rotated_in, q_offset), k_linear)
    (d_q_linear,) = rope_q_back(d_query.reshape(rows_here, kv_heads * query_groups, HEAD_SIZE))
    (d_k_linear,) = rope_k_back(d_key_own)
    d_q_low = d_q_linear.reshape(rows_here, kv_heads * query_groups * HEAD_SIZE).astype(
        jnp.bfloat16
    )
    d_k_low = d_k_linear.reshape(rows_here, kv_heads * HEAD_SIZE).astype(jnp.bfloat16)
    d_v_low = d_value_own.reshape(rows_here, kv_heads * HEAD_SIZE).astype(jnp.bfloat16)
    d_wq = contract_first(normed_low, d_q_low)
    d_wk = contract_first(normed_low, d_k_low)
    d_wv = contract_first(normed_low, d_v_low)
    d_normed_one = lax.psum(
        (
            contract_last(d_q_low, wq_full)
            + contract_last(d_k_low, wk_full)
            + contract_last(d_v_low, wv_full)
        ).astype(jnp.bfloat16),
        "tp",
    ).astype(jnp.float32)
    _, norm_one_back = jax.vjp(normalize, inputs, gain_one)
    d_inputs_norm, d_gain_one = norm_one_back(d_normed_one)
    in_grad = (d_middle + d_inputs_norm).astype(jnp.bfloat16)
    weight_grads = (d_gain_one, d_wq, d_wk, d_wv, d_wo, d_gain_two, d_wg, d_wu, d_wd)
    shares = (
        lax.psum_scatter(weight_grads[0], ("fsdp", "ctx"), scatter_dimension=0, tiled=True),
        lax.psum_scatter(weight_grads[1], ("fsdp", "ctx"), scatter_dimension=0, tiled=True),
        lax.psum_scatter(weight_grads[2], ("fsdp", "ctx"), scatter_dimension=0, tiled=True),
        lax.psum_scatter(weight_grads[3], ("fsdp", "ctx"), scatter_dimension=0, tiled=True),
        lax.psum_scatter(weight_grads[4], ("fsdp", "ctx"), scatter_dimension=0, tiled=True),
        lax.psum_scatter(weight_grads[5], ("fsdp", "ctx"), scatter_dimension=0, tiled=True),
        lax.psum_scatter(weight_grads[6], ("fsdp", "ctx"), scatter_dimension=0, tiled=True),
        lax.psum_scatter(weight_grads[7], ("fsdp", "ctx"), scatter_dimension=0, tiled=True),
        lax.psum_scatter(weight_grads[8], ("fsdp", "ctx"), scatter_dimension=0, tiled=True),
    )
    owned_grads = (
        lax.all_gather(shares[0].astype(jnp.bfloat16), "ctx", axis=0, tiled=True).astype(
            jnp.float32
        ),
        lax.all_gather(shares[1].astype(jnp.bfloat16), "ctx", axis=0, tiled=True).astype(
            jnp.float32
        ),
        lax.all_gather(shares[2].astype(jnp.bfloat16), "ctx", axis=0, tiled=True).astype(
            jnp.float32
        ),
        lax.all_gather(shares[3].astype(jnp.bfloat16), "ctx", axis=0, tiled=True).astype(
            jnp.float32
        ),
        lax.all_gather(shares[4].astype(jnp.bfloat16), "ctx", axis=0, tiled=True).astype(
            jnp.float32
        ),
        lax.all_gather(shares[5].astype(jnp.bfloat16), "ctx", axis=0, tiled=True).astype(
            jnp.float32
        ),
        lax.all_gather(shares[6].astype(jnp.bfloat16), "ctx", axis=0, tiled=True).astype(
            jnp.float32
        ),
        lax.all_gather(shares[7].astype(jnp.bfloat16), "ctx", axis=0, tiled=True).astype(
            jnp.float32
        ),
        lax.all_gather(shares[8].astype(jnp.bfloat16), "ctx", axis=0, tiled=True).astype(
            jnp.float32
        ),
    )
    return (
        result,
        in_grad,
        owned_grads[0],
        owned_grads[1],
        owned_grads[2],
        owned_grads[3],
        owned_grads[4],
        owned_grads[5],
        owned_grads[6],
        owned_grads[7],
        owned_grads[8],
    )


def solution(mesh):
    placed = (
        P(("fsdp", "ctx"), None),
        P(("fsdp", "ctx"), None),
        P("fsdp"),
        P("fsdp", "tp"),
        P("fsdp", "tp"),
        P("fsdp", "tp"),
        P("fsdp", "tp"),
        P("fsdp"),
        P("fsdp", "tp"),
        P("fsdp", "tp"),
        P("fsdp", "tp"),
        P("fsdp", None),
        P("fsdp", None),
    )
    return jax.shard_map(
        shards,
        mesh=mesh,
        in_specs=placed,
        out_specs=(
            P(("fsdp", "ctx"), None),
            P(("fsdp", "ctx"), None),
            P("fsdp"),
            P("fsdp", "tp"),
            P("fsdp", "tp"),
            P("fsdp", "tp"),
            P("fsdp", "tp"),
            P("fsdp"),
            P("fsdp", "tp"),
            P("fsdp", "tp"),
            P("fsdp", "tp"),
        ),
        check_vma=False,
    )
```

profile of v0, /device:TPU:0, one launch (start us, length us, event | category | flops | bytes accessed | tf_op | source)
XLA Modules:
  0.0 3791.9 jit_solution(17390938088742770877)
XLA Ops:
  10.7 9.5 all-gather
  20.9 18.3 all-gather.17.cloned.1.call-done
  41.2 15.6 all_gather.64
  57.3 10.5 all-gather.21.cloned.1.call-done
  69.5 15.6 all_gather.67
  86.9 35.5 all-gather.19.cloned.1.call-done
  122.3 4.0 fusion.112
  127.6 29.3 while.30
  127.8 5.0 fusion.190
  132.8 4.8 fusion.191
  142.3 4.8 fusion.190
  147.1 4.6 fusion.191
  157.9 18.9 all-gather.23.cloned.1.call-done
  176.8 4.6 convolution_convert_fusion.1
  183.6 8.0 all-gather.1
  191.6 9.6 all-reduce.12.cloned.1.call-done
  203.4 158.2 %all-gather.25.cloned.1.call-done = bf16[2048,4096]{1,0:T(8,128)(2,1)} async-done(((bf16[512,4096]{1,0:T(8,128)(2,1)}), bf16[2048,4096]{1,0:T(8,128)(2,1)}) %all-gather.25.cloned.1.call-update) | async-done | bytes 16777232 | tf_op jit(solution)/shard_map/all_gather | solution.py:194
  361.7 10.7 fusion.118
  372.4 148.7 %all-gather.27.cloned.1.call-done = bf16[2048,4096]{1,0:T(8,128)(2,1)} async-done(((bf16[512,4096]{1,0:T(8,128)(2,1)}), bf16[2048,4096]{1,0:T(8,128)(2,1)}) %all-gather.27.cloned.1.call-update) | async-done | bytes 16777232 | tf_op jit(solution)/shard_map/all_gather | solution.py:195
  521.1 12.9 fusion.119
  534.0 146.5 %all-gather.29.cloned.1.call-done = bf16[2048,4096]{1,0:T(8,128)(2,1)} async-done(((bf16[512,4096]{1,0:T(8,128)(2,1)}), bf16[2048,4096]{1,0:T(8,128)(2,1)}) %all-gather.29.cloned.1.call-update) | async-done | bytes 16777232 | tf_op jit(solution)/shard_map/all_gather | solution.py:196
  680.5 16.5 multiply_convert_fusion
  697.0 12.3 fusion.120
  709.3 12.5 fusion.61
  721.8 19.7 all-reduce.14.cloned.1.call-done
  741.5 3.2 fusion.69
  744.8 4.6 convolution_convert_fusion.2
  755.2 39.3 %while.31 = (s32[]{:T(128)}, f32[256,4,4,64]{0,3,2,1:T(8,128)S(1)}, f32[1024,4,64]{0,2,1:T(8,128)}, f32[1024,4,64]{0,2,1:T(8,128)}, bf16[2,512,4,64]{1,3,2,0:T(8...) while((s32[]{:T(128)}, f32[256,4,4,64]{0,3,2,1:T(8,128)S(1)}, ...), condition=%wide.region_17.18_spmd.clone, body=%wide.region_16.17_spmd.clone.sunk | while | flops 1368915968 | bytes 116586880 | solution.py:287
  756.9 4.4 fusion.205
  765.8 4.6 fusion.207
  770.5 4.4 fusion.208
  776.5 4.4 fusion.205
  785.3 4.6 fusion.207
  790.1 4.4 fusion.208
  798.8 4.8 fusion.109
  805.2 6.8 fusion.77
  812.3 17.7 fusion.122
  830.0 17.6 fusion.123
  847.7 14.9 convolution_bitcast_fusion.1
  862.9 12.0 convolution_convert_fusion
  874.9 5.0 fusion.121
  881.2 3.4 convolution_add_fusion.1
  884.7 3.4 fusion.62
  892.2 133.7 %reduce-scatter.14.cloned.1.call-done = f32[128,1024]{1,0:T(8,128)} async-done(((f32[2048,1024]{1,0:T(8,128)}), f32[128,1024]{1,0:T(8,128)}) %reduce-scatter.14.cloned.1.call-update) | async-done | bytes 524304 | tf_op jit(solution)/shard_map/reduce_scatter | solution.py:323
  1027.7 180.9 %reduce-scatter.20.cloned.1.call-done = f32[128,1024]{1,0:T(8,128)} async-done(((f32[2048,1024]{1,0:T(8,128)}), f32[128,1024]{1,0:T(8,128)}) %reduce-scatter.20.cloned.1.call-update) | async-done | bytes 524304 | tf_op jit(solution)/shard_map/reduce_scatter | solution.py:326
  1210.4 687.7 %reduce-scatter.22.cloned.1.call-done = f32[128,4096]{1,0:T(8,128)} async-done(((f32[2048,4096]{1,0:T(8,128)}), f32[128,4096]{1,0:T(8,128)}) %reduce-scatter.22.cloned.1.call-update) | async-done | bytes 2097168 | tf_op jit(solution)/shard_map/reduce_scatter | solution.py:328
  1900.8 688.1 %reduce-scatter.24.cloned.1.call-done = f32[128,4096]{1,0:T(8,128)} async-done(((f32[2048,4096]{1,0:T(8,128)}), f32[128,4096]{1,0:T(8,128)}) %reduce-scatter.24.cloned.1.call-update) | async-done | bytes 2097168 | tf_op jit(solution)/shard_map/reduce_scatter | solution.py:329
  2591.7 688.1 %reduce-scatter.26.cloned.1.call-done = f32[128,4096]{0,1:T(8,128)} async-done(((f32[2048,4096]{0,1:T(8,128)}), f32[128,4096]{0,1:T(8,128)}) %reduce-scatter.26.cloned.1.call-update) | async-done | bytes 2097168 | tf_op jit(solution)/shard_map/reduce_scatter | solution.py:330
  3283.7 19.1 all-reduce.16.cloned.1.call-done
  3305.0 78.1 %all-reduce.6 = (bf16[2048]{0:T(1024)(128)(2,1)S(1)}, bf16[2048]{0:T(1024)(128)(2,1)S(1)}) all-reduce(f32[2048]{0:T(1024)S(1)} %get-tuple-element.389, f32[2048]{0:T(1024)S(1)} %copy-done.28), channel_id=4, replica_groups=mesh['fsdp'=4,'ctx'=4,'tp'=2] {'fsdp','ctx'}, use_global_device_ids=true, to_apply=%region_23.24.clone | all-reduce | flops 4096 | bytes 24576
  3383.2 7.5 all-gather.2
  3391.4 9.6 all-gather.3
  3401.6 4.8 fusion.73
  3407.3 15.3 all_gather.75
  3423.5 53.1 %reduce-scatter.18.cloned.1.call-done = f32[128,256]{1,0:T(8,128)} async-done(((f32[2048,256]{1,0:T(8,128)}), f32[128,256]{1,0:T(8,128)}) %reduce-scatter.18.cloned.1.call-update) | async-done | bytes 131088 | tf_op jit(solution)/shard_map/reduce_scatter | solution.py:325
  3477.5 15.3 all_gather.76
  3493.6 10.2 all-gather.31.cloned.1.call-done
  3506.6 26.3 all-gather.33.cloned.1.call-done
  3535.7 79.7 %all-gather.35.cloned.1.call-done = bf16[512,4096]{1,0:T(8,128)(2,1)} async-done(((bf16[128,4096]{1,0:T(8,128)(2,1)}), bf16[512,4096]{1,0:T(8,128)(2,1)}) %all-gather.35.cloned.1.call-update) | async-done | bytes 4194320 | tf_op jit(solution)/shard_map/all_gather | solution.py:351
  3615.4 6.7 convert_element_type.235
  3622.1 74.9 %all-gather.37.cloned.1.call-done = bf16[512,4096]{1,0:T(8,128)(2,1)} async-done(((bf16[128,4096]{1,0:T(8,128)(2,1)}), bf16[512,4096]{1,0:T(8,128)(2,1)}) %all-gather.37.cloned.1.call-update) | async-done | bytes 4194320 | tf_op jit(solution)/shard_map/all_gather | solution.py:354
  3697.0 6.7 convert_element_type.237
  3703.7 74.0 %all-gather.39.cloned.1.call-done = bf16[512,4096]{0,1:T(8,128)(2,1)} async-done(((bf16[128,4096]{0,1:T(8,128)(2,1)}), bf16[512,4096]{0,1:T(8,128)(2,1)}) %all-gather.39.cloned.1.call-update) | async-done | bytes 4194320 | tf_op jit(solution)/shard_map/all_gather | solution.py:357
  3777.6 7.0 copy.73
  (228 shorter events, 79.9 us)
Async XLA Ops:
  7.2 2.9 copy-start.31
  7.2 3.2 copy-start.34
  7.2 3.5 copy-start.32
  7.2 13.0 copy-start.3
  7.2 32.0 all-gather.17.cloned.1.call-start
  8.0 59.8 %all-gather.21.cloned.1.call-start = ((), (), s32[]{:S(2)}) async-start(), calls=%async_computation.11 | async-start | bytes 1310720 | tf_op jit(solution)/shard_map/all_gather | solution.py:100
  8.7 113.6 %all-gather.19.cloned.1.call-start = ((), (), s32[]{:S(2)}) async-start(), calls=%async_computation.10 | async-start | bytes 5242880 | tf_op jit(solution)/shard_map/all_gather | solution.py:98
  9.4 167.3 %all-gather.23.cloned.1.call-start = ((), (), s32[]{:S(2)}) async-start(), calls=%async_computation.12 | async-start | bytes 5242880 | tf_op jit(solution)/shard_map/all_gather | solution.py:101
  10.0 191.2 %all-reduce.12.cloned.1.call-start = ((), (), s32[]{:S(2)}) async-start(), calls=%async_computation.13 | async-start | bytes 2097152 | tf_op jit(solution)/shard_map/psum | solution.py:188
  20.2 102.1 %copy-start.24 = (f32[4,1,512]{2,1,0:T(1,128)}, f32[4,1,512]{2,1,0:T(1,128)S(1)}, u32[]{:S(2)}) copy-start(f32[4,1,512]{2,1,0:T(1,128)S(1)} %convert_element_type.240) | copy-start | bytes 24580
  20.5 36.3 copy-start.29
  20.6 101.8 %copy-start.26 = (f32[256]{0:T(256)}, f32[256]{0:T(256)S(1)}, u32[]{:S(2)}) copy-start(f32[256]{0:T(256)S(1)} %fusion.101) | copy-start | bytes 3076
  20.9 105.5 %copy-start.18 = (f32[256,32]{0,1:T(8,128)}, f32[256,32]{0,1:T(8,128)S(1)}, u32[]{:S(2)}) copy-start(f32[256,32]{0,1:T(8,128)S(1)} %get-tuple-element.470) | copy-start | bytes 98308
  20.9 105.5 %copy-start.20 = (f32[256,32]{0,1:T(8,128)}, f32[256,32]{0,1:T(8,128)S(1)}, u32[]{:S(2)}) copy-start(f32[256,32]{0,1:T(8,128)S(1)} %get-tuple-element.471) | copy-start | bytes 98308
  126.3 1.2 copy-start.12
  132.8 6.1 copy-start
  147.1 6.5 copy-start
  156.9 24.5 copy-start.13
  181.4 180.2 %all-gather.25.cloned.1.call-start = ((), (), s32[]{:S(2)}) async-start(), calls=%async_computation.14 | async-start | bytes 20971520 | tf_op jit(solution)/shard_map/all_gather | solution.py:194
  182.0 339.1 %all-gather.27.cloned.1.call-start = ((), (), s32[]{:S(2)}) async-start(), calls=%async_computation.15 | async-start | bytes 20971520 | tf_op jit(solution)/shard_map/all_gather | solution.py:195
  182.8 0.8 copy-start.33
  182.8 497.8 %all-gather.29.cloned.1.call-start = ((), (), s32[]{:S(2)}) async-start(), calls=%async_computation.16 | async-start | bytes 20971520 | tf_op jit(solution)/shard_map/all_gather | solution.py:196
  183.5 558.0 %all-reduce.14.cloned.1.call-start = ((), (), s32[]{:S(2)}) async-start(), calls=%async_computation.17 | async-start | bytes 2097152 | tf_op jit(solution)/shard_map/psum | solution.py:217
  201.2 1.7 copy-start.4
  203.4 158.2 %copy-start.11 = (bf16[256,2048]{1,0:T(8,128)(2,1)}, bf16[256,2048]{1,0:T(8,128)(2,1)S(1)}, u32[]{:S(2)}) copy-start(bf16[256,2048]{1,0:T(8,128)(2,1)S(1)} %multiply_convert_fusion.2) | copy-start | bytes 3145732
  372.4 308.2 %copy-start.7 = (bf16[256,2048]{1,0:T(8,128)(2,1)S(1)}, bf16[256,2048]{1,0:T(8,128)(2,1)}, u32[]{:S(2)}) copy-start(bf16[256,2048]{1,0:T(8,128)(2,1)} %param.18) | copy-start | bytes 3145732
  721.7 158.2 %reduce-scatter.10.cloned.1.call-start = ((), (), s32[]{:S(2)}) async-start(), calls=%async_computation.18 | async-start | bytes 655360 | tf_op jit(solution)/shard_map/reduce_scatter | solution.py:290
  741.5 3.3 copy-start.5
  741.5 3.3 copy-start.8
  741.5 3.3 copy-start.10
  755.4 1.6 copy-start.16
  755.4 1.6 copy-start.22
  756.7 4.7 copy-start.1
  765.7 4.8 copy-start.2
  774.9 1.5 copy-start.16
  774.9 1.6 copy-start.22
  776.2 4.7 copy-start.1
  785.3 4.8 copy-start.2
  794.5 2.3 copy-start.14
  794.5 3.2 copy-start.19
  794.5 3.2 copy-start.21
  796.7 87.9 %reduce-scatter.12.cloned.1.call-start = ((), (), s32[]{:S(2)}) async-start(), calls=%async_computation.19 | async-start | bytes 655360 | tf_op jit(solution)/shard_map/reduce_scatter | solution.py:293
  797.7 1.2 copy-start.25
  797.7 1.2 copy-start.27
  797.7 228.2 %reduce-scatter.14.cloned.1.call-start = ((), (), s32[]{:S(2)}) async-start(), calls=%async_computation.20 | async-start | bytes 8912896 | tf_op jit(solution)/shard_map/reduce_scatter | solution.py:323
  803.6 1.2 copy-start.6
  803.6 1.6 copy-start.9
  803.6 404.9 %reduce-scatter.20.cloned.1.call-start = ((), (), s32[]{:S(2)}) async-start(), calls=%async_computation.24 | async-start | bytes 8912896 | tf_op jit(solution)/shard_map/reduce_scatter | solution.py:326
  812.0 1086.0 %reduce-scatter.22.cloned.1.call-start = ((), (), s32[]{:S(2)}) async-start(), calls=%async_computation.26 | async-start | bytes 35651584 | tf_op jit(solution)/shard_map/reduce_scatter | solution.py:328
  830.0 1758.9 %reduce-scatter.24.cloned.1.call-start = ((), (), s32[]{:S(2)}) async-start(), calls=%async_computation.28 | async-start | bytes 35651584 | tf_op jit(solution)/shard_map/reduce_scatter | solution.py:329
  847.7 2432.1 %reduce-scatter.26.cloned.1.call-start = ((), (), s32[]{:S(2)}) async-start(), calls=%async_computation.30 | async-start | bytes 35651584 | tf_op jit(solution)/shard_map/reduce_scatter | solution.py:330
  862.6 2440.2 %all-reduce.16.cloned.1.call-start = ((), (), s32[]{:S(2)}) async-start(), calls=%async_computation.32 | async-start | bytes 4194304 | tf_op jit(solution)/shard_map/psum | solution.py:204
  879.9 1.3 copy-start.17
  888.1 2.1 copy-start.23
  888.1 2518.3 %reduce-scatter.16.cloned.1.call-start = ((), (), s32[]{:S(2)}) async-start(), calls=%async_computation.22 | async-start | bytes 2228224 | tf_op jit(solution)/shard_map/reduce_scatter | solution.py:324
  890.1 2586.5 %reduce-scatter.18.cloned.1.call-start = ((), (), s32[]{:S(2)}) async-start(), calls=%async_computation.23 | async-start | bytes 2228224 | tf_op jit(solution)/shard_map/reduce_scatter | solution.py:325
  892.1 2611.7 %all-gather.31.cloned.1.call-start = ((), (), s32[]{:S(2)}) async-start(), calls=%async_computation.21 | async-start | bytes 1310720 | tf_op jit(solution)/shard_map/all_gather | solution.py:336
  1027.6 2505.3 %all-gather.33.cloned.1.call-start = ((), (), s32[]{:S(2)}) async-start(), calls=%async_computation.25 | async-start | bytes 1310720 | tf_op jit(solution)/shard_map/all_gather | solution.py:345
  1210.4 2405.1 %all-gather.35.cloned.1.call-start = ((), (), s32[]{:S(2)}) async-start(), calls=%async_computation.27 | async-start | bytes 5242880 | tf_op jit(solution)/shard_map/all_gather | solution.py:351
  1900.8 1796.2 %all-gather.37.cloned.1.call-start = ((), (), s32[]{:S(2)}) async-start(), calls=%async_computation.29 | async-start | bytes 5242880 | tf_op jit(solution)/shard_map/all_gather | solution.py:354
  2591.6 690.9 %copy-start.35 = (u32[32]{0:T(128)S(1)}, u32[32]{0:T(128)}, u32[]{:S(2)}) copy-start(u32[32]{0:T(128)} %constant.184) | copy-start | bytes 388
  2591.6 1186.0 %all-gather.39.cloned.1.call-start = ((), (), s32[]{:S(2)}) async-start(), calls=%async_computation.31 | async-start | bytes 5242880 | tf_op jit(solution)/shard_map/all_gather | solution.py:357
  3282.4 22.6 copy-start.28
  3282.4 119.2 %copy-start.30 = (f32[256]{0:T(256)S(1)}, f32[256]{0:T(256)}, u32[]{:S(2)}) copy-start(f32[256]{0:T(256)} %copy-done.29) | copy-start | bytes 3076
  (1 other events, 0.8 us)
Sparse Core Ops, SparseCore 0:
  9.9 29.3 all-gather.16
  41.1 26.6 all-gather.20
  69.6 52.6 all-gather.18
  124.0 52.6 all-gather.22
  181.6 19.5 all-reduce.11
  203.0 158.5 all-gather.24
  363.6 157.4 all-gather.26
  523.1 157.4 all-gather.28
  721.9 19.5 all-reduce.13
  796.8 22.8 reduce-scatter.9
  822.6 19.9 reduce-scatter.11
  845.3 180.5 reduce-scatter.13
  1028.7 179.8 reduce-scatter.19
  1210.8 687.2 reduce-scatter.21
  1900.3 688.5 reduce-scatter.23
  2591.1 688.6 reduce-scatter.25
  3282.5 20.1 all-reduce.15
  3305.6 85.3 reduce-scatter.15
  3393.9 82.6 reduce-scatter.17
  3478.7 25.0 all-gather.30
  3505.5 27.4 all-gather.32
  3535.1 80.2 all-gather.34
  3617.7 79.2 all-gather.36
  3698.5 79.0 all-gather.38
where the time goes:
time: 3800 us; the launch traced here: 3790 us
  waiting for transfers between devices  3290 us (87%)
  matrix products  223 us (6%)
  blocking collectives  175 us (5%)
  other arithmetic  66.3 us (2%)
    reduce_scatter x1, waiting for transfers between devices, shards(): lax.psum_scatter(weight_grads[8], ('fsdp', 'ctx'), scatter_dimension=0, t...  688 us
    reduce_scatter x1, waiting for transfers between devices, shards(): lax.psum_scatter(weight_grads[7], ('fsdp', 'ctx'), scatter_dimension=0, t...  688 us
    reduce_scatter x1, waiting for transfers between devices, shards(): lax.psum_scatter(weight_grads[6], ('fsdp', 'ctx'), scatter_dimension=0, t...  688 us
    reduce_scatter x1, waiting for transfers between devices, shards(): lax.psum_scatter(weight_grads[4], ('fsdp', 'ctx'), scatter_dimension=0, t...  181 us
    all_gather x1, waiting for transfers between devices, shards(): lax.all_gather(gate_weight, 'fsdp', axis=0, tiled=True)  158 us
    all_gather x1, waiting for transfers between devices, shards(): lax.all_gather(up_weight, 'fsdp', axis=0, tiled=True)  149 us
    all_gather x1, waiting for transfers between devices, shards(): lax.all_gather(down_weight, 'fsdp', axis=0, tiled=True)  147 us
    reduce_scatter x1, waiting for transfers between devices, shards(): lax.psum_scatter(weight_grads[1], ('fsdp', 'ctx'), scatter_dimension=0, t...  134 us
  transfers between devices with their start and end apart: 24, of which 21 were waited for; matrix products, arithmetic and copies ran while one was open for 5% of the time, Pallas kernels for 0%

commit v1 on v0

--- a/solution.py
+++ b/solution.py
@@ -68,7 +68,324 @@
     )
 
 
-def shards(
+def swap(array, axis, distance):
+    size = lax.axis_size(axis)
+    return lax.ppermute(array, axis, [(i, i ^ distance) for i in range(size)])
+
+
+def line_sum(part, axis):
+    size = lax.axis_size(axis)
+    index = lax.axis_index(axis)
+    middle = size // 2
+    total = part
+    for step in range(middle - 1):
+        came = lax.ppermute(total, axis, [(step, step + 1), (size - 1 - step, size - 2 - step)])
+        total = add_low(total, came)
+    if size > 1:
+        came = lax.ppermute(total, axis, [(middle - 1, middle), (middle, middle - 1)])
+        total = add_low(total, came)
+    for step in range(middle - 2, -1, -1):
+        came = lax.ppermute(total, axis, [(step + 1, step), (size - 2 - step, size - 1 - step)])
+        receives = (index == step) | (index == size - 1 - step)
+        total = jnp.where(receives, came, total)
+    return total
+
+
+def add_low(left, right):
+    return (left.astype(jnp.float32) + right.astype(jnp.float32)).astype(jnp.bfloat16)
+
+
+def gather_tokens(own):
+    blocks = []
+    for k in range(lax.axis_size("fsdp")):
+        block = swap(own, "fsdp", k) if k else own
+        blocks += [block, swap(block, "tp", 1)]
+    return jnp.concatenate(blocks, axis=0)
+
+
+def scatter_tokens(partial):
+    count = lax.axis_size("fsdp")
+    blocks = partial.reshape(count, 2, -1, partial.shape[-1])
+    mine = [add_low(blocks[k, 0], swap(blocks[k, 1], "tp", 1)) for k in range(count)]
+    total = mine[0].astype(jnp.float32)
+    for k in range(1, count):
+        total = total + swap(mine[k], "fsdp", k).astype(jnp.float32)
+    return total
+
+
+def send_columns(weight, width):
+    count = lax.axis_size("fsdp")
+    index = lax.axis_index("fsdp")
+    rows = weight.shape[0]
+    whole = jnp.zeros((rows * count, width), weight.dtype)
+    for k in range(count):
+        piece = lax.dynamic_slice_in_dim(weight, (index ^ k) * width, width, 1)
+        if k:
+            piece = swap(piece, "fsdp", k)
+        whole = lax.dynamic_update_slice_in_dim(whole, piece, (index ^ k) * rows, 0)
+    return whole
+
+
+def return_rows(grad, out, column_of):
+    count = lax.axis_size("fsdp")
+    index = lax.axis_index("fsdp")
+    rows = grad.shape[0] // count
+    pieces = []
+    for k in range(count):
+        piece = lax.dynamic_slice_in_dim(grad, (index ^ k) * rows, rows, 0)
+        if k:
+            piece = swap(piece, "fsdp", k)
+        pieces.append(line_sum(piece, "ctx"))
+    return pieces
+
+
+def fill_columns(pieces, first, width):
+    count = len(pieces)
+    index = lax.axis_index("fsdp")
+    out = jnp.zeros((pieces[0].shape[0], count * width), jnp.float32)
+    for k in range(count):
+        part = pieces[k][:, first : first + width].astype(jnp.float32)
+        out = lax.dynamic_update_slice_in_dim(out, part, (index ^ k) * width, 1)
+    return out
+
+
+def sum_all(vector):
+    count = lax.axis_size("fsdp")
+    index = lax.axis_index("fsdp")
+    width = vector.shape[0] // count
+    both = vector + swap(vector, "tp", 1)
+    total = lax.dynamic_slice_in_dim(both, index * width, width, 0)
+    for k in range(1, count):
+        total = total + swap(lax.dynamic_slice_in_dim(both, (index ^ k) * width, width, 0), "fsdp", k)
+    distance = 1
+    while distance < lax.axis_size("ctx"):
+        total = total + swap(total, "ctx", distance)
+        distance *= 2
+    return total
+
+
+def gather_gain(gain):
+    count = lax.axis_size("fsdp")
+    index = lax.axis_index("fsdp")
+    width = gain.shape[0]
+    whole = jnp.zeros((count * width,), gain.dtype)
+    for k in range(count):
+        piece = swap(gain, "fsdp", k) if k else gain
+        whole = lax.dynamic_update_slice_in_dim(whole, piece, (index ^ k) * width, 0)
+    return whole.astype(jnp.float32)
+
+
+def split_heads(
+    hidden_in,
+    out_cotangent,
+    norm1_gain,
+    q_weight,
+    key_projection_weight,
+    value_projection_weight,
+    o_weight,
+    norm2_gain,
+    gate_weight,
+    up_weight,
+    down_weight,
+    seq_lengths,
+    span_order,
+):
+    packs = lax.axis_size("fsdp")
+    cycle = lax.axis_size("ctx")
+    core = lax.axis_index("tp")
+    here = lax.axis_index("ctx")
+    rows = hidden_in.shape[0]
+    half = rows // 2
+    q_width = q_weight.shape[1] // packs
+    k_width = key_projection_weight.shape[1] // packs
+    ff_width = gate_weight.shape[1] // packs
+    groups = q_width // k_width
+    kv_heads = k_width // HEAD_SIZE
+    score_scale = 1.0 / math.sqrt(HEAD_SIZE)
+
+    own_in = lax.dynamic_slice_in_dim(hidden_in, core * half, half, 0)
+    own_cot = lax.dynamic_slice_in_dim(out_cotangent, core * half, half, 0)
+    all_in = gather_tokens(own_in)
+    gain_one = gather_gain(norm1_gain)
+    gain_two = gather_gain(norm2_gain)
+    wqkv = send_columns_joined((q_weight, key_projection_weight, value_projection_weight))
+    wo = send_columns(o_weight, q_width)
+    wg = send_columns(gate_weight, ff_width)
+    wu = send_columns(up_weight, ff_width)
+    wd = send_columns(down_weight, ff_width)
+    all_cot = gather_tokens(own_cot)
+
+    order_len = span_order.shape[1]
+    meta = jnp.concatenate([span_order[0], seq_lengths[0]])
+    places, segments, offsets = [], [], []
+    within = jnp.arange(half, dtype=jnp.int32)
+    for k in range(packs):
+        meta_k = swap(meta, "fsdp", k) if k else meta
+        order_row = meta_k[:order_len]
+        length_row = meta_k[order_len:]
+        ends = jnp.cumsum(length_row, dtype=jnp.int32)
+        for j in range(cycle):
+            first = lax.dynamic_index_in_dim(order_row, here ^ j, 0, keepdims=False)
+            for h in range(2):
+                section = jnp.where((core ^ h) == 0, first, 2 * cycle - 1 - first)
+                place = section * half + within
+                passed = place[:, None] >= ends[None, :]
+                places.append(place)
+                segments.append(jnp.sum(passed.astype(jnp.int32), axis=1, dtype=jnp.int32))
+                offsets.append(
+                    place
+                    - jnp.sum(jnp.where(passed, length_row[None, :], 0), axis=1, dtype=jnp.int32)
+                )
+    places = jnp.stack(places).reshape(packs, cycle * rows)
+    segments = jnp.stack(segments).reshape(packs, cycle * rows)
+    offsets = jnp.stack(offsets).reshape(packs, cycle * rows)[:, :rows].reshape(-1)
+    visible = (
+        (places[:, :rows, None] >= places[:, None, :])
+        & (segments[:, :rows, None] == segments[:, None, :])
+    )[:, None, None]
+
+    tokens = packs * rows
+    normed_low = normalize(all_in.astype(jnp.float32), gain_one).astype(jnp.bfloat16)
+    qkv = jnp.dot(normed_low, wqkv, preferred_element_type=jnp.float32)
+    rope = lambda lin: rotary_embedding(lin.reshape(tokens, -1, HEAD_SIZE), offsets)
+    q_rot = (
+        rope(qkv[:, :q_width])
+        .astype(jnp.bfloat16)
+        .reshape(packs, rows, kv_heads, groups, HEAD_SIZE)
+    )
+    k_rot = rope(qkv[:, q_width : q_width + k_width]).astype(jnp.bfloat16).reshape(tokens, k_width)
+    v_low = qkv[:, q_width + k_width :].astype(jnp.bfloat16)
+    kv_own = jnp.concatenate([k_rot, v_low], axis=1)
+    kv_all = jnp.stack([swap(kv_own, "ctx", j) if j else kv_own for j in range(cycle)])
+    kv_all = kv_all.reshape(cycle, packs, rows, 2, kv_heads, HEAD_SIZE)
+    kv_all = jnp.transpose(kv_all, (3, 1, 0, 2, 4, 5)).reshape(
+        2, packs, cycle * rows, kv_heads, HEAD_SIZE
+    )
+    k_all, v_all = kv_all[0], kv_all[1]
+    scores = (
+        jnp.einsum("pqkgd,pskd->pkgqs", q_rot, k_all, preferred_element_type=jnp.float32)
+        * score_scale
+    )
+    scores = jnp.where(visible, scores, -1e30)
+    row_max = jnp.max(scores, axis=-1, keepdims=True)
+    weights = jnp.where(visible, jnp.exp(scores - row_max), 0.0)
+    totals = jnp.sum(weights, axis=-1, keepdims=True)
+    probs = weights / totals
+    probs_low = probs.astype(jnp.bfloat16)
+    mixed = jnp.einsum("pkgqs,pskd->pqkgd", probs_low, v_all, preferred_element_type=jnp.float32)
+    attn_low = mixed.reshape(tokens, q_width).astype(jnp.bfloat16)
+    branch = scatter_tokens(contract_last(attn_low, wo).astype(jnp.bfloat16))
+    middle = own_in.astype(jnp.float32) + branch
+
+    normed_two = normalize(middle, gain_two)
+    normed_two_low = gather_tokens(normed_two.astype(jnp.bfloat16))
+    gate_val = jnp.dot(normed_two_low, wg, preferred_element_type=jnp.float32)
+    up_val = jnp.dot(normed_two_low, wu, preferred_element_type=jnp.float32)
+    hidden = swiglu(gate_val, up_val).astype(jnp.bfloat16)
+    down_pieces = return_rows(contract_first(all_cot, hidden).astype(jnp.bfloat16), None, None)
+    d_hidden = jnp.dot(all_cot, wd, preferred_element_type=jnp.float32)
+    _, swiglu_back = jax.vjp(swiglu, gate_val, up_val)
+    d_gate, d_up = swiglu_back(d_hidden)
+    d_gate_low = d_gate.astype(jnp.bfloat16)
+    d_up_low = d_up.astype(jnp.bfloat16)
+    gate_pieces = return_rows(
+        contract_first(normed_two_low, d_gate_low).astype(jnp.bfloat16), None, None
+    )
+    up_pieces = return_rows(
+        contract_first(normed_two_low, d_up_low).astype(jnp.bfloat16), None, None
+    )
+    ffn_out = scatter_tokens(contract_last(hidden, wd).astype(jnp.bfloat16))
+    result = (middle + ffn_out).astype(jnp.bfloat16)
+    d_normed_two = scatter_tokens(
+        (contract_last(d_gate_low, wg) + contract_last(d_up_low, wu)).astype(jnp.bfloat16)
+    )
+    _, norm_two_back = jax.vjp(normalize, middle, gain_two)
+    d_middle_norm, d_gain_two = norm_two_back(d_normed_two)
+    d_middle = own_cot.astype(jnp.float32) + d_middle_norm
+
+    d_branch = gather_tokens(d_middle.astype(jnp.bfloat16))
+    d_wo = contract_first(d_branch, attn_low).astype(jnp.bfloat16)
+    d_attn = (
+        jnp.dot(d_branch, wo, preferred_element_type=jnp.float32)
+        .astype(jnp.bfloat16)
+        .reshape(packs, rows, kv_heads, groups, HEAD_SIZE)
+    )
+    row_delta = jnp.einsum("pqkgd,pqkgd->pkgq", d_attn.astype(jnp.float32), mixed)
+    d_values = jnp.einsum("pkgqs,pqkgd->pskd", probs_low, d_attn, preferred_element_type=jnp.float32)
+    d_probs = jnp.einsum("pqkgd,pskd->pkgqs", d_attn, v_all, preferred_element_type=jnp.float32)
+    d_scores = (probs * (d_probs - row_delta[..., None])).astype(jnp.bfloat16)
+    d_q_rot = (
+        jnp.einsum("pkgqs,pskd->pqkgd", d_scores, k_all, preferred_element_type=jnp.float32)
+        * score_scale
+    )
+    d_keys = (
+        jnp.einsum("pkgqs,pqkgd->pskd", d_scores, q_rot, preferred_element_type=jnp.float32)
+        * score_scale
+    )
+    d_kv = jnp.stack([d_keys, d_values]).astype(jnp.bfloat16)
+    d_kv = d_kv.reshape(2, packs, cycle, rows, k_width)
+    d_kv_own = d_kv[:, :, 0].astype(jnp.float32)
+    for j in range(1, cycle):
+        d_kv_own = d_kv_own + swap(d_kv[:, :, j], "ctx", j).astype(jnp.float32)
+    d_k_rot = d_kv_own[0].reshape(tokens, kv_heads, HEAD_SIZE)
+    d_v_low = d_kv_own[1].reshape(tokens, k_width).astype(jnp.bfloat16)
+    turn = lambda grad: rotary_embedding(grad, -offsets)
+    d_q_low = turn(d_q_rot.reshape(tokens, -1, HEAD_SIZE)).reshape(tokens, q_width)
+    d_k_low = turn(d_k_rot).reshape(tokens, k_width)
+    d_qkv = jnp.concatenate(
+        [d_q_low.astype(jnp.bfloat16), d_k_low.astype(jnp.bfloat16), d_v_low], axis=1
+    )
+    d_wqkv = contract_first(normed_low, d_qkv).astype(jnp.bfloat16)
+    qkvo_pieces = return_rows(jnp.concatenate([d_wo, d_wqkv], axis=1), None, None)
+    d_normed_one = scatter_tokens(contract_last(d_qkv, wqkv).astype(jnp.bfloat16))
+    _, norm_one_back = jax.vjp(normalize, own_in.astype(jnp.float32), gain_one)
+    d_inputs_norm, d_gain_one = norm_one_back(d_normed_one)
+    in_grad = (d_middle + d_inputs_norm).astype(jnp.bfloat16)
+
+    return (
+        both_halves(result),
+        both_halves(in_grad),
+        sum_all(d_gain_one),
+        fill_columns(qkvo_pieces, q_width, q_width),
+        fill_columns(qkvo_pieces, 2 * q_width, k_width),
+        fill_columns(qkvo_pieces, 2 * q_width + k_width, k_width),
+        fill_columns(qkvo_pieces, 0, q_width),
+        sum_all(d_gain_two),
+        fill_columns(gate_pieces, 0, ff_width),
+        fill_columns(up_pieces, 0, ff_width),
+        fill_columns(down_pieces, 0, ff_width),
+    )
+
+
+def both_halves(own):
+    core = lax.axis_index("tp")
+    other = swap(own, "tp", 1)
+    first = jnp.where(core == 0, own, other)
+    second = jnp.where(core == 0, other, own)
+    return jnp.concatenate([first, second], axis=0)
+
+
+def send_columns_joined(weights):
+    count = lax.axis_size("fsdp")
+    index = lax.axis_index("fsdp")
+    rows = weights[0].shape[0]
+    widths = [weight.shape[1] // count for weight in weights]
+    whole = jnp.zeros((rows * count, sum(widths)), weights[0].dtype)
+    for k in range(count):
+        piece = jnp.concatenate(
+            [
+                lax.dynamic_slice_in_dim(weight, (index ^ k) * width, width, 1)
+                for weight, width in zip(weights, widths)
+            ],
+            axis=1,
+        )
+        if k:
+            piece = swap(piece, "fsdp", k)
+        whole = lax.dynamic_update_slice_in_dim(whole, piece, (index ^ k) * rows, 0)
+    return whole
+
+
+def gathered_weights(
     hidden_in,
     out_cotangent,
     norm1_gain,
@@ -389,8 +706,10 @@
         P("fsdp", None),
         P("fsdp", None),
     )
+    plane = mesh.shape["fsdp"] * mesh.shape["tp"]
+    splits = mesh.shape["tp"] == 2 and KEY_VALUE_HEADS % plane == 0
     return jax.shard_map(
-        shards,
+        split_heads if splits else gathered_weights,
         mesh=mesh,
         in_specs=placed,
         out_specs=(

time: 3800 us -> 1420 us (0.37)
  waiting for transfers between devices: 3290 us -> 681 us
  starting transfers between devices: 1.65 us -> 291 us
  blocking collectives: 175 us -> 0 us
  local copies, waits for them, and re-layouts: 22.6 us -> 165 us
  matrix products: 223 us -> 120 us
  other arithmetic: 66.3 us -> 113 us
    reduce_scatter x9 -> x0, waiting for transfers between devices: 2430 us -> none  [the longest x1 688 us: shards(): lax.psum_scatter(weight_grads[8], ('fsdp', 'ctx'), scatter_dimension=0, t...]
    all_gather x12 -> x0, waiting for transfers between devices: 802 us -> none  [the longest x1 158 us: shards(): lax.all_gather(gate_weight, 'fsdp', axis=0, tiled=True)]
    ppermute x0 -> x160, waiting for transfers between devices: none -> 681 us  [the longest x112 350 us: swap(): return lax.ppermute(array, axis, [(i, i ^ distance) for i in range(size)])]
    ppermute x0 -> x160, starting transfers between devices: none -> 291 us  [the longest x112 197 us: swap(): return lax.ppermute(array, axis, [(i, i ^ distance) for i in range(size)])]
    all_gather x8 -> x0, blocking collectives: 96.5 us -> none  [the longest x1 15.6 us: shards(): value_row_block = lax.all_gather(v_low, 'ctx', axis=0, tiled=True)]
    unnamed x1 -> x0, blocking collectives: 78.1 us -> none
    psum x3 -> x0, waiting for transfers between devices: 48.3 us -> none  [the longest x1 19.7 us: shards(): lax.psum((contract_last(d_gate_low, wg_full) + contract_last(d_up_low, wu...]
    dynamic_update_slice x0 -> x39, local copies, waits for them, and re-layouts: none -> 42.4 us  [the longest x16 23.4 us: fill_columns(): out = lax.dynamic_update_slice_in_dim(out, part, (index ^ k) * width, 1)]
  transfers between devices with their start and end apart: 24 -> 160, of which waited for: 21 -> 59; matrix products, arithmetic and copies ran while one was open for 5% -> 21% of each run, Pallas kernels for 0% -> 0%
where the time goes in v1:
time: 1420 us; the launch traced here: 1400 us
  waiting for transfers between devices  681 us (48%)
  starting transfers between devices  291 us (20%)
  local copies, waits for them, and re-layouts  165 us (12%)
  matrix products  120 us (8%)
  other arithmetic  113 us (8%)
  between operations  35.1 us (2%)
    ppermute x112, waiting for transfers between devices, swap(): return lax.ppermute(array, axis, [(i, i ^ distance) for i in range(size)])  350 us
    ppermute x16, waiting for transfers between devices, line_sum(): lax.ppermute(total, axis, [(step + 1, step), (size - 2 - step, size - 1 -...  236 us
    ppermute x112, starting transfers between devices, swap(): return lax.ppermute(array, axis, [(i, i ^ distance) for i in range(size)])  197 us
    ppermute x16, waiting for transfers between devices, line_sum(): lax.ppermute(total, axis, [(step, step + 1), (size - 1 - step, size - 2 -...  95.2 us
    ppermute x16, starting transfers between devices, line_sum(): lax.ppermute(total, axis, [(step, step + 1), (size - 1 - step, size - 2 -...  56.6 us
    convert_element_type x36, other arithmetic, add_low(): (left.astype(jnp.float32) + right.astype(jnp.float32)).astype(jnp.bfloat16)  48.1 us
    unnamed x218, local copies, waits for them, and re-layouts  34 us
    dot_general x5, matrix products, contract_last(): lax.dot_general(left, right, (((1,), (1,)), ((), ())), preferred_element_...  31 us
  transfers between devices with their start and end apart: 160, of which 59 were waited for; matrix products, arithmetic and copies ran while one was open for 21% of the time, Pallas kernels for 0%

profile of v1, /device:TPU:0, one launch (start us, length us, event | category | flops | bytes accessed | tf_op | source)
XLA Modules:
  0.0 1404.9 jit_solution(8254491995825875322)
XLA Ops:
  105.1 10.5 collective-permute-done.21
  124.5 10.7 collective-permute-done.12
  141.7 11.3 collective-permute-done.3
  162.5 12.2 collective-permute-done.59
  203.5 8.0 collective-permute-done.17
  234.0 6.3 bitcast_convert_fusion
  252.3 7.0 fusion.188
  265.4 10.3 collective-permute-done.26
  278.9 41.7 %collective-permute-done.43 = bf16[512,1024]{1,0:T(8,128)(2,1)S(1)} collective-permute-done((bf16[512,1024]{1,0:T(8,128)(2,1)S(1)}, bf16[512,1024]{1,0:T(8,128)(2,1)S(1)}, u32[]{:S(2)}, u32[]{:S(2)}) %collective-permute-start.43) | collective-permute-done | bytes 1048608 | tf_op jit(solution)/shard_map/ppermute | solution.py:73
  324.0 41.0 %collective-permute-done.40 = bf16[512,1024]{1,0:T(8,128)(2,1)S(1)} collective-permute-done((bf16[512,1024]{1,0:T(8,128)(2,1)S(1)}, bf16[512,1024]{1,0:T(8,128)(2,1)S(1)}, u32[]{:S(2)}, u32[]{:S(2)}) %collective-permute-start.40) | collective-permute-done | bytes 1048608 | tf_op jit(solution)/shard_map/ppermute | solution.py:73
  368.7 18.8 %collective-permute-done.35 = bf16[128,2048]{1,0:T(8,128)(2,1)S(1)} collective-permute-done((bf16[128,2048]{1,0:T(8,128)(2,1)S(1)}, bf16[128,2048]{1,0:T(8,128)(2,1)S(1)}, u32[]{:S(2)}, u32[]{:S(2)}) %collective-permute-start.35) | collective-permute-done | bytes 524320 | tf_op jit(solution)/shard_map/ppermute | solution.py:73
  390.2 4.5 fusion.187
  394.7 10.1 fusion.19
  406.1 6.8 fusion.189
  412.9 7.0 convolution_convert_fusion.3
  419.9 7.1 convolution_convert_fusion.5
  427.0 5.0 convolution_convert_fusion.2
  432.0 5.1 convolution_convert_fusion.4
  437.1 11.8 add_convert_fusion
  467.3 9.3 collective-permute-done.69
  478.0 9.1 collective-permute-done.67
  496.2 9.9 collective-permute-done.130
  510.0 18.2 %collective-permute-done.113 = f32[512]{0:T(512)S(1)} collective-permute-done((f32[512]{0:T(512)S(1)}, f32[512]{0:T(512)S(1)}, u32[]{:S(2)}, u32[]{:S(2)}) %collective-permute-start.113) | collective-permute-done | bytes 2080 | tf_op jit(solution)/shard_map/ppermute | solution.py:73
  537.4 6.5 collective-permute-done.75
  559.4 12.3 fusion.1
  571.7 9.6 fusion.45
  581.3 4.5 fusion.42
  596.6 4.6 convolution_convert_fusion.7
  603.9 7.2 collective-permute-done.133
  611.0 5.7 collective-permute-start.119
  621.3 12.8 collective-permute-done.141
  634.0 4.4 collective-permute-start.123
  640.7 14.0 collective-permute-done.148
  692.1 13.3 collective-permute-done.134
  713.8 14.2 %collective-permute-done.138 = bf16[512,1024]{1,0:T(8,128)(2,1)S(1)} collective-permute-done((bf16[512,1024]{1,0:T(8,128)(2,1)}, bf16[512,1024]{1,0:T(8,128)(2,1)S(1)}, u32[]{:S(2)}, u32[]{:S(2)}) %collective-permute-start.138) | collective-permute-done | bytes 1048608 | tf_op jit(solution)/shard_map/ppermute | solution.py:82
  727.9 5.3 collective-permute-start.157
  735.8 14.6 %collective-permute-done.142 = bf16[512,1024]{1,0:T(8,128)(2,1)S(1)} collective-permute-done((bf16[512,1024]{1,0:T(8,128)(2,1)}, bf16[512,1024]{1,0:T(8,128)(2,1)S(1)}, u32[]{:S(2)}, u32[]{:S(2)}) %collective-permute-start.142) | collective-permute-done | bytes 1048608 | tf_op jit(solution)/shard_map/ppermute | solution.py:82
  758.2 14.6 %collective-permute-done.149 = bf16[512,1024]{1,0:T(8,128)(2,1)S(1)} collective-permute-done((bf16[512,1024]{1,0:T(8,128)(2,1)}, bf16[512,1024]{1,0:T(8,128)(2,1)S(1)}, u32[]{:S(2)}, u32[]{:S(2)}) %collective-permute-start.149) | collective-permute-done | bytes 1048608 | tf_op jit(solution)/shard_map/ppermute | solution.py:82
  777.9 17.3 %collective-permute-done.153 = bf16[512,1024]{1,0:T(8,128)(2,1)S(1)} collective-permute-done((bf16[512,1024]{1,0:T(8,128)(2,1)S(1)}, bf16[512,1024]{1,0:T(8,128)(2,1)S(1)}, u32[]{:S(2)}, u32[]{:S(2)}) %collective-permute-start.153) | collective-permute-done | bytes 1048608 | tf_op jit(solution)/shard_map/ppermute | solution.py:82
  797.1 29.3 %collective-permute-done.79 = bf16[2,4,256,64]{2,1,3,0:T(4,128)(2,1)S(1)} collective-permute-done((bf16[2,4,256,64]{2,1,3,0:T(4,128)(2,1)S(1)}, bf16[2,4,256,64]{2,1,3,0:T(4,128)(2,1)S(1)}, u32[]{:S(2)}, u32[]{:S(2)}) %collective-permute-start.79) | collective-permute-done | bytes 262176 | tf_op jit(solution)/shard_map/ppermute | solution.py:73
  846.9 4.7 collective-permute-start.94
  858.5 6.9 collective-permute-done.94
  870.8 11.5 collective-permute-done.132
  885.4 17.7 %collective-permute-done.147 = bf16[512,1024]{1,0:T(8,128)(2,1)S(1)} collective-permute-done((bf16[512,1024]{1,0:T(8,128)(2,1)S(1)}, bf16[512,1024]{1,0:T(8,128)(2,1)S(1)}, u32[]{:S(2)}, u32[]{:S(2)}) %collective-permute-start.147) | collective-permute-done | bytes 1048608 | tf_op jit(solution)/shard_map/ppermute | solution.py:88
  921.4 8.9 collective-permute-done.86
  930.3 10.8 collective-permute-done.84
  948.0 8.1 collective-permute-done.54
  959.5 7.7 collective-permute-done.90
  970.9 88.5 %collective-permute-start.92 = (f32[512]{0:T(512)S(1)}, f32[512]{0:T(512)S(1)}, u32[]{:S(2)}, u32[]{:S(2)}) collective-permute-start(f32[512]{0:T(512)S(1)} %add_add_fusion.3), channel_id=1, source_target_pairs={{0,2},{2,0},{4,6},{6,4},{1,3},{3,1},{5,7},{7,5},{8,10},{10,8},{12,... | collective-permute-start | bytes 6152 | tf_op jit(solution)/shard_map/ppermute | solution.py:73
  1061.7 7.7 collective-permute-start.98
  1073.8 6.2 collective-permute-start.93
  1082.6 25.9 %collective-permute-done.93 = f32[512]{0:T(512)S(1)} collective-permute-done((f32[512]{0:T(512)S(1)}, f32[512]{0:T(512)S(1)}, u32[]{:S(2)}, u32[]{:S(2)}) %collective-permute-start.93) | collective-permute-done | bytes 2080 | tf_op jit(solution)/shard_map/ppermute | solution.py:73
  1123.0 13.5 collective-permute-done.121
  1138.2 20.7 %collective-permute-done.125 = bf16[512,1024]{1,0:T(8,128)(2,1)S(1)} collective-permute-done((bf16[512,1024]{1,0:T(8,128)(2,1)S(1)}, bf16[512,1024]{1,0:T(8,128)(2,1)S(1)}, u32[]{:S(2)}, u32[]{:S(2)}) %collective-permute-start.125) | collective-permute-done | bytes 1048608 | tf_op jit(solution)/shard_map/ppermute | solution.py:88
  1160.7 20.7 %collective-permute-done.129 = bf16[512,1024]{1,0:T(8,128)(2,1)S(1)} collective-permute-done((bf16[512,1024]{1,0:T(8,128)(2,1)S(1)}, bf16[512,1024]{1,0:T(8,128)(2,1)S(1)}, u32[]{:S(2)}, u32[]{:S(2)}) %collective-permute-start.129) | collective-permute-done | bytes 1048608 | tf_op jit(solution)/shard_map/ppermute | solution.py:88
  1183.4 20.5 %collective-permute-done.136 = bf16[512,1024]{1,0:T(8,128)(2,1)S(1)} collective-permute-done((bf16[512,1024]{1,0:T(8,128)(2,1)S(1)}, bf16[512,1024]{1,0:T(8,128)(2,1)S(1)}, u32[]{:S(2)}, u32[]{:S(2)}) %collective-permute-start.136) | collective-permute-done | bytes 1048608 | tf_op jit(solution)/shard_map/ppermute | solution.py:88
  1205.6 20.7 %collective-permute-done.140 = bf16[512,1024]{1,0:T(8,128)(2,1)S(1)} collective-permute-done((bf16[512,1024]{1,0:T(8,128)(2,1)S(1)}, bf16[512,1024]{1,0:T(8,128)(2,1)S(1)}, u32[]{:S(2)}, u32[]{:S(2)}) %collective-permute-start.140) | collective-permute-done | bytes 1048608 | tf_op jit(solution)/shard_map/ppermute | solution.py:88
  1228.1 20.7 %collective-permute-done.144 = bf16[512,1024]{1,0:T(8,128)(2,1)S(1)} collective-permute-done((bf16[512,1024]{1,0:T(8,128)(2,1)S(1)}, bf16[512,1024]{1,0:T(8,128)(2,1)S(1)}, u32[]{:S(2)}, u32[]{:S(2)}) %collective-permute-start.144) | collective-permute-done | bytes 1048608 | tf_op jit(solution)/shard_map/ppermute | solution.py:88
  1250.0 21.3 %collective-permute-done.151 = bf16[512,1024]{1,0:T(8,128)(2,1)S(1)} collective-permute-done((bf16[512,1024]{1,0:T(8,128)(2,1)S(1)}, bf16[512,1024]{1,0:T(8,128)(2,1)S(1)}, u32[]{:S(2)}, u32[]{:S(2)}) %collective-permute-start.151) | collective-permute-done | bytes 1048608 | tf_op jit(solution)/shard_map/ppermute | solution.py:88
  1274.5 19.3 %collective-permute-done.155 = bf16[512,1024]{1,0:T(8,128)(2,1)S(1)} collective-permute-done((bf16[512,1024]{1,0:T(8,128)(2,1)S(1)}, bf16[512,1024]{1,0:T(8,128)(2,1)S(1)}, u32[]{:S(2)}, u32[]{:S(2)}) %collective-permute-start.155) | collective-permute-done | bytes 1048608 | tf_op jit(solution)/shard_map/ppermute | solution.py:88
  1297.0 19.3 %collective-permute-done.159 = bf16[512,1024]{1,0:T(8,128)(2,1)S(1)} collective-permute-done((bf16[512,1024]{1,0:T(8,128)(2,1)S(1)}, bf16[512,1024]{1,0:T(8,128)(2,1)S(1)}, u32[]{:S(2)}, u32[]{:S(2)}) %collective-permute-start.159) | collective-permute-done | bytes 1048608 | tf_op jit(solution)/shard_map/ppermute | solution.py:88
  1318.0 8.0 collective-permute-done.96
  1349.7 12.2 collective-permute-done.104
  1364.1 6.6 collective-permute-done.108
  (819 shorter events, 489.8 us)
Async XLA Ops:
  0.7 91.2 %collective-permute-start.7 = (bf16[512]{0:T(512)(128)(2,1)}, bf16[512]{0:T(512)(128)(2,1)S(1)}, u32[]{:S(2)}, u32[]{:S(2)}) collective-permute-start(bf16[512]{0:T(512)(128)(2,1)} %param.15), channel_id=1, source_target_pairs={{0,8},{8,0},{16,24},{24,16},{1,9},{9,1},{17,25},{25,17},{2,10},{10... | collective-permute-start | bytes 3080 | tf_op jit(solution)/shard_map/ppermute | solution.py:73
  3.7 88.8 %collective-permute-start.8 = (bf16[512]{0:T(512)(128)(2,1)}, bf16[512]{0:T(512)(128)(2,1)S(1)}, u32[]{:S(2)}, u32[]{:S(2)}) collective-permute-start(bf16[512]{0:T(512)(128)(2,1)} %param.15), channel_id=1, source_target_pairs={{0,16},{8,24},{16,0},{24,8},{1,17},{9,25},{17,1},{25,9},{2,18},{10... | collective-permute-start | bytes 3080 | tf_op jit(solution)/shard_map/ppermute | solution.py:73
  5.2 88.9 %collective-permute-start.9 = (bf16[512]{0:T(512)(128)(2,1)}, bf16[512]{0:T(512)(128)(2,1)S(1)}, u32[]{:S(2)}, u32[]{:S(2)}) collective-permute-start(bf16[512]{0:T(512)(128)(2,1)} %param.15), channel_id=1, source_target_pairs={{0,24},{8,16},{16,8},{24,0},{1,25},{9,17},{17,9},{25,1},{2,26},{10... | collective-permute-start | bytes 3080 | tf_op jit(solution)/shard_map/ppermute | solution.py:73
  5.9 47.0 %collective-permute-start.13 = (s32[8]{0:T(128)S(1)}, s32[8]{0:T(128)S(1)}, u32[]{:S(2)}, u32[]{:S(2)}) collective-permute-start(s32[8]{0:T(128)S(1)} %pad_add_fusion), channel_id=1, source_target_pairs={{0,8},{8,0},{16,24},{24,16},{1,9},{9,1},{17,25},{25,17},{2,10},{10... | collective-permute-start | bytes 104 | tf_op jit(solution)/shard_map/ppermute | solution.py:73
  7.9 53.6 %collective-permute-start.15 = (s32[8]{0:T(128)S(1)}, s32[8]{0:T(128)S(1)}, u32[]{:S(2)}, u32[]{:S(2)}) collective-permute-start(s32[8]{0:T(128)S(1)} %pad_add_fusion), channel_id=1, source_target_pairs={{0,24},{8,16},{16,8},{24,0},{1,25},{9,17},{17,9},{25,1},{2,26},{10... | collective-permute-start | bytes 104 | tf_op jit(solution)/shard_map/ppermute | solution.py:73
  153.1 47.8 %collective-permute-start.61 = (bf16[128,2048]{1,0:T(8,128)(2,1)S(1)}, bf16[128,2048]{1,0:T(8,128)(2,1)}, u32[]{:S(2)}, u32[]{:S(2)}) collective-permute-start(bf16[128,2048]{1,0:T(8,128)(2,1)S(1)} %get-tuple-element.86), channel_id=1, source_target_pairs={{0,24},{8,16},{16,8},{24,0},{1,25},{9,17},{17,9},{25,1},{2,26},{10... | collective-permute-start | bytes 1572872 | tf_op jit(solution)/shard_map/ppermute | solution.py:73
  197.6 45.3 %collective-permute-start.47 = (bf16[512,1024]{1,0:T(8,128)(2,1)}, bf16[512,1024]{1,0:T(8,128)(2,1)}, u32[]{:S(2)}, u32[]{:S(2)}) collective-permute-start(bf16[512,1024]{1,0:T(8,128)(2,1)} %get-tuple-element.127), channel_id=1, source_target_pairs={{0,24},{8,16},{16,8},{24,0},{1,25},{9,17},{17,9},{25,1},{2,26},{10... | collective-permute-start | bytes 3145736 | tf_op jit(solution)/shard_map/ppermute | solution.py:73
  200.8 58.5 %collective-permute-start.42 = (bf16[512,1024]{1,0:T(8,128)(2,1)}, bf16[512,1024]{1,0:T(8,128)(2,1)}, u32[]{:S(2)}, u32[]{:S(2)}) collective-permute-start(bf16[512,1024]{1,0:T(8,128)(2,1)} %get-tuple-element.136), channel_id=1, source_target_pairs={{0,8},{8,0},{16,24},{24,16},{1,9},{9,1},{17,25},{25,17},{2,10},{10... | collective-permute-start | bytes 3145736 | tf_op jit(solution)/shard_map/ppermute | solution.py:73
  202.4 44.4 %collective-permute-start.62 = (bf16[128,2048]{1,0:T(8,128)(2,1)}, bf16[128,2048]{1,0:T(8,128)(2,1)}, u32[]{:S(2)}, u32[]{:S(2)}) collective-permute-start(bf16[128,2048]{1,0:T(8,128)(2,1)} %collective-permute-done.61), channel_id=1, source_target_pairs={{0,1},{1,0},{2,3},{3,2},{4,5},{5,4},{6,7},{7,6},{8,9},{9,8},{10,11... | collective-permute-start | bytes 1572872 | tf_op jit(solution)/shard_map/ppermute | solution.py:73
  259.4 61.2 %collective-permute-start.43 = (bf16[512,1024]{1,0:T(8,128)(2,1)S(1)}, bf16[512,1024]{1,0:T(8,128)(2,1)S(1)}, u32[]{:S(2)}, u32[]{:S(2)}) collective-permute-start(bf16[512,1024]{1,0:T(8,128)(2,1)S(1)} %copy-done.45), channel_id=1, source_target_pairs={{0,16},{8,24},{16,0},{24,8},{1,17},{9,25},{17,1},{25,9},{2,18},{10... | collective-permute-start | bytes 3145736 | tf_op jit(solution)/shard_map/ppermute | solution.py:73
  261.7 60.0 %collective-permute-start.44 = (bf16[512,1024]{1,0:T(8,128)(2,1)S(1)}, bf16[512,1024]{1,0:T(8,128)(2,1)S(1)}, u32[]{:S(2)}, u32[]{:S(2)}) collective-permute-start(bf16[512,1024]{1,0:T(8,128)(2,1)S(1)} %copy-done.44), channel_id=1, source_target_pairs={{0,24},{8,16},{16,8},{24,0},{1,25},{9,17},{17,9},{25,1},{2,26},{10... | collective-permute-start | bytes 3145736 | tf_op jit(solution)/shard_map/ppermute | solution.py:73
  264.4 57.4 %collective-permute-start.39 = (bf16[512,1024]{1,0:T(8,128)(2,1)S(1)}, bf16[512,1024]{1,0:T(8,128)(2,1)S(1)}, u32[]{:S(2)}, u32[]{:S(2)}) collective-permute-start(bf16[512,1024]{1,0:T(8,128)(2,1)S(1)} %copy-done.43), channel_id=1, source_target_pairs={{0,8},{8,0},{16,24},{24,16},{1,9},{9,1},{17,25},{25,17},{2,10},{10... | collective-permute-start | bytes 3145736 | tf_op jit(solution)/shard_map/ppermute | solution.py:73
  275.7 89.4 %collective-permute-start.40 = (bf16[512,1024]{1,0:T(8,128)(2,1)S(1)}, bf16[512,1024]{1,0:T(8,128)(2,1)S(1)}, u32[]{:S(2)}, u32[]{:S(2)}) collective-permute-start(bf16[512,1024]{1,0:T(8,128)(2,1)S(1)} %copy-done.42), channel_id=1, source_target_pairs={{0,16},{8,24},{16,0},{24,8},{1,17},{9,25},{17,1},{25,9},{2,18},{10... | collective-permute-start | bytes 3145736 | tf_op jit(solution)/shard_map/ppermute | solution.py:73
  276.6 90.9 %collective-permute-start.41 = (bf16[512,1024]{1,0:T(8,128)(2,1)S(1)}, bf16[512,1024]{1,0:T(8,128)(2,1)S(1)}, u32[]{:S(2)}, u32[]{:S(2)}) collective-permute-start(bf16[512,1024]{1,0:T(8,128)(2,1)S(1)} %copy-done.41), channel_id=1, source_target_pairs={{0,24},{8,16},{16,8},{24,0},{1,25},{9,17},{17,9},{25,1},{2,26},{10... | collective-permute-start | bytes 3145736 | tf_op jit(solution)/shard_map/ppermute | solution.py:73
  320.6 47.0 %collective-permute-start.33 = (bf16[128,2048]{1,0:T(8,128)(2,1)S(1)}, bf16[128,2048]{1,0:T(8,128)(2,1)S(1)}, u32[]{:S(2)}, u32[]{:S(2)}) collective-permute-start(bf16[128,2048]{1,0:T(8,128)(2,1)S(1)} %get-tuple-element.88), channel_id=1, source_target_pairs={{0,8},{8,0},{16,24},{24,16},{1,9},{9,1},{17,25},{25,17},{2,10},{10... | collective-permute-start | bytes 1572872 | tf_op jit(solution)/shard_map/ppermute | solution.py:73
  321.7 65.8 %collective-permute-start.32 = (bf16[128,2048]{1,0:T(8,128)(2,1)S(1)}, bf16[128,2048]{1,0:T(8,128)(2,1)S(1)}, u32[]{:S(2)}, u32[]{:S(2)}) collective-permute-start(bf16[128,2048]{1,0:T(8,128)(2,1)S(1)} %get-tuple-element.88), channel_id=1, source_target_pairs={{0,1},{1,0},{2,3},{3,2},{4,5},{5,4},{6,7},{7,6},{8,9},{9,8},{10,11... | collective-permute-start | bytes 1572872 | tf_op jit(solution)/shard_map/ppermute | solution.py:73
  321.8 65.7 %collective-permute-start.35 = (bf16[128,2048]{1,0:T(8,128)(2,1)S(1)}, bf16[128,2048]{1,0:T(8,128)(2,1)S(1)}, u32[]{:S(2)}, u32[]{:S(2)}) collective-permute-start(bf16[128,2048]{1,0:T(8,128)(2,1)S(1)} %get-tuple-element.88), channel_id=1, source_target_pairs={{0,16},{8,24},{16,0},{24,8},{1,17},{9,25},{17,1},{25,9},{2,18},{10... | collective-permute-start | bytes 1572872 | tf_op jit(solution)/shard_map/ppermute | solution.py:73
  476.6 53.0 %collective-permute-start.145 = (bf16[512,1024]{1,0:T(8,128)(2,1)S(1)}, bf16[512,1024]{1,0:T(8,128)(2,1)S(1)}, u32[]{:S(2)}, u32[]{:S(2)}) collective-permute-start(bf16[512,1024]{1,0:T(8,128)(2,1)S(1)} %get-tuple-element.97), channel_id=1, source_target_pairs={{0,2},{6,4},{1,3},{7,5},{8,10},{14,12},{9,11},{15,13},{16,18},{22,... | collective-permute-start | bytes 3145736 | tf_op jit(solution)/shard_map/ppermute | solution.py:82
  493.9 42.3 %collective-permute-start.70 = (bf16[128,2048]{1,0:T(8,128)(2,1)S(1)}, bf16[128,2048]{1,0:T(8,128)(2,1)S(1)}, u32[]{:S(2)}, u32[]{:S(2)}) collective-permute-start(bf16[128,2048]{1,0:T(8,128)(2,1)S(1)} %get-tuple-element.83), channel_id=1, source_target_pairs={{0,1},{1,0},{2,3},{3,2},{4,5},{5,4},{6,7},{7,6},{8,9},{9,8},{10,11... | collective-permute-start | bytes 1572872 | tf_op jit(solution)/shard_map/ppermute | solution.py:73
  495.1 42.3 %collective-permute-start.73 = (bf16[128,2048]{1,0:T(8,128)(2,1)S(1)}, bf16[128,2048]{1,0:T(8,128)(2,1)S(1)}, u32[]{:S(2)}, u32[]{:S(2)}) collective-permute-start(bf16[128,2048]{1,0:T(8,128)(2,1)S(1)} %get-tuple-element.83), channel_id=1, source_target_pairs={{0,16},{8,24},{16,0},{24,8},{1,17},{9,25},{17,1},{25,9},{2,18},{10... | collective-permute-start | bytes 1572872 | tf_op jit(solution)/shard_map/ppermute | solution.py:73
  534.7 51.1 %collective-permute-start.118 = (bf16[512,1024]{1,0:T(8,128)(2,1)}, bf16[512,1024]{1,0:T(8,128)(2,1)}, u32[]{:S(2)}, u32[]{:S(2)}) collective-permute-start(bf16[512,1024]{1,0:T(8,128)(2,1)} %get-tuple-element.104), channel_id=1, source_target_pairs={{0,8},{8,0},{16,24},{24,16},{1,9},{9,1},{17,25},{25,17},{2,10},{10... | collective-permute-start | bytes 3145736 | tf_op jit(solution)/shard_map/ppermute | solution.py:73
  536.2 59.2 %collective-permute-start.122 = (bf16[512,1024]{1,0:T(8,128)(2,1)}, bf16[512,1024]{1,0:T(8,128)(2,1)}, u32[]{:S(2)}, u32[]{:S(2)}) collective-permute-start(bf16[512,1024]{1,0:T(8,128)(2,1)} %get-tuple-element.103), channel_id=1, source_target_pairs={{0,16},{8,24},{16,0},{24,8},{1,17},{9,25},{17,1},{25,9},{2,18},{10... | collective-permute-start | bytes 3145736 | tf_op jit(solution)/shard_map/ppermute | solution.py:73
  544.0 57.3 %collective-permute-start.126 = (bf16[512,1024]{1,0:T(8,128)(2,1)}, bf16[512,1024]{1,0:T(8,128)(2,1)}, u32[]{:S(2)}, u32[]{:S(2)}) collective-permute-start(bf16[512,1024]{1,0:T(8,128)(2,1)} %get-tuple-element.102), channel_id=1, source_target_pairs={{0,24},{8,16},{16,8},{24,0},{1,25},{9,17},{17,9},{25,1},{2,26},{10... | collective-permute-start | bytes 3145736 | tf_op jit(solution)/shard_map/ppermute | solution.py:73
  545.5 65.5 %collective-permute-start.133 = (bf16[512,1024]{1,0:T(8,128)(2,1)}, bf16[512,1024]{1,0:T(8,128)(2,1)}, u32[]{:S(2)}, u32[]{:S(2)}) collective-permute-start(bf16[512,1024]{1,0:T(8,128)(2,1)} %get-tuple-element.100), channel_id=1, source_target_pairs={{0,8},{8,0},{16,24},{24,16},{1,9},{9,1},{17,25},{25,17},{2,10},{10... | collective-permute-start | bytes 3145736 | tf_op jit(solution)/shard_map/ppermute | solution.py:73
  547.3 72.9 %collective-permute-start.137 = (bf16[512,1024]{1,0:T(8,128)(2,1)}, bf16[512,1024]{1,0:T(8,128)(2,1)}, u32[]{:S(2)}, u32[]{:S(2)}) collective-permute-start(bf16[512,1024]{1,0:T(8,128)(2,1)} %get-tuple-element.99), channel_id=1, source_target_pairs={{0,16},{8,24},{16,0},{24,8},{1,17},{9,25},{17,1},{25,9},{2,18},{10... | collective-permute-start | bytes 3145736 | tf_op jit(solution)/shard_map/ppermute | solution.py:73
  585.8 48.2 %collective-permute-start.141 = (bf16[512,1024]{1,0:T(8,128)(2,1)}, bf16[512,1024]{1,0:T(8,128)(2,1)}, u32[]{:S(2)}, u32[]{:S(2)}) collective-permute-start(bf16[512,1024]{1,0:T(8,128)(2,1)} %get-tuple-element.98), channel_id=1, source_target_pairs={{0,24},{8,16},{16,8},{24,0},{1,25},{9,17},{17,9},{25,1},{2,26},{10... | collective-permute-start | bytes 3145736 | tf_op jit(solution)/shard_map/ppermute | solution.py:73
  595.5 59.2 %collective-permute-start.148 = (bf16[512,1024]{1,0:T(8,128)(2,1)}, bf16[512,1024]{1,0:T(8,128)(2,1)}, u32[]{:S(2)}, u32[]{:S(2)}) collective-permute-start(bf16[512,1024]{1,0:T(8,128)(2,1)} %get-tuple-element.96), channel_id=1, source_target_pairs={{0,8},{8,0},{16,24},{24,16},{1,9},{9,1},{17,25},{25,17},{2,10},{10... | collective-permute-start | bytes 3145736 | tf_op jit(solution)/shard_map/ppermute | solution.py:73
  601.2 61.1 %collective-permute-start.116 = (bf16[512,1024]{1,0:T(8,128)(2,1)}, bf16[512,1024]{1,0:T(8,128)(2,1)}, u32[]{:S(2)}, u32[]{:S(2)}) collective-permute-start(bf16[512,1024]{1,0:T(8,128)(2,1)} %add_convert_fusion.24), channel_id=1, source_target_pairs={{2,4},{4,2},{3,5},{5,3},{10,12},{12,10},{11,13},{13,11},{18,20},{2... | collective-permute-start | bytes 3145736 | tf_op jit(solution)/shard_map/ppermute | solution.py:85
  611.0 54.9 %collective-permute-start.119 = (bf16[512,1024]{1,0:T(8,128)(2,1)}, bf16[512,1024]{1,0:T(8,128)(2,1)}, u32[]{:S(2)}, u32[]{:S(2)}) collective-permute-start(bf16[512,1024]{1,0:T(8,128)(2,1)} %collective-permute-done.118), channel_id=1, source_target_pairs={{0,2},{6,4},{1,3},{7,5},{8,10},{14,12},{9,11},{15,13},{16,18},{22,... | collective-permute-start | bytes 3145736 | tf_op jit(solution)/shard_map/ppermute | solution.py:82
  620.2 53.0 %collective-permute-start.152 = (bf16[512,1024]{1,0:T(8,128)(2,1)}, bf16[512,1024]{1,0:T(8,128)(2,1)S(1)}, u32[]{:S(2)}, u32[]{:S(2)}) collective-permute-start(bf16[512,1024]{1,0:T(8,128)(2,1)} %get-tuple-element.95), channel_id=1, source_target_pairs={{0,16},{8,24},{16,0},{24,8},{1,17},{9,25},{17,1},{25,9},{2,18},{10... | collective-permute-start | bytes 3145736 | tf_op jit(solution)/shard_map/ppermute | solution.py:73
  674.6 53.3 %collective-permute-start.138 = (bf16[512,1024]{1,0:T(8,128)(2,1)}, bf16[512,1024]{1,0:T(8,128)(2,1)S(1)}, u32[]{:S(2)}, u32[]{:S(2)}) collective-permute-start(bf16[512,1024]{1,0:T(8,128)(2,1)} %collective-permute-done.137), channel_id=1, source_target_pairs={{0,2},{6,4},{1,3},{7,5},{8,10},{14,12},{9,11},{15,13},{16,18},{22,... | collective-permute-start | bytes 3145736 | tf_op jit(solution)/shard_map/ppermute | solution.py:82
  683.0 67.4 %collective-permute-start.142 = (bf16[512,1024]{1,0:T(8,128)(2,1)}, bf16[512,1024]{1,0:T(8,128)(2,1)S(1)}, u32[]{:S(2)}, u32[]{:S(2)}) collective-permute-start(bf16[512,1024]{1,0:T(8,128)(2,1)} %collective-permute-done.141), channel_id=1, source_target_pairs={{0,2},{6,4},{1,3},{7,5},{8,10},{14,12},{9,11},{15,13},{16,18},{22,... | collective-permute-start | bytes 3145736 | tf_op jit(solution)/shard_map/ppermute | solution.py:82
  689.9 65.6 %collective-permute-start.146 = (bf16[512,1024]{1,0:T(8,128)(2,1)S(1)}, bf16[512,1024]{1,0:T(8,128)(2,1)S(1)}, u32[]{:S(2)}, u32[]{:S(2)}) collective-permute-start(bf16[512,1024]{1,0:T(8,128)(2,1)S(1)} %copy-done.12), channel_id=1, source_target_pairs={{2,4},{4,2},{3,5},{5,3},{10,12},{12,10},{11,13},{13,11},{18,20},{2... | collective-permute-start | bytes 3145736 | tf_op jit(solution)/shard_map/ppermute | solution.py:85
  705.4 67.4 %collective-permute-start.149 = (bf16[512,1024]{1,0:T(8,128)(2,1)}, bf16[512,1024]{1,0:T(8,128)(2,1)S(1)}, u32[]{:S(2)}, u32[]{:S(2)}) collective-permute-start(bf16[512,1024]{1,0:T(8,128)(2,1)} %collective-permute-done.148), channel_id=1, source_target_pairs={{0,2},{6,4},{1,3},{7,5},{8,10},{14,12},{9,11},{15,13},{16,18},{22,... | collective-permute-start | bytes 3145736 | tf_op jit(solution)/shard_map/ppermute | solution.py:82
  712.4 82.8 %collective-permute-start.153 = (bf16[512,1024]{1,0:T(8,128)(2,1)S(1)}, bf16[512,1024]{1,0:T(8,128)(2,1)S(1)}, u32[]{:S(2)}, u32[]{:S(2)}) collective-permute-start(bf16[512,1024]{1,0:T(8,128)(2,1)S(1)} %collective-permute-done.152), channel_id=1, source_target_pairs={{0,2},{6,4},{1,3},{7,5},{8,10},{14,12},{9,11},{15,13},{16,18},{22,... | collective-permute-start | bytes 3145736 | tf_op jit(solution)/shard_map/ppermute | solution.py:82
  727.9 118.9 %collective-permute-start.157 = (bf16[512,1024]{1,0:T(8,128)(2,1)}, bf16[512,1024]{1,0:T(8,128)(2,1)}, u32[]{:S(2)}, u32[]{:S(2)}) collective-permute-start(bf16[512,1024]{1,0:T(8,128)(2,1)} %collective-permute-done.156), channel_id=1, source_target_pairs={{0,2},{6,4},{1,3},{7,5},{8,10},{14,12},{9,11},{15,13},{16,18},{22,... | collective-permute-start | bytes 3145736 | tf_op jit(solution)/shard_map/ppermute | solution.py:82
  750.4 76.0 %collective-permute-start.79 = (bf16[2,4,256,64]{2,1,3,0:T(4,128)(2,1)S(1)}, bf16[2,4,256,64]{2,1,3,0:T(4,128)(2,1)S(1)}, u32[]{:S(2)}, u32[]{:S(2)}) collective-permute-start(bf16[2,4,256,64]{2,1,3,0:T(4,128)(2,1)S(1)} %get-tuple-element.159), channel_id=1, source_target_pairs={{0,6},{2,4},{4,2},{6,0},{1,7},{3,5},{5,3},{7,1},{8,14},{10,12},{12... | collective-permute-start | bytes 786440 | tf_op jit(solution)/shard_map/ppermute | solution.py:73
  755.6 73.4 %collective-permute-start.78 = (bf16[2,4,256,64]{2,1,3,0:T(4,128)(2,1)S(1)}, bf16[2,4,256,64]{2,1,3,0:T(4,128)(2,1)S(1)}, u32[]{:S(2)}, u32[]{:S(2)}) collective-permute-start(bf16[2,4,256,64]{2,1,3,0:T(4,128)(2,1)S(1)} %get-tuple-element.160), channel_id=1, source_target_pairs={{0,4},{2,6},{4,0},{6,2},{1,5},{3,7},{5,1},{7,3},{8,12},{10,14},{12... | collective-permute-start | bytes 786440 | tf_op jit(solution)/shard_map/ppermute | solution.py:73
  772.9 59.9 %collective-permute-start.77 = (bf16[2,4,256,64]{2,1,3,0:T(4,128)(2,1)S(1)}, bf16[2,4,256,64]{2,1,3,0:T(4,128)(2,1)S(1)}, u32[]{:S(2)}, u32[]{:S(2)}) collective-permute-start(bf16[2,4,256,64]{2,1,3,0:T(4,128)(2,1)S(1)} %get-tuple-element.158), channel_id=1, source_target_pairs={{0,2},{2,0},{4,6},{6,4},{1,3},{3,1},{5,7},{7,5},{8,10},{10,8},{12,... | collective-permute-start | bytes 786440 | tf_op jit(solution)/shard_map/ppermute | solution.py:73
  795.2 72.0 %collective-permute-start.117 = (bf16[512,1024]{1,0:T(8,128)(2,1)}, bf16[512,1024]{1,0:T(8,128)(2,1)}, u32[]{:S(2)}, u32[]{:S(2)}) collective-permute-start(bf16[512,1024]{1,0:T(8,128)(2,1)} %add_convert_fusion.23), channel_id=1, source_target_pairs={{2,0},{4,6},{3,1},{5,7},{10,8},{12,14},{11,9},{13,15},{18,16},{20,... | collective-permute-start | bytes 3145736 | tf_op jit(solution)/shard_map/ppermute | solution.py:88
  853.5 56.5 %collective-permute-start.120 = (bf16[512,1024]{1,0:T(8,128)(2,1)S(1)}, bf16[512,1024]{1,0:T(8,128)(2,1)S(1)}, u32[]{:S(2)}, u32[]{:S(2)}) collective-permute-start(bf16[512,1024]{1,0:T(8,128)(2,1)S(1)} %copy-done.15), channel_id=1, source_target_pairs={{2,4},{4,2},{3,5},{5,3},{10,12},{12,10},{11,13},{13,11},{18,20},{2... | collective-permute-start | bytes 3145736 | tf_op jit(solution)/shard_map/ppermute | solution.py:85
  855.6 47.5 %collective-permute-start.147 = (bf16[512,1024]{1,0:T(8,128)(2,1)S(1)}, bf16[512,1024]{1,0:T(8,128)(2,1)S(1)}, u32[]{:S(2)}, u32[]{:S(2)}) collective-permute-start(bf16[512,1024]{1,0:T(8,128)(2,1)S(1)} %copy-done.22), channel_id=1, source_target_pairs={{2,0},{4,6},{3,1},{5,7},{10,8},{12,14},{11,9},{13,15},{18,16},{20,... | collective-permute-start | bytes 3145736 | tf_op jit(solution)/shard_map/ppermute | solution.py:88
  865.3 46.2 %collective-permute-start.124 = (bf16[512,1024]{1,0:T(8,128)(2,1)S(1)}, bf16[512,1024]{1,0:T(8,128)(2,1)}, u32[]{:S(2)}, u32[]{:S(2)}) collective-permute-start(bf16[512,1024]{1,0:T(8,128)(2,1)S(1)} %copy-done.17), channel_id=1, source_target_pairs={{2,4},{4,2},{3,5},{5,3},{10,12},{12,10},{11,13},{13,11},{18,20},{2... | collective-permute-start | bytes 3145736 | tf_op jit(solution)/shard_map/ppermute | solution.py:85
  867.3 46.8 %collective-permute-start.128 = (bf16[512,1024]{1,0:T(8,128)(2,1)S(1)}, bf16[512,1024]{1,0:T(8,128)(2,1)S(1)}, u32[]{:S(2)}, u32[]{:S(2)}) collective-permute-start(bf16[512,1024]{1,0:T(8,128)(2,1)S(1)} %copy-done.16), channel_id=1, source_target_pairs={{2,4},{4,2},{3,5},{5,3},{10,12},{12,10},{11,13},{13,11},{18,20},{2... | collective-permute-start | bytes 3145736 | tf_op jit(solution)/shard_map/ppermute | solution.py:85
  958.5 103.2 %collective-permute-start.97 = (bf16[512,640]{0,1:T(8,128)(2,1)S(1)}, bf16[512,640]{0,1:T(8,128)(2,1)S(1)}, u32[]{:S(2)}, u32[]{:S(2)}) collective-permute-start(bf16[512,640]{0,1:T(8,128)(2,1)S(1)} %copy-done.55), channel_id=1, source_target_pairs={{0,8},{8,0},{16,24},{24,16},{1,9},{9,1},{17,25},{25,17},{2,10},{10... | collective-permute-start | bytes 1966088 | tf_op jit(solution)/shard_map/ppermute | solution.py:73
  967.2 102.2 %collective-permute-start.101 = (bf16[512,640]{0,1:T(8,128)(2,1)S(1)}, bf16[512,640]{0,1:T(8,128)(2,1)S(1)}, u32[]{:S(2)}, u32[]{:S(2)}) collective-permute-start(bf16[512,640]{0,1:T(8,128)(2,1)S(1)} %copy-done.54), channel_id=1, source_target_pairs={{0,16},{8,24},{16,0},{24,8},{1,17},{9,25},{17,1},{25,9},{2,18},{10... | collective-permute-start | bytes 1966088 | tf_op jit(solution)/shard_map/ppermute | solution.py:73
  968.2 102.6 %collective-permute-start.105 = (bf16[512,640]{0,1:T(8,128)(2,1)S(1)}, bf16[512,640]{0,1:T(8,128)(2,1)S(1)}, u32[]{:S(2)}, u32[]{:S(2)}) collective-permute-start(bf16[512,640]{0,1:T(8,128)(2,1)S(1)} %copy-done.53), channel_id=1, source_target_pairs={{0,24},{8,16},{16,8},{24,0},{1,25},{9,17},{17,9},{25,1},{2,26},{10... | collective-permute-start | bytes 1966088 | tf_op jit(solution)/shard_map/ppermute | solution.py:73
  969.8 104.0 %collective-permute-start.50 = (bf16[128,2048]{1,0:T(8,128)(2,1)S(1)}, bf16[128,2048]{1,0:T(8,128)(2,1)S(1)}, u32[]{:S(2)}, u32[]{:S(2)}) collective-permute-start(bf16[128,2048]{1,0:T(8,128)(2,1)S(1)} %copy-done.59), channel_id=1, source_target_pairs={{0,8},{8,0},{16,24},{24,16},{1,9},{9,1},{17,25},{25,17},{2,10},{10... | collective-permute-start | bytes 1572872 | tf_op jit(solution)/shard_map/ppermute | solution.py:73
  970.9 90.1 %collective-permute-start.92 = (f32[512]{0:T(512)S(1)}, f32[512]{0:T(512)S(1)}, u32[]{:S(2)}, u32[]{:S(2)}) collective-permute-start(f32[512]{0:T(512)S(1)} %add_add_fusion.3), channel_id=1, source_target_pairs={{0,2},{2,0},{4,6},{6,4},{1,3},{3,1},{5,7},{7,5},{8,10},{10,8},{12,... | collective-permute-start | bytes 6152 | tf_op jit(solution)/shard_map/ppermute | solution.py:73
  1061.0 49.4 %collective-permute-start.95 = (bf16[512,640]{0,1:T(8,128)(2,1)S(1)}, bf16[512,640]{0,1:T(8,128)(2,1)S(1)}, u32[]{:S(2)}, u32[]{:S(2)}) collective-permute-start(bf16[512,640]{0,1:T(8,128)(2,1)S(1)} %add_convert_fusion.32), channel_id=1, source_target_pairs={{2,4},{4,2},{3,5},{5,3},{10,12},{12,10},{11,13},{13,11},{18,20},{2... | collective-permute-start | bytes 1966088 | tf_op jit(solution)/shard_map/ppermute | solution.py:85
  1061.7 50.1 %collective-permute-start.98 = (bf16[512,640]{0,1:T(8,128)(2,1)S(1)}, bf16[512,640]{0,1:T(8,128)(2,1)}, u32[]{:S(2)}, u32[]{:S(2)}) collective-permute-start(bf16[512,640]{0,1:T(8,128)(2,1)S(1)} %collective-permute-done.97), channel_id=1, source_target_pairs={{0,2},{6,4},{1,3},{7,5},{8,10},{14,12},{9,11},{15,13},{16,18},{22,... | collective-permute-start | bytes 1966088 | tf_op jit(solution)/shard_map/ppermute | solution.py:82
  1069.4 45.0 %collective-permute-start.102 = (bf16[512,640]{0,1:T(8,128)(2,1)S(1)}, bf16[512,640]{0,1:T(8,128)(2,1)S(1)}, u32[]{:S(2)}, u32[]{:S(2)}) collective-permute-start(bf16[512,640]{0,1:T(8,128)(2,1)S(1)} %collective-permute-done.101), channel_id=1, source_target_pairs={{0,2},{6,4},{1,3},{7,5},{8,10},{14,12},{9,11},{15,13},{16,18},{22,... | collective-permute-start | bytes 1966088 | tf_op jit(solution)/shard_map/ppermute | solution.py:82
  1070.8 45.8 %collective-permute-start.106 = (bf16[512,640]{0,1:T(8,128)(2,1)S(1)}, bf16[512,640]{0,1:T(8,128)(2,1)S(1)}, u32[]{:S(2)}, u32[]{:S(2)}) collective-permute-start(bf16[512,640]{0,1:T(8,128)(2,1)S(1)} %collective-permute-done.105), channel_id=1, source_target_pairs={{0,2},{6,4},{1,3},{7,5},{8,10},{14,12},{9,11},{15,13},{16,18},{22,... | collective-permute-start | bytes 1966088 | tf_op jit(solution)/shard_map/ppermute | solution.py:82
  1110.4 48.6 %collective-permute-start.125 = (bf16[512,1024]{1,0:T(8,128)(2,1)S(1)}, bf16[512,1024]{1,0:T(8,128)(2,1)S(1)}, u32[]{:S(2)}, u32[]{:S(2)}) collective-permute-start(bf16[512,1024]{1,0:T(8,128)(2,1)S(1)} %add_convert_fusion.19), channel_id=1, source_target_pairs={{2,0},{4,6},{3,1},{5,7},{10,8},{12,14},{11,9},{13,15},{18,16},{20,... | collective-permute-start | bytes 3145736 | tf_op jit(solution)/shard_map/ppermute | solution.py:88
  1111.9 69.6 %collective-permute-start.129 = (bf16[512,1024]{1,0:T(8,128)(2,1)S(1)}, bf16[512,1024]{1,0:T(8,128)(2,1)S(1)}, u32[]{:S(2)}, u32[]{:S(2)}) collective-permute-start(bf16[512,1024]{1,0:T(8,128)(2,1)S(1)} %add_convert_fusion.17), channel_id=1, source_target_pairs={{2,0},{4,6},{3,1},{5,7},{10,8},{12,14},{11,9},{13,15},{18,16},{20,... | collective-permute-start | bytes 3145736 | tf_op jit(solution)/shard_map/ppermute | solution.py:88
  1118.1 85.8 %collective-permute-start.136 = (bf16[512,1024]{1,0:T(8,128)(2,1)S(1)}, bf16[512,1024]{1,0:T(8,128)(2,1)S(1)}, u32[]{:S(2)}, u32[]{:S(2)}) collective-permute-start(bf16[512,1024]{1,0:T(8,128)(2,1)S(1)} %add_convert_fusion.13), channel_id=1, source_target_pairs={{2,0},{4,6},{3,1},{5,7},{10,8},{12,14},{11,9},{13,15},{18,16},{20,... | collective-permute-start | bytes 3145736 | tf_op jit(solution)/shard_map/ppermute | solution.py:88
  1119.5 106.9 %collective-permute-start.140 = (bf16[512,1024]{1,0:T(8,128)(2,1)S(1)}, bf16[512,1024]{1,0:T(8,128)(2,1)S(1)}, u32[]{:S(2)}, u32[]{:S(2)}) collective-permute-start(bf16[512,1024]{1,0:T(8,128)(2,1)S(1)} %add_convert_fusion.11), channel_id=1, source_target_pairs={{2,0},{4,6},{3,1},{5,7},{10,8},{12,14},{11,9},{13,15},{18,16},{20,... | collective-permute-start | bytes 3145736 | tf_op jit(solution)/shard_map/ppermute | solution.py:88
  1136.5 112.4 %collective-permute-start.144 = (bf16[512,1024]{1,0:T(8,128)(2,1)S(1)}, bf16[512,1024]{1,0:T(8,128)(2,1)S(1)}, u32[]{:S(2)}, u32[]{:S(2)}) collective-permute-start(bf16[512,1024]{1,0:T(8,128)(2,1)S(1)} %add_convert_fusion.9), channel_id=1, source_target_pairs={{2,0},{4,6},{3,1},{5,7},{10,8},{12,14},{11,9},{13,15},{18,16},{20,... | collective-permute-start | bytes 3145736 | tf_op jit(solution)/shard_map/ppermute | solution.py:88
  1159.0 112.4 %collective-permute-start.151 = (bf16[512,1024]{1,0:T(8,128)(2,1)S(1)}, bf16[512,1024]{1,0:T(8,128)(2,1)S(1)}, u32[]{:S(2)}, u32[]{:S(2)}) collective-permute-start(bf16[512,1024]{1,0:T(8,128)(2,1)S(1)} %add_convert_fusion.5), channel_id=1, source_target_pairs={{2,0},{4,6},{3,1},{5,7},{10,8},{12,14},{11,9},{13,15},{18,16},{20,... | collective-permute-start | bytes 3145736 | tf_op jit(solution)/shard_map/ppermute | solution.py:88
  1181.4 112.4 %collective-permute-start.155 = (bf16[512,1024]{1,0:T(8,128)(2,1)S(1)}, bf16[512,1024]{1,0:T(8,128)(2,1)S(1)}, u32[]{:S(2)}, u32[]{:S(2)}) collective-permute-start(bf16[512,1024]{1,0:T(8,128)(2,1)S(1)} %add_convert_fusion.3), channel_id=1, source_target_pairs={{2,0},{4,6},{3,1},{5,7},{10,8},{12,14},{11,9},{13,15},{18,16},{20,... | collective-permute-start | bytes 3145736 | tf_op jit(solution)/shard_map/ppermute | solution.py:88
  1203.9 112.4 %collective-permute-start.159 = (bf16[512,1024]{1,0:T(8,128)(2,1)S(1)}, bf16[512,1024]{1,0:T(8,128)(2,1)S(1)}, u32[]{:S(2)}, u32[]{:S(2)}) collective-permute-start(bf16[512,1024]{1,0:T(8,128)(2,1)S(1)} %add_convert_fusion.1), channel_id=1, source_target_pairs={{2,0},{4,6},{3,1},{5,7},{10,8},{12,14},{11,9},{13,15},{18,16},{20,... | collective-permute-start | bytes 3145736 | tf_op jit(solution)/shard_map/ppermute | solution.py:88
  1226.4 99.6 %collective-permute-start.96 = (bf16[512,640]{0,1:T(8,128)(2,1)S(1)}, bf16[512,640]{0,1:T(8,128)(2,1)S(1)}, u32[]{:S(2)}, u32[]{:S(2)}) collective-permute-start(bf16[512,640]{0,1:T(8,128)(2,1)S(1)} %add_convert_fusion.31), channel_id=1, source_target_pairs={{2,0},{4,6},{3,1},{5,7},{10,8},{12,14},{11,9},{13,15},{18,16},{20,... | collective-permute-start | bytes 1966088 | tf_op jit(solution)/shard_map/ppermute | solution.py:88
  1248.8 79.2 %collective-permute-start.99 = (bf16[512,640]{0,1:T(8,128)(2,1)S(1)}, bf16[512,640]{0,1:T(8,128)(2,1)S(1)}, u32[]{:S(2)}, u32[]{:S(2)}) collective-permute-start(bf16[512,640]{0,1:T(8,128)(2,1)S(1)} %add_convert_fusion.30), channel_id=1, source_target_pairs={{2,4},{4,2},{3,5},{5,3},{10,12},{12,10},{11,13},{13,11},{18,20},{2... | collective-permute-start | bytes 1966088 | tf_op jit(solution)/shard_map/ppermute | solution.py:85
  1271.3 58.2 %collective-permute-start.103 = (bf16[512,640]{0,1:T(8,128)(2,1)S(1)}, bf16[512,640]{0,1:T(8,128)(2,1)}, u32[]{:S(2)}, u32[]{:S(2)}) collective-permute-start(bf16[512,640]{0,1:T(8,128)(2,1)S(1)} %add_convert_fusion.28), channel_id=1, source_target_pairs={{2,4},{4,2},{3,5},{5,3},{10,12},{12,10},{11,13},{13,11},{18,20},{2... | collective-permute-start | bytes 1966088 | tf_op jit(solution)/shard_map/ppermute | solution.py:85
  (189 other events, 4388.1 us)

commit v2 on v0

--- a/solution.py
+++ b/solution.py
@@ -1,8 +1,11 @@
+import functools
 import math
 
 import jax
 import jax.numpy as jnp
 from jax import lax
+from jax.experimental import pallas as pl
+from jax.experimental.pallas import tpu as pltpu
 from jax.sharding import PartitionSpec as P
 
 QUERY_HEADS = 32
@@ -68,7 +71,686 @@
     )
 
 
-def shards(
+VMEM_LIMIT = 48 * 1024 * 1024
+
+
+def pairs_by(distance, size):
+    return [(i, i ^ distance) for i in range(size)]
+
+
+def swap(array, axis, distance):
+    return lax.ppermute(array, axis, pairs_by(distance, lax.axis_size(axis)))
+
+
+def add_low(left, right):
+    return (left.astype(jnp.float32) + right.astype(jnp.float32)).astype(jnp.bfloat16)
+
+
+def reorder(array, index, count):
+    width = array.shape[-1] // count
+    return jnp.concatenate(
+        [
+            lax.dynamic_slice_in_dim(array, (index ^ block) * width, width, array.ndim - 1)
+            for block in range(count)
+        ],
+        axis=-1,
+    )
+
+
+def as_seen(array, distance, count):
+    width = array.shape[-1] // count
+    return jnp.concatenate(
+        [
+            array[..., (block ^ distance) * width : ((block ^ distance) + 1) * width]
+            for block in range(count)
+        ],
+        axis=-1,
+    )
+
+
+class Line:
+    def __init__(self, axis):
+        size = lax.axis_size(axis)
+        index = lax.axis_index(axis)
+        middle = size // 2
+        self.axis = axis
+        self.size = size
+        self.hops = middle
+        self.outer = [(index == h) | (index == size - 1 - h) for h in range(middle)]
+        self.moving = []
+        self.sums = {}
+
+    def pairs(self, hop):
+        size = self.size
+        if hop == self.hops - 1:
+            return [(hop, hop + 1), (hop + 1, hop)]
+        return [
+            (hop, hop + 1),
+            (hop + 1, hop),
+            (size - 1 - hop, size - 2 - hop),
+            (size - 2 - hop, size - 1 - hop),
+        ]
+
+    def advance(self, got, entering):
+        last = self.hops - 1
+        still = []
+        for name, value, stage in self.moving:
+            hop = stage if stage <= last else 2 * last - stage
+            came = got["line", hop][:, : value.shape[1]]
+            if stage <= last:
+                value = add_low(value, came)
+            else:
+                value = jnp.where(self.outer[hop], came, value)
+            if stage == 2 * last:
+                self.sums[name] = value
+            else:
+                still.append((name, value, stage + 1))
+        if entering is not None:
+            if self.hops:
+                still.append((entering[0], entering[1], 0))
+            else:
+                self.sums[entering[0]] = entering[1]
+        self.moving = still
+        moves = []
+        for hop in range(self.hops):
+            inward = [value for _, value, stage in still if stage == hop]
+            outward = [value for _, value, stage in still if stage == 2 * last - hop and hop < last]
+            if not inward and not outward:
+                continue
+            if inward and outward and inward[0].shape == outward[0].shape:
+                value = jnp.where(self.outer[hop], inward[0], outward[0])
+                moves.append((("line", hop), value, self.axis, self.pairs(hop)))
+            elif inward and outward:
+                wide = max(inward[0].shape[1], outward[0].shape[1])
+                grown = [
+                    jnp.pad(array, ((0, 0), (0, wide - array.shape[1])))
+                    for array in (inward[0], outward[0])
+                ]
+                value = jnp.where(self.outer[hop], grown[0], grown[1])
+                moves.append((("line", hop), value, self.axis, self.pairs(hop)))
+            else:
+                value = (inward or outward)[0]
+                pairs = self.pairs(hop)
+                if hop < last:
+                    pairs = pairs[0::2] if inward else pairs[1::2]
+                moves.append((("line", hop), value, self.axis, pairs))
+        return moves
+
+
+class Steps:
+    def __init__(self, line):
+        self.line = line
+        self.got = {}
+        self.names = []
+        self.flying = []
+
+    def step(self, moves=(), summed=None, late=None):
+        moves = list(moves)
+        fresh = [summed[1]] if summed is not None and summed[1] is not None else []
+        if not self.flying and not moves and not fresh:
+            return
+        held = lax.optimization_barrier(
+            tuple(self.flying) + tuple(move[1] for move in moves) + tuple(fresh)
+        )
+        count = len(self.flying)
+        for name, value in zip(self.names, held[:count]):
+            self.got[name] = value
+        moves = [
+            (name, value, axis, pairs)
+            for (name, _, axis, pairs), value in zip(moves, held[count:])
+        ]
+        entering = summed
+        if summed is not None:
+            entering = (summed[0], held[-1] if fresh else self.take(summed[0]))
+        moves = self.line.advance(self.got, entering) + moves
+        moves += late() if late is not None else []
+        self.names = [move[0] for move in moves]
+        self.flying = [lax.ppermute(value, axis, pairs) for _, value, axis, pairs in moves]
+
+    def take(self, name):
+        return self.got.pop(name)
+
+
+def turned(lin, cosine, sine):
+    width = lin.shape[-1]
+    quarter = HEAD_SIZE // 2
+    lane = lax.broadcasted_iota(jnp.int32, lin.shape, lin.ndim - 1)
+    low = lax.rem(lane, HEAD_SIZE) < quarter
+    partner = jnp.where(
+        low, -pltpu.roll(lin, width - quarter, lin.ndim - 1), pltpu.roll(lin, quarter, lin.ndim - 1)
+    )
+    return lin * cosine + partner * sine
+
+
+def side_by_side(table, width):
+    return jnp.concatenate([table] * (width // table.shape[-1]), axis=-1)
+
+
+def of_keys(cosine, sine):
+    keys = lax.broadcasted_iota(jnp.int32, cosine.shape, 1) < HEAD_SIZE
+    return jnp.where(keys, cosine, 1.0), jnp.where(keys, sine, 0.0)
+
+
+def qkv_kernel(x_ref, gain_ref, w_ref, cos_ref, sin_ref, normed_ref, q_ref, kv_ref):
+    x = x_ref[...].astype(jnp.float32)
+    mean = jnp.mean(x * x, axis=-1, keepdims=True)
+    normed = (x * lax.rsqrt(mean + 1e-05) * gain_ref[...]).astype(jnp.bfloat16)
+    normed_ref[...] = normed
+    lin = jnp.dot(normed, w_ref[...], preferred_element_type=jnp.float32)
+    cosine, sine = cos_ref[...], sin_ref[...]
+    q_width = q_ref.shape[-1]
+    q = turned(lin[:, :q_width], side_by_side(cosine, q_width), side_by_side(sine, q_width))
+    q_ref[...] = q.astype(jnp.bfloat16)
+    kv = turned(lin[:, q_width:], *of_keys(cosine, sine))
+    kv_ref[...] = kv.astype(jnp.bfloat16)
+
+
+def project_qkv(x, gain, weight, cosine, sine, q_width):
+    tokens, depth = x.shape
+    kv_width = weight.shape[1] - q_width
+    block = math.gcd(tokens, 256)
+
+    def by_rows(width):
+        return pl.BlockSpec((block, width), lambda i: (i, 0))
+
+    def whole(shape):
+        return pl.BlockSpec(shape, lambda i: (0, 0))
+
+    return pl.pallas_call(
+        qkv_kernel,
+        grid=(tokens // block,),
+        in_specs=[
+            by_rows(depth),
+            whole((1, depth)),
+            whole(weight.shape),
+            by_rows(cosine.shape[1]),
+            by_rows(cosine.shape[1]),
+        ],
+        out_specs=[by_rows(depth), by_rows(q_width), by_rows(kv_width)],
+        out_shape=[
+            jax.ShapeDtypeStruct((tokens, depth), jnp.bfloat16),
+            jax.ShapeDtypeStruct((tokens, q_width), jnp.bfloat16),
+            jax.ShapeDtypeStruct((tokens, kv_width), jnp.bfloat16),
+        ],
+        compiler_params=pltpu.CompilerParams(vmem_limit_bytes=VMEM_LIMIT),
+        cost_estimate=pl.CostEstimate(
+            flops=2 * tokens * depth * weight.shape[1],
+            bytes_accessed=4 * tokens * depth + 2 * weight.size,
+            transcendentals=0,
+        ),
+        name="qkv",
+    )(x, gain, weight, cosine, sine)
+
+
+def shares(q, k, visible):
+    scores = lax.dot_general(
+        q, k, (((1,), (1,)), ((), ())), preferred_element_type=jnp.float32
+    ) * (1.0 / math.sqrt(HEAD_SIZE))
+    scores = jnp.where(visible, scores, -1e30)
+    weights = jnp.exp(scores - jnp.max(scores, axis=-1, keepdims=True))
+    weights = jnp.where(visible, weights, 0.0)
+    return weights, jnp.sum(weights, axis=-1, keepdims=True)
+
+
+def load_attention(q_ref, place_ref, start_ref, key_place_ref, kv_refs):
+    q = q_ref[...]
+    q = q.reshape(q.shape[0] * q.shape[2], q.shape[3])
+    kv = jnp.concatenate(
+        [ref[...].reshape(q.shape[0], 2 * HEAD_SIZE) for ref in kv_refs], axis=0
+    )
+    key_place = key_place_ref[0]
+    visible = (key_place <= place_ref[0]) & (key_place >= start_ref[0])
+    return q, kv[:, :HEAD_SIZE], kv[:, HEAD_SIZE:], visible
+
+
+def attend_kernel(groups, q_ref, place_ref, start_ref, key_place_ref, *refs):
+    kv_refs, out_ref = refs[:-1], refs[-1]
+    q, k, v, visible = load_attention(q_ref, place_ref, start_ref, key_place_ref, kv_refs)
+    mixed = []
+    for g in range(groups):
+        weights, totals = shares(q[:, g * HEAD_SIZE : (g + 1) * HEAD_SIZE], k, visible)
+        probs = (weights / totals).astype(jnp.bfloat16)
+        mixed.append(jnp.dot(probs, v, preferred_element_type=jnp.float32))
+    out = jnp.concatenate(mixed, axis=1).astype(jnp.bfloat16)
+    out_ref[...] = out.reshape(out_ref.shape)
+
+
+def attend_back_kernel(
+    groups, q_ref, d_ref, cos_ref, sin_ref, place_ref, start_ref, key_place_ref, *refs
+):
+    kv_refs, (dq_ref, dkv_ref) = refs[:-2], refs[-2:]
+    q, k, v, visible = load_attention(q_ref, place_ref, start_ref, key_place_ref, kv_refs)
+    d_out = d_ref[...].reshape(q.shape)
+    scale = 1.0 / math.sqrt(HEAD_SIZE)
+    d_q, d_k, d_v = [], 0.0, 0.0
+    for g in range(groups):
+        q_head = q[:, g * HEAD_SIZE : (g + 1) * HEAD_SIZE]
+        d_head = d_out[:, g * HEAD_SIZE : (g + 1) * HEAD_SIZE]
+        weights, totals = shares(q_head, k, visible)
+        probs = weights / totals
+        d_probs = lax.dot_general(
+            d_head, v, (((1,), (1,)), ((), ())), preferred_element_type=jnp.float32
+        )
+        row_delta = jnp.sum(probs * d_probs, axis=-1, keepdims=True)
+        d_scores = (probs * (d_probs - row_delta)).astype(jnp.bfloat16)
+        d_q.append(jnp.dot(d_scores, k, preferred_element_type=jnp.float32) * scale)
+        d_k = d_k + contract_first(d_scores, q_head) * scale
+        d_v = d_v + contract_first(probs.astype(jnp.bfloat16), d_head)
+    d_q = jnp.concatenate(d_q, axis=1)
+    cosine = cos_ref[...].reshape(q.shape[0], -1)
+    sine = sin_ref[...].reshape(q.shape[0], -1)
+    d_q = turned(d_q, side_by_side(cosine, q.shape[1]), -side_by_side(sine, q.shape[1]))
+    dq_ref[...] = d_q.astype(jnp.bfloat16).reshape(dq_ref.shape)
+    d_kv = jnp.concatenate([d_k, d_v], axis=1).astype(jnp.bfloat16)
+    dkv_ref[...] = d_kv.reshape(dkv_ref.shape)
+
+
+def attention_specs(packs, rows, cycle):
+    def of_pack(width):
+        return pl.BlockSpec((2, 1, rows // 2, width), lambda p: (0, p, 0, 0))
+
+    places = [
+        pl.BlockSpec((1, rows, 1), lambda p: (p, 0, 0)),
+        pl.BlockSpec((1, rows, 1), lambda p: (p, 0, 0)),
+        pl.BlockSpec((1, 1, cycle * rows), lambda p: (p, 0, 0)),
+    ]
+    return of_pack, places
+
+
+def attend(q, places, kvs, groups):
+    _, packs, half, width = q.shape
+    rows, cycle = 2 * half, len(kvs)
+    of_pack, place_specs = attention_specs(packs, rows, cycle)
+    work = packs * groups * rows * cycle * rows
+    return pl.pallas_call(
+        functools.partial(attend_kernel, groups),
+        grid=(packs,),
+        in_specs=[of_pack(width)] + place_specs + [of_pack(2 * HEAD_SIZE)] * cycle,
+        out_specs=of_pack(width),
+        out_shape=jax.ShapeDtypeStruct(q.shape, jnp.bfloat16),
+        compiler_params=pltpu.CompilerParams(vmem_limit_bytes=VMEM_LIMIT),
+        cost_estimate=pl.CostEstimate(
+            flops=40 * 4 * work, bytes_accessed=4 * q.size * 3, transcendentals=work
+        ),
+        name="attend",
+    )(q, *places, *kvs)
+
+
+def attend_back(q, d_out, cosine, sine, places, kvs, groups):
+    _, packs, half, width = q.shape
+    rows, cycle = 2 * half, len(kvs)
+    of_pack, place_specs = attention_specs(packs, rows, cycle)
+    work = packs * groups * rows * cycle * rows
+    kv_out = (cycle, 2, packs, half, 2 * HEAD_SIZE)
+    return pl.pallas_call(
+        functools.partial(attend_back_kernel, groups),
+        grid=(packs,),
+        in_specs=[of_pack(width)] * 2
+        + [of_pack(cosine.shape[-1])] * 2
+        + place_specs
+        + [of_pack(2 * HEAD_SIZE)] * cycle,
+        out_specs=[
+            of_pack(width),
+            pl.BlockSpec((cycle, 2, 1, half, 2 * HEAD_SIZE), lambda p: (0, 0, p, 0, 0)),
+        ],
+        out_shape=[
+            jax.ShapeDtypeStruct(q.shape, jnp.bfloat16),
+            jax.ShapeDtypeStruct(kv_out, jnp.bfloat16),
+        ],
+        compiler_params=pltpu.CompilerParams(vmem_limit_bytes=VMEM_LIMIT),
+        cost_estimate=pl.CostEstimate(
+            flops=40 * 10 * work, bytes_accessed=4 * q.size * 4, transcendentals=work
+        ),
+        name="attend_back",
+    )(q, d_out, cosine, sine, *places, *kvs)
+
+
+def split_heads(
+    hidden_in,
+    out_cotangent,
+    norm1_gain,
+    q_weight,
+    key_projection_weight,
+    value_projection_weight,
+    o_weight,
+    norm2_gain,
+    gate_weight,
+    up_weight,
+    down_weight,
+    seq_lengths,
+    span_order,
+):
+    packs = lax.axis_size("fsdp")
+    cycle = lax.axis_size("ctx")
+    pack = lax.axis_index("fsdp")
+    core = lax.axis_index("tp")
+    here = lax.axis_index("ctx")
+    rows = hidden_in.shape[0]
+    half = rows // 2
+    tokens = packs * rows
+    depth = q_weight.shape[0]
+    width = depth * packs
+    q_width = q_weight.shape[1] // packs
+    k_width = key_projection_weight.shape[1] // packs
+    ff_width = gate_weight.shape[1] // packs
+    ff_half = ff_width // 2
+    groups = q_width // k_width
+    far = range(1, packs)
+    steps = Steps(Line("ctx"))
+    kept = {}
+
+
+    def columns(weight, k, count, first=0, of=None):
+        return lax.dynamic_slice_in_dim(weight, (pack ^ k) * (of or count) + first, count, 1)
+
+    def to_pack(name, k, array):
+        return ((name, k), array, "fsdp", pairs_by(k, packs))
+
+    def spread(name, array):
+        return [to_pack(name, k, as_seen(array, k, packs)) for k in far]
+
+    def gathered(own, others):
+        mine = jnp.concatenate([own] + others, axis=0)
+        return jnp.concatenate([mine, swap(mine, "tp", 1)], axis=0)
+
+    def arrived(name):
+        return [steps.take((name, k)) for k in far]
+
+    def to_rows(name, partial):
+        mine = add_low(partial[: tokens // 2], swap(partial[tokens // 2 :], "tp", 1))
+        blocks = mine.reshape(packs, half, width)
+        return blocks[0], [to_pack(name, k, as_seen(blocks[k], k, packs)) for k in far]
+
+    def summed_rows(name, own):
+        total = own.astype(jnp.float32)
+        for k in far:
+            total = total + steps.take((name, k)).astype(jnp.float32)
+        return total
+
+    own_in = reorder(lax.dynamic_slice_in_dim(hidden_in, core * half, half, 0), pack, packs)
+    own_cot = reorder(lax.dynamic_slice_in_dim(out_cotangent, core * half, half, 0), pack, packs)
+
+    meta = jnp.concatenate([span_order[0], seq_lengths[0]])
+    order_len, meta_len = span_order.shape[1], meta.shape[0]
+    info = jnp.concatenate(
+        [norm1_gain, norm2_gain, (meta // 32).astype(jnp.bfloat16), (meta % 32).astype(jnp.bfloat16)]
+    )
+    info = jnp.pad(info, (0, width - info.shape[0]))[None]
+    info_rows = jnp.pad(info, ((0, 15), (0, 0)))
+
+    def attention_piece(k):
+        return jnp.concatenate(
+            [
+                columns(q_weight, k, q_width),
+                columns(key_projection_weight, k, k_width),
+                columns(value_projection_weight, k, k_width),
+                columns(o_weight, k, q_width),
+            ],
+            axis=1,
+        )
+
+    steps.step(
+        [
+            to_pack("in", k, jnp.concatenate([as_seen(own_in, k, packs), info_rows], axis=0))
+            for k in far
+        ]
+    )
+    steps.step([to_pack("attention", k, attention_piece(k)) for k in far])
+    came = arrived("in")
+    all_in = gathered(own_in, [block[:half] for block in came])
+    infos = jnp.concatenate([info] + [block[half : half + 1] for block in came], axis=0)
+    all_gains = infos[:, : 2 * depth].astype(jnp.float32)
+    gain_one = all_gains[:, :depth].reshape(-1)
+    gain_two = all_gains[:, depth:].reshape(-1)
+    metas = infos[:, 2 * depth : 2 * depth + 2 * meta_len].astype(jnp.int32)
+    metas = metas[:, :meta_len] * 32 + metas[:, meta_len:]
+    orders, lengths = metas[:, :order_len], metas[:, order_len:]
+
+    others = jnp.stack([here ^ j for j in range(cycle)])
+    first = jnp.sum(
+        jnp.where(
+            others[None, :, None] == jnp.arange(order_len, dtype=jnp.int32)[None, None, :],
+            orders[:, None, :],
+            0,
+        ),
+        axis=2,
+    )
+    halves = jnp.stack([core, core ^ 1])[None, None, :]
+    section = jnp.where(halves == 0, first[:, :, None], 2 * cycle - 1 - first[:, :, None])
+    places = section[..., None] * half + jnp.arange(half, dtype=jnp.int32)
+    places = places.reshape(packs, cycle * rows)
+    starts = jnp.zeros_like(places)
+    end = jnp.zeros((packs, 1), jnp.int32)
+    for j in range(lengths.shape[1]):
+        end = end + lengths[:, j : j + 1]
+        starts = jnp.where(places >= end, end, starts)
+    place_args = (places[:, :rows, None], starts[:, :rows, None], places[:, None, :])
+    offsets = (places - starts)[:, :rows].reshape(packs, 2, half).transpose(1, 0, 2)
+    frequency = jnp.exp(
+        -math.log(500000.0)
+        * (jnp.arange(2 * HEAD_SIZE) % (HEAD_SIZE // 2)).astype(jnp.float32)
+        * 2.0
+        / HEAD_SIZE
+    )
+    angles = offsets.astype(jnp.float32).reshape(tokens, 1) * frequency[None, :]
+    cosine, sine = jnp.cos(angles), jnp.sin(angles)
+
+    side = here & 1
+
+    def fetch(name, weight):
+        return [to_pack(name, k, columns(weight, k, ff_half, side * ff_half, ff_width)) for k in far]
+
+    steps.step(fetch("gate", gate_weight))
+    w_attention = jnp.concatenate([attention_piece(0)] + arrived("attention"), axis=0)
+    wqkv, wo = w_attention[:, : q_width + 2 * k_width], w_attention[:, q_width + 2 * k_width :]
+    normed_low, q_rot, kv_own = project_qkv(all_in, gain_one[None], wqkv, cosine, sine, q_width)
+
+    by_pack = (2, packs, half, -1)
+    steps.step(
+        [(("kv", j), kv_own, "ctx", pairs_by(j, cycle)) for j in range(1, cycle)]
+        + fetch("up", up_weight)
+    )
+
+    def pass_on(k):
+        kept["both", k] = jnp.concatenate([steps.take(("gate", k)), steps.take(("up", k))], axis=1)
+        return to_neighbour(k)
+
+    def to_neighbour(k):
+        return [(("neighbour", k), kept["both", k], "ctx", pairs_by(1, cycle))]
+
+    def first_of_weights():
+        moves = [pass_on(k) for k in far]
+        return moves[0] if moves else []
+
+    steps.step(spread("cot", own_cot), late=first_of_weights)
+    kvs = [kv_own] + [steps.take(("kv", j)) for j in range(1, cycle)]
+    kvs = [kv.reshape(by_pack) for kv in kvs]
+    q_rot = q_rot.reshape(by_pack)
+    attn_low = attend(q_rot, place_args, kvs, groups).reshape(tokens, q_width)
+    branch_own, branch_moves = to_rows("branch", contract_last(attn_low, wo).astype(jnp.bfloat16))
+
+    steps.step(branch_moves + to_neighbour(2))
+    all_cot = gathered(own_cot, arrived("cot"))
+
+    def middle_moves():
+        kept["middle"] = own_in.astype(jnp.float32) + summed_rows("branch", branch_own)
+        kept["normed"] = normalize(kept["middle"], gain_two).astype(jnp.bfloat16)
+        return spread("two", kept["normed"])
+
+    steps.step(to_neighbour(3), late=middle_moves)
+    middle = kept["middle"]
+
+    def wd_moves(ks):
+        return [to_pack("down", k, columns(down_weight, k, ff_width)) for k in ks]
+
+    steps.step(wd_moves([1, 2]))
+    normed_two_low = gathered(kept["normed"], arrived("two"))
+
+    def whole_columns(weight, first):
+        out = jnp.zeros((width, ff_width), weight.dtype)
+        fetched = [kept["both", k][:, first : first + ff_half] for k in far]
+        passed = [kept["neighbour", k][:, first : first + ff_half] for k in far]
+        out = lax.dynamic_update_slice(out, columns(weight, 0, ff_width), (0, 0))
+        out = lax.dynamic_update_slice(
+            out, jnp.concatenate(fetched, axis=0), (depth, side * ff_half)
+        )
+        return lax.dynamic_update_slice(
+            out, jnp.concatenate(passed, axis=0), (depth, (1 - side) * ff_half)
+        )
+
+    for k in far:
+        kept["neighbour", k] = steps.take(("neighbour", k))
+    wg = whole_columns(gate_weight, 0)
+    wu = whole_columns(up_weight, ff_half)
+
+    gate_val = jnp.dot(normed_two_low, wg, preferred_element_type=jnp.float32)
+    up_val = jnp.dot(normed_two_low, wu, preferred_element_type=jnp.float32)
+    hidden = swiglu(gate_val, up_val).astype(jnp.bfloat16)
+    d_wd = contract_first(all_cot, hidden).astype(jnp.bfloat16)
+
+    def rows_of(grad, k):
+        return grad[k * depth : (k + 1) * depth]
+
+    def back(name, grad, ks):
+        return [to_pack(name, k, rows_of(grad, k)) for k in ks]
+
+    def entry(name, k, grad=None):
+        return ((name, k), rows_of(grad, 0) if k == 0 else None)
+
+    steps.step(back("wd", d_wd, [1, 2]), summed=entry("wd", 0, d_wd))
+    steps.step(wd_moves([3]), summed=entry("wd", 1))
+    steps.step(back("wd", d_wd, [3]), summed=entry("wd", 2))
+    wd = jnp.concatenate([columns(down_weight, 0, ff_width)] + arrived("down"), axis=0)
+    d_hidden = jnp.dot(all_cot, wd, preferred_element_type=jnp.float32)
+    _, swiglu_back = jax.vjp(swiglu, gate_val, up_val)
+    d_gate, d_up = (grad.astype(jnp.bfloat16) for grad in swiglu_back(d_hidden))
+    two_own, two_moves = to_rows(
+        "d_two", (contract_last(d_gate, wg) + contract_last(d_up, wu)).astype(jnp.bfloat16)
+    )
+    d_wg = contract_first(normed_two_low, d_gate).astype(jnp.bfloat16)
+    d_wu = contract_first(normed_two_low, d_up).astype(jnp.bfloat16)
+
+    def branch_back():
+        _, norm_two_back = jax.vjp(normalize, middle, gain_two)
+        d_middle_norm, kept["d_gain_two"] = norm_two_back(summed_rows("d_two", two_own))
+        kept["d_middle"] = own_cot.astype(jnp.float32) + d_middle_norm
+        kept["d_branch"] = kept["d_middle"].astype(jnp.bfloat16)
+        return spread("d_branch", kept["d_branch"])
+
+    steps.step(two_moves, summed=entry("wd", 3))
+    steps.step(summed=entry("wg", 0, d_wg), late=branch_back)
+    steps.step(back("wg", d_wg, [1, 2]), summed=entry("wu", 0, d_wu))
+
+    d_branch = gathered(kept["d_branch"], arrived("d_branch"))
+    d_attn = jnp.dot(d_branch, wo, preferred_element_type=jnp.float32).astype(jnp.bfloat16)
+    d_wo = contract_first(d_branch, attn_low).astype(jnp.bfloat16)
+    d_q, d_kv = attend_back(
+        q_rot,
+        d_attn.reshape(by_pack),
+        cosine.reshape(by_pack),
+        sine.reshape(by_pack),
+        place_args,
+        kvs,
+        groups,
+    )
+    d_kv = d_kv.reshape(cycle, tokens, 2 * HEAD_SIZE)
+    d_kv = jnp.concatenate(
+        [
+            lax.dynamic_index_in_dim(d_kv, here ^ j, 0, keepdims=False)[side_rows]
+            for side_rows in (slice(0, tokens // 2), slice(tokens // 2, tokens))
+            for j in range(cycle)
+        ],
+        axis=1,
+    )
+    ff_own, ff_moves = to_rows("ff", contract_last(hidden, wd).astype(jnp.bfloat16))
+
+    steps.step(back("wg", d_wg, [3]), summed=entry("wg", 1))
+    steps.step(back("wu", d_wu, [1, 2]), summed=("d_kv", d_kv))
+    steps.step(back("wu", d_wu, [3]), summed=entry("wg", 2))
+    steps.step(ff_moves, summed=entry("wg", 3))
+    steps.step(summed=entry("wu", 1))
+    d_kv_sum = steps.line.sums.pop("d_kv")
+    d_kv_own = jnp.concatenate(
+        [
+            lax.dynamic_slice_in_dim(d_kv_sum, (side * cycle + here) * 2 * HEAD_SIZE, 2 * HEAD_SIZE, 1)
+            for side in range(2)
+        ],
+        axis=0,
+    ).astype(jnp.float32)
+    k_cosine, k_sine = of_keys(cosine, sine)
+    low = (jnp.arange(2 * HEAD_SIZE) % HEAD_SIZE < HEAD_SIZE // 2)[None, :]
+    shift = HEAD_SIZE // 2
+    partner = jnp.where(low, -jnp.roll(d_kv_own, -shift, 1), jnp.roll(d_kv_own, shift, 1))
+    d_kv_low = (d_kv_own * k_cosine - partner * k_sine).astype(jnp.bfloat16)
+    d_qkv = jnp.concatenate([d_q.reshape(tokens, q_width), d_kv_low], axis=1)
+    d_wqkvo = jnp.concatenate([contract_first(normed_low, d_qkv).astype(jnp.bfloat16), d_wo], axis=1)
+    one_own, one_moves = to_rows("d_one", contract_last(d_qkv, wqkv).astype(jnp.bfloat16))
+    result = (middle + summed_rows("ff", ff_own)).astype(jnp.bfloat16)
+
+    steps.step(back("wqkvo", d_wqkvo, [1, 2]), summed=entry("wu", 2))
+    steps.step(back("wqkvo", d_wqkvo, [3]), summed=entry("wu", 3))
+    steps.step(one_moves, summed=entry("wqkvo", 0, d_wqkvo))
+
+    def gains_to_packs():
+        _, norm_one_back = jax.vjp(normalize, own_in.astype(jnp.float32), gain_one)
+        d_inputs_norm, d_gain_one = norm_one_back(summed_rows("d_one", one_own))
+        kept["in_grad"] = (kept["d_middle"] + d_inputs_norm).astype(jnp.bfloat16)
+        d_gains = jnp.stack([d_gain_one, kept["d_gain_two"]])
+        kept["gains"] = d_gains + swap(d_gains, "tp", 1)
+        return [
+            to_pack("gains", k, kept["gains"][:, k * depth : (k + 1) * depth]) for k in far
+        ]
+
+    def gains_along(distance):
+        if distance == 1:
+            kept["gains"] = kept["gains"][:, :depth]
+            for k in far:
+                kept["gains"] = kept["gains"] + steps.take(("gains", k))
+        else:
+            kept["gains"] = kept["gains"] + steps.take("gains")
+        if distance >= cycle:
+            return []
+        return [("gains", kept["gains"], "ctx", pairs_by(distance, cycle))]
+
+    tasks = [gains_to_packs]
+    tasks += [functools.partial(gains_along, 1 << bit) for bit in range(cycle.bit_length())]
+    for i in range(1, max(packs, len(tasks) + 1)):
+        summed = entry("wqkvo", i) if i < packs else None
+        steps.step(summed=summed, late=tasks[i - 1] if i <= len(tasks) else None)
+    while steps.flying:
+        steps.step()
+    sums = steps.line.sums
+
+    def assembled(name, count, first=0):
+        out = jnp.zeros((depth, count * packs), jnp.float32)
+        for k in range(packs):
+            piece = sums[name, k][:, first : first + count].astype(jnp.float32)
+            out = lax.dynamic_update_slice(out, piece, (0, (pack ^ k) * count))
+        return out
+
+    def both_halves(own):
+        own = reorder(own, pack, packs)
+        other = swap(own, "tp", 1)
+        return jnp.concatenate(
+            [jnp.where(core == 0, own, other), jnp.where(core == 0, other, own)], axis=0
+        )
+
+    return (
+        both_halves(result),
+        both_halves(kept["in_grad"]),
+        kept["gains"][0],
+        assembled("wqkvo", q_width),
+        assembled("wqkvo", k_width, q_width),
+        assembled("wqkvo", k_width, q_width + k_width),
+        assembled("wqkvo", q_width, q_width + 2 * k_width),
+        kept["gains"][1],
+        assembled("wg", ff_width),
+        assembled("wu", ff_width),
+        assembled("wd", ff_width),
+    )
+
+
+def gathered_weights(
     hidden_in,
     out_cotangent,
     norm1_gain,
@@ -389,8 +1071,10 @@
         P("fsdp", None),
         P("fsdp", None),
     )
+    plane = mesh.shape["fsdp"] * mesh.shape["tp"]
+    splits = mesh.shape["tp"] == 2 and KEY_VALUE_HEADS == plane and mesh.shape["ctx"] % 2 == 0
     return jax.shard_map(
-        shards,
+        split_heads if splits else gathered_weights,
         mesh=mesh,
         in_specs=placed,
         out_specs=(

time: 3800 us -> 848 us (0.22)
  waiting for transfers between devices: 3290 us -> 347 us
  blocking collectives: 175 us -> 0 us
  matrix products: 223 us -> 69.4 us
  starting transfers between devices: 1.65 us -> 145 us
  local copies, waits for them, and re-layouts: 22.6 us -> 104 us
  other arithmetic: 66.3 us -> 131 us
  Pallas kernels: 0 us -> 42.3 us
    reduce_scatter x9 -> x0, waiting for transfers between devices: 2430 us -> none  [the longest x1 688 us: shards(): lax.psum_scatter(weight_grads[8], ('fsdp', 'ctx'), scatter_dimension=0, t...]
    all_gather x12 -> x0, waiting for transfers between devices: 802 us -> none  [the longest x1 158 us: shards(): lax.all_gather(gate_weight, 'fsdp', axis=0, tiled=True)]
    ppermute x0 -> x106, waiting for transfers between devices: none -> 347 us  [the longest x95 347 us: step(): lax.ppermute(value, axis, pairs)]
    ppermute x0 -> x106, starting transfers between devices: none -> 145 us  [the longest x95 145 us: step(): lax.ppermute(value, axis, pairs)]
    all_gather x8 -> x0, blocking collectives: 96.5 us -> none  [the longest x1 15.6 us: shards(): value_row_block = lax.all_gather(v_low, 'ctx', axis=0, tiled=True)]
    dot_general x21 -> x4, matrix products: 104 us -> 22.7 us  [the longest x1 10.3 us: split_heads(): d_hidden = jnp.dot(all_cot, wd, preferred_element_type=jnp.float32)]
    unnamed x1 -> x0, blocking collectives: 78.1 us -> none
    psum x3 -> x0, waiting for transfers between devices: 48.3 us -> none  [the longest x1 19.7 us: shards(): lax.psum((contract_last(d_gate_low, wg_full) + contract_last(d_up_low, wu...]
  transfers between devices with their start and end apart: 24 -> 106, of which waited for: 21 -> 58; matrix products, arithmetic and copies ran while one was open for 5% -> 24% of each run, Pallas kernels for 0% -> 3%
where the time goes in v2:
time: 848 us; the launch traced here: 842 us
  waiting for transfers between devices  347 us (41%)
  starting transfers between devices  145 us (17%)
  other arithmetic  131 us (15%)
  local copies, waits for them, and re-layouts  104 us (12%)
  matrix products  69.4 us (8%)
  Pallas kernels  42.3 us (5%)
    ppermute x95, waiting for transfers between devices, step(): lax.ppermute(value, axis, pairs)  347 us
    ppermute x95, starting transfers between devices, step(): lax.ppermute(value, axis, pairs)  145 us
    dynamic_update_slice x17, other arithmetic, assembled(): out = lax.dynamic_update_slice(out, piece, (0, (pack ^ k) * count))  28.7 us
    unnamed x328, local copies, waits for them, and re-layouts  27.5 us
    dot_general x5, matrix products, contract_last(): lax.dot_general(left, right, (((1,), (1,)), ((), ())), preferred_element_...  24.3 us
    dot_general x5, matrix products, contract_first(): lax.dot_general(left, right, (((0,), (0,)), ((), ())), preferred_element_...  22.4 us
    pallas_call x1, Pallas kernels, attend_back(): pl.pallas_call(functools.partial(attend_back_kernel, groups), grid=(packs...  21.6 us
    convert_element_type x13, other arithmetic, add_low(): (left.astype(jnp.float32) + right.astype(jnp.float32)).astype(jnp.bfloat16)  17.7 us
  transfers between devices with their start and end apart: 106, of which 58 were waited for; matrix products, arithmetic and copies ran while one was open for 24% of the time, Pallas kernels for 3%

profile of v2, /device:TPU:0, one launch (start us, length us, event | category | flops | bytes accessed | tf_op | source)
XLA Modules:
  0.0 842.1 jit_solution(8346658360409422865)
XLA Ops:
  24.9 13.2 %collective-permute-done.1 = bf16[144,2048]{1,0:T(8,128)(2,1)} collective-permute-done((bf16[144,2048]{1,0:T(8,128)(2,1)}, bf16[144,2048]{1,0:T(8,128)(2,1)}, u32[]{:S(2)}, u32[]{:S(2)}) %collective-permute-start.1) | collective-permute-done | bytes 589856 | tf_op jit(solution)/shard_map/ppermute | solution.py:208
  46.4 4.3 pad_maximum_fusion.2
  58.5 10.3 %collective-permute-done.4 = bf16[512,640]{1,0:T(8,128)(2,1)S(1)} collective-permute-done((bf16[512,640]{1,0:T(8,128)(2,1)}, bf16[512,640]{1,0:T(8,128)(2,1)S(1)}, u32[]{:S(2)}, u32[]{:S(2)}) %collective-permute-start.4) | collective-permute-done | bytes 655392 | tf_op jit(solution)/shard_map/ppermute | solution.py:208
  68.7 13.1 %collective-permute-done.5 = bf16[512,640]{1,0:T(8,128)(2,1)S(1)} collective-permute-done((bf16[512,640]{1,0:T(8,128)(2,1)}, bf16[512,640]{1,0:T(8,128)(2,1)S(1)}, u32[]{:S(2)}, u32[]{:S(2)}) %collective-permute-start.5) | collective-permute-done | bytes 655392 | tf_op jit(solution)/shard_map/ppermute | solution.py:208
  86.8 7.7 pad_maximum_fusion.1
  94.7 3.9 constant_dynamic-update-slice_fusion.x_ref
  98.7 7.3 qkv.1
  116.4 4.0 collective-permute-start.12
  123.6 9.5 %collective-permute-done.11 = bf16[1024,128]{1,0:T(8,128)(2,1)S(1)} collective-permute-done((bf16[1024,128]{1,0:T(8,128)(2,1)S(1)}, bf16[1024,128]{1,0:T(8,128)(2,1)S(1)}, u32[]{:S(2)}, u32[]{:S(2)}) %collective-permute-start.11) | collective-permute-done | bytes 262176 | tf_op jit(solution)/shard_map/ppermute | solution.py:208
  134.8 13.4 %attend.1 = bf16[2,4,128,256]{3,2,1,0:T(8,128)(2,1)S(1)} custom-call(bf16[2,4,128,256]{3,2,1,0:T(8,128)(2,1)S(1)} %bitcast.105, s32[4,256,1]{2,1,0:T(8,128)S(1)} %copy.42.place_ref, s32[4,256,1]{2,1,0:T(8,128)S(1)} %copy.43.start_ref, s32[4,1,1024]{2,1,0:T(1,128)S(1)} %broadcast_add_fusion.key_place_ref, bf16[2,4,128,128]{3,2,1,0:T(8,128)(2,1)S(1)} %bitcast.107, ...), custom_call_target="tpu_custom_call" | custom-call | flops 671088640 | bytes 3145728 | tf_op jit(solution)/shard_map/attend/pallas_call | solution.py:365
  154.6 4.4 constant_dynamic-slice_fusion.11
  174.3 3.5 collective-permute-done.17
  177.8 9.8 %collective-permute-done.18 = bf16[128,2048]{1,0:T(8,128)(2,1)} collective-permute-done((bf16[128,2048]{1,0:T(8,128)(2,1)S(1)}, bf16[128,2048]{1,0:T(8,128)(2,1)}, u32[]{:S(2)}, u32[]{:S(2)}) %collective-permute-start.18) | collective-permute-done | bytes 524320 | tf_op jit(solution)/shard_map/ppermute | solution.py:208
  192.2 3.9 dynamic_update_slice.105
  208.8 4.5 pad_maximum_fusion.4
  213.3 3.0 collective-permute-done.21
  216.4 9.7 %collective-permute-done.22 = bf16[128,2048]{1,0:T(8,128)(2,1)S(1)} collective-permute-done((bf16[128,2048]{1,0:T(8,128)(2,1)S(1)}, bf16[128,2048]{1,0:T(8,128)(2,1)S(1)}, u32[]{:S(2)}, u32[]{:S(2)}) %collective-permute-start.22) | collective-permute-done | bytes 524320 | tf_op jit(solution)/shard_map/ppermute | solution.py:208
  237.8 6.6 collective-permute-done.27
  247.4 7.4 collective-permute-done.28
  263.3 4.5 fusion.78
  267.9 6.5 multiply_convert_fusion.1
  275.7 5.0 convolution_convert_fusion.5
  289.8 19.1 %collective-permute-done.33 = bf16[512,1024]{1,0:T(8,128)(2,1)S(1)} collective-permute-done((bf16[512,1024]{1,0:T(8,128)(2,1)S(1)}, bf16[512,1024]{1,0:T(8,128)(2,1)S(1)}, u32[]{:S(2)}, u32[]{:S(2)}) %collective-permute-start.33) | collective-permute-done | bytes 1048608 | tf_op jit(solution)/shard_map/ppermute | solution.py:208
  314.9 4.6 collective-permute-start.36
  321.4 18.2 %collective-permute-done.36 = bf16[512,1024]{1,0:T(8,128)(2,1)S(1)} collective-permute-done((bf16[512,1024]{1,0:T(8,128)(2,1)S(1)}, bf16[512,1024]{1,0:T(8,128)(2,1)S(1)}, u32[]{:S(2)}, u32[]{:S(2)}) %collective-permute-start.36) | collective-permute-done | bytes 1048608 | tf_op jit(solution)/shard_map/ppermute | solution.py:208
  339.7 3.4 collective-permute-done.38
  343.1 10.3 %multiply_convert_fusion = (bf16[1024,1024]{1,0:T(8,128)(2,1)}, bf16[1024,1024]{1,0:T(8,128)(2,1)S(1)}) fusion(f32[1024,1024]{1,0:T(8,128)} %copy-done.149, f32[1024,1024]{1,0:T(8,128)} %get-tuple-element.528, bf16[1024,2048]{1,0:T(8,128)(2,1)} %copy-done.127, bf16[512,1024]{1,0:T(8,128)(2,1)S(1)} %collective-permute-done.38, ...), kind=kOutput, calls=%fused_computation.8 | convolution fusion | flops 4326424576 | bytes 20971520 | tf_op jit(solution)/shard_map/dot_general | solution.py:624
  353.5 6.8 fusion.79
  360.3 7.0 add_convert_fusion
  381.4 19.7 %collective-permute-done.40 = bf16[512,1024]{1,0:T(8,128)(2,1)S(1)} collective-permute-done((bf16[512,1024]{1,0:T(8,128)(2,1)S(1)}, bf16[512,1024]{1,0:T(8,128)(2,1)S(1)}, u32[]{:S(2)}, u32[]{:S(2)}) %collective-permute-start.40) | collective-permute-done | bytes 1048608 | tf_op jit(solution)/shard_map/ppermute | solution.py:208
  406.8 3.3 collective-permute-start.44
  413.6 6.4 convolution_convert_fusion.3
  421.9 3.1 collective-permute-done.46
  425.0 8.7 %collective-permute-done.47 = bf16[128,2048]{1,0:T(8,128)(2,1)S(1)} collective-permute-done((bf16[128,2048]{1,0:T(8,128)(2,1)S(1)}, bf16[128,2048]{1,0:T(8,128)(2,1)S(1)}, u32[]{:S(2)}, u32[]{:S(2)}) %collective-permute-start.47) | collective-permute-done | bytes 524320 | tf_op jit(solution)/shard_map/ppermute | solution.py:208
  446.3 4.9 convolution_convert_fusion.2
  453.7 7.9 collective-permute-done.53
  461.7 5.0 collective-permute-done.49
  468.0 3.4 copy-done.14
  473.1 4.0 collective-permute-start.54
  478.8 6.7 convolution_convert_fusion.4
  488.7 11.9 %collective-permute-done.54 = bf16[512,1024]{1,0:T(8,128)(2,1)S(1)} collective-permute-done((bf16[512,1024]{1,0:T(8,128)(2,1)S(1)}, bf16[512,1024]{1,0:T(8,128)(2,1)S(1)}, u32[]{:S(2)}, u32[]{:S(2)}) %collective-permute-start.54) | collective-permute-done | bytes 1048608 | tf_op jit(solution)/shard_map/ppermute | solution.py:208
  515.4 21.6 %attend_back.1 = (bf16[2,4,128,256]{3,2,1,0:T(8,128)(2,1)S(1)}, bf16[4,2,4,128,128]{4,3,2,1,0:T(8,128)(2,1)S(1)}) custom-call(bf16[2,4,128,256]{3,2,1,0:T(8,128)(2,1)S(1)} %bitcast.106, bf16[2,4,128,256]{3,2,1,0:T(8,128)(2,1)S(1)} %bitcast.119, f32[2,4,128,128]{3,2,1,0:T(8,128)S(1)} %get-tuple-element.522.cos_ref, ...), custom_call_target="tpu_custom_call" | custom-call | flops 1677721600 | bytes 4194304 | tf_op jit(solution)/shard_map/attend_back/pallas_call | solution.py:385
  550.4 16.7 %collective-permute-done.62 = bf16[512,1024]{1,0:T(8,128)(2,1)S(1)} collective-permute-done((bf16[512,1024]{1,0:T(8,128)(2,1)S(1)}, bf16[512,1024]{1,0:T(8,128)(2,1)S(1)}, u32[]{:S(2)}, u32[]{:S(2)}) %collective-permute-start.62) | collective-permute-done | bytes 1048608 | tf_op jit(solution)/shard_map/ppermute | solution.py:208
  580.7 15.6 %collective-permute-done.66 = bf16[512,1024]{1,0:T(8,128)(2,1)S(1)} collective-permute-done((bf16[512,1024]{1,0:T(8,128)(2,1)S(1)}, bf16[512,1024]{1,0:T(8,128)(2,1)S(1)}, u32[]{:S(2)}, u32[]{:S(2)}) %collective-permute-start.66) | collective-permute-done | bytes 1048608 | tf_op jit(solution)/shard_map/ppermute | solution.py:208
  599.8 3.4 copy-done.15
  611.7 3.6 convolution_convert_fusion.7
  615.3 7.8 collective-permute-done.71
  623.1 5.3 collective-permute-done.72
  648.8 7.7 collective-permute-done.76
  656.5 3.6 convert_dynamic-update-slice_fusion.9
  661.6 3.2 collective-permute-start.78
  670.3 6.7 collective-permute-done.80
  684.4 4.2 collective-permute-start.82
  693.0 7.3 collective-permute-done.84
  708.8 3.3 collective-permute-start.85
  718.5 3.5 collective-permute-done.87
  722.1 6.3 collective-permute-done.88
  729.8 3.2 convert_dynamic-update-slice_fusion.5
  745.2 16.5 %collective-permute-done.92 = bf16[512,1024]{1,0:T(8,128)(2,1)S(1)} collective-permute-done((bf16[512,1024]{1,0:T(8,128)(2,1)S(1)}, bf16[512,1024]{1,0:T(8,128)(2,1)S(1)}, u32[]{:S(2)}, u32[]{:S(2)}) %collective-permute-start.92) | collective-permute-done | bytes 1048608 | tf_op jit(solution)/shard_map/ppermute | solution.py:208
  766.9 3.1 convert_dynamic-update-slice_fusion.4
  770.0 9.8 %collective-permute-done.99 = f32[2,512]{1,0:T(2,128)S(1)} collective-permute-done((f32[2,512]{1,0:T(2,128)S(1)}, f32[2,512]{1,0:T(2,128)S(1)}, u32[]{:S(2)}, u32[]{:S(2)}) %collective-permute-start.99) | collective-permute-done | bytes 4128 | tf_op jit(solution)/shard_map/ppermute | solution.py:208
  782.8 3.5 collective-permute-start.100
  812.3 8.0 collective-permute-done.103
  827.0 9.5 %collective-permute-done.105 = bf16[512,640]{1,0:T(8,128)(2,1)} collective-permute-done((bf16[512,640]{1,0:T(8,128)(2,1)S(1)}, bf16[512,640]{1,0:T(8,128)(2,1)}, u32[]{:S(2)}, u32[]{:S(2)}) %collective-permute-start.105) | collective-permute-done | bytes 655392 | tf_op jit(solution)/shard_map/ppermute | solution.py:208
  (700 shorter events, 354.7 us)
Async XLA Ops:
  10.4 27.7 %collective-permute-start.1 = (bf16[144,2048]{1,0:T(8,128)(2,1)}, bf16[144,2048]{1,0:T(8,128)(2,1)}, u32[]{:S(2)}, u32[]{:S(2)}) collective-permute-start(bf16[144,2048]{1,0:T(8,128)(2,1)} %get-tuple-element.163), channel_id=1, source_target_pairs={{0,16},{8,24},{16,0},{24,8},{1,17},{9,25},{17,1},{25,9},{2,18},{10... | collective-permute-start | bytes 1769480 | tf_op jit(solution)/shard_map/ppermute | solution.py:208
  12.0 26.2 %collective-permute-start.2 = (bf16[144,2048]{1,0:T(8,128)(2,1)}, bf16[144,2048]{1,0:T(8,128)(2,1)}, u32[]{:S(2)}, u32[]{:S(2)}) collective-permute-start(bf16[144,2048]{1,0:T(8,128)(2,1)} %get-tuple-element.164), channel_id=1, source_target_pairs={{0,24},{8,16},{16,8},{24,0},{1,25},{9,17},{17,9},{25,1},{2,26},{10... | collective-permute-start | bytes 1769480 | tf_op jit(solution)/shard_map/ppermute | solution.py:208
  50.7 44.0 %collective-permute-start.3 = (bf16[512,2048]{1,0:T(8,128)(2,1)}, bf16[512,2048]{1,0:T(8,128)(2,1)}, u32[]{:S(2)}, u32[]{:S(2)}) collective-permute-start(bf16[512,2048]{1,0:T(8,128)(2,1)} %pad_maximum_fusion.2), channel_id=1, source_target_pairs={{0,1},{1,0},{2,3},{3,2},{4,5},{5,4},{6,7},{7,6},{8,9},{9,8},{10,11... | collective-permute-start | bytes 6291464 | tf_op jit(solution)/shard_map/ppermute | solution.py:82
  52.2 29.6 %collective-permute-start.5 = (bf16[512,640]{1,0:T(8,128)(2,1)}, bf16[512,640]{1,0:T(8,128)(2,1)S(1)}, u32[]{:S(2)}, u32[]{:S(2)}) collective-permute-start(bf16[512,640]{1,0:T(8,128)(2,1)} %pad_maximum_fusion.17), channel_id=1, source_target_pairs={{0,16},{8,24},{16,0},{24,8},{1,17},{9,25},{17,1},{25,9},{2,18},{10... | collective-permute-start | bytes 1966088 | tf_op jit(solution)/shard_map/ppermute | solution.py:208
  53.0 30.3 %collective-permute-start.6 = (bf16[512,640]{1,0:T(8,128)(2,1)}, bf16[512,640]{1,0:T(8,128)(2,1)S(1)}, u32[]{:S(2)}, u32[]{:S(2)}) collective-permute-start(bf16[512,640]{1,0:T(8,128)(2,1)} %pad_maximum_fusion.18), channel_id=1, source_target_pairs={{0,24},{8,16},{16,8},{24,0},{1,25},{9,17},{17,9},{25,1},{2,26},{10... | collective-permute-start | bytes 1966088 | tf_op jit(solution)/shard_map/ppermute | solution.py:208
  83.3 22.7 %collective-permute-start.7 = (bf16[512,512]{1,0:T(8,128)(2,1)}, bf16[512,512]{1,0:T(8,128)(2,1)S(1)}, u32[]{:S(2)}, u32[]{:S(2)}) collective-permute-start(bf16[512,512]{1,0:T(8,128)(2,1)} %get-tuple-element.176), channel_id=1, source_target_pairs={{0,8},{8,0},{16,24},{24,16},{1,9},{9,1},{17,25},{25,17},{2,10},{10... | collective-permute-start | bytes 1572872 | tf_op jit(solution)/shard_map/ppermute | solution.py:208
  84.2 24.4 %collective-permute-start.8 = (bf16[512,512]{1,0:T(8,128)(2,1)}, bf16[512,512]{1,0:T(8,128)(2,1)S(1)}, u32[]{:S(2)}, u32[]{:S(2)}) collective-permute-start(bf16[512,512]{1,0:T(8,128)(2,1)} %get-tuple-element.177), channel_id=1, source_target_pairs={{0,16},{8,24},{16,0},{24,8},{1,17},{9,25},{17,1},{25,9},{2,18},{10... | collective-permute-start | bytes 1572872 | tf_op jit(solution)/shard_map/ppermute | solution.py:208
  85.7 22.9 %collective-permute-start.9 = (bf16[512,512]{1,0:T(8,128)(2,1)}, bf16[512,512]{1,0:T(8,128)(2,1)S(1)}, u32[]{:S(2)}, u32[]{:S(2)}) collective-permute-start(bf16[512,512]{1,0:T(8,128)(2,1)} %get-tuple-element.178), channel_id=1, source_target_pairs={{0,24},{8,16},{16,8},{24,0},{1,25},{9,17},{17,9},{25,1},{2,26},{10... | collective-permute-start | bytes 1572872 | tf_op jit(solution)/shard_map/ppermute | solution.py:208
  110.3 22.9 %collective-permute-start.13 = (bf16[512,512]{1,0:T(8,128)(2,1)}, bf16[512,512]{1,0:T(8,128)(2,1)}, u32[]{:S(2)}, u32[]{:S(2)}) collective-permute-start(bf16[512,512]{1,0:T(8,128)(2,1)} %get-tuple-element.182), channel_id=1, source_target_pairs={{0,8},{8,0},{16,24},{24,16},{1,9},{9,1},{17,25},{25,17},{2,10},{10... | collective-permute-start | bytes 1572872 | tf_op jit(solution)/shard_map/ppermute | solution.py:208
  111.7 21.4 %collective-permute-start.14 = (bf16[512,512]{1,0:T(8,128)(2,1)}, bf16[512,512]{1,0:T(8,128)(2,1)}, u32[]{:S(2)}, u32[]{:S(2)}) collective-permute-start(bf16[512,512]{1,0:T(8,128)(2,1)} %get-tuple-element.183), channel_id=1, source_target_pairs={{0,16},{8,24},{16,0},{24,8},{1,17},{9,25},{17,1},{25,9},{2,18},{10... | collective-permute-start | bytes 1572872 | tf_op jit(solution)/shard_map/ppermute | solution.py:208
  112.3 22.5 %collective-permute-start.15 = (bf16[512,512]{1,0:T(8,128)(2,1)}, bf16[512,512]{1,0:T(8,128)(2,1)}, u32[]{:S(2)}, u32[]{:S(2)}) collective-permute-start(bf16[512,512]{1,0:T(8,128)(2,1)} %get-tuple-element.184), channel_id=1, source_target_pairs={{0,24},{8,16},{16,8},{24,0},{1,25},{9,17},{17,9},{25,1},{2,26},{10... | collective-permute-start | bytes 1572872 | tf_op jit(solution)/shard_map/ppermute | solution.py:208
  113.8 19.4 %collective-permute-start.11 = (bf16[1024,128]{1,0:T(8,128)(2,1)S(1)}, bf16[1024,128]{1,0:T(8,128)(2,1)S(1)}, u32[]{:S(2)}, u32[]{:S(2)}) collective-permute-start(bf16[1024,128]{1,0:T(8,128)(2,1)S(1)} %get-tuple-element.181), channel_id=1, source_target_pairs={{0,4},{2,6},{4,0},{6,2},{1,5},{3,7},{5,1},{7,3},{8,12},{10,14},{12... | collective-permute-start | bytes 786440 | tf_op jit(solution)/shard_map/ppermute | solution.py:208
  160.3 29.3 %collective-permute-start.20 = (bf16[512,1024]{1,0:T(8,128)(2,1)S(1)}, bf16[512,1024]{1,0:T(8,128)(2,1)}, u32[]{:S(2)}, u32[]{:S(2)}) collective-permute-start(bf16[512,1024]{1,0:T(8,128)(2,1)S(1)} %pad_maximum_fusion.7), channel_id=1, source_target_pairs={{0,2},{2,0},{4,6},{6,4},{1,3},{3,1},{5,7},{7,5},{8,10},{10,8},{12,... | collective-permute-start | bytes 3145736 | tf_op jit(solution)/shard_map/ppermute | solution.py:208
  163.9 23.8 %collective-permute-start.18 = (bf16[128,2048]{1,0:T(8,128)(2,1)S(1)}, bf16[128,2048]{1,0:T(8,128)(2,1)}, u32[]{:S(2)}, u32[]{:S(2)}) collective-permute-start(bf16[128,2048]{1,0:T(8,128)(2,1)S(1)} %copy-done.108), channel_id=1, source_target_pairs={{0,16},{8,24},{16,0},{24,8},{1,17},{9,25},{17,1},{25,9},{2,18},{10... | collective-permute-start | bytes 1572872 | tf_op jit(solution)/shard_map/ppermute | solution.py:208
  165.1 24.5 %collective-permute-start.19 = (bf16[128,2048]{1,0:T(8,128)(2,1)S(1)}, bf16[128,2048]{1,0:T(8,128)(2,1)}, u32[]{:S(2)}, u32[]{:S(2)}) collective-permute-start(bf16[128,2048]{1,0:T(8,128)(2,1)S(1)} %copy-done.107), channel_id=1, source_target_pairs={{0,24},{8,16},{16,8},{24,0},{1,25},{9,17},{17,9},{25,1},{2,26},{10... | collective-permute-start | bytes 1572872 | tf_op jit(solution)/shard_map/ppermute | solution.py:208
  189.6 36.5 %collective-permute-start.24 = (bf16[512,1024]{1,0:T(8,128)(2,1)}, bf16[512,1024]{1,0:T(8,128)(2,1)}, u32[]{:S(2)}, u32[]{:S(2)}) collective-permute-start(bf16[512,1024]{1,0:T(8,128)(2,1)} %pad_maximum_fusion.8), channel_id=1, source_target_pairs={{0,2},{2,0},{4,6},{6,4},{1,3},{3,1},{5,7},{7,5},{8,10},{10,8},{12,... | collective-permute-start | bytes 3145736 | tf_op jit(solution)/shard_map/ppermute | solution.py:208
  202.1 24.0 %collective-permute-start.22 = (bf16[128,2048]{1,0:T(8,128)(2,1)S(1)}, bf16[128,2048]{1,0:T(8,128)(2,1)S(1)}, u32[]{:S(2)}, u32[]{:S(2)}) collective-permute-start(bf16[128,2048]{1,0:T(8,128)(2,1)S(1)} %copy-done.115), channel_id=1, source_target_pairs={{0,16},{8,24},{16,0},{24,8},{1,17},{9,25},{17,1},{25,9},{2,18},{10... | collective-permute-start | bytes 1572872 | tf_op jit(solution)/shard_map/ppermute | solution.py:208
  203.8 22.3 %collective-permute-start.23 = (bf16[128,2048]{1,0:T(8,128)(2,1)S(1)}, bf16[128,2048]{1,0:T(8,128)(2,1)S(1)}, u32[]{:S(2)}, u32[]{:S(2)}) collective-permute-start(bf16[128,2048]{1,0:T(8,128)(2,1)S(1)} %copy-done.114), channel_id=1, source_target_pairs={{0,24},{8,16},{16,8},{24,0},{1,25},{9,17},{17,9},{25,1},{2,26},{10... | collective-permute-start | bytes 1572872 | tf_op jit(solution)/shard_map/ppermute | solution.py:208
  213.2 49.6 %collective-permute-start.32 = (bf16[512,2048]{1,0:T(8,128)(2,1)S(1)}, bf16[512,2048]{1,0:T(8,128)(2,1)S(1)}, u32[]{:S(2)}, u32[]{:S(2)}) collective-permute-start(bf16[512,2048]{1,0:T(8,128)(2,1)S(1)} %pad_maximum_fusion.4), channel_id=1, source_target_pairs={{0,1},{1,0},{2,3},{3,2},{4,5},{5,4},{6,7},{7,6},{8,9},{9,8},{10,11... | collective-permute-start | bytes 6291464 | tf_op jit(solution)/shard_map/ppermute | solution.py:82
  229.2 25.5 %collective-permute-start.25 = (bf16[512,1024]{1,0:T(8,128)(2,1)S(1)}, bf16[512,1024]{1,0:T(8,128)(2,1)S(1)}, u32[]{:S(2)}, u32[]{:S(2)}) collective-permute-start(bf16[512,1024]{1,0:T(8,128)(2,1)S(1)} %pad_maximum_fusion.9), channel_id=1, source_target_pairs={{0,2},{2,0},{4,6},{6,4},{1,3},{3,1},{5,7},{7,5},{8,10},{10,8},{12,... | collective-permute-start | bytes 3145736 | tf_op jit(solution)/shard_map/ppermute | solution.py:208
  232.9 21.9 %collective-permute-start.28 = (bf16[128,2048]{1,0:T(8,128)(2,1)S(1)}, bf16[128,2048]{1,0:T(8,128)(2,1)S(1)}, u32[]{:S(2)}, u32[]{:S(2)}) collective-permute-start(bf16[128,2048]{1,0:T(8,128)(2,1)S(1)} %get-tuple-element.496), channel_id=1, source_target_pairs={{0,24},{8,16},{16,8},{24,0},{1,25},{9,17},{17,9},{25,1},{2,26},{10... | collective-permute-start | bytes 1572872 | tf_op jit(solution)/shard_map/ppermute | solution.py:208
  258.0 25.3 %collective-permute-start.30 = (bf16[512,1024]{1,0:T(8,128)(2,1)S(1)}, bf16[512,1024]{1,0:T(8,128)(2,1)S(1)}, u32[]{:S(2)}, u32[]{:S(2)}) collective-permute-start(bf16[512,1024]{1,0:T(8,128)(2,1)S(1)} %copy-done.81), channel_id=1, source_target_pairs={{0,8},{8,0},{16,24},{24,16},{1,9},{9,1},{17,25},{25,17},{2,10},{10... | collective-permute-start | bytes 3145736 | tf_op jit(solution)/shard_map/ppermute | solution.py:208
  259.4 24.9 %collective-permute-start.31 = (bf16[512,1024]{1,0:T(8,128)(2,1)S(1)}, bf16[512,1024]{1,0:T(8,128)(2,1)S(1)}, u32[]{:S(2)}, u32[]{:S(2)}) collective-permute-start(bf16[512,1024]{1,0:T(8,128)(2,1)S(1)} %copy-done.80), channel_id=1, source_target_pairs={{0,16},{8,24},{16,0},{24,8},{1,17},{9,25},{17,1},{25,9},{2,18},{10... | collective-permute-start | bytes 3145736 | tf_op jit(solution)/shard_map/ppermute | solution.py:208
  284.4 24.5 %collective-permute-start.33 = (bf16[512,1024]{1,0:T(8,128)(2,1)S(1)}, bf16[512,1024]{1,0:T(8,128)(2,1)S(1)}, u32[]{:S(2)}, u32[]{:S(2)}) collective-permute-start(bf16[512,1024]{1,0:T(8,128)(2,1)S(1)} %get-tuple-element.218), channel_id=1, source_target_pairs={{0,2},{6,4},{1,3},{7,5},{8,10},{14,12},{9,11},{15,13},{16,18},{22,... | collective-permute-start | bytes 3145736 | tf_op jit(solution)/shard_map/ppermute | solution.py:208
  287.4 23.9 %collective-permute-start.34 = (bf16[512,1024]{1,0:T(8,128)(2,1)S(1)}, bf16[512,1024]{1,0:T(8,128)(2,1)S(1)}, u32[]{:S(2)}, u32[]{:S(2)}) collective-permute-start(bf16[512,1024]{1,0:T(8,128)(2,1)S(1)} %get-tuple-element.219), channel_id=1, source_target_pairs={{0,8},{8,0},{16,24},{24,16},{1,9},{9,1},{17,25},{25,17},{2,10},{10... | collective-permute-start | bytes 3145736 | tf_op jit(solution)/shard_map/ppermute | solution.py:208
  288.1 23.7 %collective-permute-start.35 = (bf16[512,1024]{1,0:T(8,128)(2,1)S(1)}, bf16[512,1024]{1,0:T(8,128)(2,1)S(1)}, u32[]{:S(2)}, u32[]{:S(2)}) collective-permute-start(bf16[512,1024]{1,0:T(8,128)(2,1)S(1)} %get-tuple-element.220), channel_id=1, source_target_pairs={{0,16},{8,24},{16,0},{24,8},{1,17},{9,25},{17,1},{25,9},{2,18},{10... | collective-permute-start | bytes 3145736 | tf_op jit(solution)/shard_map/ppermute | solution.py:208
  314.9 24.8 %collective-permute-start.36 = (bf16[512,1024]{1,0:T(8,128)(2,1)S(1)}, bf16[512,1024]{1,0:T(8,128)(2,1)S(1)}, u32[]{:S(2)}, u32[]{:S(2)}) collective-permute-start(bf16[512,1024]{1,0:T(8,128)(2,1)S(1)} %collective-permute-done.34), channel_id=1, source_target_pairs={{0,2},{6,4},{1,3},{7,5},{8,10},{14,12},{9,11},{15,13},{16,18},{22,... | collective-permute-start | bytes 3145736 | tf_op jit(solution)/shard_map/ppermute | solution.py:208
  319.5 23.6 %collective-permute-start.38 = (bf16[512,1024]{1,0:T(8,128)(2,1)S(1)}, bf16[512,1024]{1,0:T(8,128)(2,1)S(1)}, u32[]{:S(2)}, u32[]{:S(2)}) collective-permute-start(bf16[512,1024]{1,0:T(8,128)(2,1)S(1)} %copy-done.79), channel_id=1, source_target_pairs={{0,24},{8,16},{16,8},{24,0},{1,25},{9,17},{17,9},{25,1},{2,26},{10... | collective-permute-start | bytes 3145736 | tf_op jit(solution)/shard_map/ppermute | solution.py:208
  375.5 25.6 %collective-permute-start.40 = (bf16[512,1024]{1,0:T(8,128)(2,1)S(1)}, bf16[512,1024]{1,0:T(8,128)(2,1)S(1)}, u32[]{:S(2)}, u32[]{:S(2)}) collective-permute-start(bf16[512,1024]{1,0:T(8,128)(2,1)S(1)} %broadcast_select_fusion.11), channel_id=1, source_target_pairs={{0,2},{2,0},{6,4},{4,6},{1,3},{3,1},{7,5},{5,7},{8,10},{10,8},{14,... | collective-permute-start | bytes 3145736 | tf_op jit(solution)/shard_map/ppermute | solution.py:208
  376.9 25.9 %collective-permute-start.42 = (bf16[512,1024]{1,0:T(8,128)(2,1)S(1)}, bf16[512,1024]{1,0:T(8,128)(2,1)S(1)}, u32[]{:S(2)}, u32[]{:S(2)}) collective-permute-start(bf16[512,1024]{1,0:T(8,128)(2,1)S(1)} %copy-done.91), channel_id=1, source_target_pairs={{0,24},{8,16},{16,8},{24,0},{1,25},{9,17},{17,9},{25,1},{2,26},{10... | collective-permute-start | bytes 3145736 | tf_op jit(solution)/shard_map/ppermute | solution.py:208
  404.9 29.9 %collective-permute-start.45 = (bf16[512,1024]{1,0:T(8,128)(2,1)S(1)}, bf16[512,1024]{1,0:T(8,128)(2,1)S(1)}, u32[]{:S(2)}, u32[]{:S(2)}) collective-permute-start(bf16[512,1024]{1,0:T(8,128)(2,1)S(1)} %get-tuple-element.407), channel_id=1, source_target_pairs={{2,4},{4,2},{3,5},{5,3},{10,12},{12,10},{11,13},{13,11},{18,20},{2... | collective-permute-start | bytes 3145736 | tf_op jit(solution)/shard_map/ppermute | solution.py:208
  406.8 28.0 %collective-permute-start.44 = (bf16[512,1024]{1,0:T(8,128)(2,1)S(1)}, bf16[512,1024]{1,0:T(8,128)(2,1)S(1)}, u32[]{:S(2)}, u32[]{:S(2)}) collective-permute-start(bf16[512,1024]{1,0:T(8,128)(2,1)S(1)} %broadcast_select_fusion.10), channel_id=1, source_target_pairs={{0,2},{2,0},{6,4},{4,6},{1,3},{3,1},{7,5},{5,7},{8,10},{10,8},{14,... | collective-permute-start | bytes 3145736 | tf_op jit(solution)/shard_map/ppermute | solution.py:208
  411.1 22.6 %collective-permute-start.47 = (bf16[128,2048]{1,0:T(8,128)(2,1)S(1)}, bf16[128,2048]{1,0:T(8,128)(2,1)S(1)}, u32[]{:S(2)}, u32[]{:S(2)}) collective-permute-start(bf16[128,2048]{1,0:T(8,128)(2,1)S(1)} %pad_maximum_fusion.31), channel_id=1, source_target_pairs={{0,16},{8,24},{16,0},{24,8},{1,17},{9,25},{17,1},{25,9},{2,18},{10... | collective-permute-start | bytes 1572872 | tf_op jit(solution)/shard_map/ppermute | solution.py:208
  412.5 22.3 %collective-permute-start.48 = (bf16[128,2048]{1,0:T(8,128)(2,1)S(1)}, bf16[128,2048]{1,0:T(8,128)(2,1)S(1)}, u32[]{:S(2)}, u32[]{:S(2)}) collective-permute-start(bf16[128,2048]{1,0:T(8,128)(2,1)S(1)} %pad_maximum_fusion.32), channel_id=1, source_target_pairs={{0,24},{8,16},{16,8},{24,0},{1,25},{9,17},{17,9},{25,1},{2,26},{10... | collective-permute-start | bytes 1572872 | tf_op jit(solution)/shard_map/ppermute | solution.py:208
  439.8 21.8 %collective-permute-start.53 = (bf16[128,2048]{1,0:T(8,128)(2,1)S(1)}, bf16[128,2048]{1,0:T(8,128)(2,1)S(1)}, u32[]{:S(2)}, u32[]{:S(2)}) collective-permute-start(bf16[128,2048]{1,0:T(8,128)(2,1)S(1)} %get-tuple-element.484), channel_id=1, source_target_pairs={{0,24},{8,16},{16,8},{24,0},{1,25},{9,17},{17,9},{25,1},{2,26},{10... | collective-permute-start | bytes 1572872 | tf_op jit(solution)/shard_map/ppermute | solution.py:208
  442.0 19.6 %collective-permute-start.50 = (bf16[512,1024]{1,0:T(8,128)(2,1)S(1)}, bf16[512,1024]{1,0:T(8,128)(2,1)S(1)}, u32[]{:S(2)}, u32[]{:S(2)}) collective-permute-start(bf16[512,1024]{1,0:T(8,128)(2,1)S(1)} %get-tuple-element.405), channel_id=1, source_target_pairs={{2,4},{4,2},{3,5},{5,3},{10,12},{12,10},{11,13},{13,11},{18,20},{2... | collective-permute-start | bytes 3145736 | tf_op jit(solution)/shard_map/ppermute | solution.py:208
  443.5 23.2 %collective-permute-start.49 = (bf16[512,1024]{1,0:T(8,128)(2,1)S(1)}, bf16[512,1024]{1,0:T(8,128)(2,1)S(1)}, u32[]{:S(2)}, u32[]{:S(2)}) collective-permute-start(bf16[512,1024]{1,0:T(8,128)(2,1)S(1)} %broadcast_select_fusion.9), channel_id=1, source_target_pairs={{0,2},{2,0},{6,4},{4,6},{1,3},{3,1},{7,5},{5,7},{8,10},{10,8},{14,... | collective-permute-start | bytes 3145736 | tf_op jit(solution)/shard_map/ppermute | solution.py:208
  466.9 44.6 %collective-permute-start.61 = (bf16[512,2048]{1,0:T(8,128)(2,1)S(1)}, bf16[512,2048]{1,0:T(8,128)(2,1)}, u32[]{:S(2)}, u32[]{:S(2)}) collective-permute-start(bf16[512,2048]{1,0:T(8,128)(2,1)S(1)} %pad_maximum_fusion.5), channel_id=1, source_target_pairs={{0,1},{1,0},{2,3},{3,2},{4,5},{5,4},{6,7},{7,6},{8,9},{9,8},{10,11... | collective-permute-start | bytes 6291464 | tf_op jit(solution)/shard_map/ppermute | solution.py:82
  473.1 27.5 %collective-permute-start.54 = (bf16[512,1024]{1,0:T(8,128)(2,1)S(1)}, bf16[512,1024]{1,0:T(8,128)(2,1)S(1)}, u32[]{:S(2)}, u32[]{:S(2)}) collective-permute-start(bf16[512,1024]{1,0:T(8,128)(2,1)S(1)} %broadcast_select_fusion.8), channel_id=1, source_target_pairs={{0,2},{2,0},{6,4},{4,6},{1,3},{3,1},{7,5},{5,7},{8,10},{10,8},{14,... | collective-permute-start | bytes 3145736 | tf_op jit(solution)/shard_map/ppermute | solution.py:208
  477.1 25.2 %collective-permute-start.56 = (bf16[512,1024]{1,0:T(8,128)(2,1)}, bf16[512,1024]{1,0:T(8,128)(2,1)S(1)}, u32[]{:S(2)}, u32[]{:S(2)}) collective-permute-start(bf16[512,1024]{1,0:T(8,128)(2,1)} %get-tuple-element.244), channel_id=1, source_target_pairs={{0,8},{8,0},{16,24},{24,16},{1,9},{9,1},{17,25},{25,17},{2,10},{10... | collective-permute-start | bytes 3145736 | tf_op jit(solution)/shard_map/ppermute | solution.py:208
  478.1 24.9 %collective-permute-start.57 = (bf16[512,1024]{1,0:T(8,128)(2,1)}, bf16[512,1024]{1,0:T(8,128)(2,1)S(1)}, u32[]{:S(2)}, u32[]{:S(2)}) collective-permute-start(bf16[512,1024]{1,0:T(8,128)(2,1)} %get-tuple-element.245), channel_id=1, source_target_pairs={{0,16},{8,24},{16,0},{24,8},{1,17},{9,25},{17,1},{25,9},{2,18},{10... | collective-permute-start | bytes 3145736 | tf_op jit(solution)/shard_map/ppermute | solution.py:208
  488.6 59.3 %collective-permute-start.39 = (bf16[512,2048]{1,0:T(8,128)(2,1)}, bf16[512,2048]{1,0:T(8,128)(2,1)}, u32[]{:S(2)}, u32[]{:S(2)}) collective-permute-start(bf16[512,2048]{1,0:T(8,128)(2,1)} %slice.757), channel_id=1, source_target_pairs={{0,1},{1,0},{2,3},{3,2},{4,5},{5,4},{6,7},{7,6},{8,9},{9,8},{10,11... | collective-permute-start | bytes 6291464 | tf_op jit(solution)/shard_map/ppermute | solution.py:82
  505.3 32.1 %collective-permute-start.59 = (bf16[512,1024]{1,0:T(8,128)(2,1)S(1)}, bf16[512,1024]{1,0:T(8,128)(2,1)S(1)}, u32[]{:S(2)}, u32[]{:S(2)}) collective-permute-start(bf16[512,1024]{1,0:T(8,128)(2,1)S(1)} %get-tuple-element.401), channel_id=1, source_target_pairs={{2,4},{4,2},{3,5},{5,3},{10,12},{12,10},{11,13},{13,11},{18,20},{2... | collective-permute-start | bytes 3145736 | tf_op jit(solution)/shard_map/ppermute | solution.py:208
  507.7 29.8 %collective-permute-start.58 = (bf16[512,1024]{1,0:T(8,128)(2,1)}, bf16[512,1024]{1,0:T(8,128)(2,1)}, u32[]{:S(2)}, u32[]{:S(2)}) collective-permute-start(bf16[512,1024]{1,0:T(8,128)(2,1)} %broadcast_select_fusion.7), channel_id=1, source_target_pairs={{0,2},{2,0},{6,4},{4,6},{1,3},{3,1},{7,5},{5,7},{8,10},{10,8},{14,... | collective-permute-start | bytes 3145736 | tf_op jit(solution)/shard_map/ppermute | solution.py:208
  510.3 27.2 %collective-permute-start.60 = (bf16[512,1024]{1,0:T(8,128)(2,1)}, bf16[512,1024]{1,0:T(8,128)(2,1)S(1)}, u32[]{:S(2)}, u32[]{:S(2)}) collective-permute-start(bf16[512,1024]{1,0:T(8,128)(2,1)} %get-tuple-element.249), channel_id=1, source_target_pairs={{0,24},{8,16},{16,8},{24,0},{1,25},{9,17},{17,9},{25,1},{2,26},{10... | collective-permute-start | bytes 3145736 | tf_op jit(solution)/shard_map/ppermute | solution.py:208
  543.2 23.9 %collective-permute-start.62 = (bf16[512,1024]{1,0:T(8,128)(2,1)S(1)}, bf16[512,1024]{1,0:T(8,128)(2,1)S(1)}, u32[]{:S(2)}, u32[]{:S(2)}) collective-permute-start(bf16[512,1024]{1,0:T(8,128)(2,1)S(1)} %broadcast_select_fusion.6), channel_id=1, source_target_pairs={{0,2},{2,0},{6,4},{4,6},{1,3},{3,1},{7,5},{5,7},{8,10},{10,8},{14,... | collective-permute-start | bytes 3145736 | tf_op jit(solution)/shard_map/ppermute | solution.py:208
  545.6 23.0 %collective-permute-start.64 = (bf16[512,1024]{1,0:T(8,128)(2,1)S(1)}, bf16[512,1024]{1,0:T(8,128)(2,1)S(1)}, u32[]{:S(2)}, u32[]{:S(2)}) collective-permute-start(bf16[512,1024]{1,0:T(8,128)(2,1)S(1)} %copy-done.90), channel_id=1, source_target_pairs={{0,8},{8,0},{16,24},{24,16},{1,9},{9,1},{17,25},{25,17},{2,10},{10... | collective-permute-start | bytes 3145736 | tf_op jit(solution)/shard_map/ppermute | solution.py:208
  546.6 22.7 %collective-permute-start.65 = (bf16[512,1024]{1,0:T(8,128)(2,1)S(1)}, bf16[512,1024]{1,0:T(8,128)(2,1)S(1)}, u32[]{:S(2)}, u32[]{:S(2)}) collective-permute-start(bf16[512,1024]{1,0:T(8,128)(2,1)S(1)} %copy-done.89), channel_id=1, source_target_pairs={{0,16},{8,24},{16,0},{24,8},{1,17},{9,25},{17,1},{25,9},{2,18},{10... | collective-permute-start | bytes 3145736 | tf_op jit(solution)/shard_map/ppermute | solution.py:208
  573.5 22.8 %collective-permute-start.66 = (bf16[512,1024]{1,0:T(8,128)(2,1)S(1)}, bf16[512,1024]{1,0:T(8,128)(2,1)S(1)}, u32[]{:S(2)}, u32[]{:S(2)}) collective-permute-start(bf16[512,1024]{1,0:T(8,128)(2,1)S(1)} %broadcast_select_fusion.5), channel_id=1, source_target_pairs={{0,2},{2,0},{6,4},{4,6},{1,3},{3,1},{7,5},{5,7},{8,10},{10,8},{14,... | collective-permute-start | bytes 3145736 | tf_op jit(solution)/shard_map/ppermute | solution.py:208
  576.2 22.5 %collective-permute-start.68 = (bf16[512,1024]{1,0:T(8,128)(2,1)S(1)}, bf16[512,1024]{1,0:T(8,128)(2,1)S(1)}, u32[]{:S(2)}, u32[]{:S(2)}) collective-permute-start(bf16[512,1024]{1,0:T(8,128)(2,1)S(1)} %copy-done.88), channel_id=1, source_target_pairs={{0,24},{8,16},{16,8},{24,0},{1,25},{9,17},{17,9},{25,1},{2,26},{10... | collective-permute-start | bytes 3145736 | tf_op jit(solution)/shard_map/ppermute | solution.py:208
  603.1 26.5 %collective-permute-start.70 = (bf16[512,1024]{1,0:T(8,128)(2,1)S(1)}, bf16[512,1024]{1,0:T(8,128)(2,1)}, u32[]{:S(2)}, u32[]{:S(2)}) collective-permute-start(bf16[512,1024]{1,0:T(8,128)(2,1)S(1)} %get-tuple-element.417), channel_id=1, source_target_pairs={{2,4},{4,2},{3,5},{5,3},{10,12},{12,10},{11,13},{13,11},{18,20},{2... | collective-permute-start | bytes 3145736 | tf_op jit(solution)/shard_map/ppermute | solution.py:208
  606.5 23.1 %collective-permute-start.69 = (bf16[512,1024]{1,0:T(8,128)(2,1)}, bf16[512,1024]{1,0:T(8,128)(2,1)}, u32[]{:S(2)}, u32[]{:S(2)}) collective-permute-start(bf16[512,1024]{1,0:T(8,128)(2,1)} %broadcast_select_fusion.4), channel_id=1, source_target_pairs={{0,2},{2,0},{6,4},{4,6},{1,3},{3,1},{7,5},{5,7},{8,10},{10,8},{14,... | collective-permute-start | bytes 3145736 | tf_op jit(solution)/shard_map/ppermute | solution.py:208
  609.2 19.2 %collective-permute-start.72 = (bf16[128,2048]{1,0:T(8,128)(2,1)}, bf16[128,2048]{1,0:T(8,128)(2,1)S(1)}, u32[]{:S(2)}, u32[]{:S(2)}) collective-permute-start(bf16[128,2048]{1,0:T(8,128)(2,1)} %pad_maximum_fusion.37), channel_id=1, source_target_pairs={{0,16},{8,24},{16,0},{24,8},{1,17},{9,25},{17,1},{25,9},{2,18},{10... | collective-permute-start | bytes 1572872 | tf_op jit(solution)/shard_map/ppermute | solution.py:208
  610.5 19.2 %collective-permute-start.73 = (bf16[128,2048]{1,0:T(8,128)(2,1)}, bf16[128,2048]{1,0:T(8,128)(2,1)S(1)}, u32[]{:S(2)}, u32[]{:S(2)}) collective-permute-start(bf16[128,2048]{1,0:T(8,128)(2,1)} %pad_maximum_fusion.38), channel_id=1, source_target_pairs={{0,24},{8,16},{16,8},{24,0},{1,25},{9,17},{17,9},{25,1},{2,26},{10... | collective-permute-start | bytes 1572872 | tf_op jit(solution)/shard_map/ppermute | solution.py:208
  637.4 19.1 %collective-permute-start.76 = (bf16[512,1024]{1,0:T(8,128)(2,1)S(1)}, bf16[512,1024]{1,0:T(8,128)(2,1)S(1)}, u32[]{:S(2)}, u32[]{:S(2)}) collective-permute-start(bf16[512,1024]{1,0:T(8,128)(2,1)S(1)} %broadcast_select_fusion.2), channel_id=1, source_target_pairs={{0,2},{2,0},{6,4},{4,6},{1,3},{3,1},{7,5},{5,7},{8,10},{10,8},{14,... | collective-permute-start | bytes 3145736 | tf_op jit(solution)/shard_map/ppermute | solution.py:208
  644.1 25.2 %collective-permute-start.75 = (bf16[512,2048]{1,0:T(8,128)(2,1)S(1)}, bf16[512,2048]{1,0:T(8,128)(2,1)S(1)}, u32[]{:S(2)}, u32[]{:S(2)}) collective-permute-start(bf16[512,2048]{1,0:T(8,128)(2,1)S(1)} %slice.801), channel_id=1, source_target_pairs={{0,1},{1,0},{2,3},{3,2},{4,5},{5,4},{6,7},{7,6},{8,9},{9,8},{10,11... | collective-permute-start | bytes 6291464 | tf_op jit(solution)/shard_map/ppermute | solution.py:82
  660.1 18.0 %collective-permute-start.79 = (bf16[512,1024]{1,0:T(8,128)(2,1)S(1)}, bf16[512,1024]{1,0:T(8,128)(2,1)S(1)}, u32[]{:S(2)}, u32[]{:S(2)}) collective-permute-start(bf16[512,1024]{1,0:T(8,128)(2,1)S(1)} %get-tuple-element.415), channel_id=1, source_target_pairs={{2,4},{4,2},{3,5},{5,3},{10,12},{12,10},{11,13},{13,11},{18,20},{2... | collective-permute-start | bytes 3145736 | tf_op jit(solution)/shard_map/ppermute | solution.py:208
  661.6 19.0 %collective-permute-start.78 = (bf16[512,1024]{1,0:T(8,128)(2,1)S(1)}, bf16[512,1024]{1,0:T(8,128)(2,1)S(1)}, u32[]{:S(2)}, u32[]{:S(2)}) collective-permute-start(bf16[512,1024]{1,0:T(8,128)(2,1)S(1)} %broadcast_select_fusion.1), channel_id=1, source_target_pairs={{0,2},{2,0},{6,4},{4,6},{1,3},{3,1},{7,5},{5,7},{8,10},{10,8},{14,... | collective-permute-start | bytes 3145736 | tf_op jit(solution)/shard_map/ppermute | solution.py:208
  669.3 45.8 %collective-permute-start.74 = (bf16[128,2048]{1,0:T(8,128)(2,1)}, bf16[128,2048]{1,0:T(8,128)(2,1)}, u32[]{:S(2)}, u32[]{:S(2)}) collective-permute-start(bf16[128,2048]{1,0:T(8,128)(2,1)} %pad_maximum_fusion.39), channel_id=1, source_target_pairs={{0,1},{1,0},{2,3},{3,2},{4,5},{5,4},{6,7},{7,6},{8,9},{9,8},{10,11... | collective-permute-start | bytes 1572872 | tf_op jit(solution)/shard_map/ppermute | solution.py:82
  684.4 18.9 %collective-permute-start.82 = (bf16[512,1024]{1,0:T(8,128)(2,1)S(1)}, bf16[512,1024]{1,0:T(8,128)(2,1)S(1)}, u32[]{:S(2)}, u32[]{:S(2)}) collective-permute-start(bf16[512,1024]{1,0:T(8,128)(2,1)S(1)} %broadcast_select_fusion), channel_id=1, source_target_pairs={{0,2},{2,0},{6,4},{4,6},{1,3},{3,1},{7,5},{5,7},{8,10},{10,8},{14,... | collective-permute-start | bytes 3145736 | tf_op jit(solution)/shard_map/ppermute | solution.py:208
  705.6 22.9 %collective-permute-start.86 = (bf16[512,1024]{1,0:T(8,128)(2,1)S(1)}, bf16[512,1024]{1,0:T(8,128)(2,1)}, u32[]{:S(2)}, u32[]{:S(2)}) collective-permute-start(bf16[512,1024]{1,0:T(8,128)(2,1)S(1)} %get-tuple-element.409), channel_id=1, source_target_pairs={{2,4},{4,2},{3,5},{5,3},{10,12},{12,10},{11,13},{13,11},{18,20},{2... | collective-permute-start | bytes 3145736 | tf_op jit(solution)/shard_map/ppermute | solution.py:208
  708.8 19.6 %collective-permute-start.85 = (bf16[512,1024]{1,0:T(8,128)(2,1)}, bf16[512,1024]{1,0:T(8,128)(2,1)}, u32[]{:S(2)}, u32[]{:S(2)}) collective-permute-start(bf16[512,1024]{1,0:T(8,128)(2,1)} %pad_select_fusion.1), channel_id=1, source_target_pairs={{0,2},{2,0},{6,4},{4,6},{1,3},{3,1},{7,5},{5,7},{8,10},{10,8},{14,... | collective-permute-start | bytes 3145736 | tf_op jit(solution)/shard_map/ppermute | solution.py:208
  736.3 25.5 %collective-permute-start.92 = (bf16[512,1024]{1,0:T(8,128)(2,1)S(1)}, bf16[512,1024]{1,0:T(8,128)(2,1)S(1)}, u32[]{:S(2)}, u32[]{:S(2)}) collective-permute-start(bf16[512,1024]{1,0:T(8,128)(2,1)S(1)} %pad_select_fusion), channel_id=1, source_target_pairs={{0,2},{2,0},{6,4},{4,6},{1,3},{3,1},{7,5},{5,7},{8,10},{10,8},{14,... | collective-permute-start | bytes 3145736 | tf_op jit(solution)/shard_map/ppermute | solution.py:208
  780.2 18.3 %collective-permute-start.101 = (bf16[512,640]{1,0:T(8,128)(2,1)S(1)}, bf16[512,640]{1,0:T(8,128)(2,1)}, u32[]{:S(2)}, u32[]{:S(2)}) collective-permute-start(bf16[512,640]{1,0:T(8,128)(2,1)S(1)} %add_convert_fusion.34), channel_id=1, source_target_pairs={{2,4},{4,2},{3,5},{5,3},{10,12},{12,10},{11,13},{13,11},{18,20},{2... | collective-permute-start | bytes 1966088 | tf_op jit(solution)/shard_map/ppermute | solution.py:208
  (196 other events, 3195.3 us)

commit v3 on v0

--- a/solution.py
+++ b/solution.py
@@ -1,8 +1,11 @@
+import functools
 import math
 
 import jax
 import jax.numpy as jnp
 from jax import lax
+from jax.experimental import pallas as pl
+from jax.experimental.pallas import tpu as pltpu
 from jax.sharding import PartitionSpec as P
 
 QUERY_HEADS = 32
@@ -68,7 +71,1051 @@
     )
 
 
-def shards(
+VMEM_LIMIT = 32 * 1024 * 1024
+SMALL_LIMIT = 12 * 1024 * 1024
+SMALL = pl.CostEstimate(flops=1, bytes_accessed=1, transcendentals=0)
+
+
+def pairs_by(distance, size):
+    return [(i, i ^ distance) for i in range(size)]
+
+
+def swap(array, axis, distance):
+    return lax.ppermute(array, axis, pairs_by(distance, lax.axis_size(axis)))
+
+
+class Line:
+    def __init__(self, axis):
+        index = lax.axis_index(axis)
+        size = lax.axis_size(axis)
+        self.axis = axis
+        self.at_end = ((index == 0) | (index == size - 1)).astype(jnp.int32)[None]
+        self.entered = self.halfway = self.leaving = None
+        self.sums = {}
+
+    def advance(self, got, entering):
+        if self.leaving is not None:
+            name, sent = self.leaving
+            self.sums[name] = (got["ends"], sent)
+        moves = []
+        halfway = None
+        if self.entered is not None:
+            name, value = self.entered
+            halfway = (name, add_low(value, got["ends"]))
+            moves.append(("middle", halfway[1], self.axis, [(1, 2), (2, 1)]))
+        leaving = None
+        inwards, outwards = [(0, 1), (3, 2)], [(1, 0), (2, 3)]
+        if self.halfway is not None:
+            name, value = self.halfway
+            if entering is None:
+                sent, pairs = add_low(value, got["middle"]), outwards
+            else:
+                sent = either_way(self.at_end, entering[1], value, got["middle"])
+                pairs = inwards + outwards
+            leaving = (name, sent)
+            moves.append(("ends", sent, self.axis, pairs))
+        elif entering is not None:
+            moves.append(("ends", entering[1], self.axis, inwards))
+        self.entered, self.halfway, self.leaving = entering, halfway, leaving
+        return moves
+
+
+class Steps:
+    def __init__(self, line):
+        self.line = line
+        self.got = {}
+        self.names = []
+        self.flying = []
+
+    def step(self, moves=(), summed=None, late=None, carry=()):
+        moves = list(moves)
+        fresh = [summed[1]] if summed is not None and summed[1] is not None else []
+        held = lax.optimization_barrier(
+            tuple(self.flying) + tuple(move[1] for move in moves) + tuple(fresh) + tuple(carry)
+        )
+        count = len(self.flying)
+        for name, value in zip(self.names, held[:count]):
+            self.got[name] = value
+        moves = [
+            (name, value, axis, pairs)
+            for (name, _, axis, pairs), value in zip(moves, held[count:])
+        ]
+        entering = summed
+        if summed is not None:
+            entering = (summed[0], held[count + len(moves)] if fresh else self.take(summed[0]))
+        on_line = self.line.advance(self.got, entering)
+        moves = on_line + moves + (late() if late is not None else [])
+        self.names = [move[0] for move in moves]
+        self.flying = [lax.ppermute(value, axis, pairs) for _, value, axis, pairs in moves]
+        return held[len(held) - len(carry) :]
+
+    def take(self, name):
+        return self.got.pop(name)
+
+
+def in_vmem(kernel, out_shape, *args, scalars=0):
+    specs = [pl.BlockSpec(memory_space=pltpu.SMEM)] * scalars
+    specs += [pl.BlockSpec(memory_space=pltpu.VMEM)] * (len(args) - scalars)
+    return pl.pallas_call(
+        kernel,
+        out_shape=out_shape,
+        in_specs=specs,
+        out_specs=[pl.BlockSpec(memory_space=pltpu.VMEM)] * len(out_shape),
+        compiler_params=pltpu.CompilerParams(vmem_limit_bytes=SMALL_LIMIT),
+        cost_estimate=SMALL,
+    )(*args)
+
+
+def low(*shape):
+    return jax.ShapeDtypeStruct(shape, jnp.bfloat16)
+
+
+def full(*shape):
+    return jax.ShapeDtypeStruct(shape, jnp.float32)
+
+
+def store_seen(ref, value, distance, count):
+    width = value.shape[-1] // count
+    for block in range(count):
+        there = block ^ distance
+        ref[: value.shape[0], block * width : (block + 1) * width] = value[
+            :, there * width : (there + 1) * width
+        ]
+
+
+def prepare_kernel(count, index_ref, x_ref, *refs):
+    extra_ref = refs[0] if len(refs) > count else None
+    own_ref, *sends = refs[-count:]
+    rows, width = own_ref.shape[0], own_ref.shape[1] // count
+    first = pl.multiple_of(index_ref[1] * rows, rows)
+    for block in range(count):
+        column = pl.multiple_of((index_ref[0] ^ block) * width, width)
+        own_ref[:, block * width : (block + 1) * width] = x_ref[
+            pl.ds(first, rows), pl.ds(column, width)
+        ]
+    for k in range(1, count):
+        store_seen(sends[k - 1], own_ref[...], k, count)
+        if extra_ref is not None:
+            sends[k - 1][rows:, :] = extra_ref[...]
+
+
+def prepare(x, index, count, extra=()):
+    rows, width = x.shape[0] // 2, x.shape[1]
+    more = extra[0].shape[0] if extra else 0
+    return in_vmem(
+        functools.partial(prepare_kernel, count),
+        [low(rows, width)] + [low(rows + more, width)] * (count - 1),
+        index,
+        x,
+        *extra,
+        scalars=1,
+    )
+
+
+def join_kernel(*refs):
+    out_ref = refs[-1]
+    rows = refs[0].shape[0]
+    for i, ref in enumerate(refs[:-1]):
+        out_ref[i * rows : (i + 1) * rows, :] = ref[:rows, :]
+
+
+def join(own, others):
+    rows, width = own.shape
+    return in_vmem(join_kernel, [low(rows * (1 + len(others)), width)], own, *others)[0]
+
+
+def fold_kernel(count, first_ref, came_ref, own_ref, *sends):
+    rows = own_ref.shape[0]
+    for k in range(count):
+        here = slice(k * rows, (k + 1) * rows)
+        total = first_ref[here, :].astype(jnp.float32) + came_ref[here, :].astype(jnp.float32)
+        total = total.astype(jnp.bfloat16)
+        if k == 0:
+            own_ref[...] = total
+        else:
+            store_seen(sends[k - 1], total, k, count)
+
+
+def fold(first, came, count):
+    rows, width = first.shape[0] // count, first.shape[1]
+    return in_vmem(
+        functools.partial(fold_kernel, count), [low(rows, width)] * count, first, came
+    )
+
+
+def total_of(refs):
+    total = refs[0][...].astype(jnp.float32)
+    for ref in refs[1:]:
+        total = total + ref[...].astype(jnp.float32)
+    return total
+
+
+def middle_kernel(count, in_ref, gain_ref, *refs):
+    parts, (middle_ref, normed_ref, *sends) = refs[:count], refs[count:]
+    middle = in_ref[...].astype(jnp.float32) + total_of(parts)
+    middle_ref[...] = middle
+    mean = jnp.mean(middle * middle, axis=-1, keepdims=True)
+    normed = (middle * lax.rsqrt(mean + 1e-05) * gain_ref[...]).astype(jnp.bfloat16)
+    normed_ref[...] = normed
+    for k in range(1, count):
+        store_seen(sends[k - 1], normed, k, count)
+
+
+def norm_back(d_normed, x, gain):
+    scale = lax.rsqrt(jnp.mean(x * x, axis=-1, keepdims=True) + 1e-05)
+    unit = x * scale
+    d_unit = d_normed * gain
+    d_x = scale * (d_unit - unit * jnp.mean(d_unit * unit, axis=-1, keepdims=True))
+    return d_x, jnp.sum(d_normed * unit, axis=0, keepdims=True)
+
+
+def branch_back_kernel(count, middle_ref, gain_ref, cot_ref, *refs):
+    parts, (d_middle_ref, d_gain_ref, branch_ref, *sends) = refs[:count], refs[count:]
+    d_x, d_gain_ref[...] = norm_back(total_of(parts), middle_ref[...], gain_ref[...])
+    d_middle = cot_ref[...].astype(jnp.float32) + d_x
+    d_middle_ref[...] = d_middle
+    branch = d_middle.astype(jnp.bfloat16)
+    branch_ref[...] = branch
+    for k in range(1, count):
+        store_seen(sends[k - 1], branch, k, count)
+
+
+def in_grad_kernel(count, in_ref, gain_ref, d_middle_ref, *refs):
+    parts, (grad_ref, d_gain_ref) = refs[:count], refs[count:]
+    x = in_ref[...].astype(jnp.float32)
+    d_x, d_gain_ref[...] = norm_back(total_of(parts), x, gain_ref[...])
+    grad_ref[...] = (d_middle_ref[...] + d_x).astype(jnp.bfloat16)
+
+
+def gridded(kernel, steps, ins, outs, scalars=()):
+    return pl.pallas_call(
+        kernel,
+        grid=(steps,),
+        in_specs=[pl.BlockSpec(memory_space=pltpu.SMEM)] * len(scalars)
+        + [pl.BlockSpec(block, index) for _, block, index in ins],
+        out_specs=[pl.BlockSpec(block, index) for _, block, index in outs],
+        out_shape=[shape for shape, _, _ in outs],
+        compiler_params=pltpu.CompilerParams(vmem_limit_bytes=VMEM_LIMIT),
+        cost_estimate=SMALL,
+    )(*scalars, *[array for array, _, _ in ins])
+
+
+def row_blocks(array, rows):
+    return (array, (rows, array.shape[1]), lambda i: (i, 0))
+
+
+def add_low(left, right):
+    right = right[:, : left.shape[1]]
+    return (left.astype(jnp.float32) + right.astype(jnp.float32)).astype(jnp.bfloat16)
+
+
+def either_way(at_end, fresh, value, came):
+    total = add_low(value, came)
+    width = max(fresh.shape[1], value.shape[1])
+    if fresh.shape[1] < width:
+        fresh = jnp.pad(fresh, ((0, 0), (0, width - fresh.shape[1])))
+    if total.shape[1] < width:
+        total = jnp.pad(total, ((0, 0), (0, width - total.shape[1])))
+    return jnp.where(at_end[0] == 1, fresh, total)
+
+
+def settled(at_end, came_ref, sent_ref, columns):
+    return jnp.where(at_end == 1, came_ref[:, columns], sent_ref[:, columns]).astype(jnp.float32)
+
+
+def settle_kernel(count, at_end_ref, index_ref, *refs):
+    out_ref = refs[-1]
+    width = out_ref.shape[1] // count
+    for k in range(count):
+        column = pl.multiple_of((index_ref[0] ^ k) * width, width)
+        out_ref[:, pl.ds(column, width)] = settled(
+            at_end_ref[0], refs[2 * k], refs[2 * k + 1], slice(0, width)
+        )
+
+
+def settle(at_end, index, pairs, width):
+    count = len(pairs)
+    arrays = [array for pair in pairs for array in pair]
+    depth = arrays[0].shape[0]
+    rows = math.gcd(depth, 128)
+    ins = [(array, (rows, width), lambda i: (i, 0)) for array in arrays]
+    outs = [row_blocks(full(depth, width * count), rows)]
+    kernel = functools.partial(settle_kernel, count)
+    return gridded(kernel, depth // rows, ins, outs, scalars=(at_end, index))[0]
+
+
+def settle_attention_kernel(count, q_width, kv_width, at_end_ref, index_ref, *refs):
+    q_ref, k_ref, v_ref, o_ref = refs[-4:]
+    o_width = o_ref.shape[1] // count
+    o_first = q_width + kv_width
+    kvs = []
+    for k in range(count):
+        came_ref, sent_ref = refs[2 * k], refs[2 * k + 1]
+        column = pl.multiple_of((index_ref[0] ^ k) * q_width, q_width)
+        q_ref[:, pl.ds(column, q_width)] = settled(
+            at_end_ref[0], came_ref, sent_ref, slice(0, q_width)
+        )
+        column = pl.multiple_of((index_ref[0] ^ k) * o_width, o_width)
+        o_ref[:, pl.ds(column, o_width)] = settled(
+            at_end_ref[0], came_ref, sent_ref, slice(o_first, o_first + o_width)
+        )
+        kvs.append(settled(at_end_ref[0], came_ref, sent_ref, slice(q_width, o_first)))
+    ordered = []
+    for place in range(count):
+        kv = kvs[0]
+        for k in range(1, count):
+            kv = jnp.where((index_ref[0] ^ k) == place, kvs[k], kv)
+        ordered.append(kv)
+    k_ref[...] = jnp.concatenate([kv[:, : kv_width // 2] for kv in ordered], axis=1)
+    v_ref[...] = jnp.concatenate([kv[:, kv_width // 2 :] for kv in ordered], axis=1)
+
+
+def settle_attention(at_end, index, pairs, q_width, kv_width):
+    count = len(pairs)
+    arrays = [array for pair in pairs for array in pair]
+    depth = arrays[0].shape[0]
+    width = min(array.shape[1] for array in arrays)
+    o_width = width - q_width - kv_width
+    rows = math.gcd(depth, 128)
+    ins = [(array, (rows, width), lambda i: (i, 0)) for array in arrays]
+    widths = (q_width, kv_width // 2, kv_width // 2, o_width)
+    outs = [row_blocks(full(depth, each * count), rows) for each in widths]
+    kernel = functools.partial(settle_attention_kernel, count, q_width, kv_width)
+    return gridded(kernel, depth // rows, ins, outs, scalars=(at_end, index))
+
+
+def d_qkv_kernel(at_end_ref, here_ref, came_ref, sent_ref, dq_ref, cos_ref, sin_ref, out_ref):
+    lanes = 2 * HEAD_SIZE
+    half, q_width = dq_ref.shape[1], dq_ref.shape[2]
+    cycle = came_ref.shape[1] // lanes // 2
+    for core_side in range(2):
+        column = pl.multiple_of((core_side * cycle + here_ref[0]) * lanes, lanes)
+        d_kv = settled(at_end_ref[0], came_ref, sent_ref, pl.ds(column, lanes))
+        cosine, sine = of_keys(cos_ref[core_side], sin_ref[core_side])
+        d_kv = turned(d_kv, cosine, -sine).astype(jnp.bfloat16)
+        rows = slice(core_side * half, (core_side + 1) * half)
+        out_ref[rows, :q_width] = dq_ref[core_side]
+        out_ref[rows, q_width:] = d_kv
+
+
+def rows_back_kernel(count, index_ref, own_ref, other_ref, out_ref):
+    rows, width = own_ref.shape[0], own_ref.shape[1] // count
+    for ref, core in ((own_ref, index_ref[1]), (other_ref, 1 - index_ref[1])):
+        first = pl.multiple_of(core * rows, rows)
+        for block in range(count):
+            column = pl.multiple_of((index_ref[0] ^ block) * width, width)
+            out_ref[pl.ds(first, rows), pl.ds(column, width)] = ref[
+                :, block * width : (block + 1) * width
+            ]
+
+
+def result_kernel(middle_ref, *refs):
+    refs[-1][...] = (middle_ref[...] + total_of(refs[:-1])).astype(jnp.bfloat16)
+
+
+def still(array):
+    zeros = (0,) * len(array.shape)
+    return (array, array.shape, lambda i: zeros)
+
+
+def dot(left, right):
+    return jnp.dot(left, right, preferred_element_type=jnp.float32)
+
+
+def both(mine_ref, other_ref):
+    return jnp.concatenate([mine_ref[...], other_ref[...]], axis=0)
+
+
+def gate_up_kernel(count, here_steps, *refs):
+    x = both(refs[0], refs[1])
+    refs = refs[2:]
+    own, fetched, passed = refs[:2], refs[2 : 2 * count], refs[2 * count : 4 * count - 2]
+    gate_ref, up_ref, hidden_ref, wg_ref, wu_ref = refs[4 * count - 2 :]
+    here = pl.program_id(0) < here_steps
+    lins = []
+    for which, out_ref in ((0, wg_ref), (1, wu_ref)):
+        pieces = [own[which][...]]
+        for k in range(count - 1):
+            pieces.append(
+                jnp.where(here, fetched[2 * k + which][...], passed[2 * k + which][...])
+            )
+        weight = jnp.concatenate(pieces, axis=0)
+        out_ref[...] = weight
+        lins.append(dot(x, weight))
+    gate, up = lins
+    gate_ref[...] = gate
+    up_ref[...] = up
+    hidden_ref[...] = (gate * jax.nn.sigmoid(gate) * up).astype(jnp.bfloat16)
+
+
+def gate_up(x, own_gate, own_up, fetched, passed):
+    tokens, depth = 2 * x[0].shape[0], own_gate.shape[0]
+    width, units = x[0].shape[1], own_gate.shape[1]
+    count = len(fetched) + 1
+    block = math.gcd(units // 2, 256)
+    steps, half = units // block, units // block // 2
+    ins = [still(x[0]), still(x[1])]
+    ins += [(w, (depth, block), lambda i: (0, i)) for w in (own_gate, own_up)]
+    for arrays in (fetched, passed):
+        for array in arrays:
+            ins.append((array, (depth, block), lambda i: (0, lax.rem(i, half))))
+            ins.append((array, (depth, block), lambda i: (0, half + lax.rem(i, half))))
+    outs = [
+        (full(tokens, units), (tokens, block), lambda i: (0, i)),
+        (full(tokens, units), (tokens, block), lambda i: (0, i)),
+        (low(tokens, units), (tokens, block), lambda i: (0, i)),
+        (low(width, units), (width, block), lambda i: (0, i)),
+        (low(width, units), (width, block), lambda i: (0, i)),
+    ]
+    return gridded(functools.partial(gate_up_kernel, count, half), steps, ins, outs)
+
+
+def units_back_kernel(count, *refs):
+    d_out = both(refs[0], refs[1])
+    refs = refs[2:]
+    pieces, (gate_ref, up_ref, d_gate_ref, d_up_ref, wd_ref) = refs[:count], refs[count:]
+    weight = jnp.concatenate([ref[...] for ref in pieces], axis=0)
+    wd_ref[...] = weight
+    d_hidden = dot(d_out, weight)
+    gate, up = gate_ref[...], up_ref[...]
+    chance = jax.nn.sigmoid(gate)
+    d_up_ref[...] = (d_hidden * (gate * chance)).astype(jnp.bfloat16)
+    slope = chance + gate * chance * (1.0 - chance)
+    d_gate_ref[...] = (d_hidden * up * slope).astype(jnp.bfloat16)
+
+
+def units_back(d_out, pieces, gate, up):
+    tokens, units = gate.shape
+    depth, width = pieces[0].shape[0], d_out[0].shape[1]
+    block = math.gcd(units, 256)
+
+    def by_columns(array, rows):
+        return (array, (rows, block), lambda i: (0, i))
+
+    ins = [still(d_out[0]), still(d_out[1])] + [by_columns(piece, depth) for piece in pieces]
+    ins += [by_columns(gate, tokens), by_columns(up, tokens)]
+    outs = [by_columns(low(tokens, units), tokens)] * 2 + [by_columns(low(width, units), width)]
+    return gridded(functools.partial(units_back_kernel, len(pieces)), units // block, ins, outs)
+
+
+def rows_sum_kernel(terms, *refs):
+    first_ref, second_ref = refs[-2:]
+    total = 0.0
+    for left_ref, right_ref in zip(refs[:terms], refs[terms : 2 * terms]):
+        total = total + contract_last(left_ref[...], right_ref[...])
+    total = total.astype(jnp.bfloat16)
+    half = first_ref.shape[0]
+    first_ref[...] = total[:half]
+    second_ref[...] = total[half:]
+
+
+def rows_sum(lefts, rights):
+    tokens, width = lefts[0].shape[0], rights[0].shape[0]
+    block = math.gcd(width, 512)
+    ins = [still(left) for left in lefts]
+    ins += [(right, (block, right.shape[1]), lambda i: (i, 0)) for right in rights]
+    outs = [(low(tokens // 2, width), (tokens // 2, block), lambda i: (0, i))] * 2
+    return gridded(functools.partial(rows_sum_kernel, len(lefts)), width // block, ins, outs)
+
+
+def weight_grad_kernel(count, terms, turn, *refs):
+    if turn:
+        side, refs = refs[0][0], refs[1:]
+    outs = refs[3 * terms :]
+    step = pl.program_id(0)
+    first = 0
+    for term in range(terms):
+        mine_ref, other_ref, right_ref = refs[3 * term : 3 * term + 3]
+        half = mine_ref.shape[0]
+        grad = contract_first(mine_ref[...], right_ref[:half, :])
+        grad = grad + contract_first(other_ref[...], right_ref[half:, :])
+        grad = grad.astype(jnp.bfloat16)
+        columns = grad.shape[1]
+        for k in range(count):
+
+            @pl.when(step == k)
+            def _(k=k, first=first, grad=grad, columns=columns):
+                if turn:
+                    part = columns // 2
+                    outs[k][:, pl.ds(pl.multiple_of(side * part, part), part)] = grad[:, :part]
+                    outs[k][:, pl.ds(pl.multiple_of((1 - side) * part, part), part)] = grad[:, part:]
+                else:
+                    outs[k][:, first : first + columns] = grad
+
+        first += columns
+
+
+def weight_grad(terms, count, side=None):
+    columns = sum(right.shape[1] for _, _, right in terms)
+    depth = terms[0][0].shape[1] // count
+    ins = []
+    if side is not None:
+        ins.append((side, None, None))
+    for mine, other, right in terms:
+        ins += [(left, (left.shape[0], depth), lambda i: (0, i)) for left in (mine, other)]
+        ins.append(still(right))
+    specs = [
+        pl.BlockSpec(memory_space=pltpu.SMEM) if block is None else pl.BlockSpec(block, index)
+        for _, block, index in ins
+    ]
+    return pl.pallas_call(
+        functools.partial(weight_grad_kernel, count, len(terms), side is not None),
+        grid=(count,),
+        in_specs=specs,
+        out_specs=[pl.BlockSpec((depth, columns), lambda i: (0, 0))] * count,
+        out_shape=[low(depth, columns)] * count,
+        compiler_params=pltpu.CompilerParams(vmem_limit_bytes=VMEM_LIMIT),
+        cost_estimate=SMALL,
+    )(*[array for array, _, _ in ins])
+
+
+def turned(lin, cosine, sine):
+    width = lin.shape[-1]
+    quarter = HEAD_SIZE // 2
+    lane = lax.broadcasted_iota(jnp.int32, lin.shape, lin.ndim - 1)
+    first = lax.rem(lane, HEAD_SIZE) < quarter
+    partner = jnp.where(
+        first,
+        -pltpu.roll(lin, width - quarter, lin.ndim - 1),
+        pltpu.roll(lin, quarter, lin.ndim - 1),
+    )
+    return lin * cosine + partner * sine
+
+
+def side_by_side(table, width):
+    return jnp.concatenate([table] * (width // table.shape[-1]), axis=-1)
+
+
+def of_keys(cosine, sine):
+    keys = lax.broadcasted_iota(jnp.int32, cosine.shape, 1) < HEAD_SIZE
+    return jnp.where(keys, cosine, 1.0), jnp.where(keys, sine, 0.0)
+
+
+def qkv_kernel(count, q_width, kv_width, *refs):
+    x_refs, (gain_ref, cos_ref, sin_ref), refs = refs[:2], refs[2:5], refs[5:]
+    pieces, refs = refs[:count], refs[count:]
+    normed_refs, (q_ref, kv_ref, wqkv_ref, wo_ref) = refs[:2], refs[2:]
+    weight = jnp.concatenate([ref[...] for ref in pieces], axis=0)
+    qkv_width = q_width + kv_width
+
+    @pl.when(pl.program_id(0) == 0)
+    def _():
+        wqkv_ref[...] = weight[:, :qkv_width]
+        wo_ref[...] = weight[:, qkv_width:]
+
+    for i in range(2):
+        x = x_refs[i][...].astype(jnp.float32)
+        mean = jnp.mean(x * x, axis=-1, keepdims=True)
+        normed = (x * lax.rsqrt(mean + 1e-05) * gain_ref[...]).astype(jnp.bfloat16)
+        normed_refs[i][...] = normed
+        lin = dot(normed, weight[:, :qkv_width])
+        cosine, sine = cos_ref[i], sin_ref[i]
+        q = turned(lin[:, :q_width], side_by_side(cosine, q_width), side_by_side(sine, q_width))
+        q_ref[i] = q.astype(jnp.bfloat16)
+        kv = turned(lin[:, q_width:], *of_keys(cosine, sine))
+        kv_ref[i] = kv.astype(jnp.bfloat16)
+
+
+def project_qkv(x, gain, cosine, sine, pieces, q_width, kv_width):
+    half_rows, width = x[0].shape
+    qkv_width = q_width + kv_width
+    block = math.gcd(half_rows, 128)
+
+    def rows_of(array, columns):
+        return (array, (block, columns), lambda i: (i, 0))
+
+    def of_both(array, columns):
+        return (array, (2, block, columns), lambda i: (0, i, 0))
+
+    lanes = cosine.shape[-1]
+    ins = [rows_of(x[0], width), rows_of(x[1], width), still(gain)]
+    ins += [of_both(cosine, lanes), of_both(sine, lanes)] + [still(piece) for piece in pieces]
+    o_width = pieces[0].shape[1] - qkv_width
+    outs = [rows_of(low(half_rows, width), width)] * 2
+    outs += [of_both(low(2, half_rows, q_width), q_width), of_both(low(2, half_rows, kv_width), kv_width)]
+    outs += [still(low(width, qkv_width)), still(low(width, o_width))]
+    kernel = functools.partial(qkv_kernel, len(pieces), q_width, kv_width)
+    return gridded(kernel, half_rows // block, ins, outs)
+
+
+def shares(q, k, visible):
+    scores = contract_last(q, k) * (1.0 / math.sqrt(HEAD_SIZE))
+    scores = jnp.where(visible, scores, -1e30)
+    weights = jnp.exp(scores - jnp.max(scores, axis=-1, keepdims=True))
+    weights = jnp.where(visible, weights, 0.0)
+    return weights, jnp.sum(weights, axis=-1, keepdims=True)
+
+
+def load_attention(q_ref, place_ref, start_ref, key_place_ref, kv_refs):
+    q = q_ref[...]
+    q = q.reshape(q.shape[0] * q.shape[1], q.shape[2])
+    kv = jnp.concatenate([ref[...].reshape(q.shape[0], 2 * HEAD_SIZE) for ref in kv_refs], axis=0)
+    key_place = key_place_ref[0]
+    visible = (key_place <= place_ref[0]) & (key_place >= start_ref[0])
+    return q, kv[:, :HEAD_SIZE], kv[:, HEAD_SIZE:], visible
+
+
+def attend_kernel(groups, q_ref, place_ref, start_ref, key_place_ref, wo_ref, *refs):
+    kv_refs, (out_ref, first_ref, second_ref) = refs[:-3], refs[-3:]
+    q, k, v, visible = load_attention(q_ref, place_ref, start_ref, key_place_ref, kv_refs)
+    mixed = []
+    for g in range(groups):
+        weights, totals = shares(q[:, g * HEAD_SIZE : (g + 1) * HEAD_SIZE], k, visible)
+        mixed.append(dot(weights.astype(jnp.bfloat16), v) / totals)
+    out = jnp.concatenate(mixed, axis=1).astype(jnp.bfloat16)
+    out_ref[...] = out.reshape(out_ref.shape)
+    branch = contract_last(out, wo_ref[...]).astype(jnp.bfloat16)
+    half = first_ref.shape[0]
+    first_ref[...] = branch[:half]
+    second_ref[...] = branch[half:]
+
+
+def attend_back_kernel(
+    groups,
+    here_ref,
+    q_ref,
+    mine_ref,
+    other_ref,
+    cos_ref,
+    sin_ref,
+    place_ref,
+    start_ref,
+    key_place_ref,
+    wo_ref,
+    *refs,
+):
+    kv_refs, (dq_ref, dkv_ref) = refs[:-2], refs[-2:]
+    q, k, v, visible = load_attention(q_ref, place_ref, start_ref, key_place_ref, kv_refs)
+    d_out = dot(both(mine_ref, other_ref), wo_ref[...]).astype(jnp.bfloat16)
+    scale = 1.0 / math.sqrt(HEAD_SIZE)
+    d_q, d_k, d_v = [], 0.0, 0.0
+    for g in range(groups):
+        q_head = q[:, g * HEAD_SIZE : (g + 1) * HEAD_SIZE]
+        d_head = d_out[:, g * HEAD_SIZE : (g + 1) * HEAD_SIZE]
+        weights, totals = shares(q_head, k, visible)
+        probs = weights / totals
+        d_probs = contract_last(d_head, v)
+        row_delta = jnp.sum(probs * d_probs, axis=-1, keepdims=True)
+        d_scores = (probs * (d_probs - row_delta)).astype(jnp.bfloat16)
+        d_q.append(dot(d_scores, k) * scale)
+        d_k = d_k + contract_first(d_scores, q_head) * scale
+        d_v = d_v + contract_first(probs.astype(jnp.bfloat16), d_head)
+    d_q = jnp.concatenate(d_q, axis=1)
+    cosine = cos_ref[...].reshape(q.shape[0], -1)
+    sine = sin_ref[...].reshape(q.shape[0], -1)
+    d_q = turned(d_q, side_by_side(cosine, q.shape[1]), -side_by_side(sine, q.shape[1]))
+    dq_ref[...] = d_q.astype(jnp.bfloat16).reshape(dq_ref.shape)
+    d_kv = jnp.concatenate([d_k, d_v], axis=1).astype(jnp.bfloat16)
+    half, lanes, cycle = dkv_ref.shape[0], 2 * HEAD_SIZE, len(kv_refs)
+    for j in range(cycle):
+        for core_side in range(2):
+            first = (2 * j + core_side) * half
+            column = pl.multiple_of((core_side * cycle + (here_ref[0] ^ j)) * lanes, lanes)
+            dkv_ref[:, pl.ds(column, lanes)] = d_kv[first : first + half]
+
+
+def of_pack(array, half):
+    return (array, (2, half, array.shape[-1]), lambda p: (0, p, 0))
+
+
+def place_blocks(places):
+    return [(array, (1,) + array.shape[1:], lambda p: (p, 0, 0)) for array in places]
+
+
+def attend(q, places, wo, kvs, packs, groups):
+    half = q.shape[1] // packs
+    width = wo.shape[0]
+    ins = [of_pack(q, half)] + place_blocks(places) + [still(wo)] + [of_pack(kv, half) for kv in kvs]
+    outs = [of_pack(low(*q.shape), half)]
+    outs += [(low(q.shape[1], width), (half, width), lambda p: (p, 0))] * 2
+    return gridded(functools.partial(attend_kernel, groups), packs, ins, outs)
+
+
+def attend_back(here, q, d_branch, cosine, sine, places, wo, kvs, packs, groups):
+    half = q.shape[1] // packs
+    cycle = len(kvs)
+    ins = [of_pack(q, half)]
+    ins += [(array, (half, array.shape[1]), lambda p: (p, 0)) for array in d_branch]
+    ins += [of_pack(cosine, half), of_pack(sine, half)] + place_blocks(places) + [still(wo)]
+    ins += [of_pack(kv, half) for kv in kvs]
+    lanes = 2 * HEAD_SIZE
+    outs = [of_pack(low(*q.shape), half)]
+    outs.append((low(q.shape[1], 2 * cycle * lanes), (half, 2 * cycle * lanes), lambda p: (p, 0)))
+    kernel = functools.partial(attend_back_kernel, groups)
+    return gridded(kernel, packs, ins, outs, scalars=(here,))
+
+
+def split_heads(
+    hidden_in,
+    out_cotangent,
+    norm1_gain,
+    q_weight,
+    key_projection_weight,
+    value_projection_weight,
+    o_weight,
+    norm2_gain,
+    gate_weight,
+    up_weight,
+    down_weight,
+    seq_lengths,
+    span_order,
+):
+    packs = lax.axis_size("fsdp")
+    cycle = lax.axis_size("ctx")
+    pack = lax.axis_index("fsdp")
+    core = lax.axis_index("tp")
+    here = lax.axis_index("ctx")
+    rows = hidden_in.shape[0]
+    half = rows // 2
+    tokens = packs * rows
+    depth = q_weight.shape[0]
+    width = depth * packs
+    q_width = q_weight.shape[1] // packs
+    k_width = key_projection_weight.shape[1] // packs
+    ff_width = gate_weight.shape[1] // packs
+    ff_half = ff_width // 2
+    groups = q_width // k_width
+    far = range(1, packs)
+    steps = Steps(Line("ctx"))
+    kept = {}
+
+
+    def columns(weight, k, count, first=0, of=None):
+        return lax.dynamic_slice_in_dim(weight, (pack ^ k) * (of or count) + first, count, 1)
+
+    def to_pack(name, k, array):
+        return ((name, k), array, "fsdp", pairs_by(k, packs))
+
+    def send_all(name, arrays):
+        return [to_pack(name, k, array) for k, array in zip(far, arrays)]
+
+    def arrived(name):
+        return [steps.take((name, k)) for k in far]
+
+    def to_core(name, array):
+        return [(name, array, "tp", pairs_by(1, 2))]
+
+    def to_rows(name, first):
+        kept[name], *others = fold(first, steps.take(name), packs)
+        return send_all(name, others)
+
+    def joined(name, own, others):
+        kept[name] = join(own, others)
+        return to_core(name, kept[name])
+
+    def both_of(name):
+        return kept[name], steps.take(name)
+
+    index = jnp.stack([pack, core]).astype(jnp.int32)
+    here_arg = here.astype(jnp.int32)[None]
+    side_arg = here_arg & 1
+    at_end = steps.line.at_end
+
+    meta = jnp.concatenate([span_order[0], seq_lengths[0]])
+    order_len, meta_len = span_order.shape[1], meta.shape[0]
+    info = jnp.concatenate(
+        [norm1_gain, norm2_gain, (meta // 32).astype(jnp.bfloat16), (meta % 32).astype(jnp.bfloat16)]
+    )
+    info = jnp.pad(info, (0, width - info.shape[0]))[None]
+    own_in, *in_moves = prepare(
+        hidden_in, index, packs, (jnp.pad(info, ((0, 15), (0, 0))),)
+    )
+    own_cot, *cot_moves = prepare(out_cotangent, index, packs)
+
+    def attention_piece(k):
+        return jnp.concatenate(
+            [
+                columns(q_weight, k, q_width),
+                columns(key_projection_weight, k, k_width),
+                columns(value_projection_weight, k, k_width),
+                columns(o_weight, k, q_width),
+            ],
+            axis=1,
+        )
+
+    steps.step(send_all("in", in_moves))
+    steps.step([to_pack("attention", k, attention_piece(k)) for k in far])
+    came = arrived("in")
+    all_in = join(own_in, came)
+    all_in = (all_in, swap(all_in, "tp", 1))
+    infos = jnp.concatenate([info] + [block[half : half + 1] for block in came], axis=0)
+    all_gains = infos[:, : 2 * depth].astype(jnp.float32)
+    gain_one = all_gains[:, :depth].reshape(1, -1)
+    gain_two = all_gains[:, depth:].reshape(1, -1)
+    metas = infos[:, 2 * depth : 2 * depth + 2 * meta_len].astype(jnp.int32)
+    metas = metas[:, :meta_len] * 32 + metas[:, meta_len:]
+    orders, lengths = metas[:, :order_len], metas[:, order_len:]
+
+    others = jnp.stack([here ^ j for j in range(cycle)])
+    first = jnp.sum(
+        jnp.where(
+            others[None, :, None] == jnp.arange(order_len, dtype=jnp.int32)[None, None, :],
+            orders[:, None, :],
+            0,
+        ),
+        axis=2,
+    )
+    halves = jnp.stack([core, core ^ 1])[None, None, :]
+    section = jnp.where(halves == 0, first[:, :, None], 2 * cycle - 1 - first[:, :, None])
+    places = section[..., None] * half + jnp.arange(half, dtype=jnp.int32)
+    places = places.reshape(packs, cycle * rows)
+    starts = jnp.zeros_like(places)
+    end = jnp.zeros((packs, 1), jnp.int32)
+    for j in range(lengths.shape[1]):
+        end = end + lengths[:, j : j + 1]
+        starts = jnp.where(places >= end, end, starts)
+    place_args = (places[:, :rows, None], starts[:, :rows, None], places[:, None, :])
+    offsets = (places - starts)[:, :rows].reshape(packs, 2, half).transpose(1, 0, 2)
+    frequency = jnp.exp(
+        -math.log(500000.0)
+        * (jnp.arange(2 * HEAD_SIZE) % (HEAD_SIZE // 2)).astype(jnp.float32)
+        * 2.0
+        / HEAD_SIZE
+    )
+    angles = offsets.astype(jnp.float32).reshape(2, tokens // 2, 1) * frequency[None, None, :]
+    cosine, sine = jnp.cos(angles), jnp.sin(angles)
+
+    side = here & 1
+
+    def two_halves(weight, k):
+        return jnp.concatenate(
+            [
+                columns(weight, k, ff_half, side * ff_half, ff_width),
+                columns(weight, k, ff_half, (1 - side) * ff_half, ff_width),
+            ],
+            axis=1,
+        )
+
+    def fetch(ks):
+        return [
+            to_pack(
+                "gate_up",
+                k,
+                jnp.concatenate(
+                    [
+                        columns(weight, k, ff_half, side * ff_half, ff_width)
+                        for weight in (gate_weight, up_weight)
+                    ],
+                    axis=1,
+                ),
+            )
+            for k in ks
+        ]
+
+    def to_neighbour(k):
+        return [(("neighbour", k), fetched[k], "ctx", pairs_by(1, cycle))]
+
+    fetched = {}
+    _, cosine, sine, *place_args = steps.step(
+        fetch([1, 2]), carry=(all_in[1], cosine, sine, *place_args)
+    )
+    attention_pieces = [attention_piece(0)] + arrived("attention")
+    normed_mine, normed_other, q_rot, kv_own, wqkv, wo = project_qkv(
+        all_in, gain_one, cosine, sine, attention_pieces, q_width, 2 * k_width
+    )
+    normed_one = (normed_mine, normed_other)
+    steps.step(
+        [(("kv", j), kv_own, "ctx", pairs_by(j, cycle)) for j in range(1, cycle)] + fetch([3])
+    )
+    fetched[1], fetched[2] = steps.take(("gate_up", 1)), steps.take(("gate_up", 2))
+    steps.step(send_all("cot", cot_moves) + to_neighbour(1))
+    fetched[3] = steps.take(("gate_up", 3))
+    kvs = [kv_own] + [steps.take(("kv", j)) for j in range(1, cycle)]
+    attn, first, second = attend(q_rot, place_args, wo, kvs, packs, groups)
+    attn_low = attn.reshape(tokens, q_width)
+    steps.step(to_core("branch", second))
+    steps.step(to_neighbour(2), late=lambda: to_rows("branch", first))
+    kept["cot"] = join(own_cot, arrived("cot"))
+
+    def middle_moves():
+        kept["middle"], kept["normed"], *sends = in_vmem(
+            functools.partial(middle_kernel, packs),
+            [full(half, width)] + [low(half, width)] * packs,
+            own_in,
+            gain_two,
+            kept["branch"],
+            *arrived("branch"),
+        )
+        return send_all("two", sends)
+
+    steps.step(to_neighbour(3) + to_core("cot", kept["cot"]), late=middle_moves)
+
+    def wd_moves(ks):
+        return [to_pack("down", k, two_halves(down_weight, k)) for k in ks]
+
+    own_columns = [two_halves(weight, 0) for weight in (gate_weight, up_weight, down_weight)]
+    own_gate, own_up, own_down = steps.step(
+        wd_moves([1, 2]),
+        late=lambda: joined("two", kept["normed"], arrived("two")),
+        carry=own_columns,
+    )
+    all_cot = both_of("cot")
+    neighbours = [steps.take(("neighbour", k)) for k in far]
+    names = [name for name in steps.names]
+    kept_two = steps.flying[names.index("two")]
+    normed_two = (kept["two"], kept_two)
+
+    gate_val, up_val, hidden, wg, wu = gate_up(
+        normed_two, own_gate, own_up, [fetched[k] for k in far], neighbours
+    )
+    d_wd = weight_grad([(*all_cot, hidden)], packs, side_arg)
+
+    def back(name, grad, ks):
+        return [to_pack(name, k, grad[k]) for k in ks]
+
+    def entry(name, k, grad=None):
+        return ((name, k), grad[0] if k == 0 else None)
+
+    steps.step(back("wd", d_wd, [1, 2]), summed=entry("wd", 0, d_wd))
+    steps.step(wd_moves([3]), summed=entry("wd", 1))
+    steps.step(back("wd", d_wd, [3]), summed=entry("wd", 2))
+    d_gate, d_up, wd = units_back(all_cot, [own_down] + arrived("down"), gate_val, up_val)
+    first, second = rows_sum([d_gate, d_up], [wg, wu])
+    steps.step(to_core("d_two", second), summed=entry("wd", 3))
+    d_wg = weight_grad([(*normed_two, d_gate)], packs, side_arg)
+    steps.step(back("wg", d_wg, [1, 2]), summed=entry("wg", 0, d_wg))
+    d_wu = weight_grad([(*normed_two, d_up)], packs, side_arg)
+    steps.step(
+        summed=entry("wu", 0, d_wu), late=functools.partial(to_rows, "d_two", first)
+    )
+
+    def branch_back():
+        kept["d_middle"], kept["d_gain_two"], kept["d_branch"], *sends = in_vmem(
+            functools.partial(branch_back_kernel, packs),
+            [full(half, width), full(1, width)] + [low(half, width)] * packs,
+            kept["middle"],
+            gain_two,
+            own_cot,
+            kept["d_two"],
+            *arrived("d_two"),
+        )
+        return send_all("d_branch", sends)
+
+    first, second = rows_sum([hidden], [wd])
+    steps.step(summed=entry("wg", 1), late=branch_back, carry=(first, second))
+    steps.step(
+        back("wg", d_wg, [3]),
+        summed=entry("wg", 2),
+        late=lambda: joined("all_branch", kept["d_branch"], arrived("d_branch")),
+    )
+    d_branch = None
+
+    def attention_back():
+        return attend_back(
+            here_arg, q_rot, d_branch, cosine, sine, place_args, wo, kvs, packs, groups
+        )
+
+    sums = steps.line.sums
+
+    def settle_all(name):
+        return settle(at_end, index, [sums[name, k] for k in range(packs)], ff_width)
+
+    steps.step(back("wu", d_wu, [1, 2]), summed=entry("wg", 3))
+    d_branch = both_of("all_branch")
+    d_q, d_kv = attention_back()
+    steps.step(back("wu", d_wu, [3]), summed=("d_kv", d_kv))
+    down_grad = settle_all("wd")
+    steps.step(to_core("ff", second), summed=entry("wu", 1))
+    (down_grad,) = steps.step(
+        summed=entry("wu", 2),
+        late=functools.partial(to_rows, "ff", first),
+        carry=(down_grad,),
+    )
+    steps.step(summed=entry("wu", 3))
+    d_qkv = in_vmem(
+        d_qkv_kernel,
+        [low(tokens, q_width + 2 * k_width)],
+        at_end,
+        here_arg,
+        *sums["d_kv"],
+        d_q,
+        cosine,
+        sine,
+        scalars=2,
+    )[0]
+    d_wqkvo = weight_grad([(*normed_one, d_qkv), (*d_branch, attn_low)], packs)
+    first, second = rows_sum([d_qkv], [wqkv])
+    result = in_vmem(
+        result_kernel, [low(half, width)], kept["middle"], kept["ff"], *arrived("ff")
+    )[0]
+    steps.step(
+        back("wqkvo", d_wqkvo, [1, 2]) + to_core("d_one", second) + to_core("result", result),
+        summed=entry("wqkvo", 0, d_wqkvo),
+    )
+    steps.step(back("wqkvo", d_wqkvo, [3]), summed=entry("wqkvo", 1))
+
+    def both_rows(own, other):
+        return in_vmem(
+            functools.partial(rows_back_kernel, packs),
+            [low(rows, width)],
+            index,
+            own,
+            other,
+            scalars=1,
+        )[0]
+
+    out_hidden = both_rows(result, steps.take("result"))
+    gate_grad = settle_all("wg")
+    out_hidden, gate_grad = steps.step(
+        summed=entry("wqkvo", 2),
+        late=functools.partial(to_rows, "d_one", first),
+        carry=(out_hidden, gate_grad),
+    )
+    up_grad = settle_all("wu")
+
+    def gains_to_core():
+        kept["in_grad"], d_gain_one = in_vmem(
+            functools.partial(in_grad_kernel, packs),
+            [low(half, width), full(1, width)],
+            own_in,
+            gain_one,
+            kept["d_middle"],
+            kept["d_one"],
+            *arrived("d_one"),
+        )
+        kept["gains"] = jnp.concatenate([d_gain_one, kept["d_gain_two"]], axis=0)
+        return to_core("gains", kept["gains"]) + to_core("in_grad", kept["in_grad"])
+
+    def gains_to_packs():
+        kept["gains"] = kept["gains"] + steps.take("gains")
+        return [to_pack("gains", k, kept["gains"][:, k * depth : (k + 1) * depth]) for k in far]
+
+    def gains_along():
+        kept["gains"] = kept["gains"][:, :depth]
+        for k in far:
+            kept["gains"] = kept["gains"] + steps.take(("gains", k))
+        return [(("gains", j), kept["gains"], "ctx", pairs_by(j, cycle)) for j in range(1, cycle)]
+
+    (up_grad,) = steps.step(summed=entry("wqkvo", 3), late=gains_to_core, carry=(up_grad,))
+    steps.step(late=gains_to_packs)
+    in_grad = both_rows(kept["in_grad"], steps.take("in_grad"))
+    (in_grad,) = steps.step(late=gains_along, carry=(in_grad,))
+    steps.step()
+    shares_of_gains = jnp.stack(
+        [kept["gains"]] + [steps.take(("gains", j)) for j in range(1, cycle)]
+    )
+    gains = 0.0
+    for place in range(cycle):
+        gains = gains + lax.dynamic_index_in_dim(shares_of_gains, here ^ place, 0, keepdims=False)
+    q_grad, k_grad, v_grad, o_grad = settle_attention(
+        at_end, index, [sums["wqkvo", k] for k in range(packs)], q_width, 2 * k_width
+    )
+    return (
+        out_hidden,
+        in_grad,
+        gains[0],
+        q_grad,
+        k_grad,
+        v_grad,
+        o_grad,
+        gains[1],
+        gate_grad,
+        up_grad,
+        down_grad,
+    )
+
+
+def gathered_weights(
     hidden_in,
     out_cotangent,
     norm1_gain,
@@ -389,8 +1436,10 @@
         P("fsdp", None),
         P("fsdp", None),
     )
+    plane = mesh.shape["fsdp"] * mesh.shape["tp"]
+    splits = mesh.shape["tp"] == 2 and KEY_VALUE_HEADS == plane and mesh.shape["ctx"] == 4
     return jax.shard_map(
-        shards,
+        split_heads if splits else gathered_weights,
         mesh=mesh,
         in_specs=placed,
         out_specs=(

time: 3800 us -> 767 us (0.20)
  waiting for transfers between devices: 3290 us -> 382 us
  matrix products: 223 us -> 0 us
  blocking collectives: 175 us -> 0 us
  Pallas kernels: 0 us -> 146 us
  starting transfers between devices: 1.65 us -> 143 us
    reduce_scatter x9 -> x0, waiting for transfers between devices: 2430 us -> none  [the longest x1 688 us: shards(): lax.psum_scatter(weight_grads[8], ('fsdp', 'ctx'), scatter_dimension=0, t...]
    all_gather x12 -> x0, waiting for transfers between devices: 802 us -> none  [the longest x1 158 us: shards(): lax.all_gather(gate_weight, 'fsdp', axis=0, tiled=True)]
    ppermute x0 -> x104, waiting for transfers between devices: none -> 382 us  [the longest x103 382 us: step(): lax.ppermute(value, axis, pairs)]
    dot_general x35 -> x0, matrix products: 223 us -> none  [the longest x7 65.7 us: contract_first(): lax.dot_general(left, right, (((0,), (0,)), ((), ())), preferred_element_...]
    pallas_call x0 -> x33, Pallas kernels: none -> 146 us  [the longest x12 105 us: gridded(): pl.pallas_call(kernel, grid=(steps,), in_specs=[pl.BlockSpec(memory_space...]
    ppermute x0 -> x104, starting transfers between devices: none -> 143 us  [the longest x103 142 us: step(): lax.ppermute(value, axis, pairs)]
    all_gather x8 -> x0, blocking collectives: 96.5 us -> none  [the longest x1 15.6 us: shards(): value_row_block = lax.all_gather(v_low, 'ctx', axis=0, tiled=True)]
    unnamed x1 -> x0, blocking collectives: 78.1 us -> none
  transfers between devices with their start and end apart: 24 -> 104, of which waited for: 21 -> 54; matrix products, arithmetic and copies ran while one was open for 5% -> 5% of each run, Pallas kernels for 0% -> 18%
where the time goes in v3:
time: 767 us; the launch traced here: 760 us
  waiting for transfers between devices  382 us (50%)
  Pallas kernels  146 us (19%)
  starting transfers between devices  143 us (19%)
  local copies, waits for them, and re-layouts  50.1 us (7%)
  other arithmetic  37.5 us (5%)
    ppermute x103, waiting for transfers between devices, step(): lax.ppermute(value, axis, pairs)  382 us
    ppermute x103, starting transfers between devices, step(): lax.ppermute(value, axis, pairs)  142 us
    pallas_call x12, Pallas kernels, gridded(): pl.pallas_call(kernel, grid=(steps,), in_specs=[pl.BlockSpec(memory_space...  105 us
    unnamed x233, local copies, waits for them, and re-layouts  36.6 us
    pallas_call x4, Pallas kernels, weight_grad(): pl.pallas_call(functools.partial(weight_grad_kernel, count, len(terms), s...  26.5 us
  transfers between devices with their start and end apart: 104, of which 54 were waited for; matrix products, arithmetic and copies ran while one was open for 5% of the time, Pallas kernels for 18%

profile of v3, /device:TPU:0, one launch (start us, length us, event | category | flops | bytes accessed | tf_op | source)
XLA Modules:
  0.0 760.4 jit_solution(13185057257263574553)
XLA Ops:
  6.6 2.9 collective-permute-start
  20.7 2.9 constant_dynamic-slice_fusion.11
  24.9 12.3 %collective-permute-done.1.refs_2_ = bf16[144,2048]{1,0:T(8,128)(2,1)S(1)} collective-permute-done((bf16[144,2048]{1,0:T(8,128)(2,1)}, bf16[144,2048]{1,0:T(8,128)(2,1)S(1)}, u32[]{:S(2)}, u32[]{:S(2)}) %collective-permute-start.1) | collective-permute-done | bytes 589856 | tf_op jit(solution)/shard_map/ppermute | solution.py:149
  50.9 12.2 %collective-permute-done.3.refs_6_ = bf16[512,640]{1,0:T(8,128)(2,1)} collective-permute-done((bf16[512,640]{1,0:T(8,128)(2,1)}, bf16[512,640]{1,0:T(8,128)(2,1)}, u32[]{:S(2)}, u32[]{:S(2)}) %collective-permute-start.3) | collective-permute-done | bytes 655392 | tf_op jit(solution)/shard_map/ppermute | solution.py:149
  63.1 12.1 %collective-permute-done.4.refs_7_ = bf16[512,640]{1,0:T(8,128)(2,1)} collective-permute-done((bf16[512,640]{1,0:T(8,128)(2,1)}, bf16[512,640]{1,0:T(8,128)(2,1)}, u32[]{:S(2)}, u32[]{:S(2)}) %collective-permute-start.4) | collective-permute-done | bytes 655392 | tf_op jit(solution)/shard_map/ppermute | solution.py:149
  81.9 8.0 %shard_map.214 = (bf16[512,2048]{1,0:T(8,128)(2,1)S(1)}, bf16[512,2048]{1,0:T(8,128)(2,1)S(1)}, bf16[2,512,256]{2,1,0:T(8,128)(2,1)S(1)}, bf16[2,512,128]{2,1,0:...) custom-call(bf16[512,2048]{1,0:T(8,128)(2,1)S(1)} %shard_map.213.refs_0_, ...), custom_call_target="tpu_custom_call" | custom-call | flops 1 | bytes 1 | tf_op jit(solution)/shard_map/pallas_call | solution.py:291
  94.5 6.7 collective-permute-done.7.refs_4_.refs_5_
  109.6 12.0 %collective-permute-done.10.refs_2_ = bf16[2,512,128]{2,1,0:T(8,128)(2,1)S(1)} collective-permute-done((bf16[2,512,128]{2,1,0:T(8,128)(2,1)S(1)}, bf16[2,512,128]{2,1,0:T(8,128)(2,1)S(1)}, u32[]{:S(2)}, u32[]{:S(2)}) %collective-permute-start.10) | collective-permute-done | bytes 262176 | tf_op jit(solution)/shard_map/ppermute | solution.py:149
  125.1 3.0 collective-permute-start.16
  137.5 12.9 %shard_map.216 = (bf16[2,512,256]{2,1,0:T(8,128)(2,1)S(1)}, bf16[512,2048]{1,0:T(8,128)(2,1)S(1)}, bf16[512,2048]{1,0:T(8,128)(2,1)S(1)}) custom-call(bf16[2,512,256]{2,1,0:T(8,128)(2,1)S(1)} %copy-done.36, s32[4,256,1]{2,1,0:T(8,128)S(1)} %copy.32.place_ref, s32[4,256,1]{2,1,0:T(8,128)S(1)} %copy.33.start_ref, ...), custom_call_target="tpu_custom_call" | custom-call | flops 1 | bytes 1 | tf_op jit(solution)/shard_map/pallas_call | solution.py:291
  154.4 4.2 collective-permute-done.17.came_ref
  164.6 9.6 %collective-permute-done.19.refs_1_ = bf16[128,2048]{1,0:T(8,128)(2,1)S(1)} collective-permute-done((bf16[128,2048]{1,0:T(8,128)(2,1)S(1)}, bf16[128,2048]{1,0:T(8,128)(2,1)S(1)}, u32[]{:S(2)}, u32[]{:S(2)}) %collective-permute-start.19) | collective-permute-done | bytes 524320 | tf_op jit(solution)/shard_map/ppermute | solution.py:149
  174.3 9.7 %collective-permute-done.20.refs_2_ = bf16[128,2048]{1,0:T(8,128)(2,1)S(1)} collective-permute-done((bf16[128,2048]{1,0:T(8,128)(2,1)S(1)}, bf16[128,2048]{1,0:T(8,128)(2,1)S(1)}, u32[]{:S(2)}, u32[]{:S(2)}) %collective-permute-start.20) | collective-permute-done | bytes 524320 | tf_op jit(solution)/shard_map/ppermute | solution.py:149
  194.3 8.8 %collective-permute-done.24.refs_1_ = bf16[128,2048]{1,0:T(8,128)(2,1)S(1)} collective-permute-done((bf16[128,2048]{1,0:T(8,128)(2,1)S(1)}, bf16[128,2048]{1,0:T(8,128)(2,1)S(1)}, u32[]{:S(2)}, u32[]{:S(2)}) %collective-permute-start.24) | collective-permute-done | bytes 524320 | tf_op jit(solution)/shard_map/ppermute | solution.py:149
  203.1 10.0 %collective-permute-done.25.refs_2_ = bf16[128,2048]{1,0:T(8,128)(2,1)S(1)} collective-permute-done((bf16[128,2048]{1,0:T(8,128)(2,1)S(1)}, bf16[128,2048]{1,0:T(8,128)(2,1)S(1)}, u32[]{:S(2)}, u32[]{:S(2)}) %collective-permute-start.25) | collective-permute-done | bytes 524320 | tf_op jit(solution)/shard_map/ppermute | solution.py:149
  219.1 14.5 %shard_map.221 = (f32[1024,1024]{1,0:T(8,128)S(1)}, f32[1024,1024]{1,0:T(8,128)}, bf16[1024,1024]{1,0:T(8,128)(2,1)S(1)}, bf16[2048,1024]{1,0:T(8,128)(2,1)}, bf16[2048,1024]{1,0:T(8,128)(2,1)}) custom-call(bf16[512,2048]{1,0:T(8,128)(2,1)S(1)} %shard_map.220.refs_0_.refs_1_, bf16[512,2048]{1,0:T(8,128)(2,1)S(1)} %collective-permute-done.29.refs_1_.refs_2_, ...), custom_call_target="tpu_custom_call" | custom-call | flops 1 | bytes 1 | tf_op jit(solution)/shard_map/pallas_call | solution.py:291
  233.6 6.4 shard_map.222
  246.6 18.5 %collective-permute-done.30 = bf16[512,1024]{1,0:T(8,128)(2,1)S(1)} collective-permute-done((bf16[512,1024]{1,0:T(8,128)(2,1)S(1)}, bf16[512,1024]{1,0:T(8,128)(2,1)S(1)}, u32[]{:S(2)}, u32[]{:S(2)}) %collective-permute-start.30) | collective-permute-done | bytes 1048608 | tf_op jit(solution)/shard_map/ppermute | solution.py:149
  271.6 5.2 collective-permute-start.34
  278.6 18.1 %collective-permute-done.34 = bf16[512,1024]{1,0:T(8,128)(2,1)} collective-permute-done((bf16[512,1024]{1,0:T(8,128)(2,1)}, bf16[512,1024]{1,0:T(8,128)(2,1)}, u32[]{:S(2)}, u32[]{:S(2)}) %collective-permute-start.34) | collective-permute-done | bytes 1048608 | tf_op jit(solution)/shard_map/ppermute | solution.py:149
  296.7 4.1 collective-permute-done.35.refs_5_
  300.8 3.7 fusion.refs_1_
  311.3 8.7 %shard_map.223 = (bf16[1024,1024]{1,0:T(8,128)(2,1)S(1)}, bf16[1024,1024]{1,0:T(8,128)(2,1)S(1)}, bf16[2048,1024]{1,0:T(8,128)(2,1)S(1)}) custom-call(bf16[512,2048]{1,0:T(8,128)(2,1)S(1)} %copy-done.3, bf16[512,2048]{1,0:T(8,128)(2,1)S(1)} %copy-done.7, bf16[512,1024]{1,0:T(8,128)(2,1)S(1)} %copy-done.26, bf16[512,1024]{1,0:T(8,128)(2,1)S(1)} %copy-done.57, ...), custom_call_target="tpu_custom_call" | custom-call | flops 1 | bytes 1 | tf_op jit(solution)/shard_map/pallas_call | solution.py:291
  324.2 9.7 %shard_map.224 = (bf16[512,2048]{1,0:T(8,128)(2,1)S(1)}, bf16[512,2048]{1,0:T(8,128)(2,1)S(1)}) custom-call(bf16[1024,1024]{1,0:T(8,128)(2,1)S(1)} %get-tuple-element.349.refs_0_.refs_3_, bf16[1024,1024]{1,0:T(8,128)(2,1)S(1)} %get-tuple-element.350.refs_1_.refs_3_, bf16[2048,1024]{1,0:T(8,128)(2,1)S(1)} %copy-done.15, bf16[2048,1024]{1,0:T(8,128)(2,1)S(1)} %copy-done.16), custom_call_target="tpu_custom_call" | custom-call | flops 1 | bytes 1 | tf_op jit(solution)/shard_map/pallas_call | solution.py:291
  334.8 3.4 collective-permute-start.40
  340.4 6.0 shard_map.225
  346.5 15.5 %collective-permute-done.40.refs_2_ = bf16[512,1024]{1,0:T(8,128)(2,1)S(1)} collective-permute-done((bf16[512,1024]{1,0:T(8,128)(2,1)S(1)}, bf16[512,1024]{1,0:T(8,128)(2,1)S(1)}, u32[]{:S(2)}, u32[]{:S(2)}) %collective-permute-start.40) | collective-permute-done | bytes 1048608 | tf_op jit(solution)/shard_map/ppermute | solution.py:149
  362.6 5.4 collective-permute-start.43
  371.0 6.2 shard_map.226
  377.2 13.4 %collective-permute-done.43.refs_4_ = bf16[512,1024]{1,0:T(8,128)(2,1)S(1)} collective-permute-done((bf16[512,1024]{1,0:T(8,128)(2,1)S(1)}, bf16[512,1024]{1,0:T(8,128)(2,1)S(1)}, u32[]{:S(2)}, u32[]{:S(2)}) %collective-permute-start.43) | collective-permute-done | bytes 1048608 | tf_op jit(solution)/shard_map/ppermute | solution.py:149
  403.4 6.1 shard_map.228
  409.5 5.3 collective-permute-done.48.refs_1_
  414.8 8.3 %collective-permute-done.49.refs_2_ = bf16[128,2048]{1,0:T(8,128)(2,1)S(1)} collective-permute-done((bf16[128,2048]{1,0:T(8,128)(2,1)S(1)}, bf16[128,2048]{1,0:T(8,128)(2,1)S(1)}, u32[]{:S(2)}, u32[]{:S(2)}) %collective-permute-start.49) | collective-permute-done | bytes 524320 | tf_op jit(solution)/shard_map/ppermute | solution.py:149
  431.6 11.4 %collective-permute-done.53.refs_1_ = bf16[128,2048]{1,0:T(8,128)(2,1)S(1)} collective-permute-done((bf16[128,2048]{1,0:T(8,128)(2,1)S(1)}, bf16[128,2048]{1,0:T(8,128)(2,1)S(1)}, u32[]{:S(2)}, u32[]{:S(2)}) %collective-permute-start.53) | collective-permute-done | bytes 524320 | tf_op jit(solution)/shard_map/ppermute | solution.py:149
  443.0 6.7 collective-permute-done.54.refs_2_
  457.4 19.9 %collective-permute-done.57.refs_0_ = bf16[512,1024]{1,0:T(8,128)(2,1)S(1)} collective-permute-done((bf16[512,1024]{1,0:T(8,128)(2,1)S(1)}, bf16[512,1024]{1,0:T(8,128)(2,1)S(1)}, u32[]{:S(2)}, u32[]{:S(2)}) %collective-permute-start.57) | collective-permute-done | bytes 1048608 | tf_op jit(solution)/shard_map/ppermute | solution.py:149
  477.3 3.6 collective-permute-done.58
  486.9 23.8 %shard_map.231 = (bf16[2,512,256]{2,1,0:T(8,128)(2,1)S(1)}, bf16[512,1024]{1,0:T(8,128)(2,1)S(1)}) custom-call(s32[1]{0:T(128)} %bitcast.5.here_ref, bf16[2,512,256]{2,1,0:T(8,128)(2,1)S(1)} %copy-done.37, bf16[512,2048]{1,0:T(8,128)(2,1)S(1)} %shard_map.230.mine_ref.refs_3_, bf16[512,2048]{1,0:T(8,128)(2,1)S(1)} %collective-permute-done.59.other_ref.refs_4_, ...), custom_call_target="tpu_custom_call" | custom-call | flops 1 | bytes 1 | tf_op jit(solution)/shard_map/pallas_call | solution.py:291
  517.8 18.4 %collective-permute-done.65.refs_4_ = bf16[512,1024]{1,0:T(8,128)(2,1)S(1)} collective-permute-done((bf16[512,1024]{1,0:T(8,128)(2,1)S(1)}, bf16[512,1024]{1,0:T(8,128)(2,1)S(1)}, u32[]{:S(2)}, u32[]{:S(2)}) %collective-permute-start.65) | collective-permute-done | bytes 1048608 | tf_op jit(solution)/shard_map/ppermute | solution.py:149
  536.2 3.6 collective-permute-done.66
  544.3 5.5 shard_map.232
  549.8 17.2 %collective-permute-done.68.refs_6_ = bf16[512,1024]{1,0:T(8,128)(2,1)S(1)} collective-permute-done((bf16[512,1024]{1,0:T(8,128)(2,1)S(1)}, bf16[512,1024]{1,0:T(8,128)(2,1)S(1)}, u32[]{:S(2)}, u32[]{:S(2)}) %collective-permute-start.68) | collective-permute-done | bytes 1048608 | tf_op jit(solution)/shard_map/ppermute | solution.py:149
  567.7 4.1 collective-permute-start.71
  577.1 11.4 %collective-permute-done.72.refs_1_ = bf16[128,2048]{1,0:T(8,128)(2,1)S(1)} collective-permute-done((bf16[128,2048]{1,0:T(8,128)(2,1)S(1)}, bf16[128,2048]{1,0:T(8,128)(2,1)S(1)}, u32[]{:S(2)}, u32[]{:S(2)}) %collective-permute-start.72) | collective-permute-done | bytes 524320 | tf_op jit(solution)/shard_map/ppermute | solution.py:149
  588.5 10.0 %collective-permute-done.73.refs_2_ = bf16[128,2048]{1,0:T(8,128)(2,1)S(1)} collective-permute-done((bf16[128,2048]{1,0:T(8,128)(2,1)S(1)}, bf16[128,2048]{1,0:T(8,128)(2,1)S(1)}, u32[]{:S(2)}, u32[]{:S(2)}) %collective-permute-start.73) | collective-permute-done | bytes 524320 | tf_op jit(solution)/shard_map/ppermute | solution.py:149
  599.5 3.0 collective-permute-start.76
  605.3 3.2 shard_map.236
  611.5 7.8 %shard_map.235 = (bf16[512,640]{1,0:T(8,128)(2,1)S(1)}, bf16[512,640]{1,0:T(8,128)(2,1)S(1)}, bf16[512,640]{1,0:T(8,128)(2,1)S(1)}, bf16[512,640]{1,0:T(8,128)(2,1)S(1)}) custom-call(bf16[512,2048]{1,0:T(8,128)(2,1)S(1)} %copy-done.32, bf16[512,2048]{1,0:T(8,128)(2,1)S(1)} %copy-done.34, bf16[1024,384]{1,0:T(8,128)(2,1)S(1)} %shard_map.234.refs_2_.refs_0_, ...), custom_call_target="tpu_custom_call" | custom-call | flops 1 | bytes 1 | tf_op jit(solution)/shard_map/pallas_call | solution.py:561
  619.7 4.0 collective-permute-done.76.refs_2_
  624.1 4.1 collective-permute-start.78
  631.9 14.7 %collective-permute-done.79 = bf16[512,640]{1,0:T(8,128)(2,1)S(1)} collective-permute-done((bf16[512,640]{1,0:T(8,128)(2,1)S(1)}, bf16[512,640]{1,0:T(8,128)(2,1)S(1)}, u32[]{:S(2)}, u32[]{:S(2)}) %collective-permute-start.79) | collective-permute-done | bytes 655392 | tf_op jit(solution)/shard_map/ppermute | solution.py:149
  647.4 4.6 collective-permute-done.78.refs_4_
  652.6 4.2 collective-permute-start.84
  659.4 4.2 shard_map.239
  665.2 9.0 %collective-permute-done.85 = bf16[512,640]{1,0:T(8,128)(2,1)S(1)} collective-permute-done((bf16[512,640]{1,0:T(8,128)(2,1)S(1)}, bf16[512,640]{1,0:T(8,128)(2,1)S(1)}, u32[]{:S(2)}, u32[]{:S(2)}) %collective-permute-start.85) | collective-permute-done | bytes 655392 | tf_op jit(solution)/shard_map/ppermute | solution.py:149
  674.2 5.1 collective-permute-done.84.refs_6_
  686.3 4.2 shard_map.241
  690.4 7.2 collective-permute-done.88.refs_1_
  697.6 7.7 %collective-permute-done.89.refs_2_ = bf16[128,2048]{1,0:T(8,128)(2,1)S(1)} collective-permute-done((bf16[128,2048]{1,0:T(8,128)(2,1)S(1)}, bf16[128,2048]{1,0:T(8,128)(2,1)S(1)}, u32[]{:S(2)}, u32[]{:S(2)}) %collective-permute-start.89) | collective-permute-done | bytes 524320 | tf_op jit(solution)/shard_map/ppermute | solution.py:149
  713.0 7.9 %collective-permute-done.92.refs_2_ = bf16[512,640]{1,0:T(8,128)(2,1)S(1)} collective-permute-done((bf16[512,640]{1,0:T(8,128)(2,1)S(1)}, bf16[512,640]{1,0:T(8,128)(2,1)S(1)}, u32[]{:S(2)}, u32[]{:S(2)}) %collective-permute-start.92) | collective-permute-done | bytes 655392 | tf_op jit(solution)/shard_map/ppermute | solution.py:149
  729.7 7.4 collective-permute-done.96.refs_4_
  740.3 3.9 collective-permute-start.101
  746.6 7.3 collective-permute-done.101
  755.6 4.4 shard_map.244
  (499 shorter events, 222.1 us)
Async XLA Ops:
  9.6 27.6 %collective-permute-start.1 = (bf16[144,2048]{1,0:T(8,128)(2,1)}, bf16[144,2048]{1,0:T(8,128)(2,1)S(1)}, u32[]{:S(2)}, u32[]{:S(2)}) collective-permute-start(bf16[144,2048]{1,0:T(8,128)(2,1)} %get-tuple-element.256), channel_id=1, source_target_pairs={{0,16},{8,24},{16,0},{24,8},{1,17},{9,25},{17,1},{25,9},{2,18},{10... | collective-permute-start | bytes 1769480 | tf_op jit(solution)/shard_map/ppermute | solution.py:149
  11.1 26.9 %collective-permute-start.2 = (bf16[144,2048]{1,0:T(8,128)(2,1)S(1)}, bf16[144,2048]{1,0:T(8,128)(2,1)S(1)}, u32[]{:S(2)}, u32[]{:S(2)}) collective-permute-start(bf16[144,2048]{1,0:T(8,128)(2,1)S(1)} %get-tuple-element.257), channel_id=1, source_target_pairs={{0,24},{8,16},{16,8},{24,0},{1,25},{9,17},{17,9},{25,1},{2,26},{10... | collective-permute-start | bytes 1769480 | tf_op jit(solution)/shard_map/ppermute | solution.py:149
  41.1 35.8 %collective-permute-start.6 = (bf16[512,2048]{1,0:T(8,128)(2,1)S(1)}, bf16[512,2048]{1,0:T(8,128)(2,1)}, u32[]{:S(2)}, u32[]{:S(2)}) collective-permute-start(bf16[512,2048]{1,0:T(8,128)(2,1)S(1)} %shard_map.213.refs_0_), channel_id=1, source_target_pairs={{0,1},{1,0},{2,3},{3,2},{4,5},{5,4},{6,7},{7,6},{8,9},{9,8},{10,11... | collective-permute-start | bytes 6291464 | tf_op jit(solution)/shard_map/ppermute | solution.py:84
  45.6 29.7 %collective-permute-start.4 = (bf16[512,640]{1,0:T(8,128)(2,1)}, bf16[512,640]{1,0:T(8,128)(2,1)}, u32[]{:S(2)}, u32[]{:S(2)}) collective-permute-start(bf16[512,640]{1,0:T(8,128)(2,1)} %pad_maximum_fusion.10), channel_id=1, source_target_pairs={{0,16},{8,24},{16,0},{24,8},{1,17},{9,25},{17,1},{25,9},{2,18},{10... | collective-permute-start | bytes 1966088 | tf_op jit(solution)/shard_map/ppermute | solution.py:149
  47.2 29.7 %collective-permute-start.5 = (bf16[512,640]{1,0:T(8,128)(2,1)}, bf16[512,640]{1,0:T(8,128)(2,1)}, u32[]{:S(2)}, u32[]{:S(2)}) collective-permute-start(bf16[512,640]{1,0:T(8,128)(2,1)} %pad_maximum_fusion.11), channel_id=1, source_target_pairs={{0,24},{8,16},{16,8},{24,0},{1,25},{9,17},{17,9},{25,1},{2,26},{10... | collective-permute-start | bytes 1966088 | tf_op jit(solution)/shard_map/ppermute | solution.py:149
  76.9 24.3 %collective-permute-start.7 = (bf16[512,1024]{1,0:T(8,128)(2,1)}, bf16[512,1024]{1,0:T(8,128)(2,1)}, u32[]{:S(2)}, u32[]{:S(2)}) collective-permute-start(bf16[512,1024]{1,0:T(8,128)(2,1)} %pad_maximum_fusion), channel_id=1, source_target_pairs={{0,8},{8,0},{16,24},{24,16},{1,9},{9,1},{17,25},{25,17},{2,10},{10... | collective-permute-start | bytes 3145736 | tf_op jit(solution)/shard_map/ppermute | solution.py:149
  77.7 23.7 %collective-permute-start.8 = (bf16[512,1024]{1,0:T(8,128)(2,1)}, bf16[512,1024]{1,0:T(8,128)(2,1)S(1)}, u32[]{:S(2)}, u32[]{:S(2)}) collective-permute-start(bf16[512,1024]{1,0:T(8,128)(2,1)} %pad_maximum_fusion.1), channel_id=1, source_target_pairs={{0,16},{8,24},{16,0},{24,8},{1,17},{9,25},{17,1},{25,9},{2,18},{10... | collective-permute-start | bytes 3145736 | tf_op jit(solution)/shard_map/ppermute | solution.py:149
  101.4 23.7 %collective-permute-start.12 = (bf16[512,1024]{1,0:T(8,128)(2,1)S(1)}, bf16[512,1024]{1,0:T(8,128)(2,1)S(1)}, u32[]{:S(2)}, u32[]{:S(2)}) collective-permute-start(bf16[512,1024]{1,0:T(8,128)(2,1)S(1)} %pad_maximum_fusion.2), channel_id=1, source_target_pairs={{0,24},{8,16},{16,8},{24,0},{1,25},{9,17},{17,9},{25,1},{2,26},{10... | collective-permute-start | bytes 3145736 | tf_op jit(solution)/shard_map/ppermute | solution.py:149
  125.1 29.3 %collective-permute-start.16 = (bf16[512,1024]{1,0:T(8,128)(2,1)}, bf16[512,1024]{1,0:T(8,128)(2,1)}, u32[]{:S(2)}, u32[]{:S(2)}) collective-permute-start(bf16[512,1024]{1,0:T(8,128)(2,1)} %collective-permute-done.7.refs_4_.refs_5_), channel_id=1, source_target_pairs={{0,2},{2,0},{4,6},{6,4},{1,3},{3,1},{5,7},{7,5},{8,10},{10,8},{12,... | collective-permute-start | bytes 3145736 | tf_op jit(solution)/shard_map/ppermute | solution.py:149
  128.1 22.3 %collective-permute-start.13 = (bf16[128,2048]{1,0:T(8,128)(2,1)}, bf16[128,2048]{1,0:T(8,128)(2,1)}, u32[]{:S(2)}, u32[]{:S(2)}) collective-permute-start(bf16[128,2048]{1,0:T(8,128)(2,1)} %get-tuple-element.281), channel_id=1, source_target_pairs={{0,8},{8,0},{16,24},{24,16},{1,9},{9,1},{17,25},{25,17},{2,10},{10... | collective-permute-start | bytes 1572872 | tf_op jit(solution)/shard_map/ppermute | solution.py:149
  128.7 24.1 %collective-permute-start.14 = (bf16[128,2048]{1,0:T(8,128)(2,1)}, bf16[128,2048]{1,0:T(8,128)(2,1)}, u32[]{:S(2)}, u32[]{:S(2)}) collective-permute-start(bf16[128,2048]{1,0:T(8,128)(2,1)} %get-tuple-element.282), channel_id=1, source_target_pairs={{0,16},{8,24},{16,0},{24,8},{1,17},{9,25},{17,1},{25,9},{2,18},{10... | collective-permute-start | bytes 1572872 | tf_op jit(solution)/shard_map/ppermute | solution.py:149
  130.4 24.0 %collective-permute-start.15 = (bf16[128,2048]{1,0:T(8,128)(2,1)}, bf16[128,2048]{1,0:T(8,128)(2,1)}, u32[]{:S(2)}, u32[]{:S(2)}) collective-permute-start(bf16[128,2048]{1,0:T(8,128)(2,1)} %get-tuple-element.283), channel_id=1, source_target_pairs={{0,24},{8,16},{16,8},{24,0},{1,25},{9,17},{17,9},{25,1},{2,26},{10... | collective-permute-start | bytes 1572872 | tf_op jit(solution)/shard_map/ppermute | solution.py:149
  158.6 26.2 %collective-permute-start.18 = (bf16[512,1024]{1,0:T(8,128)(2,1)S(1)}, bf16[512,1024]{1,0:T(8,128)(2,1)S(1)}, u32[]{:S(2)}, u32[]{:S(2)}) collective-permute-start(bf16[512,1024]{1,0:T(8,128)(2,1)S(1)} %copy-done.23), channel_id=1, source_target_pairs={{0,2},{2,0},{4,6},{6,4},{1,3},{3,1},{5,7},{7,5},{8,10},{10,8},{12,... | collective-permute-start | bytes 3145736 | tf_op jit(solution)/shard_map/ppermute | solution.py:149
  160.1 23.9 %collective-permute-start.20 = (bf16[128,2048]{1,0:T(8,128)(2,1)S(1)}, bf16[128,2048]{1,0:T(8,128)(2,1)S(1)}, u32[]{:S(2)}, u32[]{:S(2)}) collective-permute-start(bf16[128,2048]{1,0:T(8,128)(2,1)S(1)} %get-tuple-element.300), channel_id=1, source_target_pairs={{0,16},{8,24},{16,0},{24,8},{1,17},{9,25},{17,1},{25,9},{2,18},{10... | collective-permute-start | bytes 1572872 | tf_op jit(solution)/shard_map/ppermute | solution.py:149
  161.8 22.9 %collective-permute-start.21 = (bf16[128,2048]{1,0:T(8,128)(2,1)S(1)}, bf16[128,2048]{1,0:T(8,128)(2,1)S(1)}, u32[]{:S(2)}, u32[]{:S(2)}) collective-permute-start(bf16[128,2048]{1,0:T(8,128)(2,1)S(1)} %get-tuple-element.301), channel_id=1, source_target_pairs={{0,24},{8,16},{16,8},{24,0},{1,25},{9,17},{17,9},{25,1},{2,26},{10... | collective-permute-start | bytes 1572872 | tf_op jit(solution)/shard_map/ppermute | solution.py:149
  184.7 30.0 %collective-permute-start.23 = (bf16[512,2048]{1,0:T(8,128)(2,1)S(1)}, bf16[512,2048]{1,0:T(8,128)(2,1)S(1)}, u32[]{:S(2)}, u32[]{:S(2)}) collective-permute-start(bf16[512,2048]{1,0:T(8,128)(2,1)S(1)} %shard_map.218.refs_1_.refs_0_), channel_id=1, source_target_pairs={{0,1},{1,0},{2,3},{3,2},{4,5},{5,4},{6,7},{7,6},{8,9},{9,8},{10,11... | collective-permute-start | bytes 6291464 | tf_op jit(solution)/shard_map/ppermute | solution.py:149
  184.7 30.0 %collective-permute-start.22 = (bf16[512,1024]{1,0:T(8,128)(2,1)S(1)}, bf16[512,1024]{1,0:T(8,128)(2,1)S(1)}, u32[]{:S(2)}, u32[]{:S(2)}) collective-permute-start(bf16[512,1024]{1,0:T(8,128)(2,1)S(1)} %copy-done.25), channel_id=1, source_target_pairs={{0,2},{2,0},{4,6},{6,4},{1,3},{3,1},{5,7},{7,5},{8,10},{10,8},{12,... | collective-permute-start | bytes 3145736 | tf_op jit(solution)/shard_map/ppermute | solution.py:149
  189.8 23.4 %collective-permute-start.25 = (bf16[128,2048]{1,0:T(8,128)(2,1)S(1)}, bf16[128,2048]{1,0:T(8,128)(2,1)S(1)}, u32[]{:S(2)}, u32[]{:S(2)}) collective-permute-start(bf16[128,2048]{1,0:T(8,128)(2,1)S(1)} %get-tuple-element.314), channel_id=1, source_target_pairs={{0,16},{8,24},{16,0},{24,8},{1,17},{9,25},{17,1},{25,9},{2,18},{10... | collective-permute-start | bytes 1572872 | tf_op jit(solution)/shard_map/ppermute | solution.py:149
  190.6 24.1 %collective-permute-start.26 = (bf16[128,2048]{1,0:T(8,128)(2,1)S(1)}, bf16[128,2048]{1,0:T(8,128)(2,1)S(1)}, u32[]{:S(2)}, u32[]{:S(2)}) collective-permute-start(bf16[128,2048]{1,0:T(8,128)(2,1)S(1)} %get-tuple-element.315), channel_id=1, source_target_pairs={{0,24},{8,16},{16,8},{24,0},{1,25},{9,17},{17,9},{25,1},{2,26},{10... | collective-permute-start | bytes 1572872 | tf_op jit(solution)/shard_map/ppermute | solution.py:149
  215.0 25.6 %collective-permute-start.27 = (bf16[512,1024]{1,0:T(8,128)(2,1)S(1)}, bf16[512,1024]{1,0:T(8,128)(2,1)S(1)}, u32[]{:S(2)}, u32[]{:S(2)}) collective-permute-start(bf16[512,1024]{1,0:T(8,128)(2,1)S(1)} %pad_maximum_fusion.3), channel_id=1, source_target_pairs={{0,8},{8,0},{16,24},{24,16},{1,9},{9,1},{17,25},{25,17},{2,10},{10... | collective-permute-start | bytes 3145736 | tf_op jit(solution)/shard_map/ppermute | solution.py:149
  215.6 25.2 %collective-permute-start.28 = (bf16[512,1024]{1,0:T(8,128)(2,1)S(1)}, bf16[512,1024]{1,0:T(8,128)(2,1)S(1)}, u32[]{:S(2)}, u32[]{:S(2)}) collective-permute-start(bf16[512,1024]{1,0:T(8,128)(2,1)S(1)} %pad_maximum_fusion.4), channel_id=1, source_target_pairs={{0,16},{8,24},{16,0},{24,8},{1,17},{9,25},{17,1},{25,9},{2,18},{10... | collective-permute-start | bytes 3145736 | tf_op jit(solution)/shard_map/ppermute | solution.py:149
  240.8 24.3 %collective-permute-start.30 = (bf16[512,1024]{1,0:T(8,128)(2,1)S(1)}, bf16[512,1024]{1,0:T(8,128)(2,1)S(1)}, u32[]{:S(2)}, u32[]{:S(2)}) collective-permute-start(bf16[512,1024]{1,0:T(8,128)(2,1)S(1)} %get-tuple-element.332), channel_id=1, source_target_pairs={{0,2},{6,4},{1,3},{7,5},{8,10},{14,12},{9,11},{15,13},{16,18},{22,... | collective-permute-start | bytes 3145736 | tf_op jit(solution)/shard_map/ppermute | solution.py:149
  243.1 24.4 %collective-permute-start.31 = (bf16[512,1024]{1,0:T(8,128)(2,1)S(1)}, bf16[512,1024]{1,0:T(8,128)(2,1)}, u32[]{:S(2)}, u32[]{:S(2)}) collective-permute-start(bf16[512,1024]{1,0:T(8,128)(2,1)S(1)} %get-tuple-element.333), channel_id=1, source_target_pairs={{0,8},{8,0},{16,24},{24,16},{1,9},{9,1},{17,25},{25,17},{2,10},{10... | collective-permute-start | bytes 3145736 | tf_op jit(solution)/shard_map/ppermute | solution.py:149
  244.7 23.8 %collective-permute-start.32 = (bf16[512,1024]{1,0:T(8,128)(2,1)S(1)}, bf16[512,1024]{1,0:T(8,128)(2,1)S(1)}, u32[]{:S(2)}, u32[]{:S(2)}) collective-permute-start(bf16[512,1024]{1,0:T(8,128)(2,1)S(1)} %get-tuple-element.334), channel_id=1, source_target_pairs={{0,16},{8,24},{16,0},{24,8},{1,17},{9,25},{17,1},{25,9},{2,18},{10... | collective-permute-start | bytes 3145736 | tf_op jit(solution)/shard_map/ppermute | solution.py:149
  271.6 25.1 %collective-permute-start.34 = (bf16[512,1024]{1,0:T(8,128)(2,1)}, bf16[512,1024]{1,0:T(8,128)(2,1)}, u32[]{:S(2)}, u32[]{:S(2)}) collective-permute-start(bf16[512,1024]{1,0:T(8,128)(2,1)} %collective-permute-done.31), channel_id=1, source_target_pairs={{0,2},{6,4},{1,3},{7,5},{8,10},{14,12},{9,11},{15,13},{16,18},{22,... | collective-permute-start | bytes 3145736 | tf_op jit(solution)/shard_map/ppermute | solution.py:149
  276.8 24.0 %collective-permute-start.35 = (bf16[512,1024]{1,0:T(8,128)(2,1)}, bf16[512,1024]{1,0:T(8,128)(2,1)}, u32[]{:S(2)}, u32[]{:S(2)}) collective-permute-start(bf16[512,1024]{1,0:T(8,128)(2,1)} %pad_maximum_fusion.8), channel_id=1, source_target_pairs={{0,24},{8,16},{16,8},{24,0},{1,25},{9,17},{17,9},{25,1},{2,26},{10... | collective-permute-start | bytes 3145736 | tf_op jit(solution)/shard_map/ppermute | solution.py:149
  304.4 29.5 %collective-permute-start.37 = (bf16[512,1024]{1,0:T(8,128)(2,1)}, bf16[512,1024]{1,0:T(8,128)(2,1)}, u32[]{:S(2)}, u32[]{:S(2)}) collective-permute-start(bf16[512,1024]{1,0:T(8,128)(2,1)} %fusion.refs_1_), channel_id=1, source_target_pairs={{0,2},{6,4},{2,0},{4,6},{1,3},{7,5},{3,1},{5,7},{8,10},{14,12},{10... | collective-permute-start | bytes 3145736 | tf_op jit(solution)/shard_map/ppermute | solution.py:149
  306.5 27.4 %collective-permute-start.36 = (bf16[512,1024]{1,0:T(8,128)(2,1)S(1)}, bf16[512,1024]{1,0:T(8,128)(2,1)S(1)}, u32[]{:S(2)}, u32[]{:S(2)}) collective-permute-start(bf16[512,1024]{1,0:T(8,128)(2,1)S(1)} %add_convert_fusion.24), channel_id=1, source_target_pairs={{2,4},{4,2},{3,5},{5,3},{10,12},{12,10},{11,13},{13,11},{18,20},{2... | collective-permute-start | bytes 3145736 | tf_op jit(solution)/shard_map/ppermute | solution.py:149
  307.3 26.7 %collective-permute-start.38 = (bf16[512,1024]{1,0:T(8,128)(2,1)}, bf16[512,1024]{1,0:T(8,128)(2,1)S(1)}, u32[]{:S(2)}, u32[]{:S(2)}) collective-permute-start(bf16[512,1024]{1,0:T(8,128)(2,1)} %copy-done.84), channel_id=1, source_target_pairs={{0,24},{8,16},{16,8},{24,0},{1,25},{9,17},{17,9},{25,1},{2,26},{10... | collective-permute-start | bytes 3145736 | tf_op jit(solution)/shard_map/ppermute | solution.py:149
  334.0 28.0 %collective-permute-start.41 = (bf16[512,2048]{1,0:T(8,128)(2,1)S(1)}, bf16[512,2048]{1,0:T(8,128)(2,1)S(1)}, u32[]{:S(2)}, u32[]{:S(2)}) collective-permute-start(bf16[512,2048]{1,0:T(8,128)(2,1)S(1)} %get-tuple-element.357), channel_id=1, source_target_pairs={{0,1},{1,0},{2,3},{3,2},{4,5},{5,4},{6,7},{7,6},{8,9},{9,8},{10,11... | collective-permute-start | bytes 6291464 | tf_op jit(solution)/shard_map/ppermute | solution.py:149
  334.8 27.2 %collective-permute-start.40 = (bf16[512,1024]{1,0:T(8,128)(2,1)S(1)}, bf16[512,1024]{1,0:T(8,128)(2,1)S(1)}, u32[]{:S(2)}, u32[]{:S(2)}) collective-permute-start(bf16[512,1024]{1,0:T(8,128)(2,1)S(1)} %fusion.1.refs_3_), channel_id=1, source_target_pairs={{0,2},{6,4},{2,0},{4,6},{1,3},{7,5},{3,1},{5,7},{8,10},{14,12},{10... | collective-permute-start | bytes 3145736 | tf_op jit(solution)/shard_map/ppermute | solution.py:149
  339.7 22.3 %collective-permute-start.39 = (bf16[512,1024]{1,0:T(8,128)(2,1)S(1)}, bf16[512,1024]{1,0:T(8,128)(2,1)S(1)}, u32[]{:S(2)}, u32[]{:S(2)}) collective-permute-start(bf16[512,1024]{1,0:T(8,128)(2,1)S(1)} %add_convert_fusion.22), channel_id=1, source_target_pairs={{2,4},{4,2},{3,5},{5,3},{10,12},{12,10},{11,13},{13,11},{18,20},{2... | collective-permute-start | bytes 3145736 | tf_op jit(solution)/shard_map/ppermute | solution.py:149
  362.6 28.0 %collective-permute-start.43 = (bf16[512,1024]{1,0:T(8,128)(2,1)S(1)}, bf16[512,1024]{1,0:T(8,128)(2,1)S(1)}, u32[]{:S(2)}, u32[]{:S(2)}) collective-permute-start(bf16[512,1024]{1,0:T(8,128)(2,1)S(1)} %fusion.2.refs_5_), channel_id=1, source_target_pairs={{0,2},{6,4},{2,0},{4,6},{1,3},{7,5},{3,1},{5,7},{8,10},{14,12},{10... | collective-permute-start | bytes 3145736 | tf_op jit(solution)/shard_map/ppermute | solution.py:149
  369.2 24.1 %collective-permute-start.44 = (bf16[512,1024]{1,0:T(8,128)(2,1)S(1)}, bf16[512,1024]{1,0:T(8,128)(2,1)S(1)}, u32[]{:S(2)}, u32[]{:S(2)}) collective-permute-start(bf16[512,1024]{1,0:T(8,128)(2,1)S(1)} %get-tuple-element.364), channel_id=1, source_target_pairs={{0,8},{8,0},{16,24},{24,16},{1,9},{9,1},{17,25},{25,17},{2,10},{10... | collective-permute-start | bytes 3145736 | tf_op jit(solution)/shard_map/ppermute | solution.py:149
  370.3 23.8 %collective-permute-start.45 = (bf16[512,1024]{1,0:T(8,128)(2,1)S(1)}, bf16[512,1024]{1,0:T(8,128)(2,1)S(1)}, u32[]{:S(2)}, u32[]{:S(2)}) collective-permute-start(bf16[512,1024]{1,0:T(8,128)(2,1)S(1)} %get-tuple-element.365), channel_id=1, source_target_pairs={{0,16},{8,24},{16,0},{24,8},{1,17},{9,25},{17,1},{25,9},{2,18},{10... | collective-permute-start | bytes 3145736 | tf_op jit(solution)/shard_map/ppermute | solution.py:149
  395.2 28.0 %collective-permute-start.47 = (bf16[512,1024]{1,0:T(8,128)(2,1)S(1)}, bf16[512,1024]{1,0:T(8,128)(2,1)S(1)}, u32[]{:S(2)}, u32[]{:S(2)}) collective-permute-start(bf16[512,1024]{1,0:T(8,128)(2,1)S(1)} %fusion.3.refs_7_), channel_id=1, source_target_pairs={{0,2},{6,4},{2,0},{4,6},{1,3},{7,5},{3,1},{5,7},{8,10},{14,12},{10... | collective-permute-start | bytes 3145736 | tf_op jit(solution)/shard_map/ppermute | solution.py:149
  398.5 24.6 %collective-permute-start.46 = (bf16[512,1024]{1,0:T(8,128)(2,1)S(1)}, bf16[512,1024]{1,0:T(8,128)(2,1)S(1)}, u32[]{:S(2)}, u32[]{:S(2)}) collective-permute-start(bf16[512,1024]{1,0:T(8,128)(2,1)S(1)} %add_convert_fusion.18), channel_id=1, source_target_pairs={{2,4},{4,2},{3,5},{5,3},{10,12},{12,10},{11,13},{13,11},{18,20},{2... | collective-permute-start | bytes 3145736 | tf_op jit(solution)/shard_map/ppermute | solution.py:149
  400.9 22.3 %collective-permute-start.49 = (bf16[128,2048]{1,0:T(8,128)(2,1)S(1)}, bf16[128,2048]{1,0:T(8,128)(2,1)S(1)}, u32[]{:S(2)}, u32[]{:S(2)}) collective-permute-start(bf16[128,2048]{1,0:T(8,128)(2,1)S(1)} %get-tuple-element.375), channel_id=1, source_target_pairs={{0,16},{8,24},{16,0},{24,8},{1,17},{9,25},{17,1},{25,9},{2,18},{10... | collective-permute-start | bytes 1572872 | tf_op jit(solution)/shard_map/ppermute | solution.py:149
  423.9 25.8 %collective-permute-start.52 = (bf16[512,1024]{1,0:T(8,128)(2,1)S(1)}, bf16[512,1024]{1,0:T(8,128)(2,1)S(1)}, u32[]{:S(2)}, u32[]{:S(2)}) collective-permute-start(bf16[512,1024]{1,0:T(8,128)(2,1)S(1)} %fusion.4.refs_1_), channel_id=1, source_target_pairs={{0,2},{6,4},{2,0},{4,6},{1,3},{7,5},{3,1},{5,7},{8,10},{14,12},{10... | collective-permute-start | bytes 3145736 | tf_op jit(solution)/shard_map/ppermute | solution.py:149
  426.2 23.5 %collective-permute-start.51 = (bf16[512,1024]{1,0:T(8,128)(2,1)S(1)}, bf16[512,1024]{1,0:T(8,128)(2,1)S(1)}, u32[]{:S(2)}, u32[]{:S(2)}) collective-permute-start(bf16[512,1024]{1,0:T(8,128)(2,1)S(1)} %add_convert_fusion.16), channel_id=1, source_target_pairs={{2,4},{4,2},{3,5},{5,3},{10,12},{12,10},{11,13},{13,11},{18,20},{2... | collective-permute-start | bytes 3145736 | tf_op jit(solution)/shard_map/ppermute | solution.py:149
  449.9 31.0 %collective-permute-start.59 = (bf16[512,2048]{1,0:T(8,128)(2,1)S(1)}, bf16[512,2048]{1,0:T(8,128)(2,1)S(1)}, u32[]{:S(2)}, u32[]{:S(2)}) collective-permute-start(bf16[512,2048]{1,0:T(8,128)(2,1)S(1)} %shard_map.230.mine_ref.refs_3_), channel_id=1, source_target_pairs={{0,1},{1,0},{2,3},{3,2},{4,5},{5,4},{6,7},{7,6},{8,9},{9,8},{10,11... | collective-permute-start | bytes 6291464 | tf_op jit(solution)/shard_map/ppermute | solution.py:149
  451.6 25.7 %collective-permute-start.57 = (bf16[512,1024]{1,0:T(8,128)(2,1)S(1)}, bf16[512,1024]{1,0:T(8,128)(2,1)S(1)}, u32[]{:S(2)}, u32[]{:S(2)}) collective-permute-start(bf16[512,1024]{1,0:T(8,128)(2,1)S(1)} %fusion.5.refs_1_), channel_id=1, source_target_pairs={{0,2},{6,4},{2,0},{4,6},{1,3},{7,5},{3,1},{5,7},{8,10},{14,12},{10... | collective-permute-start | bytes 3145736 | tf_op jit(solution)/shard_map/ppermute | solution.py:149
  454.8 22.4 %collective-permute-start.56 = (bf16[512,1024]{1,0:T(8,128)(2,1)S(1)}, bf16[512,1024]{1,0:T(8,128)(2,1)S(1)}, u32[]{:S(2)}, u32[]{:S(2)}) collective-permute-start(bf16[512,1024]{1,0:T(8,128)(2,1)S(1)} %add_convert_fusion.14), channel_id=1, source_target_pairs={{2,4},{4,2},{3,5},{5,3},{10,12},{12,10},{11,13},{13,11},{18,20},{2... | collective-permute-start | bytes 3145736 | tf_op jit(solution)/shard_map/ppermute | solution.py:149
  455.6 25.3 %collective-permute-start.58 = (bf16[512,1024]{1,0:T(8,128)(2,1)S(1)}, bf16[512,1024]{1,0:T(8,128)(2,1)S(1)}, u32[]{:S(2)}, u32[]{:S(2)}) collective-permute-start(bf16[512,1024]{1,0:T(8,128)(2,1)S(1)} %copy-done.83), channel_id=1, source_target_pairs={{0,24},{8,16},{16,8},{24,0},{1,25},{9,17},{17,9},{25,1},{2,26},{10... | collective-permute-start | bytes 3145736 | tf_op jit(solution)/shard_map/ppermute | solution.py:149
  481.6 29.2 %collective-permute-start.61 = (bf16[512,1024]{1,0:T(8,128)(2,1)S(1)}, bf16[512,1024]{1,0:T(8,128)(2,1)S(1)}, u32[]{:S(2)}, u32[]{:S(2)}) collective-permute-start(bf16[512,1024]{1,0:T(8,128)(2,1)S(1)} %fusion.6.refs_3_), channel_id=1, source_target_pairs={{0,2},{6,4},{2,0},{4,6},{1,3},{7,5},{3,1},{5,7},{8,10},{14,12},{10... | collective-permute-start | bytes 3145736 | tf_op jit(solution)/shard_map/ppermute | solution.py:149
  483.9 26.9 %collective-permute-start.60 = (bf16[512,1024]{1,0:T(8,128)(2,1)S(1)}, bf16[512,1024]{1,0:T(8,128)(2,1)S(1)}, u32[]{:S(2)}, u32[]{:S(2)}) collective-permute-start(bf16[512,1024]{1,0:T(8,128)(2,1)S(1)} %add_convert_fusion.12), channel_id=1, source_target_pairs={{2,4},{4,2},{3,5},{5,3},{10,12},{12,10},{11,13},{13,11},{18,20},{2... | collective-permute-start | bytes 3145736 | tf_op jit(solution)/shard_map/ppermute | solution.py:149
  484.6 26.2 %collective-permute-start.62 = (bf16[512,1024]{1,0:T(8,128)(2,1)S(1)}, bf16[512,1024]{1,0:T(8,128)(2,1)S(1)}, u32[]{:S(2)}, u32[]{:S(2)}) collective-permute-start(bf16[512,1024]{1,0:T(8,128)(2,1)S(1)} %copy-done.81), channel_id=1, source_target_pairs={{0,8},{8,0},{16,24},{24,16},{1,9},{9,1},{17,25},{25,17},{2,10},{10... | collective-permute-start | bytes 3145736 | tf_op jit(solution)/shard_map/ppermute | solution.py:149
  485.6 25.2 %collective-permute-start.63 = (bf16[512,1024]{1,0:T(8,128)(2,1)S(1)}, bf16[512,1024]{1,0:T(8,128)(2,1)S(1)}, u32[]{:S(2)}, u32[]{:S(2)}) collective-permute-start(bf16[512,1024]{1,0:T(8,128)(2,1)S(1)} %copy-done.79), channel_id=1, source_target_pairs={{0,16},{8,24},{16,0},{24,8},{1,17},{9,25},{17,1},{25,9},{2,18},{10... | collective-permute-start | bytes 3145736 | tf_op jit(solution)/shard_map/ppermute | solution.py:149
  512.5 23.7 %collective-permute-start.65 = (bf16[512,1024]{1,0:T(8,128)(2,1)S(1)}, bf16[512,1024]{1,0:T(8,128)(2,1)S(1)}, u32[]{:S(2)}, u32[]{:S(2)}) collective-permute-start(bf16[512,1024]{1,0:T(8,128)(2,1)S(1)} %fusion.7.refs_5_), channel_id=1, source_target_pairs={{0,2},{6,4},{2,0},{4,6},{1,3},{7,5},{3,1},{5,7},{8,10},{14,12},{10... | collective-permute-start | bytes 3145736 | tf_op jit(solution)/shard_map/ppermute | solution.py:149
  516.5 23.2 %collective-permute-start.66 = (bf16[512,1024]{1,0:T(8,128)(2,1)S(1)}, bf16[512,1024]{1,0:T(8,128)(2,1)S(1)}, u32[]{:S(2)}, u32[]{:S(2)}) collective-permute-start(bf16[512,1024]{1,0:T(8,128)(2,1)S(1)} %copy-done.77), channel_id=1, source_target_pairs={{0,24},{8,16},{16,8},{24,0},{1,25},{9,17},{17,9},{25,1},{2,26},{10... | collective-permute-start | bytes 3145736 | tf_op jit(solution)/shard_map/ppermute | solution.py:149
  540.7 26.3 %collective-permute-start.69 = (bf16[512,2048]{1,0:T(8,128)(2,1)}, bf16[512,2048]{1,0:T(8,128)(2,1)S(1)}, u32[]{:S(2)}, u32[]{:S(2)}) collective-permute-start(bf16[512,2048]{1,0:T(8,128)(2,1)} %get-tuple-element.416), channel_id=1, source_target_pairs={{0,1},{1,0},{2,3},{3,2},{4,5},{5,4},{6,7},{7,6},{8,9},{9,8},{10,11... | collective-permute-start | bytes 6291464 | tf_op jit(solution)/shard_map/ppermute | solution.py:149
  541.4 25.6 %collective-permute-start.68 = (bf16[512,1024]{1,0:T(8,128)(2,1)S(1)}, bf16[512,1024]{1,0:T(8,128)(2,1)S(1)}, u32[]{:S(2)}, u32[]{:S(2)}) collective-permute-start(bf16[512,1024]{1,0:T(8,128)(2,1)S(1)} %fusion.8.refs_7_), channel_id=1, source_target_pairs={{0,2},{6,4},{2,0},{4,6},{1,3},{7,5},{3,1},{5,7},{8,10},{14,12},{10... | collective-permute-start | bytes 3145736 | tf_op jit(solution)/shard_map/ppermute | solution.py:149
  543.6 23.4 %collective-permute-start.67 = (bf16[512,1024]{1,0:T(8,128)(2,1)S(1)}, bf16[512,1024]{1,0:T(8,128)(2,1)S(1)}, u32[]{:S(2)}, u32[]{:S(2)}) collective-permute-start(bf16[512,1024]{1,0:T(8,128)(2,1)S(1)} %add_convert_fusion.8), channel_id=1, source_target_pairs={{2,4},{4,2},{3,5},{5,3},{10,12},{12,10},{11,13},{13,11},{18,20},{2... | collective-permute-start | bytes 3145736 | tf_op jit(solution)/shard_map/ppermute | solution.py:149
  567.7 30.8 %collective-permute-start.71 = (bf16[512,1024]{1,0:T(8,128)(2,1)S(1)}, bf16[512,1024]{1,0:T(8,128)(2,1)S(1)}, u32[]{:S(2)}, u32[]{:S(2)}) collective-permute-start(bf16[512,1024]{1,0:T(8,128)(2,1)S(1)} %fusion.9.sent_ref), channel_id=1, source_target_pairs={{0,2},{6,4},{2,0},{4,6},{1,3},{7,5},{3,1},{5,7},{8,10},{14,12},{10... | collective-permute-start | bytes 3145736 | tf_op jit(solution)/shard_map/ppermute | solution.py:149
  572.2 26.3 %collective-permute-start.70 = (bf16[512,1024]{1,0:T(8,128)(2,1)S(1)}, bf16[512,1024]{1,0:T(8,128)(2,1)S(1)}, u32[]{:S(2)}, u32[]{:S(2)}) collective-permute-start(bf16[512,1024]{1,0:T(8,128)(2,1)S(1)} %add_convert_fusion.6), channel_id=1, source_target_pairs={{2,4},{4,2},{3,5},{5,3},{10,12},{12,10},{11,13},{13,11},{18,20},{2... | collective-permute-start | bytes 3145736 | tf_op jit(solution)/shard_map/ppermute | solution.py:149
  574.6 23.9 %collective-permute-start.73 = (bf16[128,2048]{1,0:T(8,128)(2,1)S(1)}, bf16[128,2048]{1,0:T(8,128)(2,1)S(1)}, u32[]{:S(2)}, u32[]{:S(2)}) collective-permute-start(bf16[128,2048]{1,0:T(8,128)(2,1)S(1)} %get-tuple-element.421), channel_id=1, source_target_pairs={{0,16},{8,24},{16,0},{24,8},{1,17},{9,25},{17,1},{25,9},{2,18},{10... | collective-permute-start | bytes 1572872 | tf_op jit(solution)/shard_map/ppermute | solution.py:149
  575.4 23.1 %collective-permute-start.74 = (bf16[128,2048]{1,0:T(8,128)(2,1)S(1)}, bf16[128,2048]{1,0:T(8,128)(2,1)S(1)}, u32[]{:S(2)}, u32[]{:S(2)}) collective-permute-start(bf16[128,2048]{1,0:T(8,128)(2,1)S(1)} %get-tuple-element.422), channel_id=1, source_target_pairs={{0,24},{8,16},{16,8},{24,0},{1,25},{9,17},{17,9},{25,1},{2,26},{10... | collective-permute-start | bytes 1572872 | tf_op jit(solution)/shard_map/ppermute | solution.py:149
  599.5 24.2 %collective-permute-start.76 = (bf16[512,1024]{1,0:T(8,128)(2,1)S(1)}, bf16[512,1024]{1,0:T(8,128)(2,1)S(1)}, u32[]{:S(2)}, u32[]{:S(2)}) collective-permute-start(bf16[512,1024]{1,0:T(8,128)(2,1)S(1)} %fusion.10.refs_3_), channel_id=1, source_target_pairs={{0,2},{6,4},{2,0},{4,6},{1,3},{7,5},{3,1},{5,7},{8,10},{14,12},{10... | collective-permute-start | bytes 3145736 | tf_op jit(solution)/shard_map/ppermute | solution.py:149
  623.6 28.4 %collective-permute-start.81 = (bf16[512,2048]{1,0:T(8,128)(2,1)S(1)}, bf16[512,2048]{1,0:T(8,128)(2,1)S(1)}, u32[]{:S(2)}, u32[]{:S(2)}) collective-permute-start(bf16[512,2048]{1,0:T(8,128)(2,1)S(1)} %copy-done.75), channel_id=1, source_target_pairs={{0,1},{1,0},{2,3},{3,2},{4,5},{5,4},{6,7},{7,6},{8,9},{9,8},{10,11... | collective-permute-start | bytes 6291464 | tf_op jit(solution)/shard_map/ppermute | solution.py:149
  624.1 27.9 %collective-permute-start.78 = (bf16[512,1024]{1,0:T(8,128)(2,1)S(1)}, bf16[512,1024]{1,0:T(8,128)(2,1)S(1)}, u32[]{:S(2)}, u32[]{:S(2)}) collective-permute-start(bf16[512,1024]{1,0:T(8,128)(2,1)S(1)} %fusion.11.refs_5_), channel_id=1, source_target_pairs={{0,2},{6,4},{2,0},{4,6},{1,3},{7,5},{3,1},{5,7},{8,10},{14,12},{10... | collective-permute-start | bytes 3145736 | tf_op jit(solution)/shard_map/ppermute | solution.py:149
  628.9 23.2 %collective-permute-start.77 = (bf16[512,1024]{1,0:T(8,128)(2,1)S(1)}, bf16[512,1024]{1,0:T(8,128)(2,1)S(1)}, u32[]{:S(2)}, u32[]{:S(2)}) collective-permute-start(bf16[512,1024]{1,0:T(8,128)(2,1)S(1)} %add_convert_fusion.2), channel_id=1, source_target_pairs={{2,4},{4,2},{3,5},{5,3},{10,12},{12,10},{11,13},{13,11},{18,20},{2... | collective-permute-start | bytes 3145736 | tf_op jit(solution)/shard_map/ppermute | solution.py:149
  652.6 26.7 %collective-permute-start.84 = (bf16[512,1024]{1,0:T(8,128)(2,1)S(1)}, bf16[512,1024]{1,0:T(8,128)(2,1)S(1)}, u32[]{:S(2)}, u32[]{:S(2)}) collective-permute-start(bf16[512,1024]{1,0:T(8,128)(2,1)S(1)} %fusion.12.refs_7_), channel_id=1, source_target_pairs={{0,2},{6,4},{2,0},{4,6},{1,3},{7,5},{3,1},{5,7},{8,10},{14,12},{10... | collective-permute-start | bytes 3145736 | tf_op jit(solution)/shard_map/ppermute | solution.py:149
  679.5 27.1 %collective-permute-start.87 = (bf16[512,640]{1,0:T(8,128)(2,1)S(1)}, bf16[512,640]{1,0:T(8,128)(2,1)S(1)}, u32[]{:S(2)}, u32[]{:S(2)}) collective-permute-start(bf16[512,640]{1,0:T(8,128)(2,1)S(1)} %fusion.13.refs_1_), channel_id=1, source_target_pairs={{0,2},{6,4},{2,0},{4,6},{1,3},{7,5},{3,1},{5,7},{8,10},{14,12},{10... | collective-permute-start | bytes 1966088 | tf_op jit(solution)/shard_map/ppermute | solution.py:149
  681.5 25.1 %collective-permute-start.86 = (bf16[512,640]{1,0:T(8,128)(2,1)S(1)}, bf16[512,640]{1,0:T(8,128)(2,1)S(1)}, u32[]{:S(2)}, u32[]{:S(2)}) collective-permute-start(bf16[512,640]{1,0:T(8,128)(2,1)S(1)} %add_convert_fusion.32), channel_id=1, source_target_pairs={{2,4},{4,2},{3,5},{5,3},{10,12},{12,10},{11,13},{13,11},{18,20},{2... | collective-permute-start | bytes 1966088 | tf_op jit(solution)/shard_map/ppermute | solution.py:149
  (155 other events, 1619.7 us)

commit v4 on v3

--- a/solution.py
+++ b/solution.py
@@ -124,30 +124,47 @@
     def __init__(self, line):
         self.line = line
         self.got = {}
-        self.names = []
-        self.flying = []
+        self.on_line = []
+        self.others = []
+        self.token = jnp.zeros((8, 128), jnp.float32)
+
+    def wait(self, flying, arrays):
+        count = len(flying)
+        held = lax.optimization_barrier(
+            (self.token,) + tuple(value for _, value in flying) + tuple(arrays)
+        )
+        self.token = held[0]
+        for (name, _), value in zip(flying, held[1:]):
+            self.got[name] = value
+        return list(held[1 + count :])
+
+    def start(self, moves):
+        return [(name, lax.ppermute(value, axis, pairs)) for name, value, axis, pairs in moves]
 
     def step(self, moves=(), summed=None, late=None, carry=()):
-        moves = list(moves)
+        moves, carry = list(moves), list(carry)
+        arrays = [move[1] for move in moves] + carry
         fresh = [summed[1]] if summed is not None and summed[1] is not None else []
-        held = lax.optimization_barrier(
-            tuple(self.flying) + tuple(move[1] for move in moves) + tuple(fresh) + tuple(carry)
-        )
-        count = len(self.flying)
-        for name, value in zip(self.names, held[:count]):
-            self.got[name] = value
-        moves = [
-            (name, value, axis, pairs)
-            for (name, _, axis, pairs), value in zip(moves, held[count:])
-        ]
+        together = summed is not None and not fresh and summed[0] not in self.got
+        if together or not self.on_line:
+            held = self.wait(self.on_line + self.others, fresh + arrays)
+            held_fresh, held = held[: len(fresh)], held[len(fresh) :]
+        else:
+            held_fresh = self.wait(self.on_line, fresh)
         entering = summed
         if summed is not None:
-            entering = (summed[0], held[count + len(moves)] if fresh else self.take(summed[0]))
-        on_line = self.line.advance(self.got, entering)
-        moves = on_line + moves + (late() if late is not None else [])
-        self.names = [move[0] for move in moves]
-        self.flying = [lax.ppermute(value, axis, pairs) for _, value, axis, pairs in moves]
-        return held[len(held) - len(carry) :]
+            entering = (summed[0], held_fresh[0] if fresh else self.take(summed[0]))
+        along = self.line.advance(self.got, entering)
+        if not together and self.on_line:
+            self.on_line = self.start(along)
+            held = self.wait(self.others, arrays)
+        else:
+            self.on_line = self.start(along)
+        moves = [
+            (name, value, axis, pairs) for (name, _, axis, pairs), value in zip(moves, held)
+        ]
+        self.others = self.start(moves + (late() if late is not None else []))
+        return held[len(moves) :]
 
     def take(self, name):
         return self.got.pop(name)
@@ -951,9 +968,7 @@
     )
     all_cot = both_of("cot")
     neighbours = [steps.take(("neighbour", k)) for k in far]
-    names = [name for name in steps.names]
-    kept_two = steps.flying[names.index("two")]
-    normed_two = (kept["two"], kept_two)
+    normed_two = (kept["two"], dict(steps.others)["two"])
 
     gate_val, up_val, hidden, wg, wu = gate_up(
         normed_two, own_gate, own_up, [fetched[k] for k in far], neighbours
@@ -1042,7 +1057,7 @@
         back("wqkvo", d_wqkvo, [1, 2]) + to_core("d_one", second) + to_core("result", result),
         summed=entry("wqkvo", 0, d_wqkvo),
     )
-    steps.step(back("wqkvo", d_wqkvo, [3]), summed=entry("wqkvo", 1))
+    steps.step(late=functools.partial(to_rows, "d_one", first), summed=entry("wqkvo", 1))
 
     def both_rows(own, other):
         return in_vmem(
@@ -1056,13 +1071,6 @@
 
     out_hidden = both_rows(result, steps.take("result"))
     gate_grad = settle_all("wg")
-    out_hidden, gate_grad = steps.step(
-        summed=entry("wqkvo", 2),
-        late=functools.partial(to_rows, "d_one", first),
-        carry=(out_hidden, gate_grad),
-    )
-    up_grad = settle_all("wu")
-
     def gains_to_core():
         kept["in_grad"], d_gain_one = in_vmem(
             functools.partial(in_grad_kernel, packs),
@@ -1086,15 +1094,23 @@
             kept["gains"] = kept["gains"] + steps.take(("gains", k))
         return [(("gains", j), kept["gains"], "ctx", pairs_by(j, cycle)) for j in range(1, cycle)]
 
-    (up_grad,) = steps.step(summed=entry("wqkvo", 3), late=gains_to_core, carry=(up_grad,))
-    steps.step(late=gains_to_packs)
+    out_hidden, gate_grad = steps.step(
+        back("wqkvo", d_wqkvo, [3]),
+        summed=entry("wqkvo", 2),
+        late=gains_to_core,
+        carry=(out_hidden, gate_grad),
+    )
+    up_grad = settle_all("wu")
+
+    (up_grad,) = steps.step(summed=entry("wqkvo", 3), late=gains_to_packs, carry=(up_grad,))
     in_grad = both_rows(kept["in_grad"], steps.take("in_grad"))
     (in_grad,) = steps.step(late=gains_along, carry=(in_grad,))
     steps.step()
+    steps.step()
     shares_of_gains = jnp.stack(
         [kept["gains"]] + [steps.take(("gains", j)) for j in range(1, cycle)]
     )
-    gains = 0.0
+    gains = steps.token[0, 0]
     for place in range(cycle):
         gains = gains + lax.dynamic_index_in_dim(shares_of_gains, here ^ place, 0, keepdims=False)
     q_grad, k_grad, v_grad, o_grad = settle_attention(

time: 767 us -> 734 us (0.957)
  waiting for transfers between devices: 382 us -> 350 us
    ppermute x103, waiting for transfers between devices: 382 us -> 350 us  [start(): lax.ppermute(value, axis, pairs)]
    unnamed x233 -> x217, local copies, waits for them, and re-layouts: 36.6 us -> 32 us
  transfers between devices with their start and end apart: 104 -> 104, of which waited for: 54 -> 53; matrix products, arithmetic and copies ran while one was open for 5% -> 5% of each run, Pallas kernels for 18% -> 19%
where the time goes in v4:
time: 734 us; the launch traced here: 728 us
  waiting for transfers between devices  350 us (48%)
  Pallas kernels  148 us (20%)
  starting transfers between devices  143 us (19%)
  local copies, waits for them, and re-layouts  45.9 us (6%)
  other arithmetic  38 us (5%)
    ppermute x103, waiting for transfers between devices, start(): lax.ppermute(value, axis, pairs)  350 us
    ppermute x103, starting transfers between devices, start(): lax.ppermute(value, axis, pairs)  143 us
    pallas_call x12, Pallas kernels, gridded(): pl.pallas_call(kernel, grid=(steps,), in_specs=[pl.BlockSpec(memory_space...  105 us
    unnamed x217, local copies, waits for them, and re-layouts  32 us
    pallas_call x4, Pallas kernels, weight_grad(): pl.pallas_call(functools.partial(weight_grad_kernel, count, len(terms), s...  27.4 us
    pallas_call x17, Pallas kernels, in_vmem(): pl.pallas_call(kernel, out_shape=out_shape, in_specs=specs, out_specs=[pl...  15.1 us
  transfers between devices with their start and end apart: 104, of which 53 were waited for; matrix products, arithmetic and copies ran while one was open for 5% of the time, Pallas kernels for 19%

profile of v4, /device:TPU:0, one launch (start us, length us, event | category | flops | bytes accessed | tf_op | source)
XLA Modules:
  0.0 727.7 jit_solution(13880069928217859874)
XLA Ops:
  6.6 2.9 collective-permute-start
  18.0 2.7 constant_dynamic-slice_fusion.5
  20.8 2.9 constant_dynamic-slice_fusion.11
  24.9 12.3 %collective-permute-done.1.refs_2_ = bf16[144,2048]{1,0:T(8,128)(2,1)S(1)} collective-permute-done((bf16[144,2048]{1,0:T(8,128)(2,1)}, bf16[144,2048]{1,0:T(8,128)(2,1)S(1)}, u32[]{:S(2)}, u32[]{:S(2)}) %collective-permute-start.1) | collective-permute-done | bytes 589856 | tf_op jit(solution)/shard_map/ppermute | solution.py:142
  50.9 12.2 %collective-permute-done.3.refs_6_ = bf16[512,640]{1,0:T(8,128)(2,1)} collective-permute-done((bf16[512,640]{1,0:T(8,128)(2,1)}, bf16[512,640]{1,0:T(8,128)(2,1)}, u32[]{:S(2)}, u32[]{:S(2)}) %collective-permute-start.3) | collective-permute-done | bytes 655392 | tf_op jit(solution)/shard_map/ppermute | solution.py:142
  63.1 12.1 %collective-permute-done.4.refs_7_ = bf16[512,640]{1,0:T(8,128)(2,1)} collective-permute-done((bf16[512,640]{1,0:T(8,128)(2,1)}, bf16[512,640]{1,0:T(8,128)(2,1)}, u32[]{:S(2)}, u32[]{:S(2)}) %collective-permute-start.4) | collective-permute-done | bytes 655392 | tf_op jit(solution)/shard_map/ppermute | solution.py:142
  81.9 8.0 %shard_map.214 = (bf16[512,2048]{1,0:T(8,128)(2,1)S(1)}, bf16[512,2048]{1,0:T(8,128)(2,1)S(1)}, bf16[2,512,256]{2,1,0:T(8,128)(2,1)S(1)}, bf16[2,512,128]{2,1,0:...) custom-call(bf16[512,2048]{1,0:T(8,128)(2,1)S(1)} %shard_map.213.refs_0_, ...), custom_call_target="tpu_custom_call" | custom-call | flops 1 | bytes 1 | tf_op jit(solution)/shard_map/pallas_call | solution.py:308
  94.5 6.7 collective-permute-done.7.refs_4_.refs_5_
  112.5 12.1 %collective-permute-done.10.refs_2_ = bf16[2,512,128]{2,1,0:T(8,128)(2,1)S(1)} collective-permute-done((bf16[2,512,128]{2,1,0:T(8,128)(2,1)S(1)}, bf16[2,512,128]{2,1,0:T(8,128)(2,1)S(1)}, u32[]{:S(2)}, u32[]{:S(2)}) %collective-permute-start.10) | collective-permute-done | bytes 262176 | tf_op jit(solution)/shard_map/ppermute | solution.py:142
  138.0 12.9 %shard_map.216 = (bf16[2,512,256]{2,1,0:T(8,128)(2,1)S(1)}, bf16[512,2048]{1,0:T(8,128)(2,1)S(1)}, bf16[512,2048]{1,0:T(8,128)(2,1)S(1)}) custom-call(bf16[2,512,256]{2,1,0:T(8,128)(2,1)S(1)} %copy-done.40, s32[4,256,1]{2,1,0:T(8,128)S(1)} %copy.32.place_ref, s32[4,256,1]{2,1,0:T(8,128)S(1)} %copy.33.start_ref, ...), custom_call_target="tpu_custom_call" | custom-call | flops 1 | bytes 1 | tf_op jit(solution)/shard_map/pallas_call | solution.py:308
  152.2 4.2 collective-permute-done.17.came_ref
  162.4 9.6 %collective-permute-done.19.refs_1_ = bf16[128,2048]{1,0:T(8,128)(2,1)S(1)} collective-permute-done((bf16[128,2048]{1,0:T(8,128)(2,1)S(1)}, bf16[128,2048]{1,0:T(8,128)(2,1)S(1)}, u32[]{:S(2)}, u32[]{:S(2)}) %collective-permute-start.19) | collective-permute-done | bytes 524320 | tf_op jit(solution)/shard_map/ppermute | solution.py:142
  172.0 9.7 %collective-permute-done.20.refs_2_ = bf16[128,2048]{1,0:T(8,128)(2,1)S(1)} collective-permute-done((bf16[128,2048]{1,0:T(8,128)(2,1)S(1)}, bf16[128,2048]{1,0:T(8,128)(2,1)S(1)}, u32[]{:S(2)}, u32[]{:S(2)}) %collective-permute-start.20) | collective-permute-done | bytes 524320 | tf_op jit(solution)/shard_map/ppermute | solution.py:142
  192.1 8.7 %collective-permute-done.24.refs_1_ = bf16[128,2048]{1,0:T(8,128)(2,1)S(1)} collective-permute-done((bf16[128,2048]{1,0:T(8,128)(2,1)S(1)}, bf16[128,2048]{1,0:T(8,128)(2,1)S(1)}, u32[]{:S(2)}, u32[]{:S(2)}) %collective-permute-start.24) | collective-permute-done | bytes 524320 | tf_op jit(solution)/shard_map/ppermute | solution.py:142
  200.8 10.1 %collective-permute-done.25.refs_2_ = bf16[128,2048]{1,0:T(8,128)(2,1)S(1)} collective-permute-done((bf16[128,2048]{1,0:T(8,128)(2,1)S(1)}, bf16[128,2048]{1,0:T(8,128)(2,1)S(1)}, u32[]{:S(2)}, u32[]{:S(2)}) %collective-permute-start.25) | collective-permute-done | bytes 524320 | tf_op jit(solution)/shard_map/ppermute | solution.py:142
  216.9 14.5 %shard_map.221 = (f32[1024,1024]{1,0:T(8,128)S(1)}, f32[1024,1024]{1,0:T(8,128)}, bf16[1024,1024]{1,0:T(8,128)(2,1)S(1)}, bf16[2048,1024]{1,0:T(8,128)(2,1)}, bf16[2048,1024]{1,0:T(8,128)(2,1)}) custom-call(bf16[512,2048]{1,0:T(8,128)(2,1)S(1)} %shard_map.220.refs_0_.refs_1_, bf16[512,2048]{1,0:T(8,128)(2,1)S(1)} %collective-permute-done.29.refs_1_.refs_2_, ...), custom_call_target="tpu_custom_call" | custom-call | flops 1 | bytes 1 | tf_op jit(solution)/shard_map/pallas_call | solution.py:308
  231.4 6.4 shard_map.222
  244.4 18.9 %collective-permute-done.31 = bf16[512,1024]{1,0:T(8,128)(2,1)} collective-permute-done((bf16[512,1024]{1,0:T(8,128)(2,1)S(1)}, bf16[512,1024]{1,0:T(8,128)(2,1)}, u32[]{:S(2)}, u32[]{:S(2)}) %collective-permute-start.31) | collective-permute-done | bytes 1048608 | tf_op jit(solution)/shard_map/ppermute | solution.py:142
  267.7 7.8 %collective-permute-start.34 = (bf16[512,1024]{1,0:T(8,128)(2,1)}, bf16[512,1024]{1,0:T(8,128)(2,1)}, u32[]{:S(2)}, u32[]{:S(2)}) collective-permute-start(bf16[512,1024]{1,0:T(8,128)(2,1)} %collective-permute-done.31), channel_id=1, source_target_pairs={{0,2},{6,4},{1,3},{7,5},{8,10},{14,12},{9,11},{15,13},{16,18},{22,... | collective-permute-start | bytes 3145736 | tf_op jit(solution)/shard_map/ppermute | solution.py:142
  276.7 18.5 %collective-permute-done.34 = bf16[512,1024]{1,0:T(8,128)(2,1)} collective-permute-done((bf16[512,1024]{1,0:T(8,128)(2,1)}, bf16[512,1024]{1,0:T(8,128)(2,1)}, u32[]{:S(2)}, u32[]{:S(2)}) %collective-permute-start.34) | collective-permute-done | bytes 1048608 | tf_op jit(solution)/shard_map/ppermute | solution.py:142
  301.4 3.5 fusion.refs_1_
  308.6 8.7 %shard_map.223 = (bf16[1024,1024]{1,0:T(8,128)(2,1)S(1)}, bf16[1024,1024]{1,0:T(8,128)(2,1)S(1)}, bf16[2048,1024]{1,0:T(8,128)(2,1)S(1)}) custom-call(bf16[512,2048]{1,0:T(8,128)(2,1)S(1)} %copy-done.3, bf16[512,2048]{1,0:T(8,128)(2,1)S(1)} %copy-done.7, bf16[512,1024]{1,0:T(8,128)(2,1)S(1)} %copy-done.30, bf16[512,1024]{1,0:T(8,128)(2,1)S(1)} %copy-done.61, ...), custom_call_target="tpu_custom_call" | custom-call | flops 1 | bytes 1 | tf_op jit(solution)/shard_map/pallas_call | solution.py:308
  321.6 9.7 %shard_map.224 = (bf16[512,2048]{1,0:T(8,128)(2,1)S(1)}, bf16[512,2048]{1,0:T(8,128)(2,1)S(1)}) custom-call(bf16[1024,1024]{1,0:T(8,128)(2,1)S(1)} %get-tuple-element.404.refs_0_.refs_3_, bf16[1024,1024]{1,0:T(8,128)(2,1)S(1)} %get-tuple-element.405.refs_1_.refs_3_, bf16[2048,1024]{1,0:T(8,128)(2,1)S(1)} %copy-done.15, bf16[2048,1024]{1,0:T(8,128)(2,1)S(1)} %copy-done.16), custom_call_target="tpu_custom_call" | custom-call | flops 1 | bytes 1 | tf_op jit(solution)/shard_map/pallas_call | solution.py:308
  334.9 6.1 shard_map.225
  340.9 14.2 %collective-permute-done.40.refs_2_ = bf16[512,1024]{1,0:T(8,128)(2,1)S(1)} collective-permute-done((bf16[512,1024]{1,0:T(8,128)(2,1)S(1)}, bf16[512,1024]{1,0:T(8,128)(2,1)S(1)}, u32[]{:S(2)}, u32[]{:S(2)}) %collective-permute-start.40) | collective-permute-done | bytes 1048608 | tf_op jit(solution)/shard_map/ppermute | solution.py:142
  356.2 3.7 collective-permute-start.43
  360.6 6.2 shard_map.226
  369.1 9.3 %collective-permute-done.43.refs_4_ = bf16[512,1024]{1,0:T(8,128)(2,1)S(1)} collective-permute-done((bf16[512,1024]{1,0:T(8,128)(2,1)S(1)}, bf16[512,1024]{1,0:T(8,128)(2,1)S(1)}, u32[]{:S(2)}, u32[]{:S(2)}) %collective-permute-start.43) | collective-permute-done | bytes 1048608 | tf_op jit(solution)/shard_map/ppermute | solution.py:142
  379.5 3.7 collective-permute-start.47
  385.3 7.4 %collective-permute-done.44 = bf16[512,1024]{1,0:T(8,128)(2,1)S(1)} collective-permute-done((bf16[512,1024]{1,0:T(8,128)(2,1)S(1)}, bf16[512,1024]{1,0:T(8,128)(2,1)S(1)}, u32[]{:S(2)}, u32[]{:S(2)}) %collective-permute-start.44) | collective-permute-done | bytes 1048608 | tf_op jit(solution)/shard_map/ppermute | solution.py:142
  395.0 6.8 collective-permute-done.47.refs_6_
  402.8 3.6 collective-permute-start.52
  407.2 6.1 shard_map.228
  418.0 5.3 collective-permute-done.52.refs_0_
  423.4 3.1 collective-permute-done.53.refs_1_
  426.4 7.1 collective-permute-done.54.refs_2_
  439.7 21.0 %collective-permute-done.57.refs_0_ = bf16[512,1024]{1,0:T(8,128)(2,1)S(1)} collective-permute-done((bf16[512,1024]{1,0:T(8,128)(2,1)S(1)}, bf16[512,1024]{1,0:T(8,128)(2,1)S(1)}, u32[]{:S(2)}, u32[]{:S(2)}) %collective-permute-start.57) | collective-permute-done | bytes 1048608 | tf_op jit(solution)/shard_map/ppermute | solution.py:142
  460.7 3.6 collective-permute-done.58
  468.4 23.8 %shard_map.231 = (bf16[2,512,256]{2,1,0:T(8,128)(2,1)S(1)}, bf16[512,1024]{1,0:T(8,128)(2,1)S(1)}) custom-call(s32[1]{0:T(128)} %bitcast.5.here_ref, bf16[2,512,256]{2,1,0:T(8,128)(2,1)S(1)} %copy-done.41, bf16[512,2048]{1,0:T(8,128)(2,1)S(1)} %shard_map.230.mine_ref.refs_3_, bf16[512,2048]{1,0:T(8,128)(2,1)S(1)} %collective-permute-done.59.other_ref.refs_4_, ...), custom_call_target="tpu_custom_call" | custom-call | flops 1 | bytes 1 | tf_op jit(solution)/shard_map/pallas_call | solution.py:308
  499.0 17.1 %collective-permute-done.62 = bf16[512,1024]{1,0:T(8,128)(2,1)S(1)} collective-permute-done((bf16[512,1024]{1,0:T(8,128)(2,1)S(1)}, bf16[512,1024]{1,0:T(8,128)(2,1)S(1)}, u32[]{:S(2)}, u32[]{:S(2)}) %collective-permute-start.62) | collective-permute-done | bytes 1048608 | tf_op jit(solution)/shard_map/ppermute | solution.py:142
  520.8 3.7 collective-permute-start.68
  525.3 15.2 %collective-permute-done.66 = bf16[512,1024]{1,0:T(8,128)(2,1)S(1)} collective-permute-done((bf16[512,1024]{1,0:T(8,128)(2,1)S(1)}, bf16[512,1024]{1,0:T(8,128)(2,1)S(1)}, u32[]{:S(2)}, u32[]{:S(2)}) %collective-permute-start.66) | collective-permute-done | bytes 1048608 | tf_op jit(solution)/shard_map/ppermute | solution.py:142
  540.5 4.6 collective-permute-done.68.refs_6_
  546.2 3.7 collective-permute-start.71
  550.6 5.4 shard_map.232
  556.0 13.5 %collective-permute-done.71.came_ref = bf16[512,1024]{1,0:T(8,128)(2,1)S(1)} collective-permute-done((bf16[512,1024]{1,0:T(8,128)(2,1)S(1)}, bf16[512,1024]{1,0:T(8,128)(2,1)S(1)}, u32[]{:S(2)}, u32[]{:S(2)}) %collective-permute-start.71) | collective-permute-done | bytes 1048608 | tf_op jit(solution)/shard_map/ppermute | solution.py:142
  570.6 3.7 collective-permute-start.76
  581.6 3.2 shard_map.236
  586.5 8.7 %shard_map.235 = (bf16[512,640]{1,0:T(8,128)(2,1)S(1)}, bf16[512,640]{1,0:T(8,128)(2,1)S(1)}, bf16[512,640]{1,0:T(8,128)(2,1)S(1)}, bf16[512,640]{1,0:T(8,128)(2,1)}) custom-call(bf16[512,2048]{1,0:T(8,128)(2,1)S(1)} %copy-done.36, bf16[512,2048]{1,0:T(8,128)(2,1)S(1)} %copy-done.38, bf16[1024,384]{1,0:T(8,128)(2,1)S(1)} %shard_map.234.refs_2_.refs_0_, ...), custom_call_target="tpu_custom_call" | custom-call | flops 1 | bytes 1 | tf_op jit(solution)/shard_map/pallas_call | solution.py:578
  595.1 2.9 collective-permute-done.73.refs_2_
  604.5 14.5 %collective-permute-done.79 = bf16[512,640]{1,0:T(8,128)(2,1)S(1)} collective-permute-done((bf16[512,640]{1,0:T(8,128)(2,1)S(1)}, bf16[512,640]{1,0:T(8,128)(2,1)S(1)}, u32[]{:S(2)}, u32[]{:S(2)}) %collective-permute-start.79) | collective-permute-done | bytes 655392 | tf_op jit(solution)/shard_map/ppermute | solution.py:142
  620.1 5.1 collective-permute-done.78.refs_4_
  625.7 3.7 collective-permute-start.84
  634.4 4.2 shard_map.240
  640.1 11.8 %collective-permute-done.84.refs_6_ = bf16[512,1024]{1,0:T(8,128)(2,1)S(1)} collective-permute-done((bf16[512,1024]{1,0:T(8,128)(2,1)S(1)}, bf16[512,1024]{1,0:T(8,128)(2,1)S(1)}, u32[]{:S(2)}, u32[]{:S(2)}) %collective-permute-start.84) | collective-permute-done | bytes 1048608 | tf_op jit(solution)/shard_map/ppermute | solution.py:142
  652.1 3.2 collective-permute-done.86.refs_2_
  662.1 4.2 shard_map.242
  666.2 4.5 collective-permute-done.90
  672.6 3.7 collective-permute-start.94
  677.0 10.9 %collective-permute-done.94.refs_2_ = bf16[512,640]{1,0:T(8,128)(2,1)S(1)} collective-permute-done((bf16[512,640]{1,0:T(8,128)(2,1)S(1)}, bf16[512,640]{1,0:T(8,128)(2,1)S(1)}, u32[]{:S(2)}, u32[]{:S(2)}) %collective-permute-start.94) | collective-permute-done | bytes 655392 | tf_op jit(solution)/shard_map/ppermute | solution.py:142
  696.6 7.2 collective-permute-done.99.refs_4_
  708.0 4.2 collective-permute-start.101
  713.9 6.2 collective-permute-done.100
  722.9 4.4 shard_map.244
  (485 shorter events, 209.6 us)
Async XLA Ops:
  9.6 27.6 %collective-permute-start.1 = (bf16[144,2048]{1,0:T(8,128)(2,1)}, bf16[144,2048]{1,0:T(8,128)(2,1)S(1)}, u32[]{:S(2)}, u32[]{:S(2)}) collective-permute-start(bf16[144,2048]{1,0:T(8,128)(2,1)} %get-tuple-element.299), channel_id=1, source_target_pairs={{0,16},{8,24},{16,0},{24,8},{1,17},{9,25},{17,1},{25,9},{2,18},{10... | collective-permute-start | bytes 1769480 | tf_op jit(solution)/shard_map/ppermute | solution.py:142
  11.1 26.9 %collective-permute-start.2 = (bf16[144,2048]{1,0:T(8,128)(2,1)S(1)}, bf16[144,2048]{1,0:T(8,128)(2,1)S(1)}, u32[]{:S(2)}, u32[]{:S(2)}) collective-permute-start(bf16[144,2048]{1,0:T(8,128)(2,1)S(1)} %get-tuple-element.300), channel_id=1, source_target_pairs={{0,24},{8,16},{16,8},{24,0},{1,25},{9,17},{17,9},{25,1},{2,26},{10... | collective-permute-start | bytes 1769480 | tf_op jit(solution)/shard_map/ppermute | solution.py:142
  41.1 35.8 %collective-permute-start.6 = (bf16[512,2048]{1,0:T(8,128)(2,1)S(1)}, bf16[512,2048]{1,0:T(8,128)(2,1)}, u32[]{:S(2)}, u32[]{:S(2)}) collective-permute-start(bf16[512,2048]{1,0:T(8,128)(2,1)S(1)} %shard_map.213.refs_0_), channel_id=1, source_target_pairs={{0,1},{1,0},{2,3},{3,2},{4,5},{5,4},{6,7},{7,6},{8,9},{9,8},{10,11... | collective-permute-start | bytes 6291464 | tf_op jit(solution)/shard_map/ppermute | solution.py:84
  45.6 29.7 %collective-permute-start.4 = (bf16[512,640]{1,0:T(8,128)(2,1)}, bf16[512,640]{1,0:T(8,128)(2,1)}, u32[]{:S(2)}, u32[]{:S(2)}) collective-permute-start(bf16[512,640]{1,0:T(8,128)(2,1)} %pad_maximum_fusion.10), channel_id=1, source_target_pairs={{0,16},{8,24},{16,0},{24,8},{1,17},{9,25},{17,1},{25,9},{2,18},{10... | collective-permute-start | bytes 1966088 | tf_op jit(solution)/shard_map/ppermute | solution.py:142
  47.2 29.7 %collective-permute-start.5 = (bf16[512,640]{1,0:T(8,128)(2,1)}, bf16[512,640]{1,0:T(8,128)(2,1)}, u32[]{:S(2)}, u32[]{:S(2)}) collective-permute-start(bf16[512,640]{1,0:T(8,128)(2,1)} %pad_maximum_fusion.11), channel_id=1, source_target_pairs={{0,24},{8,16},{16,8},{24,0},{1,25},{9,17},{17,9},{25,1},{2,26},{10... | collective-permute-start | bytes 1966088 | tf_op jit(solution)/shard_map/ppermute | solution.py:142
  76.9 24.3 %collective-permute-start.7 = (bf16[512,1024]{1,0:T(8,128)(2,1)}, bf16[512,1024]{1,0:T(8,128)(2,1)}, u32[]{:S(2)}, u32[]{:S(2)}) collective-permute-start(bf16[512,1024]{1,0:T(8,128)(2,1)} %pad_maximum_fusion), channel_id=1, source_target_pairs={{0,8},{8,0},{16,24},{24,16},{1,9},{9,1},{17,25},{25,17},{2,10},{10... | collective-permute-start | bytes 3145736 | tf_op jit(solution)/shard_map/ppermute | solution.py:142
  77.7 23.7 %collective-permute-start.8 = (bf16[512,1024]{1,0:T(8,128)(2,1)}, bf16[512,1024]{1,0:T(8,128)(2,1)S(1)}, u32[]{:S(2)}, u32[]{:S(2)}) collective-permute-start(bf16[512,1024]{1,0:T(8,128)(2,1)} %pad_maximum_fusion.1), channel_id=1, source_target_pairs={{0,16},{8,24},{16,0},{24,8},{1,17},{9,25},{17,1},{25,9},{2,18},{10... | collective-permute-start | bytes 3145736 | tf_op jit(solution)/shard_map/ppermute | solution.py:142
  101.4 24.6 %collective-permute-start.12 = (bf16[512,1024]{1,0:T(8,128)(2,1)S(1)}, bf16[512,1024]{1,0:T(8,128)(2,1)S(1)}, u32[]{:S(2)}, u32[]{:S(2)}) collective-permute-start(bf16[512,1024]{1,0:T(8,128)(2,1)S(1)} %pad_maximum_fusion.2), channel_id=1, source_target_pairs={{0,24},{8,16},{16,8},{24,0},{1,25},{9,17},{17,9},{25,1},{2,26},{10... | collective-permute-start | bytes 3145736 | tf_op jit(solution)/shard_map/ppermute | solution.py:142
  104.4 20.2 %collective-permute-start.10 = (bf16[2,512,128]{2,1,0:T(8,128)(2,1)S(1)}, bf16[2,512,128]{2,1,0:T(8,128)(2,1)S(1)}, u32[]{:S(2)}, u32[]{:S(2)}) collective-permute-start(bf16[2,512,128]{2,1,0:T(8,128)(2,1)S(1)} %get-tuple-element.321.refs_0_), channel_id=1, source_target_pairs={{0,4},{2,6},{4,0},{6,2},{1,5},{3,7},{5,1},{7,3},{8,12},{10,14},{12... | collective-permute-start | bytes 786440 | tf_op jit(solution)/shard_map/ppermute | solution.py:142
  125.9 26.2 %collective-permute-start.16 = (bf16[512,1024]{1,0:T(8,128)(2,1)}, bf16[512,1024]{1,0:T(8,128)(2,1)}, u32[]{:S(2)}, u32[]{:S(2)}) collective-permute-start(bf16[512,1024]{1,0:T(8,128)(2,1)} %collective-permute-done.7.refs_4_.refs_5_), channel_id=1, source_target_pairs={{0,2},{2,0},{4,6},{6,4},{1,3},{3,1},{5,7},{7,5},{8,10},{10,8},{12,... | collective-permute-start | bytes 3145736 | tf_op jit(solution)/shard_map/ppermute | solution.py:142
  128.6 22.3 %collective-permute-start.13 = (bf16[128,2048]{1,0:T(8,128)(2,1)}, bf16[128,2048]{1,0:T(8,128)(2,1)}, u32[]{:S(2)}, u32[]{:S(2)}) collective-permute-start(bf16[128,2048]{1,0:T(8,128)(2,1)} %get-tuple-element.328), channel_id=1, source_target_pairs={{0,8},{8,0},{16,24},{24,16},{1,9},{9,1},{17,25},{25,17},{2,10},{10... | collective-permute-start | bytes 1572872 | tf_op jit(solution)/shard_map/ppermute | solution.py:142
  129.2 21.8 %collective-permute-start.14 = (bf16[128,2048]{1,0:T(8,128)(2,1)}, bf16[128,2048]{1,0:T(8,128)(2,1)}, u32[]{:S(2)}, u32[]{:S(2)}) collective-permute-start(bf16[128,2048]{1,0:T(8,128)(2,1)} %get-tuple-element.329), channel_id=1, source_target_pairs={{0,16},{8,24},{16,0},{24,8},{1,17},{9,25},{17,1},{25,9},{2,18},{10... | collective-permute-start | bytes 1572872 | tf_op jit(solution)/shard_map/ppermute | solution.py:142
  130.9 21.2 %collective-permute-start.15 = (bf16[128,2048]{1,0:T(8,128)(2,1)}, bf16[128,2048]{1,0:T(8,128)(2,1)}, u32[]{:S(2)}, u32[]{:S(2)}) collective-permute-start(bf16[128,2048]{1,0:T(8,128)(2,1)} %get-tuple-element.330), channel_id=1, source_target_pairs={{0,24},{8,16},{16,8},{24,0},{1,25},{9,17},{17,9},{25,1},{2,26},{10... | collective-permute-start | bytes 1572872 | tf_op jit(solution)/shard_map/ppermute | solution.py:142
  156.3 26.1 %collective-permute-start.18 = (bf16[512,1024]{1,0:T(8,128)(2,1)S(1)}, bf16[512,1024]{1,0:T(8,128)(2,1)S(1)}, u32[]{:S(2)}, u32[]{:S(2)}) collective-permute-start(bf16[512,1024]{1,0:T(8,128)(2,1)S(1)} %copy-done.23), channel_id=1, source_target_pairs={{0,2},{2,0},{4,6},{6,4},{1,3},{3,1},{5,7},{7,5},{8,10},{10,8},{12,... | collective-permute-start | bytes 3145736 | tf_op jit(solution)/shard_map/ppermute | solution.py:142
  157.8 23.9 %collective-permute-start.20 = (bf16[128,2048]{1,0:T(8,128)(2,1)S(1)}, bf16[128,2048]{1,0:T(8,128)(2,1)S(1)}, u32[]{:S(2)}, u32[]{:S(2)}) collective-permute-start(bf16[128,2048]{1,0:T(8,128)(2,1)S(1)} %get-tuple-element.349), channel_id=1, source_target_pairs={{0,16},{8,24},{16,0},{24,8},{1,17},{9,25},{17,1},{25,9},{2,18},{10... | collective-permute-start | bytes 1572872 | tf_op jit(solution)/shard_map/ppermute | solution.py:142
  159.5 22.9 %collective-permute-start.21 = (bf16[128,2048]{1,0:T(8,128)(2,1)S(1)}, bf16[128,2048]{1,0:T(8,128)(2,1)S(1)}, u32[]{:S(2)}, u32[]{:S(2)}) collective-permute-start(bf16[128,2048]{1,0:T(8,128)(2,1)S(1)} %get-tuple-element.350), channel_id=1, source_target_pairs={{0,24},{8,16},{16,8},{24,0},{1,25},{9,17},{17,9},{25,1},{2,26},{10... | collective-permute-start | bytes 1572872 | tf_op jit(solution)/shard_map/ppermute | solution.py:142
  182.4 30.0 %collective-permute-start.23 = (bf16[512,2048]{1,0:T(8,128)(2,1)S(1)}, bf16[512,2048]{1,0:T(8,128)(2,1)S(1)}, u32[]{:S(2)}, u32[]{:S(2)}) collective-permute-start(bf16[512,2048]{1,0:T(8,128)(2,1)S(1)} %shard_map.218.refs_1_.refs_0_), channel_id=1, source_target_pairs={{0,1},{1,0},{2,3},{3,2},{4,5},{5,4},{6,7},{7,6},{8,9},{9,8},{10,11... | collective-permute-start | bytes 6291464 | tf_op jit(solution)/shard_map/ppermute | solution.py:142
  182.5 30.0 %collective-permute-start.22 = (bf16[512,1024]{1,0:T(8,128)(2,1)S(1)}, bf16[512,1024]{1,0:T(8,128)(2,1)S(1)}, u32[]{:S(2)}, u32[]{:S(2)}) collective-permute-start(bf16[512,1024]{1,0:T(8,128)(2,1)S(1)} %copy-done.29), channel_id=1, source_target_pairs={{0,2},{2,0},{4,6},{6,4},{1,3},{3,1},{5,7},{7,5},{8,10},{10,8},{12,... | collective-permute-start | bytes 3145736 | tf_op jit(solution)/shard_map/ppermute | solution.py:142
  187.5 23.4 %collective-permute-start.25 = (bf16[128,2048]{1,0:T(8,128)(2,1)S(1)}, bf16[128,2048]{1,0:T(8,128)(2,1)S(1)}, u32[]{:S(2)}, u32[]{:S(2)}) collective-permute-start(bf16[128,2048]{1,0:T(8,128)(2,1)S(1)} %get-tuple-element.364), channel_id=1, source_target_pairs={{0,16},{8,24},{16,0},{24,8},{1,17},{9,25},{17,1},{25,9},{2,18},{10... | collective-permute-start | bytes 1572872 | tf_op jit(solution)/shard_map/ppermute | solution.py:142
  188.4 24.1 %collective-permute-start.26 = (bf16[128,2048]{1,0:T(8,128)(2,1)S(1)}, bf16[128,2048]{1,0:T(8,128)(2,1)S(1)}, u32[]{:S(2)}, u32[]{:S(2)}) collective-permute-start(bf16[128,2048]{1,0:T(8,128)(2,1)S(1)} %get-tuple-element.365), channel_id=1, source_target_pairs={{0,24},{8,16},{16,8},{24,0},{1,25},{9,17},{17,9},{25,1},{2,26},{10... | collective-permute-start | bytes 1572872 | tf_op jit(solution)/shard_map/ppermute | solution.py:142
  212.7 25.6 %collective-permute-start.27 = (bf16[512,1024]{1,0:T(8,128)(2,1)S(1)}, bf16[512,1024]{1,0:T(8,128)(2,1)S(1)}, u32[]{:S(2)}, u32[]{:S(2)}) collective-permute-start(bf16[512,1024]{1,0:T(8,128)(2,1)S(1)} %pad_maximum_fusion.3), channel_id=1, source_target_pairs={{0,8},{8,0},{16,24},{24,16},{1,9},{9,1},{17,25},{25,17},{2,10},{10... | collective-permute-start | bytes 3145736 | tf_op jit(solution)/shard_map/ppermute | solution.py:142
  213.3 25.2 %collective-permute-start.28 = (bf16[512,1024]{1,0:T(8,128)(2,1)S(1)}, bf16[512,1024]{1,0:T(8,128)(2,1)S(1)}, u32[]{:S(2)}, u32[]{:S(2)}) collective-permute-start(bf16[512,1024]{1,0:T(8,128)(2,1)S(1)} %pad_maximum_fusion.4), channel_id=1, source_target_pairs={{0,16},{8,24},{16,0},{24,8},{1,17},{9,25},{17,1},{25,9},{2,18},{10... | collective-permute-start | bytes 3145736 | tf_op jit(solution)/shard_map/ppermute | solution.py:142
  238.6 24.7 %collective-permute-start.31 = (bf16[512,1024]{1,0:T(8,128)(2,1)S(1)}, bf16[512,1024]{1,0:T(8,128)(2,1)}, u32[]{:S(2)}, u32[]{:S(2)}) collective-permute-start(bf16[512,1024]{1,0:T(8,128)(2,1)S(1)} %get-tuple-element.385), channel_id=1, source_target_pairs={{0,8},{8,0},{16,24},{24,16},{1,9},{9,1},{17,25},{25,17},{2,10},{10... | collective-permute-start | bytes 3145736 | tf_op jit(solution)/shard_map/ppermute | solution.py:142
  240.0 24.1 %collective-permute-start.32 = (bf16[512,1024]{1,0:T(8,128)(2,1)S(1)}, bf16[512,1024]{1,0:T(8,128)(2,1)S(1)}, u32[]{:S(2)}, u32[]{:S(2)}) collective-permute-start(bf16[512,1024]{1,0:T(8,128)(2,1)S(1)} %get-tuple-element.386), channel_id=1, source_target_pairs={{0,16},{8,24},{16,0},{24,8},{1,17},{9,25},{17,1},{25,9},{2,18},{10... | collective-permute-start | bytes 3145736 | tf_op jit(solution)/shard_map/ppermute | solution.py:142
  240.9 23.8 %collective-permute-start.30 = (bf16[512,1024]{1,0:T(8,128)(2,1)S(1)}, bf16[512,1024]{1,0:T(8,128)(2,1)S(1)}, u32[]{:S(2)}, u32[]{:S(2)}) collective-permute-start(bf16[512,1024]{1,0:T(8,128)(2,1)S(1)} %get-tuple-element.384), channel_id=1, source_target_pairs={{0,2},{6,4},{1,3},{7,5},{8,10},{14,12},{9,11},{15,13},{16,18},{22,... | collective-permute-start | bytes 3145736 | tf_op jit(solution)/shard_map/ppermute | solution.py:142
  267.7 27.5 %collective-permute-start.34 = (bf16[512,1024]{1,0:T(8,128)(2,1)}, bf16[512,1024]{1,0:T(8,128)(2,1)}, u32[]{:S(2)}, u32[]{:S(2)}) collective-permute-start(bf16[512,1024]{1,0:T(8,128)(2,1)} %collective-permute-done.31), channel_id=1, source_target_pairs={{0,2},{6,4},{1,3},{7,5},{8,10},{14,12},{9,11},{15,13},{16,18},{22,... | collective-permute-start | bytes 3145736 | tf_op jit(solution)/shard_map/ppermute | solution.py:142
  275.6 23.8 %collective-permute-start.35 = (bf16[512,1024]{1,0:T(8,128)(2,1)}, bf16[512,1024]{1,0:T(8,128)(2,1)}, u32[]{:S(2)}, u32[]{:S(2)}) collective-permute-start(bf16[512,1024]{1,0:T(8,128)(2,1)} %pad_maximum_fusion.8), channel_id=1, source_target_pairs={{0,24},{8,16},{16,8},{24,0},{1,25},{9,17},{17,9},{25,1},{2,26},{10... | collective-permute-start | bytes 3145736 | tf_op jit(solution)/shard_map/ppermute | solution.py:142
  299.3 32.0 %collective-permute-start.38 = (bf16[512,1024]{1,0:T(8,128)(2,1)}, bf16[512,1024]{1,0:T(8,128)(2,1)S(1)}, u32[]{:S(2)}, u32[]{:S(2)}) collective-permute-start(bf16[512,1024]{1,0:T(8,128)(2,1)} %copy-done.82), channel_id=1, source_target_pairs={{0,24},{8,16},{16,8},{24,0},{1,25},{9,17},{17,9},{25,1},{2,26},{10... | collective-permute-start | bytes 3145736 | tf_op jit(solution)/shard_map/ppermute | solution.py:142
  300.5 30.8 %collective-permute-start.36 = (bf16[512,1024]{1,0:T(8,128)(2,1)S(1)}, bf16[512,1024]{1,0:T(8,128)(2,1)S(1)}, u32[]{:S(2)}, u32[]{:S(2)}) collective-permute-start(bf16[512,1024]{1,0:T(8,128)(2,1)S(1)} %add_convert_fusion.24), channel_id=1, source_target_pairs={{2,4},{4,2},{3,5},{5,3},{10,12},{12,10},{11,13},{13,11},{18,20},{2... | collective-permute-start | bytes 3145736 | tf_op jit(solution)/shard_map/ppermute | solution.py:142
  304.8 26.5 %collective-permute-start.37 = (bf16[512,1024]{1,0:T(8,128)(2,1)}, bf16[512,1024]{1,0:T(8,128)(2,1)}, u32[]{:S(2)}, u32[]{:S(2)}) collective-permute-start(bf16[512,1024]{1,0:T(8,128)(2,1)} %fusion.refs_1_), channel_id=1, source_target_pairs={{0,2},{6,4},{2,0},{4,6},{1,3},{7,5},{3,1},{5,7},{8,10},{14,12},{10... | collective-permute-start | bytes 3145736 | tf_op jit(solution)/shard_map/ppermute | solution.py:142
  333.5 21.5 %collective-permute-start.40 = (bf16[512,1024]{1,0:T(8,128)(2,1)S(1)}, bf16[512,1024]{1,0:T(8,128)(2,1)S(1)}, u32[]{:S(2)}, u32[]{:S(2)}) collective-permute-start(bf16[512,1024]{1,0:T(8,128)(2,1)S(1)} %fusion.1.refs_3_), channel_id=1, source_target_pairs={{0,2},{6,4},{2,0},{4,6},{1,3},{7,5},{3,1},{5,7},{8,10},{14,12},{10... | collective-permute-start | bytes 3145736 | tf_op jit(solution)/shard_map/ppermute | solution.py:142
  334.0 21.1 %collective-permute-start.39 = (bf16[512,1024]{1,0:T(8,128)(2,1)S(1)}, bf16[512,1024]{1,0:T(8,128)(2,1)S(1)}, u32[]{:S(2)}, u32[]{:S(2)}) collective-permute-start(bf16[512,1024]{1,0:T(8,128)(2,1)S(1)} %add_convert_fusion.22), channel_id=1, source_target_pairs={{2,4},{4,2},{3,5},{5,3},{10,12},{12,10},{11,13},{13,11},{18,20},{2... | collective-permute-start | bytes 3145736 | tf_op jit(solution)/shard_map/ppermute | solution.py:142
  334.8 32.1 %collective-permute-start.41 = (bf16[512,2048]{1,0:T(8,128)(2,1)S(1)}, bf16[512,2048]{1,0:T(8,128)(2,1)S(1)}, u32[]{:S(2)}, u32[]{:S(2)}) collective-permute-start(bf16[512,2048]{1,0:T(8,128)(2,1)S(1)} %get-tuple-element.415), channel_id=1, source_target_pairs={{0,1},{1,0},{2,3},{3,2},{4,5},{5,4},{6,7},{7,6},{8,9},{9,8},{10,11... | collective-permute-start | bytes 6291464 | tf_op jit(solution)/shard_map/ppermute | solution.py:142
  356.2 22.2 %collective-permute-start.43 = (bf16[512,1024]{1,0:T(8,128)(2,1)S(1)}, bf16[512,1024]{1,0:T(8,128)(2,1)S(1)}, u32[]{:S(2)}, u32[]{:S(2)}) collective-permute-start(bf16[512,1024]{1,0:T(8,128)(2,1)S(1)} %fusion.2.refs_5_), channel_id=1, source_target_pairs={{0,2},{6,4},{2,0},{4,6},{1,3},{7,5},{3,1},{5,7},{8,10},{14,12},{10... | collective-permute-start | bytes 3145736 | tf_op jit(solution)/shard_map/ppermute | solution.py:142
  366.8 25.8 %collective-permute-start.44 = (bf16[512,1024]{1,0:T(8,128)(2,1)S(1)}, bf16[512,1024]{1,0:T(8,128)(2,1)S(1)}, u32[]{:S(2)}, u32[]{:S(2)}) collective-permute-start(bf16[512,1024]{1,0:T(8,128)(2,1)S(1)} %get-tuple-element.424), channel_id=1, source_target_pairs={{0,8},{8,0},{16,24},{24,16},{1,9},{9,1},{17,25},{25,17},{2,10},{10... | collective-permute-start | bytes 3145736 | tf_op jit(solution)/shard_map/ppermute | solution.py:142
  367.7 25.9 %collective-permute-start.45 = (bf16[512,1024]{1,0:T(8,128)(2,1)S(1)}, bf16[512,1024]{1,0:T(8,128)(2,1)S(1)}, u32[]{:S(2)}, u32[]{:S(2)}) collective-permute-start(bf16[512,1024]{1,0:T(8,128)(2,1)S(1)} %get-tuple-element.425), channel_id=1, source_target_pairs={{0,16},{8,24},{16,0},{24,8},{1,17},{9,25},{17,1},{25,9},{2,18},{10... | collective-permute-start | bytes 3145736 | tf_op jit(solution)/shard_map/ppermute | solution.py:142
  379.5 22.2 %collective-permute-start.47 = (bf16[512,1024]{1,0:T(8,128)(2,1)S(1)}, bf16[512,1024]{1,0:T(8,128)(2,1)S(1)}, u32[]{:S(2)}, u32[]{:S(2)}) collective-permute-start(bf16[512,1024]{1,0:T(8,128)(2,1)S(1)} %fusion.3.refs_7_), channel_id=1, source_target_pairs={{0,2},{6,4},{2,0},{4,6},{1,3},{7,5},{3,1},{5,7},{8,10},{14,12},{10... | collective-permute-start | bytes 3145736 | tf_op jit(solution)/shard_map/ppermute | solution.py:142
  384.4 28.9 %collective-permute-start.48 = (bf16[128,2048]{1,0:T(8,128)(2,1)S(1)}, bf16[128,2048]{1,0:T(8,128)(2,1)S(1)}, u32[]{:S(2)}, u32[]{:S(2)}) collective-permute-start(bf16[128,2048]{1,0:T(8,128)(2,1)S(1)} %get-tuple-element.433), channel_id=1, source_target_pairs={{0,8},{8,0},{16,24},{24,16},{1,9},{9,1},{17,25},{25,17},{2,10},{10... | collective-permute-start | bytes 1572872 | tf_op jit(solution)/shard_map/ppermute | solution.py:142
  392.7 20.6 %collective-permute-start.49 = (bf16[128,2048]{1,0:T(8,128)(2,1)S(1)}, bf16[128,2048]{1,0:T(8,128)(2,1)S(1)}, u32[]{:S(2)}, u32[]{:S(2)}) collective-permute-start(bf16[128,2048]{1,0:T(8,128)(2,1)S(1)} %get-tuple-element.434), channel_id=1, source_target_pairs={{0,16},{8,24},{16,0},{24,8},{1,17},{9,25},{17,1},{25,9},{2,18},{10... | collective-permute-start | bytes 1572872 | tf_op jit(solution)/shard_map/ppermute | solution.py:142
  402.8 20.5 %collective-permute-start.52 = (bf16[512,1024]{1,0:T(8,128)(2,1)S(1)}, bf16[512,1024]{1,0:T(8,128)(2,1)S(1)}, u32[]{:S(2)}, u32[]{:S(2)}) collective-permute-start(bf16[512,1024]{1,0:T(8,128)(2,1)S(1)} %fusion.4.refs_1_), channel_id=1, source_target_pairs={{0,2},{6,4},{2,0},{4,6},{1,3},{7,5},{3,1},{5,7},{8,10},{14,12},{10... | collective-permute-start | bytes 3145736 | tf_op jit(solution)/shard_map/ppermute | solution.py:142
  433.7 30.6 %collective-permute-start.59 = (bf16[512,2048]{1,0:T(8,128)(2,1)S(1)}, bf16[512,2048]{1,0:T(8,128)(2,1)S(1)}, u32[]{:S(2)}, u32[]{:S(2)}) collective-permute-start(bf16[512,2048]{1,0:T(8,128)(2,1)S(1)} %shard_map.230.mine_ref.refs_3_), channel_id=1, source_target_pairs={{0,1},{1,0},{2,3},{3,2},{4,5},{5,4},{6,7},{7,6},{8,9},{9,8},{10,11... | collective-permute-start | bytes 6291464 | tf_op jit(solution)/shard_map/ppermute | solution.py:142
  434.4 26.3 %collective-permute-start.57 = (bf16[512,1024]{1,0:T(8,128)(2,1)S(1)}, bf16[512,1024]{1,0:T(8,128)(2,1)S(1)}, u32[]{:S(2)}, u32[]{:S(2)}) collective-permute-start(bf16[512,1024]{1,0:T(8,128)(2,1)S(1)} %fusion.5.refs_1_), channel_id=1, source_target_pairs={{0,2},{6,4},{2,0},{4,6},{1,3},{7,5},{3,1},{5,7},{8,10},{14,12},{10... | collective-permute-start | bytes 3145736 | tf_op jit(solution)/shard_map/ppermute | solution.py:142
  437.3 23.4 %collective-permute-start.56 = (bf16[512,1024]{1,0:T(8,128)(2,1)S(1)}, bf16[512,1024]{1,0:T(8,128)(2,1)S(1)}, u32[]{:S(2)}, u32[]{:S(2)}) collective-permute-start(bf16[512,1024]{1,0:T(8,128)(2,1)S(1)} %add_convert_fusion.14), channel_id=1, source_target_pairs={{2,4},{4,2},{3,5},{5,3},{10,12},{12,10},{11,13},{13,11},{18,20},{2... | collective-permute-start | bytes 3145736 | tf_op jit(solution)/shard_map/ppermute | solution.py:142
  438.1 26.2 %collective-permute-start.58 = (bf16[512,1024]{1,0:T(8,128)(2,1)S(1)}, bf16[512,1024]{1,0:T(8,128)(2,1)S(1)}, u32[]{:S(2)}, u32[]{:S(2)}) collective-permute-start(bf16[512,1024]{1,0:T(8,128)(2,1)S(1)} %copy-done.81), channel_id=1, source_target_pairs={{0,24},{8,16},{16,8},{24,0},{1,25},{9,17},{17,9},{25,1},{2,26},{10... | collective-permute-start | bytes 3145736 | tf_op jit(solution)/shard_map/ppermute | solution.py:142
  465.5 29.0 %collective-permute-start.61 = (bf16[512,1024]{1,0:T(8,128)(2,1)S(1)}, bf16[512,1024]{1,0:T(8,128)(2,1)S(1)}, u32[]{:S(2)}, u32[]{:S(2)}) collective-permute-start(bf16[512,1024]{1,0:T(8,128)(2,1)S(1)} %fusion.6.refs_3_), channel_id=1, source_target_pairs={{0,2},{6,4},{2,0},{4,6},{1,3},{7,5},{3,1},{5,7},{8,10},{14,12},{10... | collective-permute-start | bytes 3145736 | tf_op jit(solution)/shard_map/ppermute | solution.py:142
  467.6 26.9 %collective-permute-start.60 = (bf16[512,1024]{1,0:T(8,128)(2,1)S(1)}, bf16[512,1024]{1,0:T(8,128)(2,1)S(1)}, u32[]{:S(2)}, u32[]{:S(2)}) collective-permute-start(bf16[512,1024]{1,0:T(8,128)(2,1)S(1)} %add_convert_fusion.12), channel_id=1, source_target_pairs={{2,4},{4,2},{3,5},{5,3},{10,12},{12,10},{11,13},{13,11},{18,20},{2... | collective-permute-start | bytes 3145736 | tf_op jit(solution)/shard_map/ppermute | solution.py:142
  492.2 23.8 %collective-permute-start.62 = (bf16[512,1024]{1,0:T(8,128)(2,1)S(1)}, bf16[512,1024]{1,0:T(8,128)(2,1)S(1)}, u32[]{:S(2)}, u32[]{:S(2)}) collective-permute-start(bf16[512,1024]{1,0:T(8,128)(2,1)S(1)} %copy-done.79), channel_id=1, source_target_pairs={{0,8},{8,0},{16,24},{24,16},{1,9},{9,1},{17,25},{25,17},{2,10},{10... | collective-permute-start | bytes 3145736 | tf_op jit(solution)/shard_map/ppermute | solution.py:142
  493.6 23.5 %collective-permute-start.63 = (bf16[512,1024]{1,0:T(8,128)(2,1)S(1)}, bf16[512,1024]{1,0:T(8,128)(2,1)S(1)}, u32[]{:S(2)}, u32[]{:S(2)}) collective-permute-start(bf16[512,1024]{1,0:T(8,128)(2,1)S(1)} %copy-done.77), channel_id=1, source_target_pairs={{0,16},{8,24},{16,0},{24,8},{1,17},{9,25},{17,1},{25,9},{2,18},{10... | collective-permute-start | bytes 3145736 | tf_op jit(solution)/shard_map/ppermute | solution.py:142
  495.6 24.2 %collective-permute-start.65 = (bf16[512,1024]{1,0:T(8,128)(2,1)S(1)}, bf16[512,1024]{1,0:T(8,128)(2,1)S(1)}, u32[]{:S(2)}, u32[]{:S(2)}) collective-permute-start(bf16[512,1024]{1,0:T(8,128)(2,1)S(1)} %fusion.7.refs_5_), channel_id=1, source_target_pairs={{0,2},{6,4},{2,0},{4,6},{1,3},{7,5},{3,1},{5,7},{8,10},{14,12},{10... | collective-permute-start | bytes 3145736 | tf_op jit(solution)/shard_map/ppermute | solution.py:142
  498.3 21.5 %collective-permute-start.64 = (bf16[512,1024]{1,0:T(8,128)(2,1)S(1)}, bf16[512,1024]{1,0:T(8,128)(2,1)S(1)}, u32[]{:S(2)}, u32[]{:S(2)}) collective-permute-start(bf16[512,1024]{1,0:T(8,128)(2,1)S(1)} %add_convert_fusion.10), channel_id=1, source_target_pairs={{2,4},{4,2},{3,5},{5,3},{10,12},{12,10},{11,13},{13,11},{18,20},{2... | collective-permute-start | bytes 3145736 | tf_op jit(solution)/shard_map/ppermute | solution.py:142
  517.0 23.5 %collective-permute-start.66 = (bf16[512,1024]{1,0:T(8,128)(2,1)S(1)}, bf16[512,1024]{1,0:T(8,128)(2,1)S(1)}, u32[]{:S(2)}, u32[]{:S(2)}) collective-permute-start(bf16[512,1024]{1,0:T(8,128)(2,1)S(1)} %copy-done.75), channel_id=1, source_target_pairs={{0,24},{8,16},{16,8},{24,0},{1,25},{9,17},{17,9},{25,1},{2,26},{10... | collective-permute-start | bytes 3145736 | tf_op jit(solution)/shard_map/ppermute | solution.py:142
  520.8 24.3 %collective-permute-start.68 = (bf16[512,1024]{1,0:T(8,128)(2,1)S(1)}, bf16[512,1024]{1,0:T(8,128)(2,1)S(1)}, u32[]{:S(2)}, u32[]{:S(2)}) collective-permute-start(bf16[512,1024]{1,0:T(8,128)(2,1)S(1)} %fusion.8.refs_7_), channel_id=1, source_target_pairs={{0,2},{6,4},{2,0},{4,6},{1,3},{7,5},{3,1},{5,7},{8,10},{14,12},{10... | collective-permute-start | bytes 3145736 | tf_op jit(solution)/shard_map/ppermute | solution.py:142
  524.5 20.5 %collective-permute-start.67 = (bf16[512,1024]{1,0:T(8,128)(2,1)S(1)}, bf16[512,1024]{1,0:T(8,128)(2,1)S(1)}, u32[]{:S(2)}, u32[]{:S(2)}) collective-permute-start(bf16[512,1024]{1,0:T(8,128)(2,1)S(1)} %add_convert_fusion.8), channel_id=1, source_target_pairs={{2,4},{4,2},{3,5},{5,3},{10,12},{12,10},{11,13},{13,11},{18,20},{2... | collective-permute-start | bytes 3145736 | tf_op jit(solution)/shard_map/ppermute | solution.py:142
  546.2 23.3 %collective-permute-start.71 = (bf16[512,1024]{1,0:T(8,128)(2,1)S(1)}, bf16[512,1024]{1,0:T(8,128)(2,1)S(1)}, u32[]{:S(2)}, u32[]{:S(2)}) collective-permute-start(bf16[512,1024]{1,0:T(8,128)(2,1)S(1)} %fusion.9.sent_ref), channel_id=1, source_target_pairs={{0,2},{6,4},{2,0},{4,6},{1,3},{7,5},{3,1},{5,7},{8,10},{14,12},{10... | collective-permute-start | bytes 3145736 | tf_op jit(solution)/shard_map/ppermute | solution.py:142
  570.6 27.7 %collective-permute-start.76 = (bf16[512,1024]{1,0:T(8,128)(2,1)S(1)}, bf16[512,1024]{1,0:T(8,128)(2,1)S(1)}, u32[]{:S(2)}, u32[]{:S(2)}) collective-permute-start(bf16[512,1024]{1,0:T(8,128)(2,1)S(1)} %fusion.10.refs_3_), channel_id=1, source_target_pairs={{0,2},{6,4},{2,0},{4,6},{1,3},{7,5},{3,1},{5,7},{8,10},{14,12},{10... | collective-permute-start | bytes 3145736 | tf_op jit(solution)/shard_map/ppermute | solution.py:142
  574.3 24.0 %collective-permute-start.75 = (bf16[512,1024]{1,0:T(8,128)(2,1)S(1)}, bf16[512,1024]{1,0:T(8,128)(2,1)S(1)}, u32[]{:S(2)}, u32[]{:S(2)}) collective-permute-start(bf16[512,1024]{1,0:T(8,128)(2,1)S(1)} %add_convert_fusion.4), channel_id=1, source_target_pairs={{2,4},{4,2},{3,5},{5,3},{10,12},{12,10},{11,13},{13,11},{18,20},{2... | collective-permute-start | bytes 3145736 | tf_op jit(solution)/shard_map/ppermute | solution.py:142
  577.9 20.1 %collective-permute-start.73 = (bf16[128,2048]{1,0:T(8,128)(2,1)}, bf16[128,2048]{1,0:T(8,128)(2,1)S(1)}, u32[]{:S(2)}, u32[]{:S(2)}) collective-permute-start(bf16[128,2048]{1,0:T(8,128)(2,1)} %get-tuple-element.493), channel_id=1, source_target_pairs={{0,16},{8,24},{16,0},{24,8},{1,17},{9,25},{17,1},{25,9},{2,18},{10... | collective-permute-start | bytes 1572872 | tf_op jit(solution)/shard_map/ppermute | solution.py:142
  598.3 26.9 %collective-permute-start.81 = (bf16[512,2048]{1,0:T(8,128)(2,1)S(1)}, bf16[512,2048]{1,0:T(8,128)(2,1)S(1)}, u32[]{:S(2)}, u32[]{:S(2)}) collective-permute-start(bf16[512,2048]{1,0:T(8,128)(2,1)S(1)} %get-tuple-element.519), channel_id=1, source_target_pairs={{0,1},{1,0},{2,3},{3,2},{4,5},{5,4},{6,7},{7,6},{8,9},{9,8},{10,11... | collective-permute-start | bytes 6291464 | tf_op jit(solution)/shard_map/ppermute | solution.py:142
  599.8 25.4 %collective-permute-start.78 = (bf16[512,1024]{1,0:T(8,128)(2,1)S(1)}, bf16[512,1024]{1,0:T(8,128)(2,1)S(1)}, u32[]{:S(2)}, u32[]{:S(2)}) collective-permute-start(bf16[512,1024]{1,0:T(8,128)(2,1)S(1)} %fusion.11.refs_5_), channel_id=1, source_target_pairs={{0,2},{6,4},{2,0},{4,6},{1,3},{7,5},{3,1},{5,7},{8,10},{14,12},{10... | collective-permute-start | bytes 3145736 | tf_op jit(solution)/shard_map/ppermute | solution.py:142
  601.8 23.4 %collective-permute-start.77 = (bf16[512,1024]{1,0:T(8,128)(2,1)S(1)}, bf16[512,1024]{1,0:T(8,128)(2,1)S(1)}, u32[]{:S(2)}, u32[]{:S(2)}) collective-permute-start(bf16[512,1024]{1,0:T(8,128)(2,1)S(1)} %add_convert_fusion.2), channel_id=1, source_target_pairs={{2,4},{4,2},{3,5},{5,3},{10,12},{12,10},{11,13},{13,11},{18,20},{2... | collective-permute-start | bytes 3145736 | tf_op jit(solution)/shard_map/ppermute | solution.py:142
  625.7 26.2 %collective-permute-start.84 = (bf16[512,1024]{1,0:T(8,128)(2,1)S(1)}, bf16[512,1024]{1,0:T(8,128)(2,1)S(1)}, u32[]{:S(2)}, u32[]{:S(2)}) collective-permute-start(bf16[512,1024]{1,0:T(8,128)(2,1)S(1)} %fusion.12.refs_7_), channel_id=1, source_target_pairs={{0,2},{6,4},{2,0},{4,6},{1,3},{7,5},{3,1},{5,7},{8,10},{14,12},{10... | collective-permute-start | bytes 3145736 | tf_op jit(solution)/shard_map/ppermute | solution.py:142
  630.8 21.3 %collective-permute-start.85 = (bf16[128,2048]{1,0:T(8,128)(2,1)S(1)}, bf16[128,2048]{1,0:T(8,128)(2,1)S(1)}, u32[]{:S(2)}, u32[]{:S(2)}) collective-permute-start(bf16[128,2048]{1,0:T(8,128)(2,1)S(1)} %get-tuple-element.528), channel_id=1, source_target_pairs={{0,8},{8,0},{16,24},{24,16},{1,9},{9,1},{17,25},{25,17},{2,10},{10... | collective-permute-start | bytes 1572872 | tf_op jit(solution)/shard_map/ppermute | solution.py:142
  631.6 23.6 %collective-permute-start.86 = (bf16[128,2048]{1,0:T(8,128)(2,1)S(1)}, bf16[128,2048]{1,0:T(8,128)(2,1)S(1)}, u32[]{:S(2)}, u32[]{:S(2)}) collective-permute-start(bf16[128,2048]{1,0:T(8,128)(2,1)S(1)} %get-tuple-element.529), channel_id=1, source_target_pairs={{0,16},{8,24},{16,0},{24,8},{1,17},{9,25},{17,1},{25,9},{2,18},{10... | collective-permute-start | bytes 1572872 | tf_op jit(solution)/shard_map/ppermute | solution.py:142
  632.8 22.5 %collective-permute-start.87 = (bf16[128,2048]{1,0:T(8,128)(2,1)S(1)}, bf16[128,2048]{1,0:T(8,128)(2,1)S(1)}, u32[]{:S(2)}, u32[]{:S(2)}) collective-permute-start(bf16[128,2048]{1,0:T(8,128)(2,1)S(1)} %get-tuple-element.530), channel_id=1, source_target_pairs={{0,24},{8,16},{16,8},{24,0},{1,25},{9,17},{17,9},{25,1},{2,26},{10... | collective-permute-start | bytes 1572872 | tf_op jit(solution)/shard_map/ppermute | solution.py:142
  (147 other events, 1563.8 us)

commit v5 on v4

--- a/solution.py
+++ b/solution.py
@@ -200,9 +200,7 @@
         ]
 
 
-def prepare_kernel(count, index_ref, x_ref, *refs):
-    extra_ref = refs[0] if len(refs) > count else None
-    own_ref, *sends = refs[-count:]
+def prepare_kernel(count, index_ref, x_ref, own_ref, *sends):
     rows, width = own_ref.shape[0], own_ref.shape[1] // count
     first = pl.multiple_of(index_ref[1] * rows, rows)
     for block in range(count):
@@ -210,23 +208,24 @@
         own_ref[:, block * width : (block + 1) * width] = x_ref[
             pl.ds(first, rows), pl.ds(column, width)
         ]
-    for k in range(1, count):
-        store_seen(sends[k - 1], own_ref[...], k, count)
-        if extra_ref is not None:
-            sends[k - 1][rows:, :] = extra_ref[...]
-
-
-def prepare(x, index, count, extra=()):
+    for k, send in enumerate(sends, 1):
+        store_seen(send, own_ref[...], k, count)
+
+
+def prepare(x, index, count):
     rows, width = x.shape[0] // 2, x.shape[1]
-    more = extra[0].shape[0] if extra else 0
     return in_vmem(
-        functools.partial(prepare_kernel, count),
-        [low(rows, width)] + [low(rows + more, width)] * (count - 1),
-        index,
-        x,
-        *extra,
-        scalars=1,
-    )
+        functools.partial(prepare_kernel, count), [low(rows, width)] * count, index, x, scalars=1
+    )
+
+
+def turns_kernel(offset_ref, cos_ref, sin_ref):
+    lane = lax.broadcasted_iota(jnp.int32, cos_ref.shape, 2)
+    place = lax.rem(lane, HEAD_SIZE // 2).astype(jnp.float32)
+    frequency = jnp.exp(-math.log(500000.0) * place * 2.0 / HEAD_SIZE)
+    angle = offset_ref[...] * frequency
+    cos_ref[...] = jnp.cos(angle)
+    sin_ref[...] = jnp.sin(angle)
 
 
 def join_kernel(*refs):
@@ -234,6 +233,14 @@
     rows = refs[0].shape[0]
     for i, ref in enumerate(refs[:-1]):
         out_ref[i * rows : (i + 1) * rows, :] = ref[:rows, :]
+
+
+def join_rows(arrays, rows):
+    def kernel(*refs):
+        for i, ref in enumerate(refs[:-1]):
+            refs[-1][i * rows : (i + 1) * rows, :] = ref[:rows, :]
+
+    return in_vmem(kernel, [low(rows * len(arrays), arrays[0].shape[1])], *arrays)[0]
 
 
 def join(own, others):
@@ -439,13 +446,12 @@
     return jnp.dot(left, right, preferred_element_type=jnp.float32)
 
 
-def both(mine_ref, other_ref):
-    return jnp.concatenate([mine_ref[...], other_ref[...]], axis=0)
+def both(mine_ref, other_ref, weight):
+    return jnp.concatenate([dot(mine_ref[...], weight), dot(other_ref[...], weight)], axis=0)
 
 
 def gate_up_kernel(count, here_steps, *refs):
-    x = both(refs[0], refs[1])
-    refs = refs[2:]
+    x_refs, refs = refs[:2], refs[2:]
     own, fetched, passed = refs[:2], refs[2 : 2 * count], refs[2 * count : 4 * count - 2]
     gate_ref, up_ref, hidden_ref, wg_ref, wu_ref = refs[4 * count - 2 :]
     here = pl.program_id(0) < here_steps
@@ -458,7 +464,7 @@
             )
         weight = jnp.concatenate(pieces, axis=0)
         out_ref[...] = weight
-        lins.append(dot(x, weight))
+        lins.append(both(*x_refs, weight))
     gate, up = lins
     gate_ref[...] = gate
     up_ref[...] = up
@@ -488,12 +494,11 @@
 
 
 def units_back_kernel(count, *refs):
-    d_out = both(refs[0], refs[1])
-    refs = refs[2:]
+    d_refs, refs = refs[:2], refs[2:]
     pieces, (gate_ref, up_ref, d_gate_ref, d_up_ref, wd_ref) = refs[:count], refs[count:]
     weight = jnp.concatenate([ref[...] for ref in pieces], axis=0)
     wd_ref[...] = weight
-    d_hidden = dot(d_out, weight)
+    d_hidden = both(*d_refs, weight)
     gate, up = gate_ref[...], up_ref[...]
     chance = jax.nn.sigmoid(gate)
     d_up_ref[...] = (d_hidden * (gate * chance)).astype(jnp.bfloat16)
@@ -608,24 +613,33 @@
     return jnp.where(keys, cosine, 1.0), jnp.where(keys, sine, 0.0)
 
 
-def qkv_kernel(count, q_width, kv_width, *refs):
+def qkv_kernel(count, q_width, kv_width, side_ref, *refs):
     x_refs, (gain_ref, cos_ref, sin_ref), refs = refs[:2], refs[2:5], refs[5:]
-    pieces, refs = refs[:count], refs[count:]
+    own_ref, fetched, passed_ref, refs = refs[0], refs[1:count], refs[count], refs[count + 1 :]
     normed_refs, (q_ref, kv_ref, wqkv_ref, wo_ref) = refs[:2], refs[2:]
-    weight = jnp.concatenate([ref[...] for ref in pieces], axis=0)
     qkv_width = q_width + kv_width
+    depth = own_ref.shape[0]
+    half = depth // 2
 
     @pl.when(pl.program_id(0) == 0)
     def _():
-        wqkv_ref[...] = weight[:, :qkv_width]
-        wo_ref[...] = weight[:, qkv_width:]
+        wqkv_ref[:depth, :] = own_ref[:, :qkv_width]
+        wo_ref[:depth, :] = own_ref[:, qkv_width:]
+        for k in range(1, count):
+            for which, piece in (
+                (side_ref[0], fetched[k - 1][:half, :]),
+                (1 - side_ref[0], passed_ref[(k - 1) * half : k * half, :]),
+            ):
+                first = pl.multiple_of(k * depth + which * half, half)
+                wqkv_ref[pl.ds(first, half), :] = piece[:, :qkv_width]
+                wo_ref[pl.ds(first, half), :] = piece[:, qkv_width:]
 
     for i in range(2):
         x = x_refs[i][...].astype(jnp.float32)
         mean = jnp.mean(x * x, axis=-1, keepdims=True)
         normed = (x * lax.rsqrt(mean + 1e-05) * gain_ref[...]).astype(jnp.bfloat16)
         normed_refs[i][...] = normed
-        lin = dot(normed, weight[:, :qkv_width])
+        lin = dot(normed, wqkv_ref[...])
         cosine, sine = cos_ref[i], sin_ref[i]
         q = turned(lin[:, :q_width], side_by_side(cosine, q_width), side_by_side(sine, q_width))
         q_ref[i] = q.astype(jnp.bfloat16)
@@ -633,7 +647,7 @@
         kv_ref[i] = kv.astype(jnp.bfloat16)
 
 
-def project_qkv(x, gain, cosine, sine, pieces, q_width, kv_width):
+def project_qkv(side, x, gain, cosine, sine, own, fetched, passed, q_width, kv_width):
     half_rows, width = x[0].shape
     qkv_width = q_width + kv_width
     block = math.gcd(half_rows, 128)
@@ -646,13 +660,14 @@
 
     lanes = cosine.shape[-1]
     ins = [rows_of(x[0], width), rows_of(x[1], width), still(gain)]
-    ins += [of_both(cosine, lanes), of_both(sine, lanes)] + [still(piece) for piece in pieces]
-    o_width = pieces[0].shape[1] - qkv_width
+    ins += [of_both(cosine, lanes), of_both(sine, lanes)]
+    ins += [still(array) for array in (own, *fetched, passed)]
+    o_width = own.shape[1] - qkv_width
     outs = [rows_of(low(half_rows, width), width)] * 2
     outs += [of_both(low(2, half_rows, q_width), q_width), of_both(low(2, half_rows, kv_width), kv_width)]
     outs += [still(low(width, qkv_width)), still(low(width, o_width))]
-    kernel = functools.partial(qkv_kernel, len(pieces), q_width, kv_width)
-    return gridded(kernel, half_rows // block, ins, outs)
+    kernel = functools.partial(qkv_kernel, len(fetched) + 1, q_width, kv_width)
+    return gridded(kernel, half_rows // block, ins, outs, scalars=(side,))
 
 
 def shares(q, k, visible):
@@ -703,7 +718,7 @@
 ):
     kv_refs, (dq_ref, dkv_ref) = refs[:-2], refs[-2:]
     q, k, v, visible = load_attention(q_ref, place_ref, start_ref, key_place_ref, kv_refs)
-    d_out = dot(both(mine_ref, other_ref), wo_ref[...]).astype(jnp.bfloat16)
+    d_out = both(mine_ref, other_ref, wo_ref[...]).astype(jnp.bfloat16)
     scale = 1.0 / math.sqrt(HEAD_SIZE)
     d_q, d_k, d_v = [], 0.0, 0.0
     for g in range(groups):
@@ -828,38 +843,56 @@
     side_arg = here_arg & 1
     at_end = steps.line.at_end
 
+    own_in, *in_moves = prepare(hidden_in, index, packs)
+    own_cot, *cot_moves = prepare(out_cotangent, index, packs)
+
+    side = here & 1
+    weights = (q_weight, key_projection_weight, value_projection_weight, o_weight)
+    widths = (q_width, k_width, k_width, q_width)
+
+    def attention_piece(k, first, count):
+        return jnp.concatenate(
+            [
+                lax.dynamic_slice(weight, (first, (pack ^ k) * each), (count, each))
+                for weight, each in zip(weights, widths)
+            ],
+            axis=1,
+        )
+
     meta = jnp.concatenate([span_order[0], seq_lengths[0]])
     order_len, meta_len = span_order.shape[1], meta.shape[0]
-    info = jnp.concatenate(
-        [norm1_gain, norm2_gain, (meta // 32).astype(jnp.bfloat16), (meta % 32).astype(jnp.bfloat16)]
-    )
-    info = jnp.pad(info, (0, width - info.shape[0]))[None]
-    own_in, *in_moves = prepare(
-        hidden_in, index, packs, (jnp.pad(info, ((0, 15), (0, 0))),)
-    )
-    own_cot, *cot_moves = prepare(out_cotangent, index, packs)
-
-    def attention_piece(k):
-        return jnp.concatenate(
-            [
-                columns(q_weight, k, q_width),
-                columns(key_projection_weight, k, k_width),
-                columns(value_projection_weight, k, k_width),
-                columns(o_weight, k, q_width),
-            ],
-            axis=1,
-        )
-
-    steps.step(send_all("in", in_moves))
-    steps.step([to_pack("attention", k, attention_piece(k)) for k in far])
-    came = arrived("in")
-    all_in = join(own_in, came)
-    all_in = (all_in, swap(all_in, "tp", 1))
-    infos = jnp.concatenate([info] + [block[half : half + 1] for block in came], axis=0)
-    all_gains = infos[:, : 2 * depth].astype(jnp.float32)
-    gain_one = all_gains[:, :depth].reshape(1, -1)
-    gain_two = all_gains[:, depth:].reshape(1, -1)
-    metas = infos[:, 2 * depth : 2 * depth + 2 * meta_len].astype(jnp.int32)
+    metas = jnp.concatenate([(meta // 32).astype(jnp.bfloat16), (meta % 32).astype(jnp.bfloat16)])
+    info = jnp.stack(
+        [
+            jnp.pad(jnp.concatenate([norm1_gain, metas]), (0, sum(widths) - depth - 2 * meta_len)),
+            jnp.pad(norm2_gain, (0, sum(widths) - depth)),
+        ]
+    )
+    info_rows = jnp.pad(info, ((0, 14), (0, 0)))
+    row_half = depth // 2
+    steps.step(
+        [
+            to_pack(
+                "attention",
+                k,
+                jnp.concatenate([attention_piece(k, side * row_half, row_half), info_rows], axis=0),
+            )
+            for k in far
+        ]
+    )
+    pieces = []
+
+    def pass_rows():
+        pieces.extend(arrived("attention"))
+        rows_on = join_rows(pieces, row_half)
+        return [("attention_rows", rows_on, "ctx", pairs_by(1, cycle))]
+
+    steps.step(send_all("in", in_moves), late=pass_rows)
+    infos = jnp.stack([info] + [piece[row_half : row_half + 2] for piece in pieces])
+    all_gains = infos[:, :, :depth].astype(jnp.float32)
+    gain_one = all_gains[:, 0].reshape(1, -1)
+    gain_two = all_gains[:, 1].reshape(1, -1)
+    metas = infos[:, 0, depth : depth + 2 * meta_len].astype(jnp.int32)
     metas = metas[:, :meta_len] * 32 + metas[:, meta_len:]
     orders, lengths = metas[:, :order_len], metas[:, order_len:]
 
@@ -883,16 +916,12 @@
         starts = jnp.where(places >= end, end, starts)
     place_args = (places[:, :rows, None], starts[:, :rows, None], places[:, None, :])
     offsets = (places - starts)[:, :rows].reshape(packs, 2, half).transpose(1, 0, 2)
-    frequency = jnp.exp(
-        -math.log(500000.0)
-        * (jnp.arange(2 * HEAD_SIZE) % (HEAD_SIZE // 2)).astype(jnp.float32)
-        * 2.0
-        / HEAD_SIZE
-    )
-    angles = offsets.astype(jnp.float32).reshape(2, tokens // 2, 1) * frequency[None, None, :]
-    cosine, sine = jnp.cos(angles), jnp.sin(angles)
-
-    side = here & 1
+    cosine, sine = in_vmem(
+        turns_kernel,
+        [full(2, tokens // 2, 2 * HEAD_SIZE)] * 2,
+        offsets.astype(jnp.float32).reshape(2, tokens // 2, 1),
+    )
+
 
     def two_halves(weight, k):
         return jnp.concatenate(
@@ -923,12 +952,23 @@
         return [(("neighbour", k), fetched[k], "ctx", pairs_by(1, cycle))]
 
     fetched = {}
-    _, cosine, sine, *place_args = steps.step(
-        fetch([1, 2]), carry=(all_in[1], cosine, sine, *place_args)
-    )
-    attention_pieces = [attention_piece(0)] + arrived("attention")
+    own_piece = attention_piece(0, 0, depth)
+    cosine, sine, own_piece, *place_args = steps.step(
+        fetch([1, 2]), carry=(cosine, sine, own_piece, *place_args)
+    )
+    all_in = join(own_in, arrived("in"))
+    all_in = (all_in, swap(all_in, "tp", 1))
     normed_mine, normed_other, q_rot, kv_own, wqkv, wo = project_qkv(
-        all_in, gain_one, cosine, sine, attention_pieces, q_width, 2 * k_width
+        side_arg,
+        all_in,
+        gain_one,
+        cosine,
+        sine,
+        own_piece,
+        pieces,
+        steps.take("attention_rows"),
+        q_width,
+        2 * k_width,
     )
     normed_one = (normed_mine, normed_other)
     steps.step(

time: 734 us -> 728 us (level)
  waiting for transfers between devices: 350 us -> 340 us
    ppermute x103 -> x104, waiting for transfers between devices: 350 us -> 337 us  [start(): lax.ppermute(value, axis, pairs)]
    unnamed x217 -> x210, local copies, waits for them, and re-layouts: 32 us -> 26.6 us
    pallas_call x17 -> x19, Pallas kernels: 15.1 us -> 19.5 us  [in_vmem(): pl.pallas_call(kernel, out_shape=out_shape, in_specs=specs, out_specs=[pl...]
    ppermute x103 -> x104, starting transfers between devices: 143 us -> 147 us  [start(): lax.ppermute(value, axis, pairs)]
  transfers between devices with their start and end apart: 104 -> 105, of which waited for: 53 -> 55; matrix products, arithmetic and copies ran while one was open for 5% -> 5% of each run, Pallas kernels for 19% -> 20%
where the time goes in v5:
time: 728 us; the launch traced here: 721 us
  waiting for transfers between devices  340 us (47%)
  Pallas kernels  149 us (20%)
  starting transfers between devices  147 us (20%)
  other arithmetic  42.7 us (6%)
  local copies, waits for them, and re-layouts  40.5 us (6%)
    ppermute x104, waiting for transfers between devices, start(): lax.ppermute(value, axis, pairs)  337 us
    ppermute x104, starting transfers between devices, start(): lax.ppermute(value, axis, pairs)  147 us
    pallas_call x12, Pallas kernels, gridded(): pl.pallas_call(kernel, grid=(steps,), in_specs=[pl.BlockSpec(memory_space...  103 us
    pallas_call x4, Pallas kernels, weight_grad(): pl.pallas_call(functools.partial(weight_grad_kernel, count, len(terms), s...  27 us
    unnamed x210, local copies, waits for them, and re-layouts  26.6 us
    pallas_call x19, Pallas kernels, in_vmem(): pl.pallas_call(kernel, out_shape=out_shape, in_specs=specs, out_specs=[pl...  19.5 us
    select_n x15, other arithmetic, either_way(): return jnp.where(at_end[0] == 1, fresh, total)  17.7 us
    convert_element_type x19, other arithmetic, add_low(): (left.astype(jnp.float32) + right.astype(jnp.float32)).astype(jnp.bfloat16)  15.2 us
  transfers between devices with their start and end apart: 105, of which 55 were waited for; matrix products, arithmetic and copies ran while one was open for 5% of the time, Pallas kernels for 20%

profile of v5, /device:TPU:0, one launch (start us, length us, event | category | flops | bytes accessed | tf_op | source)
XLA Modules:
  0.0 721.3 jit_solution(6545316606275482537)
XLA Ops:
  13.4 3.1 constant_dynamic-slice_fusion.11
  17.1 4.2 constant_dynamic-slice_fusion.5
  36.4 8.9 %collective-permute-done.3.refs_1_ = bf16[128,2048]{1,0:T(8,128)(2,1)} collective-permute-done((bf16[128,2048]{1,0:T(8,128)(2,1)}, bf16[128,2048]{1,0:T(8,128)(2,1)}, u32[]{:S(2)}, u32[]{:S(2)}) %collective-permute-start.3) | collective-permute-done | bytes 524320 | tf_op jit(solution)/shard_map/ppermute | solution.py:142
  45.3 9.8 %collective-permute-done.4.refs_2_ = bf16[128,2048]{1,0:T(8,128)(2,1)} collective-permute-done((bf16[128,2048]{1,0:T(8,128)(2,1)}, bf16[128,2048]{1,0:T(8,128)(2,1)}, u32[]{:S(2)}, u32[]{:S(2)}) %collective-permute-start.4) | collective-permute-done | bytes 524320 | tf_op jit(solution)/shard_map/ppermute | solution.py:142
  61.1 6.3 shard_map.216
  71.2 11.4 %collective-permute-done.7.refs_4_.refs_5_ = bf16[512,1024]{1,0:T(8,128)(2,1)} collective-permute-done((bf16[512,1024]{1,0:T(8,128)(2,1)S(1)}, bf16[512,1024]{1,0:T(8,128)(2,1)}, u32[]{:S(2)}, u32[]{:S(2)}) %collective-permute-start.7) | collective-permute-done | bytes 1048608 | tf_op jit(solution)/shard_map/ppermute | solution.py:142
  91.2 5.5 collective-permute-done.10.refs_1_
  97.4 8.7 %collective-permute-done.11.refs_2_ = bf16[2,512,128]{2,1,0:T(8,128)(2,1)S(1)} collective-permute-done((bf16[2,512,128]{2,1,0:T(8,128)(2,1)S(1)}, bf16[2,512,128]{2,1,0:T(8,128)(2,1)S(1)}, u32[]{:S(2)}, u32[]{:S(2)}) %collective-permute-start.11) | collective-permute-done | bytes 262176 | tf_op jit(solution)/shard_map/ppermute | solution.py:142
  119.4 12.9 %shard_map.218 = (bf16[2,512,256]{2,1,0:T(8,128)(2,1)S(1)}, bf16[512,2048]{1,0:T(8,128)(2,1)S(1)}, bf16[512,2048]{1,0:T(8,128)(2,1)S(1)}) custom-call(bf16[2,512,256]{2,1,0:T(8,128)(2,1)S(1)} %get-tuple-element.340.q_ref, s32[4,256,1]{2,1,0:T(8,128)S(1)} %copy.39.place_ref, s32[4,256,1]{2,1,0:T(8,128)S(1)} %copy.40.start_ref, ...), custom_call_target="tpu_custom_call" | custom-call | flops 1 | bytes 1 | tf_op jit(solution)/shard_map/pallas_call | solution.py:315
  135.4 4.2 collective-permute-done.18.came_ref
  145.6 9.7 %collective-permute-done.20.refs_1_ = bf16[128,2048]{1,0:T(8,128)(2,1)S(1)} collective-permute-done((bf16[128,2048]{1,0:T(8,128)(2,1)S(1)}, bf16[128,2048]{1,0:T(8,128)(2,1)S(1)}, u32[]{:S(2)}, u32[]{:S(2)}) %collective-permute-start.20) | collective-permute-done | bytes 524320 | tf_op jit(solution)/shard_map/ppermute | solution.py:142
  155.3 10.8 %collective-permute-done.21.refs_2_ = bf16[128,2048]{1,0:T(8,128)(2,1)S(1)} collective-permute-done((bf16[128,2048]{1,0:T(8,128)(2,1)S(1)}, bf16[128,2048]{1,0:T(8,128)(2,1)S(1)}, u32[]{:S(2)}, u32[]{:S(2)}) %collective-permute-start.21) | collective-permute-done | bytes 524320 | tf_op jit(solution)/shard_map/ppermute | solution.py:142
  175.7 8.7 %collective-permute-done.25.refs_1_ = bf16[128,2048]{1,0:T(8,128)(2,1)S(1)} collective-permute-done((bf16[128,2048]{1,0:T(8,128)(2,1)S(1)}, bf16[128,2048]{1,0:T(8,128)(2,1)S(1)}, u32[]{:S(2)}, u32[]{:S(2)}) %collective-permute-start.25) | collective-permute-done | bytes 524320 | tf_op jit(solution)/shard_map/ppermute | solution.py:142
  184.4 9.8 %collective-permute-done.26.refs_2_ = bf16[128,2048]{1,0:T(8,128)(2,1)S(1)} collective-permute-done((bf16[128,2048]{1,0:T(8,128)(2,1)S(1)}, bf16[128,2048]{1,0:T(8,128)(2,1)S(1)}, u32[]{:S(2)}, u32[]{:S(2)}) %collective-permute-start.26) | collective-permute-done | bytes 524320 | tf_op jit(solution)/shard_map/ppermute | solution.py:142
  200.1 14.5 %shard_map.223 = (f32[1024,1024]{1,0:T(8,128)S(1)}, f32[1024,1024]{1,0:T(8,128)}, bf16[1024,1024]{1,0:T(8,128)(2,1)S(1)}, bf16[2048,1024]{1,0:T(8,128)(2,1)}, bf16[2048,1024]{1,0:T(8,128)(2,1)}) custom-call(bf16[512,2048]{1,0:T(8,128)(2,1)S(1)} %shard_map.222.refs_0_.refs_1_, bf16[512,2048]{1,0:T(8,128)(2,1)S(1)} %collective-permute-done.30.refs_1_.refs_2_, ...), custom_call_target="tpu_custom_call" | custom-call | flops 1 | bytes 1 | tf_op jit(solution)/shard_map/pallas_call | solution.py:315
  214.6 6.3 shard_map.224
  227.7 19.0 %collective-permute-done.32 = bf16[512,1024]{1,0:T(8,128)(2,1)} collective-permute-done((bf16[512,1024]{1,0:T(8,128)(2,1)S(1)}, bf16[512,1024]{1,0:T(8,128)(2,1)}, u32[]{:S(2)}, u32[]{:S(2)}) %collective-permute-start.32) | collective-permute-done | bytes 1048608 | tf_op jit(solution)/shard_map/ppermute | solution.py:142
  250.9 8.2 %collective-permute-start.35 = (bf16[512,1024]{1,0:T(8,128)(2,1)}, bf16[512,1024]{1,0:T(8,128)(2,1)}, u32[]{:S(2)}, u32[]{:S(2)}) collective-permute-start(bf16[512,1024]{1,0:T(8,128)(2,1)} %collective-permute-done.32), channel_id=1, source_target_pairs={{0,2},{6,4},{1,3},{7,5},{8,10},{14,12},{9,11},{15,13},{16,18},{22,... | collective-permute-start | bytes 3145736 | tf_op jit(solution)/shard_map/ppermute | solution.py:142
  260.5 18.0 %collective-permute-done.35 = bf16[512,1024]{1,0:T(8,128)(2,1)} collective-permute-done((bf16[512,1024]{1,0:T(8,128)(2,1)}, bf16[512,1024]{1,0:T(8,128)(2,1)}, u32[]{:S(2)}, u32[]{:S(2)}) %collective-permute-start.35) | collective-permute-done | bytes 1048608 | tf_op jit(solution)/shard_map/ppermute | solution.py:142
  278.5 3.2 add_convert_fusion.24
  285.7 3.5 fusion.refs_1_
  293.3 8.9 %shard_map.225 = (bf16[1024,1024]{1,0:T(8,128)(2,1)S(1)}, bf16[1024,1024]{1,0:T(8,128)(2,1)S(1)}, bf16[2048,1024]{1,0:T(8,128)(2,1)S(1)}) custom-call(bf16[512,2048]{1,0:T(8,128)(2,1)S(1)} %copy-done.3, bf16[512,2048]{1,0:T(8,128)(2,1)S(1)} %copy-done.7, bf16[512,1024]{1,0:T(8,128)(2,1)S(1)} %copy-done.29, bf16[512,1024]{1,0:T(8,128)(2,1)S(1)} %copy-done.59, ...), custom_call_target="tpu_custom_call" | custom-call | flops 1 | bytes 1 | tf_op jit(solution)/shard_map/pallas_call | solution.py:315
  306.4 9.7 %shard_map.226 = (bf16[512,2048]{1,0:T(8,128)(2,1)S(1)}, bf16[512,2048]{1,0:T(8,128)(2,1)S(1)}) custom-call(bf16[1024,1024]{1,0:T(8,128)(2,1)S(1)} %get-tuple-element.412.refs_0_.refs_3_, bf16[1024,1024]{1,0:T(8,128)(2,1)S(1)} %get-tuple-element.413.refs_1_.refs_3_, bf16[2048,1024]{1,0:T(8,128)(2,1)S(1)} %copy-done.14, bf16[2048,1024]{1,0:T(8,128)(2,1)S(1)} %copy-done.15), custom_call_target="tpu_custom_call" | custom-call | flops 1 | bytes 1 | tf_op jit(solution)/shard_map/pallas_call | solution.py:315
  321.3 5.9 shard_map.227
  327.3 14.5 %collective-permute-done.41.refs_2_ = bf16[512,1024]{1,0:T(8,128)(2,1)S(1)} collective-permute-done((bf16[512,1024]{1,0:T(8,128)(2,1)S(1)}, bf16[512,1024]{1,0:T(8,128)(2,1)S(1)}, u32[]{:S(2)}, u32[]{:S(2)}) %collective-permute-start.41) | collective-permute-done | bytes 1048608 | tf_op jit(solution)/shard_map/ppermute | solution.py:142
  344.1 3.7 collective-permute-start.44
  348.5 6.1 shard_map.228
  357.6 8.7 %collective-permute-done.44.refs_4_ = bf16[512,1024]{1,0:T(8,128)(2,1)S(1)} collective-permute-done((bf16[512,1024]{1,0:T(8,128)(2,1)S(1)}, bf16[512,1024]{1,0:T(8,128)(2,1)S(1)}, u32[]{:S(2)}, u32[]{:S(2)}) %collective-permute-start.44) | collective-permute-done | bytes 1048608 | tf_op jit(solution)/shard_map/ppermute | solution.py:142
  367.4 3.7 collective-permute-start.48
  373.4 8.3 %collective-permute-done.45 = bf16[512,1024]{1,0:T(8,128)(2,1)S(1)} collective-permute-done((bf16[512,1024]{1,0:T(8,128)(2,1)S(1)}, bf16[512,1024]{1,0:T(8,128)(2,1)S(1)}, u32[]{:S(2)}, u32[]{:S(2)}) %collective-permute-start.45) | collective-permute-done | bytes 1048608 | tf_op jit(solution)/shard_map/ppermute | solution.py:142
  384.3 5.3 collective-permute-done.48.refs_6_
  390.7 3.6 collective-permute-start.53
  395.0 6.1 shard_map.230
  405.8 5.2 collective-permute-done.53.refs_0_
  411.0 3.8 collective-permute-done.54.refs_1_
  414.8 7.5 %collective-permute-done.55.refs_2_ = bf16[128,2048]{1,0:T(8,128)(2,1)S(1)} collective-permute-done((bf16[128,2048]{1,0:T(8,128)(2,1)S(1)}, bf16[128,2048]{1,0:T(8,128)(2,1)S(1)}, u32[]{:S(2)}, u32[]{:S(2)}) %collective-permute-start.55) | collective-permute-done | bytes 524320 | tf_op jit(solution)/shard_map/ppermute | solution.py:142
  429.6 21.2 %collective-permute-done.58.refs_0_ = bf16[512,1024]{1,0:T(8,128)(2,1)S(1)} collective-permute-done((bf16[512,1024]{1,0:T(8,128)(2,1)S(1)}, bf16[512,1024]{1,0:T(8,128)(2,1)S(1)}, u32[]{:S(2)}, u32[]{:S(2)}) %collective-permute-start.58) | collective-permute-done | bytes 1048608 | tf_op jit(solution)/shard_map/ppermute | solution.py:142
  450.8 3.6 collective-permute-done.59
  458.4 22.9 %shard_map.233 = (bf16[2,512,256]{2,1,0:T(8,128)(2,1)S(1)}, bf16[512,1024]{1,0:T(8,128)(2,1)S(1)}) custom-call(s32[1]{0:T(128)} %bitcast.5.here_ref, bf16[2,512,256]{2,1,0:T(8,128)(2,1)S(1)} %copy-done.39, bf16[512,2048]{1,0:T(8,128)(2,1)S(1)} %shard_map.232.mine_ref.refs_3_, bf16[512,2048]{1,0:T(8,128)(2,1)S(1)} %collective-permute-done.60.other_ref.refs_4_, ...), custom_call_target="tpu_custom_call" | custom-call | flops 1 | bytes 1 | tf_op jit(solution)/shard_map/pallas_call | solution.py:315
  487.7 17.7 %collective-permute-done.63 = bf16[512,1024]{1,0:T(8,128)(2,1)S(1)} collective-permute-done((bf16[512,1024]{1,0:T(8,128)(2,1)S(1)}, bf16[512,1024]{1,0:T(8,128)(2,1)S(1)}, u32[]{:S(2)}, u32[]{:S(2)}) %collective-permute-start.63) | collective-permute-done | bytes 1048608 | tf_op jit(solution)/shard_map/ppermute | solution.py:142
  509.9 3.7 collective-permute-start.69
  514.3 15.6 %collective-permute-done.67 = bf16[512,1024]{1,0:T(8,128)(2,1)S(1)} collective-permute-done((bf16[512,1024]{1,0:T(8,128)(2,1)S(1)}, bf16[512,1024]{1,0:T(8,128)(2,1)S(1)}, u32[]{:S(2)}, u32[]{:S(2)}) %collective-permute-start.67) | collective-permute-done | bytes 1048608 | tf_op jit(solution)/shard_map/ppermute | solution.py:142
  529.9 4.6 collective-permute-done.69.refs_6_
  536.5 3.7 collective-permute-start.72
  541.9 5.6 shard_map.234
  547.5 12.7 %collective-permute-done.72.came_ref = bf16[512,1024]{1,0:T(8,128)(2,1)S(1)} collective-permute-done((bf16[512,1024]{1,0:T(8,128)(2,1)S(1)}, bf16[512,1024]{1,0:T(8,128)(2,1)S(1)}, u32[]{:S(2)}, u32[]{:S(2)}) %collective-permute-start.72) | collective-permute-done | bytes 1048608 | tf_op jit(solution)/shard_map/ppermute | solution.py:142
  563.9 4.0 collective-permute-start.77
  576.2 3.2 shard_map.238
  581.1 8.6 %shard_map.237 = (bf16[512,640]{1,0:T(8,128)(2,1)S(1)}, bf16[512,640]{1,0:T(8,128)(2,1)S(1)}, bf16[512,640]{1,0:T(8,128)(2,1)S(1)}, bf16[512,640]{1,0:T(8,128)(2,1)}) custom-call(bf16[512,2048]{1,0:T(8,128)(2,1)S(1)} %copy-done.35, bf16[512,2048]{1,0:T(8,128)(2,1)S(1)} %copy-done.37, bf16[1024,384]{1,0:T(8,128)(2,1)S(1)} %shard_map.236.refs_2_.refs_0_, ...), custom_call_target="tpu_custom_call" | custom-call | flops 1 | bytes 1 | tf_op jit(solution)/shard_map/pallas_call | solution.py:583
  589.7 3.3 collective-permute-done.74.refs_2_
  600.2 14.6 %collective-permute-done.80 = bf16[512,640]{1,0:T(8,128)(2,1)S(1)} collective-permute-done((bf16[512,640]{1,0:T(8,128)(2,1)S(1)}, bf16[512,640]{1,0:T(8,128)(2,1)S(1)}, u32[]{:S(2)}, u32[]{:S(2)}) %collective-permute-start.80) | collective-permute-done | bytes 655392 | tf_op jit(solution)/shard_map/ppermute | solution.py:142
  615.2 6.3 collective-permute-done.79.refs_4_
  622.0 3.7 collective-permute-start.85
  630.6 4.2 shard_map.242
  636.4 11.5 %collective-permute-done.85.refs_6_ = bf16[512,1024]{1,0:T(8,128)(2,1)S(1)} collective-permute-done((bf16[512,1024]{1,0:T(8,128)(2,1)S(1)}, bf16[512,1024]{1,0:T(8,128)(2,1)S(1)}, u32[]{:S(2)}, u32[]{:S(2)}) %collective-permute-start.85) | collective-permute-done | bytes 1048608 | tf_op jit(solution)/shard_map/ppermute | solution.py:142
  648.1 3.3 collective-permute-done.87.refs_2_
  657.7 4.2 shard_map.244
  661.8 4.8 collective-permute-done.91
  667.7 3.7 collective-permute-start.95
  672.1 10.4 %collective-permute-done.95.refs_2_ = bf16[512,640]{1,0:T(8,128)(2,1)S(1)} collective-permute-done((bf16[512,640]{1,0:T(8,128)(2,1)S(1)}, bf16[512,640]{1,0:T(8,128)(2,1)S(1)}, u32[]{:S(2)}, u32[]{:S(2)}) %collective-permute-start.95) | collective-permute-done | bytes 655392 | tf_op jit(solution)/shard_map/ppermute | solution.py:142
  691.5 6.4 collective-permute-done.100.refs_4_
  703.2 3.0 collective-permute-start.102
  708.0 5.7 collective-permute-done.101
  716.5 4.4 shard_map.246
  (483 shorter events, 214.5 us)
Async XLA Ops:
  28.3 26.9 %collective-permute-start.6 = (bf16[768,640]{1,0:T(8,128)(2,1)}, bf16[768,640]{1,0:T(8,128)(2,1)}, u32[]{:S(2)}, u32[]{:S(2)}) collective-permute-start(bf16[768,640]{1,0:T(8,128)(2,1)} %shard_map.213), channel_id=1, source_target_pairs={{0,2},{2,0},{4,6},{6,4},{1,3},{3,1},{5,7},{7,5},{8,10},{10,8},{12,... | collective-permute-start | bytes 2949128 | tf_op jit(solution)/shard_map/ppermute | solution.py:142
  31.4 23.8 %collective-permute-start.4 = (bf16[128,2048]{1,0:T(8,128)(2,1)}, bf16[128,2048]{1,0:T(8,128)(2,1)}, u32[]{:S(2)}, u32[]{:S(2)}) collective-permute-start(bf16[128,2048]{1,0:T(8,128)(2,1)} %get-tuple-element.307), channel_id=1, source_target_pairs={{0,16},{8,24},{16,0},{24,8},{1,17},{9,25},{17,1},{25,9},{2,18},{10... | collective-permute-start | bytes 1572872 | tf_op jit(solution)/shard_map/ppermute | solution.py:142
  32.2 23.0 %collective-permute-start.5 = (bf16[128,2048]{1,0:T(8,128)(2,1)}, bf16[128,2048]{1,0:T(8,128)(2,1)}, u32[]{:S(2)}, u32[]{:S(2)}) collective-permute-start(bf16[128,2048]{1,0:T(8,128)(2,1)} %get-tuple-element.308), channel_id=1, source_target_pairs={{0,24},{8,16},{16,8},{24,0},{1,25},{9,17},{17,9},{25,1},{2,26},{10... | collective-permute-start | bytes 1572872 | tf_op jit(solution)/shard_map/ppermute | solution.py:142
  57.0 25.7 %collective-permute-start.7 = (bf16[512,1024]{1,0:T(8,128)(2,1)S(1)}, bf16[512,1024]{1,0:T(8,128)(2,1)}, u32[]{:S(2)}, u32[]{:S(2)}) collective-permute-start(bf16[512,1024]{1,0:T(8,128)(2,1)S(1)} %copy-done.102), channel_id=1, source_target_pairs={{0,8},{8,0},{16,24},{24,16},{1,9},{9,1},{17,25},{25,17},{2,10},{10... | collective-permute-start | bytes 3145736 | tf_op jit(solution)/shard_map/ppermute | solution.py:142
  57.6 25.2 %collective-permute-start.8 = (bf16[512,1024]{1,0:T(8,128)(2,1)S(1)}, bf16[512,1024]{1,0:T(8,128)(2,1)S(1)}, u32[]{:S(2)}, u32[]{:S(2)}) collective-permute-start(bf16[512,1024]{1,0:T(8,128)(2,1)S(1)} %copy-done.101), channel_id=1, source_target_pairs={{0,16},{8,24},{16,0},{24,8},{1,17},{9,25},{17,1},{25,9},{2,18},{10... | collective-permute-start | bytes 3145736 | tf_op jit(solution)/shard_map/ppermute | solution.py:142
  82.8 25.4 %collective-permute-start.13 = (bf16[512,1024]{1,0:T(8,128)(2,1)S(1)}, bf16[512,1024]{1,0:T(8,128)(2,1)S(1)}, u32[]{:S(2)}, u32[]{:S(2)}) collective-permute-start(bf16[512,1024]{1,0:T(8,128)(2,1)S(1)} %pad_maximum_fusion.2), channel_id=1, source_target_pairs={{0,24},{8,16},{16,8},{24,0},{1,25},{9,17},{17,9},{25,1},{2,26},{10... | collective-permute-start | bytes 3145736 | tf_op jit(solution)/shard_map/ppermute | solution.py:142
  84.7 21.4 %collective-permute-start.11 = (bf16[2,512,128]{2,1,0:T(8,128)(2,1)S(1)}, bf16[2,512,128]{2,1,0:T(8,128)(2,1)S(1)}, u32[]{:S(2)}, u32[]{:S(2)}) collective-permute-start(bf16[2,512,128]{2,1,0:T(8,128)(2,1)S(1)} %get-tuple-element.329.refs_0_), channel_id=1, source_target_pairs={{0,4},{2,6},{4,0},{6,2},{1,5},{3,7},{5,1},{7,3},{8,12},{10,14},{12... | collective-permute-start | bytes 786440 | tf_op jit(solution)/shard_map/ppermute | solution.py:142
  87.3 19.5 %collective-permute-start.12 = (bf16[2,512,128]{2,1,0:T(8,128)(2,1)S(1)}, bf16[2,512,128]{2,1,0:T(8,128)(2,1)S(1)}, u32[]{:S(2)}, u32[]{:S(2)}) collective-permute-start(bf16[2,512,128]{2,1,0:T(8,128)(2,1)S(1)} %get-tuple-element.329.refs_0_), channel_id=1, source_target_pairs={{0,6},{2,4},{4,2},{6,0},{1,7},{3,5},{5,3},{7,1},{8,14},{10,12},{12... | collective-permute-start | bytes 786440 | tf_op jit(solution)/shard_map/ppermute | solution.py:142
  108.2 27.1 %collective-permute-start.17 = (bf16[512,1024]{1,0:T(8,128)(2,1)}, bf16[512,1024]{1,0:T(8,128)(2,1)}, u32[]{:S(2)}, u32[]{:S(2)}) collective-permute-start(bf16[512,1024]{1,0:T(8,128)(2,1)} %collective-permute-done.7.refs_4_.refs_5_), channel_id=1, source_target_pairs={{0,2},{2,0},{4,6},{6,4},{1,3},{3,1},{5,7},{7,5},{8,10},{10,8},{12,... | collective-permute-start | bytes 3145736 | tf_op jit(solution)/shard_map/ppermute | solution.py:142
  111.1 22.0 %collective-permute-start.14 = (bf16[128,2048]{1,0:T(8,128)(2,1)}, bf16[128,2048]{1,0:T(8,128)(2,1)}, u32[]{:S(2)}, u32[]{:S(2)}) collective-permute-start(bf16[128,2048]{1,0:T(8,128)(2,1)} %get-tuple-element.336), channel_id=1, source_target_pairs={{0,8},{8,0},{16,24},{24,16},{1,9},{9,1},{17,25},{25,17},{2,10},{10... | collective-permute-start | bytes 1572872 | tf_op jit(solution)/shard_map/ppermute | solution.py:142
  112.2 21.8 %collective-permute-start.15 = (bf16[128,2048]{1,0:T(8,128)(2,1)}, bf16[128,2048]{1,0:T(8,128)(2,1)}, u32[]{:S(2)}, u32[]{:S(2)}) collective-permute-start(bf16[128,2048]{1,0:T(8,128)(2,1)} %get-tuple-element.337), channel_id=1, source_target_pairs={{0,16},{8,24},{16,0},{24,8},{1,17},{9,25},{17,1},{25,9},{2,18},{10... | collective-permute-start | bytes 1572872 | tf_op jit(solution)/shard_map/ppermute | solution.py:142
  113.2 22.2 %collective-permute-start.16 = (bf16[128,2048]{1,0:T(8,128)(2,1)}, bf16[128,2048]{1,0:T(8,128)(2,1)}, u32[]{:S(2)}, u32[]{:S(2)}) collective-permute-start(bf16[128,2048]{1,0:T(8,128)(2,1)} %get-tuple-element.338), channel_id=1, source_target_pairs={{0,24},{8,16},{16,8},{24,0},{1,25},{9,17},{17,9},{25,1},{2,26},{10... | collective-permute-start | bytes 1572872 | tf_op jit(solution)/shard_map/ppermute | solution.py:142
  139.6 26.5 %collective-permute-start.19 = (bf16[512,1024]{1,0:T(8,128)(2,1)S(1)}, bf16[512,1024]{1,0:T(8,128)(2,1)S(1)}, u32[]{:S(2)}, u32[]{:S(2)}) collective-permute-start(bf16[512,1024]{1,0:T(8,128)(2,1)S(1)} %copy-done.22), channel_id=1, source_target_pairs={{0,2},{2,0},{4,6},{6,4},{1,3},{3,1},{5,7},{7,5},{8,10},{10,8},{12,... | collective-permute-start | bytes 3145736 | tf_op jit(solution)/shard_map/ppermute | solution.py:142
  141.4 24.6 %collective-permute-start.21 = (bf16[128,2048]{1,0:T(8,128)(2,1)S(1)}, bf16[128,2048]{1,0:T(8,128)(2,1)S(1)}, u32[]{:S(2)}, u32[]{:S(2)}) collective-permute-start(bf16[128,2048]{1,0:T(8,128)(2,1)S(1)} %get-tuple-element.357), channel_id=1, source_target_pairs={{0,16},{8,24},{16,0},{24,8},{1,17},{9,25},{17,1},{25,9},{2,18},{10... | collective-permute-start | bytes 1572872 | tf_op jit(solution)/shard_map/ppermute | solution.py:142
  142.8 23.3 %collective-permute-start.22 = (bf16[128,2048]{1,0:T(8,128)(2,1)S(1)}, bf16[128,2048]{1,0:T(8,128)(2,1)S(1)}, u32[]{:S(2)}, u32[]{:S(2)}) collective-permute-start(bf16[128,2048]{1,0:T(8,128)(2,1)S(1)} %get-tuple-element.358), channel_id=1, source_target_pairs={{0,24},{8,16},{16,8},{24,0},{1,25},{9,17},{17,9},{25,1},{2,26},{10... | collective-permute-start | bytes 1572872 | tf_op jit(solution)/shard_map/ppermute | solution.py:142
  166.1 29.7 %collective-permute-start.24 = (bf16[512,2048]{1,0:T(8,128)(2,1)S(1)}, bf16[512,2048]{1,0:T(8,128)(2,1)S(1)}, u32[]{:S(2)}, u32[]{:S(2)}) collective-permute-start(bf16[512,2048]{1,0:T(8,128)(2,1)S(1)} %shard_map.220.refs_1_.refs_0_), channel_id=1, source_target_pairs={{0,1},{1,0},{2,3},{3,2},{4,5},{5,4},{6,7},{7,6},{8,9},{9,8},{10,11... | collective-permute-start | bytes 6291464 | tf_op jit(solution)/shard_map/ppermute | solution.py:142
  166.1 29.6 %collective-permute-start.23 = (bf16[512,1024]{1,0:T(8,128)(2,1)S(1)}, bf16[512,1024]{1,0:T(8,128)(2,1)S(1)}, u32[]{:S(2)}, u32[]{:S(2)}) collective-permute-start(bf16[512,1024]{1,0:T(8,128)(2,1)S(1)} %copy-done.28), channel_id=1, source_target_pairs={{0,2},{2,0},{4,6},{6,4},{1,3},{3,1},{5,7},{7,5},{8,10},{10,8},{12,... | collective-permute-start | bytes 3145736 | tf_op jit(solution)/shard_map/ppermute | solution.py:142
  170.7 23.5 %collective-permute-start.26 = (bf16[128,2048]{1,0:T(8,128)(2,1)S(1)}, bf16[128,2048]{1,0:T(8,128)(2,1)S(1)}, u32[]{:S(2)}, u32[]{:S(2)}) collective-permute-start(bf16[128,2048]{1,0:T(8,128)(2,1)S(1)} %get-tuple-element.372), channel_id=1, source_target_pairs={{0,16},{8,24},{16,0},{24,8},{1,17},{9,25},{17,1},{25,9},{2,18},{10... | collective-permute-start | bytes 1572872 | tf_op jit(solution)/shard_map/ppermute | solution.py:142
  171.8 24.0 %collective-permute-start.27 = (bf16[128,2048]{1,0:T(8,128)(2,1)S(1)}, bf16[128,2048]{1,0:T(8,128)(2,1)S(1)}, u32[]{:S(2)}, u32[]{:S(2)}) collective-permute-start(bf16[128,2048]{1,0:T(8,128)(2,1)S(1)} %get-tuple-element.373), channel_id=1, source_target_pairs={{0,24},{8,16},{16,8},{24,0},{1,25},{9,17},{17,9},{25,1},{2,26},{10... | collective-permute-start | bytes 1572872 | tf_op jit(solution)/shard_map/ppermute | solution.py:142
  195.9 25.6 %collective-permute-start.28 = (bf16[512,1024]{1,0:T(8,128)(2,1)S(1)}, bf16[512,1024]{1,0:T(8,128)(2,1)S(1)}, u32[]{:S(2)}, u32[]{:S(2)}) collective-permute-start(bf16[512,1024]{1,0:T(8,128)(2,1)S(1)} %pad_maximum_fusion.3), channel_id=1, source_target_pairs={{0,8},{8,0},{16,24},{24,16},{1,9},{9,1},{17,25},{25,17},{2,10},{10... | collective-permute-start | bytes 3145736 | tf_op jit(solution)/shard_map/ppermute | solution.py:142
  197.0 25.2 %collective-permute-start.29 = (bf16[512,1024]{1,0:T(8,128)(2,1)S(1)}, bf16[512,1024]{1,0:T(8,128)(2,1)S(1)}, u32[]{:S(2)}, u32[]{:S(2)}) collective-permute-start(bf16[512,1024]{1,0:T(8,128)(2,1)S(1)} %pad_maximum_fusion.4), channel_id=1, source_target_pairs={{0,16},{8,24},{16,0},{24,8},{1,17},{9,25},{17,1},{25,9},{2,18},{10... | collective-permute-start | bytes 3145736 | tf_op jit(solution)/shard_map/ppermute | solution.py:142
  222.2 24.5 %collective-permute-start.32 = (bf16[512,1024]{1,0:T(8,128)(2,1)S(1)}, bf16[512,1024]{1,0:T(8,128)(2,1)}, u32[]{:S(2)}, u32[]{:S(2)}) collective-permute-start(bf16[512,1024]{1,0:T(8,128)(2,1)S(1)} %get-tuple-element.393), channel_id=1, source_target_pairs={{0,8},{8,0},{16,24},{24,16},{1,9},{9,1},{17,25},{25,17},{2,10},{10... | collective-permute-start | bytes 3145736 | tf_op jit(solution)/shard_map/ppermute | solution.py:142
  223.3 24.1 %collective-permute-start.33 = (bf16[512,1024]{1,0:T(8,128)(2,1)S(1)}, bf16[512,1024]{1,0:T(8,128)(2,1)S(1)}, u32[]{:S(2)}, u32[]{:S(2)}) collective-permute-start(bf16[512,1024]{1,0:T(8,128)(2,1)S(1)} %get-tuple-element.394), channel_id=1, source_target_pairs={{0,16},{8,24},{16,0},{24,8},{1,17},{9,25},{17,1},{25,9},{2,18},{10... | collective-permute-start | bytes 3145736 | tf_op jit(solution)/shard_map/ppermute | solution.py:142
  224.3 23.6 %collective-permute-start.31 = (bf16[512,1024]{1,0:T(8,128)(2,1)S(1)}, bf16[512,1024]{1,0:T(8,128)(2,1)S(1)}, u32[]{:S(2)}, u32[]{:S(2)}) collective-permute-start(bf16[512,1024]{1,0:T(8,128)(2,1)S(1)} %get-tuple-element.392), channel_id=1, source_target_pairs={{0,2},{6,4},{1,3},{7,5},{8,10},{14,12},{9,11},{15,13},{16,18},{22,... | collective-permute-start | bytes 3145736 | tf_op jit(solution)/shard_map/ppermute | solution.py:142
  250.9 27.6 %collective-permute-start.35 = (bf16[512,1024]{1,0:T(8,128)(2,1)}, bf16[512,1024]{1,0:T(8,128)(2,1)}, u32[]{:S(2)}, u32[]{:S(2)}) collective-permute-start(bf16[512,1024]{1,0:T(8,128)(2,1)} %collective-permute-done.32), channel_id=1, source_target_pairs={{0,2},{6,4},{1,3},{7,5},{8,10},{14,12},{9,11},{15,13},{16,18},{22,... | collective-permute-start | bytes 3145736 | tf_op jit(solution)/shard_map/ppermute | solution.py:142
  259.1 23.6 %collective-permute-start.36 = (bf16[512,1024]{1,0:T(8,128)(2,1)}, bf16[512,1024]{1,0:T(8,128)(2,1)}, u32[]{:S(2)}, u32[]{:S(2)}) collective-permute-start(bf16[512,1024]{1,0:T(8,128)(2,1)} %pad_maximum_fusion.8), channel_id=1, source_target_pairs={{0,24},{8,16},{16,8},{24,0},{1,25},{9,17},{17,9},{25,1},{2,26},{10... | collective-permute-start | bytes 3145736 | tf_op jit(solution)/shard_map/ppermute | solution.py:142
  282.7 33.4 %collective-permute-start.39 = (bf16[512,1024]{1,0:T(8,128)(2,1)}, bf16[512,1024]{1,0:T(8,128)(2,1)}, u32[]{:S(2)}, u32[]{:S(2)}) collective-permute-start(bf16[512,1024]{1,0:T(8,128)(2,1)} %copy-done.76), channel_id=1, source_target_pairs={{0,24},{8,16},{16,8},{24,0},{1,25},{9,17},{17,9},{25,1},{2,26},{10... | collective-permute-start | bytes 3145736 | tf_op jit(solution)/shard_map/ppermute | solution.py:142
  284.1 32.0 %collective-permute-start.37 = (bf16[512,1024]{1,0:T(8,128)(2,1)}, bf16[512,1024]{1,0:T(8,128)(2,1)}, u32[]{:S(2)}, u32[]{:S(2)}) collective-permute-start(bf16[512,1024]{1,0:T(8,128)(2,1)} %add_convert_fusion.24), channel_id=1, source_target_pairs={{2,4},{4,2},{3,5},{5,3},{10,12},{12,10},{11,13},{13,11},{18,20},{2... | collective-permute-start | bytes 3145736 | tf_op jit(solution)/shard_map/ppermute | solution.py:142
  289.2 26.9 %collective-permute-start.38 = (bf16[512,1024]{1,0:T(8,128)(2,1)}, bf16[512,1024]{1,0:T(8,128)(2,1)}, u32[]{:S(2)}, u32[]{:S(2)}) collective-permute-start(bf16[512,1024]{1,0:T(8,128)(2,1)} %fusion.refs_1_), channel_id=1, source_target_pairs={{0,2},{6,4},{2,0},{4,6},{1,3},{7,5},{3,1},{5,7},{8,10},{14,12},{10... | collective-permute-start | bytes 3145736 | tf_op jit(solution)/shard_map/ppermute | solution.py:142
  320.4 21.4 %collective-permute-start.41 = (bf16[512,1024]{1,0:T(8,128)(2,1)S(1)}, bf16[512,1024]{1,0:T(8,128)(2,1)S(1)}, u32[]{:S(2)}, u32[]{:S(2)}) collective-permute-start(bf16[512,1024]{1,0:T(8,128)(2,1)S(1)} %fusion.1.refs_3_), channel_id=1, source_target_pairs={{0,2},{6,4},{2,0},{4,6},{1,3},{7,5},{3,1},{5,7},{8,10},{14,12},{10... | collective-permute-start | bytes 3145736 | tf_op jit(solution)/shard_map/ppermute | solution.py:142
  320.5 21.3 %collective-permute-start.40 = (bf16[512,1024]{1,0:T(8,128)(2,1)S(1)}, bf16[512,1024]{1,0:T(8,128)(2,1)S(1)}, u32[]{:S(2)}, u32[]{:S(2)}) collective-permute-start(bf16[512,1024]{1,0:T(8,128)(2,1)S(1)} %add_convert_fusion.22), channel_id=1, source_target_pairs={{2,4},{4,2},{3,5},{5,3},{10,12},{12,10},{11,13},{13,11},{18,20},{2... | collective-permute-start | bytes 3145736 | tf_op jit(solution)/shard_map/ppermute | solution.py:142
  321.2 34.4 %collective-permute-start.42 = (bf16[512,2048]{1,0:T(8,128)(2,1)S(1)}, bf16[512,2048]{1,0:T(8,128)(2,1)S(1)}, u32[]{:S(2)}, u32[]{:S(2)}) collective-permute-start(bf16[512,2048]{1,0:T(8,128)(2,1)S(1)} %get-tuple-element.423), channel_id=1, source_target_pairs={{0,1},{1,0},{2,3},{3,2},{4,5},{5,4},{6,7},{7,6},{8,9},{9,8},{10,11... | collective-permute-start | bytes 6291464 | tf_op jit(solution)/shard_map/ppermute | solution.py:142
  344.1 22.2 %collective-permute-start.44 = (bf16[512,1024]{1,0:T(8,128)(2,1)S(1)}, bf16[512,1024]{1,0:T(8,128)(2,1)S(1)}, u32[]{:S(2)}, u32[]{:S(2)}) collective-permute-start(bf16[512,1024]{1,0:T(8,128)(2,1)S(1)} %fusion.2.refs_5_), channel_id=1, source_target_pairs={{0,2},{6,4},{2,0},{4,6},{1,3},{7,5},{3,1},{5,7},{8,10},{14,12},{10... | collective-permute-start | bytes 3145736 | tf_op jit(solution)/shard_map/ppermute | solution.py:142
  355.6 26.1 %collective-permute-start.45 = (bf16[512,1024]{1,0:T(8,128)(2,1)S(1)}, bf16[512,1024]{1,0:T(8,128)(2,1)S(1)}, u32[]{:S(2)}, u32[]{:S(2)}) collective-permute-start(bf16[512,1024]{1,0:T(8,128)(2,1)S(1)} %get-tuple-element.432), channel_id=1, source_target_pairs={{0,8},{8,0},{16,24},{24,16},{1,9},{9,1},{17,25},{25,17},{2,10},{10... | collective-permute-start | bytes 3145736 | tf_op jit(solution)/shard_map/ppermute | solution.py:142
  356.7 26.3 %collective-permute-start.46 = (bf16[512,1024]{1,0:T(8,128)(2,1)S(1)}, bf16[512,1024]{1,0:T(8,128)(2,1)S(1)}, u32[]{:S(2)}, u32[]{:S(2)}) collective-permute-start(bf16[512,1024]{1,0:T(8,128)(2,1)S(1)} %get-tuple-element.433), channel_id=1, source_target_pairs={{0,16},{8,24},{16,0},{24,8},{1,17},{9,25},{17,1},{25,9},{2,18},{10... | collective-permute-start | bytes 3145736 | tf_op jit(solution)/shard_map/ppermute | solution.py:142
  367.4 22.2 %collective-permute-start.48 = (bf16[512,1024]{1,0:T(8,128)(2,1)S(1)}, bf16[512,1024]{1,0:T(8,128)(2,1)S(1)}, u32[]{:S(2)}, u32[]{:S(2)}) collective-permute-start(bf16[512,1024]{1,0:T(8,128)(2,1)S(1)} %fusion.3.refs_7_), channel_id=1, source_target_pairs={{0,2},{6,4},{2,0},{4,6},{1,3},{7,5},{3,1},{5,7},{8,10},{14,12},{10... | collective-permute-start | bytes 3145736 | tf_op jit(solution)/shard_map/ppermute | solution.py:142
  372.3 28.8 %collective-permute-start.49 = (bf16[128,2048]{1,0:T(8,128)(2,1)S(1)}, bf16[128,2048]{1,0:T(8,128)(2,1)S(1)}, u32[]{:S(2)}, u32[]{:S(2)}) collective-permute-start(bf16[128,2048]{1,0:T(8,128)(2,1)S(1)} %get-tuple-element.441), channel_id=1, source_target_pairs={{0,8},{8,0},{16,24},{24,16},{1,9},{9,1},{17,25},{25,17},{2,10},{10... | collective-permute-start | bytes 1572872 | tf_op jit(solution)/shard_map/ppermute | solution.py:142
  390.7 20.4 %collective-permute-start.53 = (bf16[512,1024]{1,0:T(8,128)(2,1)S(1)}, bf16[512,1024]{1,0:T(8,128)(2,1)S(1)}, u32[]{:S(2)}, u32[]{:S(2)}) collective-permute-start(bf16[512,1024]{1,0:T(8,128)(2,1)S(1)} %fusion.4.refs_1_), channel_id=1, source_target_pairs={{0,2},{6,4},{2,0},{4,6},{1,3},{7,5},{3,1},{5,7},{8,10},{14,12},{10... | collective-permute-start | bytes 3145736 | tf_op jit(solution)/shard_map/ppermute | solution.py:142
  422.5 31.8 %collective-permute-start.60 = (bf16[512,2048]{1,0:T(8,128)(2,1)S(1)}, bf16[512,2048]{1,0:T(8,128)(2,1)S(1)}, u32[]{:S(2)}, u32[]{:S(2)}) collective-permute-start(bf16[512,2048]{1,0:T(8,128)(2,1)S(1)} %shard_map.232.mine_ref.refs_3_), channel_id=1, source_target_pairs={{0,1},{1,0},{2,3},{3,2},{4,5},{5,4},{6,7},{7,6},{8,9},{9,8},{10,11... | collective-permute-start | bytes 6291464 | tf_op jit(solution)/shard_map/ppermute | solution.py:142
  424.6 26.2 %collective-permute-start.58 = (bf16[512,1024]{1,0:T(8,128)(2,1)S(1)}, bf16[512,1024]{1,0:T(8,128)(2,1)S(1)}, u32[]{:S(2)}, u32[]{:S(2)}) collective-permute-start(bf16[512,1024]{1,0:T(8,128)(2,1)S(1)} %fusion.5.refs_1_), channel_id=1, source_target_pairs={{0,2},{6,4},{2,0},{4,6},{1,3},{7,5},{3,1},{5,7},{8,10},{14,12},{10... | collective-permute-start | bytes 3145736 | tf_op jit(solution)/shard_map/ppermute | solution.py:142
  427.4 23.3 %collective-permute-start.57 = (bf16[512,1024]{1,0:T(8,128)(2,1)S(1)}, bf16[512,1024]{1,0:T(8,128)(2,1)S(1)}, u32[]{:S(2)}, u32[]{:S(2)}) collective-permute-start(bf16[512,1024]{1,0:T(8,128)(2,1)S(1)} %add_convert_fusion.14), channel_id=1, source_target_pairs={{2,4},{4,2},{3,5},{5,3},{10,12},{12,10},{11,13},{13,11},{18,20},{2... | collective-permute-start | bytes 3145736 | tf_op jit(solution)/shard_map/ppermute | solution.py:142
  428.2 26.2 %collective-permute-start.59 = (bf16[512,1024]{1,0:T(8,128)(2,1)S(1)}, bf16[512,1024]{1,0:T(8,128)(2,1)S(1)}, u32[]{:S(2)}, u32[]{:S(2)}) collective-permute-start(bf16[512,1024]{1,0:T(8,128)(2,1)S(1)} %copy-done.75), channel_id=1, source_target_pairs={{0,24},{8,16},{16,8},{24,0},{1,25},{9,17},{17,9},{25,1},{2,26},{10... | collective-permute-start | bytes 3145736 | tf_op jit(solution)/shard_map/ppermute | solution.py:142
  455.5 27.8 %collective-permute-start.62 = (bf16[512,1024]{1,0:T(8,128)(2,1)S(1)}, bf16[512,1024]{1,0:T(8,128)(2,1)S(1)}, u32[]{:S(2)}, u32[]{:S(2)}) collective-permute-start(bf16[512,1024]{1,0:T(8,128)(2,1)S(1)} %fusion.6.refs_3_), channel_id=1, source_target_pairs={{0,2},{6,4},{2,0},{4,6},{1,3},{7,5},{3,1},{5,7},{8,10},{14,12},{10... | collective-permute-start | bytes 3145736 | tf_op jit(solution)/shard_map/ppermute | solution.py:142
  457.6 25.6 %collective-permute-start.61 = (bf16[512,1024]{1,0:T(8,128)(2,1)S(1)}, bf16[512,1024]{1,0:T(8,128)(2,1)S(1)}, u32[]{:S(2)}, u32[]{:S(2)}) collective-permute-start(bf16[512,1024]{1,0:T(8,128)(2,1)S(1)} %add_convert_fusion.12), channel_id=1, source_target_pairs={{2,4},{4,2},{3,5},{5,3},{10,12},{12,10},{11,13},{13,11},{18,20},{2... | collective-permute-start | bytes 3145736 | tf_op jit(solution)/shard_map/ppermute | solution.py:142
  481.3 24.2 %collective-permute-start.63 = (bf16[512,1024]{1,0:T(8,128)(2,1)S(1)}, bf16[512,1024]{1,0:T(8,128)(2,1)S(1)}, u32[]{:S(2)}, u32[]{:S(2)}) collective-permute-start(bf16[512,1024]{1,0:T(8,128)(2,1)S(1)} %copy-done.73), channel_id=1, source_target_pairs={{0,8},{8,0},{16,24},{24,16},{1,9},{9,1},{17,25},{25,17},{2,10},{10... | collective-permute-start | bytes 3145736 | tf_op jit(solution)/shard_map/ppermute | solution.py:142
  482.2 23.8 %collective-permute-start.64 = (bf16[512,1024]{1,0:T(8,128)(2,1)S(1)}, bf16[512,1024]{1,0:T(8,128)(2,1)S(1)}, u32[]{:S(2)}, u32[]{:S(2)}) collective-permute-start(bf16[512,1024]{1,0:T(8,128)(2,1)S(1)} %copy-done.71), channel_id=1, source_target_pairs={{0,16},{8,24},{16,0},{24,8},{1,17},{9,25},{17,1},{25,9},{2,18},{10... | collective-permute-start | bytes 3145736 | tf_op jit(solution)/shard_map/ppermute | solution.py:142
  484.3 24.5 %collective-permute-start.66 = (bf16[512,1024]{1,0:T(8,128)(2,1)S(1)}, bf16[512,1024]{1,0:T(8,128)(2,1)S(1)}, u32[]{:S(2)}, u32[]{:S(2)}) collective-permute-start(bf16[512,1024]{1,0:T(8,128)(2,1)S(1)} %fusion.7.refs_5_), channel_id=1, source_target_pairs={{0,2},{6,4},{2,0},{4,6},{1,3},{7,5},{3,1},{5,7},{8,10},{14,12},{10... | collective-permute-start | bytes 3145736 | tf_op jit(solution)/shard_map/ppermute | solution.py:142
  487.0 21.8 %collective-permute-start.65 = (bf16[512,1024]{1,0:T(8,128)(2,1)S(1)}, bf16[512,1024]{1,0:T(8,128)(2,1)S(1)}, u32[]{:S(2)}, u32[]{:S(2)}) collective-permute-start(bf16[512,1024]{1,0:T(8,128)(2,1)S(1)} %add_convert_fusion.10), channel_id=1, source_target_pairs={{2,4},{4,2},{3,5},{5,3},{10,12},{12,10},{11,13},{13,11},{18,20},{2... | collective-permute-start | bytes 3145736 | tf_op jit(solution)/shard_map/ppermute | solution.py:142
  506.1 23.8 %collective-permute-start.67 = (bf16[512,1024]{1,0:T(8,128)(2,1)S(1)}, bf16[512,1024]{1,0:T(8,128)(2,1)S(1)}, u32[]{:S(2)}, u32[]{:S(2)}) collective-permute-start(bf16[512,1024]{1,0:T(8,128)(2,1)S(1)} %copy-done.69), channel_id=1, source_target_pairs={{0,24},{8,16},{16,8},{24,0},{1,25},{9,17},{17,9},{25,1},{2,26},{10... | collective-permute-start | bytes 3145736 | tf_op jit(solution)/shard_map/ppermute | solution.py:142
  509.9 24.6 %collective-permute-start.69 = (bf16[512,1024]{1,0:T(8,128)(2,1)S(1)}, bf16[512,1024]{1,0:T(8,128)(2,1)S(1)}, u32[]{:S(2)}, u32[]{:S(2)}) collective-permute-start(bf16[512,1024]{1,0:T(8,128)(2,1)S(1)} %fusion.8.refs_7_), channel_id=1, source_target_pairs={{0,2},{6,4},{2,0},{4,6},{1,3},{7,5},{3,1},{5,7},{8,10},{14,12},{10... | collective-permute-start | bytes 3145736 | tf_op jit(solution)/shard_map/ppermute | solution.py:142
  513.6 20.9 %collective-permute-start.68 = (bf16[512,1024]{1,0:T(8,128)(2,1)S(1)}, bf16[512,1024]{1,0:T(8,128)(2,1)S(1)}, u32[]{:S(2)}, u32[]{:S(2)}) collective-permute-start(bf16[512,1024]{1,0:T(8,128)(2,1)S(1)} %add_convert_fusion.8), channel_id=1, source_target_pairs={{2,4},{4,2},{3,5},{5,3},{10,12},{12,10},{11,13},{13,11},{18,20},{2... | collective-permute-start | bytes 3145736 | tf_op jit(solution)/shard_map/ppermute | solution.py:142
  536.5 23.7 %collective-permute-start.72 = (bf16[512,1024]{1,0:T(8,128)(2,1)S(1)}, bf16[512,1024]{1,0:T(8,128)(2,1)S(1)}, u32[]{:S(2)}, u32[]{:S(2)}) collective-permute-start(bf16[512,1024]{1,0:T(8,128)(2,1)S(1)} %fusion.9.sent_ref), channel_id=1, source_target_pairs={{0,2},{6,4},{2,0},{4,6},{1,3},{7,5},{3,1},{5,7},{8,10},{14,12},{10... | collective-permute-start | bytes 3145736 | tf_op jit(solution)/shard_map/ppermute | solution.py:142
  540.2 20.0 %collective-permute-start.71 = (bf16[512,1024]{1,0:T(8,128)(2,1)}, bf16[512,1024]{1,0:T(8,128)(2,1)}, u32[]{:S(2)}, u32[]{:S(2)}) collective-permute-start(bf16[512,1024]{1,0:T(8,128)(2,1)} %add_convert_fusion.6), channel_id=1, source_target_pairs={{2,4},{4,2},{3,5},{5,3},{10,12},{12,10},{11,13},{13,11},{18,20},{2... | collective-permute-start | bytes 3145736 | tf_op jit(solution)/shard_map/ppermute | solution.py:142
  563.9 29.3 %collective-permute-start.77 = (bf16[512,1024]{1,0:T(8,128)(2,1)S(1)}, bf16[512,1024]{1,0:T(8,128)(2,1)S(1)}, u32[]{:S(2)}, u32[]{:S(2)}) collective-permute-start(bf16[512,1024]{1,0:T(8,128)(2,1)S(1)} %fusion.10.refs_3_), channel_id=1, source_target_pairs={{0,2},{6,4},{2,0},{4,6},{1,3},{7,5},{3,1},{5,7},{8,10},{14,12},{10... | collective-permute-start | bytes 3145736 | tf_op jit(solution)/shard_map/ppermute | solution.py:142
  568.0 25.3 %collective-permute-start.76 = (bf16[512,1024]{1,0:T(8,128)(2,1)}, bf16[512,1024]{1,0:T(8,128)(2,1)}, u32[]{:S(2)}, u32[]{:S(2)}) collective-permute-start(bf16[512,1024]{1,0:T(8,128)(2,1)} %add_convert_fusion.4), channel_id=1, source_target_pairs={{2,4},{4,2},{3,5},{5,3},{10,12},{12,10},{11,13},{13,11},{18,20},{2... | collective-permute-start | bytes 3145736 | tf_op jit(solution)/shard_map/ppermute | solution.py:142
  572.6 20.4 %collective-permute-start.74 = (bf16[128,2048]{1,0:T(8,128)(2,1)}, bf16[128,2048]{1,0:T(8,128)(2,1)S(1)}, u32[]{:S(2)}, u32[]{:S(2)}) collective-permute-start(bf16[128,2048]{1,0:T(8,128)(2,1)} %get-tuple-element.501), channel_id=1, source_target_pairs={{0,16},{8,24},{16,0},{24,8},{1,17},{9,25},{17,1},{25,9},{2,18},{10... | collective-permute-start | bytes 1572872 | tf_op jit(solution)/shard_map/ppermute | solution.py:142
  573.4 19.6 %collective-permute-start.75 = (bf16[128,2048]{1,0:T(8,128)(2,1)}, bf16[128,2048]{1,0:T(8,128)(2,1)S(1)}, u32[]{:S(2)}, u32[]{:S(2)}) collective-permute-start(bf16[128,2048]{1,0:T(8,128)(2,1)} %get-tuple-element.502), channel_id=1, source_target_pairs={{0,24},{8,16},{16,8},{24,0},{1,25},{9,17},{17,9},{25,1},{2,26},{10... | collective-permute-start | bytes 1572872 | tf_op jit(solution)/shard_map/ppermute | solution.py:142
  593.3 28.2 %collective-permute-start.82 = (bf16[512,2048]{1,0:T(8,128)(2,1)S(1)}, bf16[512,2048]{1,0:T(8,128)(2,1)S(1)}, u32[]{:S(2)}, u32[]{:S(2)}) collective-permute-start(bf16[512,2048]{1,0:T(8,128)(2,1)S(1)} %get-tuple-element.527), channel_id=1, source_target_pairs={{0,1},{1,0},{2,3},{3,2},{4,5},{5,4},{6,7},{7,6},{8,9},{9,8},{10,11... | collective-permute-start | bytes 6291464 | tf_op jit(solution)/shard_map/ppermute | solution.py:142
  596.3 25.2 %collective-permute-start.79 = (bf16[512,1024]{1,0:T(8,128)(2,1)S(1)}, bf16[512,1024]{1,0:T(8,128)(2,1)S(1)}, u32[]{:S(2)}, u32[]{:S(2)}) collective-permute-start(bf16[512,1024]{1,0:T(8,128)(2,1)S(1)} %fusion.11.refs_5_), channel_id=1, source_target_pairs={{0,2},{6,4},{2,0},{4,6},{1,3},{7,5},{3,1},{5,7},{8,10},{14,12},{10... | collective-permute-start | bytes 3145736 | tf_op jit(solution)/shard_map/ppermute | solution.py:142
  597.5 24.0 %collective-permute-start.78 = (bf16[512,1024]{1,0:T(8,128)(2,1)S(1)}, bf16[512,1024]{1,0:T(8,128)(2,1)S(1)}, u32[]{:S(2)}, u32[]{:S(2)}) collective-permute-start(bf16[512,1024]{1,0:T(8,128)(2,1)S(1)} %add_convert_fusion.2), channel_id=1, source_target_pairs={{2,4},{4,2},{3,5},{5,3},{10,12},{12,10},{11,13},{13,11},{18,20},{2... | collective-permute-start | bytes 3145736 | tf_op jit(solution)/shard_map/ppermute | solution.py:142
  622.0 25.9 %collective-permute-start.85 = (bf16[512,1024]{1,0:T(8,128)(2,1)S(1)}, bf16[512,1024]{1,0:T(8,128)(2,1)S(1)}, u32[]{:S(2)}, u32[]{:S(2)}) collective-permute-start(bf16[512,1024]{1,0:T(8,128)(2,1)S(1)} %fusion.12.refs_7_), channel_id=1, source_target_pairs={{0,2},{6,4},{2,0},{4,6},{1,3},{7,5},{3,1},{5,7},{8,10},{14,12},{10... | collective-permute-start | bytes 3145736 | tf_op jit(solution)/shard_map/ppermute | solution.py:142
  627.1 21.0 %collective-permute-start.86 = (bf16[128,2048]{1,0:T(8,128)(2,1)S(1)}, bf16[128,2048]{1,0:T(8,128)(2,1)S(1)}, u32[]{:S(2)}, u32[]{:S(2)}) collective-permute-start(bf16[128,2048]{1,0:T(8,128)(2,1)S(1)} %get-tuple-element.536), channel_id=1, source_target_pairs={{0,8},{8,0},{16,24},{24,16},{1,9},{9,1},{17,25},{25,17},{2,10},{10... | collective-permute-start | bytes 1572872 | tf_op jit(solution)/shard_map/ppermute | solution.py:142
  627.9 23.4 %collective-permute-start.87 = (bf16[128,2048]{1,0:T(8,128)(2,1)S(1)}, bf16[128,2048]{1,0:T(8,128)(2,1)S(1)}, u32[]{:S(2)}, u32[]{:S(2)}) collective-permute-start(bf16[128,2048]{1,0:T(8,128)(2,1)S(1)} %get-tuple-element.537), channel_id=1, source_target_pairs={{0,16},{8,24},{16,0},{24,8},{1,17},{9,25},{17,1},{25,9},{2,18},{10... | collective-permute-start | bytes 1572872 | tf_op jit(solution)/shard_map/ppermute | solution.py:142
  629.0 22.4 %collective-permute-start.88 = (bf16[128,2048]{1,0:T(8,128)(2,1)S(1)}, bf16[128,2048]{1,0:T(8,128)(2,1)S(1)}, u32[]{:S(2)}, u32[]{:S(2)}) collective-permute-start(bf16[128,2048]{1,0:T(8,128)(2,1)S(1)} %get-tuple-element.538), channel_id=1, source_target_pairs={{0,24},{8,16},{16,8},{24,0},{1,25},{9,17},{17,9},{25,1},{2,26},{10... | collective-permute-start | bytes 1572872 | tf_op jit(solution)/shard_map/ppermute | solution.py:142
  (146 other events, 1715.6 us)

commit v6 on v5

--- a/solution.py
+++ b/solution.py
@@ -71,7 +71,8 @@
     )
 
 
-VMEM_LIMIT = 32 * 1024 * 1024
+VMEM_LIMIT = 30 * 1024 * 1024
+MIDDLE_LIMIT = 20 * 1024 * 1024
 SMALL_LIMIT = 12 * 1024 * 1024
 SMALL = pl.CostEstimate(flops=1, bytes_accessed=1, transcendentals=0)
 
@@ -141,7 +142,7 @@
     def start(self, moves):
         return [(name, lax.ppermute(value, axis, pairs)) for name, value, axis, pairs in moves]
 
-    def step(self, moves=(), summed=None, late=None, carry=()):
+    def step(self, moves=(), summed=None, late=None, carry=(), hold=False):
         moves, carry = list(moves), list(carry)
         arrays = [move[1] for move in moves] + carry
         fresh = [summed[1]] if summed is not None and summed[1] is not None else []
@@ -157,13 +158,14 @@
         along = self.line.advance(self.got, entering)
         if not together and self.on_line:
             self.on_line = self.start(along)
-            held = self.wait(self.others, arrays)
+            held = self.wait([] if hold else self.others, arrays)
         else:
             self.on_line = self.start(along)
         moves = [
             (name, value, axis, pairs) for (name, _, axis, pairs), value in zip(moves, held)
         ]
-        self.others = self.start(moves + (late() if late is not None else []))
+        before = self.others if hold else []
+        self.others = before + self.start(moves + (late() if late is not None else []))
         return held[len(moves) :]
 
     def take(self, name):
@@ -311,7 +313,7 @@
     grad_ref[...] = (d_middle_ref[...] + d_x).astype(jnp.bfloat16)
 
 
-def gridded(kernel, steps, ins, outs, scalars=()):
+def gridded(kernel, steps, ins, outs, scalars=(), limit=None):
     return pl.pallas_call(
         kernel,
         grid=(steps,),
@@ -319,7 +321,7 @@
         + [pl.BlockSpec(block, index) for _, block, index in ins],
         out_specs=[pl.BlockSpec(block, index) for _, block, index in outs],
         out_shape=[shape for shape, _, _ in outs],
-        compiler_params=pltpu.CompilerParams(vmem_limit_bytes=VMEM_LIMIT),
+        compiler_params=pltpu.CompilerParams(vmem_limit_bytes=limit or MIDDLE_LIMIT),
         cost_estimate=SMALL,
     )(*scalars, *[array for array, _, _ in ins])
 
@@ -490,7 +492,8 @@
         (low(width, units), (width, block), lambda i: (0, i)),
         (low(width, units), (width, block), lambda i: (0, i)),
     ]
-    return gridded(functools.partial(gate_up_kernel, count, half), steps, ins, outs)
+    kernel = functools.partial(gate_up_kernel, count, half)
+    return gridded(kernel, steps, ins, outs, limit=VMEM_LIMIT)
 
 
 def units_back_kernel(count, *refs):
@@ -517,7 +520,8 @@
     ins = [still(d_out[0]), still(d_out[1])] + [by_columns(piece, depth) for piece in pieces]
     ins += [by_columns(gate, tokens), by_columns(up, tokens)]
     outs = [by_columns(low(tokens, units), tokens)] * 2 + [by_columns(low(width, units), width)]
-    return gridded(functools.partial(units_back_kernel, len(pieces)), units // block, ins, outs)
+    kernel = functools.partial(units_back_kernel, len(pieces))
+    return gridded(kernel, units // block, ins, outs, limit=VMEM_LIMIT)
 
 
 def rows_sum_kernel(terms, *refs):
@@ -586,7 +590,7 @@
         in_specs=specs,
         out_specs=[pl.BlockSpec((depth, columns), lambda i: (0, 0))] * count,
         out_shape=[low(depth, columns)] * count,
-        compiler_params=pltpu.CompilerParams(vmem_limit_bytes=VMEM_LIMIT),
+        compiler_params=pltpu.CompilerParams(vmem_limit_bytes=MIDDLE_LIMIT),
         cost_estimate=SMALL,
     )(*[array for array, _, _ in ins])
 
@@ -835,6 +839,9 @@
         kept[name] = join(own, others)
         return to_core(name, kept[name])
 
+    def unwaited(name):
+        return dict(steps.others)[name]
+
     def both_of(name):
         return kept[name], steps.take(name)
 
@@ -1008,7 +1015,7 @@
     )
     all_cot = both_of("cot")
     neighbours = [steps.take(("neighbour", k)) for k in far]
-    normed_two = (kept["two"], dict(steps.others)["two"])
+    normed_two = (kept["two"], unwaited("two"))
 
     gate_val, up_val, hidden, wg, wu = gate_up(
         normed_two, own_gate, own_up, [fetched[k] for k in far], neighbours
@@ -1026,12 +1033,11 @@
     steps.step(back("wd", d_wd, [3]), summed=entry("wd", 2))
     d_gate, d_up, wd = units_back(all_cot, [own_down] + arrived("down"), gate_val, up_val)
     first, second = rows_sum([d_gate, d_up], [wg, wu])
-    steps.step(to_core("d_two", second), summed=entry("wd", 3))
     d_wg = weight_grad([(*normed_two, d_gate)], packs, side_arg)
-    steps.step(back("wg", d_wg, [1, 2]), summed=entry("wg", 0, d_wg))
+    steps.step(to_core("d_two", second) + back("wg", d_wg, [1, 2]), summed=entry("wd", 3))
     d_wu = weight_grad([(*normed_two, d_up)], packs, side_arg)
     steps.step(
-        summed=entry("wu", 0, d_wu), late=functools.partial(to_rows, "d_two", first)
+        summed=entry("wg", 0, d_wg), late=functools.partial(to_rows, "d_two", first)
     )
 
     def branch_back():
@@ -1046,37 +1052,33 @@
         )
         return send_all("d_branch", sends)
 
-    first, second = rows_sum([hidden], [wd])
-    steps.step(summed=entry("wg", 1), late=branch_back, carry=(first, second))
+    steps.step(summed=entry("wu", 0, d_wu), late=branch_back)
+    ff_first, ff_second = rows_sum([hidden], [wd])
     steps.step(
         back("wg", d_wg, [3]),
-        summed=entry("wg", 2),
+        summed=entry("wg", 1),
         late=lambda: joined("all_branch", kept["d_branch"], arrived("d_branch")),
     )
-    d_branch = None
-
-    def attention_back():
-        return attend_back(
-            here_arg, q_rot, d_branch, cosine, sine, place_args, wo, kvs, packs, groups
-        )
-
     sums = steps.line.sums
 
     def settle_all(name):
         return settle(at_end, index, [sums[name, k] for k in range(packs)], ff_width)
 
-    steps.step(back("wu", d_wu, [1, 2]), summed=entry("wg", 3))
-    d_branch = both_of("all_branch")
-    d_q, d_kv = attention_back()
+    d_branch = (kept["all_branch"], unwaited("all_branch"))
+    d_q, d_kv = attend_back(
+        here_arg, q_rot, d_branch, cosine, sine, place_args, wo, kvs, packs, groups
+    )
+    d_q, d_kv = steps.step(back("wu", d_wu, [1, 2]), summed=entry("wg", 2), carry=(d_q, d_kv))
     steps.step(back("wu", d_wu, [3]), summed=("d_kv", d_kv))
     down_grad = settle_all("wd")
-    steps.step(to_core("ff", second), summed=entry("wu", 1))
+    steps.step(to_core("ff", ff_second), summed=entry("wg", 3))
     (down_grad,) = steps.step(
-        summed=entry("wu", 2),
-        late=functools.partial(to_rows, "ff", first),
-        carry=(down_grad,),
-    )
-    steps.step(summed=entry("wu", 3))
+        summed=entry("wu", 1), late=functools.partial(to_rows, "ff", ff_first), carry=(down_grad,)
+    )
+    steps.step(summed=entry("wu", 2))
+    result = in_vmem(
+        result_kernel, [low(half, width)], kept["middle"], kept["ff"], *arrived("ff")
+    )[0]
     d_qkv = in_vmem(
         d_qkv_kernel,
         [low(tokens, q_width + 2 * k_width)],
@@ -1090,14 +1092,12 @@
     )[0]
     d_wqkvo = weight_grad([(*normed_one, d_qkv), (*d_branch, attn_low)], packs)
     first, second = rows_sum([d_qkv], [wqkv])
-    result = in_vmem(
-        result_kernel, [low(half, width)], kept["middle"], kept["ff"], *arrived("ff")
-    )[0]
     steps.step(
-        back("wqkvo", d_wqkvo, [1, 2]) + to_core("d_one", second) + to_core("result", result),
-        summed=entry("wqkvo", 0, d_wqkvo),
-    )
-    steps.step(late=functools.partial(to_rows, "d_one", first), summed=entry("wqkvo", 1))
+        back("wqkvo", d_wqkvo, [1, 2]) + to_core("d_one", second), summed=entry("wu", 3)
+    )
+    steps.step(
+        summed=entry("wqkvo", 0, d_wqkvo), late=functools.partial(to_rows, "d_one", first)
+    )
 
     def both_rows(own, other):
         return in_vmem(
@@ -1109,7 +1109,6 @@
             scalars=1,
         )[0]
 
-    out_hidden = both_rows(result, steps.take("result"))
     gate_grad = settle_all("wg")
     def gains_to_core():
         kept["in_grad"], d_gain_one = in_vmem(
@@ -1134,18 +1133,18 @@
             kept["gains"] = kept["gains"] + steps.take(("gains", k))
         return [(("gains", j), kept["gains"], "ctx", pairs_by(j, cycle)) for j in range(1, cycle)]
 
-    out_hidden, gate_grad = steps.step(
-        back("wqkvo", d_wqkvo, [3]),
-        summed=entry("wqkvo", 2),
-        late=gains_to_core,
-        carry=(out_hidden, gate_grad),
+    steps.step(back("wqkvo", d_wqkvo, [3]), summed=entry("wqkvo", 1), late=gains_to_core)
+    (gate_grad,) = steps.step(
+        summed=entry("wqkvo", 2), late=gains_to_packs, carry=(gate_grad,)
     )
     up_grad = settle_all("wu")
-
-    (up_grad,) = steps.step(summed=entry("wqkvo", 3), late=gains_to_packs, carry=(up_grad,))
     in_grad = both_rows(kept["in_grad"], steps.take("in_grad"))
-    (in_grad,) = steps.step(late=gains_along, carry=(in_grad,))
-    steps.step()
+    in_grad, up_grad = steps.step(
+        to_core("result", result), summed=entry("wqkvo", 3), carry=(in_grad, up_grad)
+    )
+    steps.step(late=gains_along)
+    out_hidden = both_rows(result, steps.take("result"))
+    (out_hidden,) = steps.step(carry=(out_hidden,))
     steps.step()
     shares_of_gains = jnp.stack(
         [kept["gains"]] + [steps.take(("gains", j)) for j in range(1, cycle)]

time: 728 us -> 709 us (0.974)
  other arithmetic: 42.7 us -> 35 us
    unnamed x210 -> x182, local copies, waits for them, and re-layouts: 26.6 us -> 22.6 us
  transfers between devices with their start and end apart: 105 -> 105, of which waited for: 55 -> 49; matrix products, arithmetic and copies ran while one was open for 5% -> 4% of each run, Pallas kernels for 20% -> 20%
where the time goes in v6:
time: 709 us; the launch traced here: 702 us
  waiting for transfers between devices  335 us (47%)
  starting transfers between devices  148 us (21%)
  Pallas kernels  146 us (21%)
  local copies, waits for them, and re-layouts  36.4 us (5%)
  other arithmetic  35 us (5%)
    ppermute x104, waiting for transfers between devices, start(): lax.ppermute(value, axis, pairs)  332 us
    ppermute x104, starting transfers between devices, start(): lax.ppermute(value, axis, pairs)  148 us
    pallas_call x12, Pallas kernels, gridded(): pl.pallas_call(kernel, grid=(steps,), in_specs=[pl.BlockSpec(memory_space...  101 us
    pallas_call x4, Pallas kernels, weight_grad(): pl.pallas_call(functools.partial(weight_grad_kernel, count, len(terms), s...  26.2 us
    unnamed x182, local copies, waits for them, and re-layouts  22.6 us
    pallas_call x19, Pallas kernels, in_vmem(): pl.pallas_call(kernel, out_shape=out_shape, in_specs=specs, out_specs=[pl...  18.6 us
  transfers between devices with their start and end apart: 105, of which 49 were waited for; matrix products, arithmetic and copies ran while one was open for 4% of the time, Pallas kernels for 20%

profile of v6, /device:TPU:0, one launch (start us, length us, event | category | flops | bytes accessed | tf_op | source)
XLA Modules:
  0.0 702.4 jit_solution(4221827995009250215)
XLA Ops:
  6.7 2.9 collective-permute-start
  13.3 3.1 constant_dynamic-slice_fusion.11
  17.1 4.2 constant_dynamic-slice_fusion.5
  36.4 8.9 %collective-permute-done.3.refs_1_ = bf16[128,2048]{1,0:T(8,128)(2,1)} collective-permute-done((bf16[128,2048]{1,0:T(8,128)(2,1)}, bf16[128,2048]{1,0:T(8,128)(2,1)}, u32[]{:S(2)}, u32[]{:S(2)}) %collective-permute-start.3) | collective-permute-done | bytes 524320 | tf_op jit(solution)/shard_map/ppermute | solution.py:143
  45.3 9.8 %collective-permute-done.4.refs_2_ = bf16[128,2048]{1,0:T(8,128)(2,1)} collective-permute-done((bf16[128,2048]{1,0:T(8,128)(2,1)}, bf16[128,2048]{1,0:T(8,128)(2,1)}, u32[]{:S(2)}, u32[]{:S(2)}) %collective-permute-start.4) | collective-permute-done | bytes 524320 | tf_op jit(solution)/shard_map/ppermute | solution.py:143
  61.1 6.3 shard_map.216
  71.3 11.3 %collective-permute-done.7.refs_4_.refs_5_ = bf16[512,1024]{1,0:T(8,128)(2,1)} collective-permute-done((bf16[512,1024]{1,0:T(8,128)(2,1)S(1)}, bf16[512,1024]{1,0:T(8,128)(2,1)}, u32[]{:S(2)}, u32[]{:S(2)}) %collective-permute-start.7) | collective-permute-done | bytes 1048608 | tf_op jit(solution)/shard_map/ppermute | solution.py:143
  91.2 5.5 collective-permute-done.10.refs_1_
  97.4 8.7 %collective-permute-done.11.refs_2_ = bf16[2,512,128]{2,1,0:T(8,128)(2,1)S(1)} collective-permute-done((bf16[2,512,128]{2,1,0:T(8,128)(2,1)S(1)}, bf16[2,512,128]{2,1,0:T(8,128)(2,1)S(1)}, u32[]{:S(2)}, u32[]{:S(2)}) %collective-permute-start.11) | collective-permute-done | bytes 262176 | tf_op jit(solution)/shard_map/ppermute | solution.py:143
  108.2 2.9 collective-permute-start.17
  119.4 12.9 %shard_map.218 = (bf16[2,512,256]{2,1,0:T(8,128)(2,1)S(1)}, bf16[512,2048]{1,0:T(8,128)(2,1)S(1)}, bf16[512,2048]{1,0:T(8,128)(2,1)S(1)}) custom-call(bf16[2,512,256]{2,1,0:T(8,128)(2,1)S(1)} %get-tuple-element.344.q_ref, s32[4,256,1]{2,1,0:T(8,128)S(1)} %copy.39.place_ref, s32[4,256,1]{2,1,0:T(8,128)S(1)} %copy.40.start_ref, ...), custom_call_target="tpu_custom_call" | custom-call | flops 1 | bytes 1 | tf_op jit(solution)/shard_map/pallas_call | solution.py:317
  135.4 4.2 collective-permute-done.18.came_ref
  145.6 9.7 %collective-permute-done.20.refs_1_ = bf16[128,2048]{1,0:T(8,128)(2,1)S(1)} collective-permute-done((bf16[128,2048]{1,0:T(8,128)(2,1)S(1)}, bf16[128,2048]{1,0:T(8,128)(2,1)S(1)}, u32[]{:S(2)}, u32[]{:S(2)}) %collective-permute-start.20) | collective-permute-done | bytes 524320 | tf_op jit(solution)/shard_map/ppermute | solution.py:143
  155.3 10.8 %collective-permute-done.21.refs_2_ = bf16[128,2048]{1,0:T(8,128)(2,1)S(1)} collective-permute-done((bf16[128,2048]{1,0:T(8,128)(2,1)S(1)}, bf16[128,2048]{1,0:T(8,128)(2,1)S(1)}, u32[]{:S(2)}, u32[]{:S(2)}) %collective-permute-start.21) | collective-permute-done | bytes 524320 | tf_op jit(solution)/shard_map/ppermute | solution.py:143
  175.7 8.7 %collective-permute-done.25.refs_1_ = bf16[128,2048]{1,0:T(8,128)(2,1)S(1)} collective-permute-done((bf16[128,2048]{1,0:T(8,128)(2,1)S(1)}, bf16[128,2048]{1,0:T(8,128)(2,1)S(1)}, u32[]{:S(2)}, u32[]{:S(2)}) %collective-permute-start.25) | collective-permute-done | bytes 524320 | tf_op jit(solution)/shard_map/ppermute | solution.py:143
  184.4 9.8 %collective-permute-done.26.refs_2_ = bf16[128,2048]{1,0:T(8,128)(2,1)S(1)} collective-permute-done((bf16[128,2048]{1,0:T(8,128)(2,1)S(1)}, bf16[128,2048]{1,0:T(8,128)(2,1)S(1)}, u32[]{:S(2)}, u32[]{:S(2)}) %collective-permute-start.26) | collective-permute-done | bytes 524320 | tf_op jit(solution)/shard_map/ppermute | solution.py:143
  200.1 14.5 %shard_map.223 = (f32[1024,1024]{1,0:T(8,128)S(1)}, f32[1024,1024]{1,0:T(8,128)S(1)}, bf16[1024,1024]{1,0:T(8,128)(2,1)S(1)}, bf16[2048,1024]{1,0:T(8,128)(2,1)}, bf16[2048,1024]{1,0:T(8,128)(2,1)}) custom-call(bf16[512,2048]{1,0:T(8,128)(2,1)S(1)} %shard_map.222.refs_0_.refs_1_, bf16[512,2048]{1,0:T(8,128)(2,1)S(1)} %collective-permute-done.30.refs_1_.refs_2_, ...), custom_call_target="tpu_custom_call" | custom-call | flops 1 | bytes 1 | tf_op jit(solution)/shard_map/pallas_call | solution.py:317
  216.6 6.3 shard_map.224
  228.9 19.5 %collective-permute-done.32 = bf16[512,1024]{1,0:T(8,128)(2,1)} collective-permute-done((bf16[512,1024]{1,0:T(8,128)(2,1)S(1)}, bf16[512,1024]{1,0:T(8,128)(2,1)}, u32[]{:S(2)}, u32[]{:S(2)}) %collective-permute-start.32) | collective-permute-done | bytes 1048608 | tf_op jit(solution)/shard_map/ppermute | solution.py:143
  252.8 8.2 %collective-permute-start.35 = (bf16[512,1024]{1,0:T(8,128)(2,1)}, bf16[512,1024]{1,0:T(8,128)(2,1)}, u32[]{:S(2)}, u32[]{:S(2)}) collective-permute-start(bf16[512,1024]{1,0:T(8,128)(2,1)} %collective-permute-done.32), channel_id=1, source_target_pairs={{0,2},{6,4},{1,3},{7,5},{8,10},{14,12},{9,11},{15,13},{16,18},{22,... | collective-permute-start | bytes 3145736 | tf_op jit(solution)/shard_map/ppermute | solution.py:143
  262.2 19.0 %collective-permute-done.35 = bf16[512,1024]{1,0:T(8,128)(2,1)} collective-permute-done((bf16[512,1024]{1,0:T(8,128)(2,1)}, bf16[512,1024]{1,0:T(8,128)(2,1)}, u32[]{:S(2)}, u32[]{:S(2)}) %collective-permute-start.35) | collective-permute-done | bytes 1048608 | tf_op jit(solution)/shard_map/ppermute | solution.py:143
  281.2 3.1 add_convert_fusion.24
  294.7 8.9 %shard_map.225 = (bf16[1024,1024]{1,0:T(8,128)(2,1)S(1)}, bf16[1024,1024]{1,0:T(8,128)(2,1)S(1)}, bf16[2048,1024]{1,0:T(8,128)(2,1)S(1)}) custom-call(bf16[512,2048]{1,0:T(8,128)(2,1)S(1)} %copy-done.3, bf16[512,2048]{1,0:T(8,128)(2,1)S(1)} %copy-done.7, bf16[512,1024]{1,0:T(8,128)(2,1)S(1)} %copy-done.25, bf16[512,1024]{1,0:T(8,128)(2,1)S(1)} %copy-done.54, ...), custom_call_target="tpu_custom_call" | custom-call | flops 1 | bytes 1 | tf_op jit(solution)/shard_map/pallas_call | solution.py:317
  303.7 9.8 %shard_map.226 = (bf16[512,2048]{1,0:T(8,128)(2,1)S(1)}, bf16[512,2048]{1,0:T(8,128)(2,1)S(1)}) custom-call(bf16[1024,1024]{1,0:T(8,128)(2,1)S(1)} %get-tuple-element.416.refs_0_.refs_3_, bf16[1024,1024]{1,0:T(8,128)(2,1)S(1)} %get-tuple-element.417.refs_1_.refs_3_, bf16[2048,1024]{1,0:T(8,128)(2,1)S(1)} %copy-done.14, bf16[2048,1024]{1,0:T(8,128)(2,1)S(1)} %copy-done.15), custom_call_target="tpu_custom_call" | custom-call | flops 1 | bytes 1 | tf_op jit(solution)/shard_map/pallas_call | solution.py:317
  313.5 5.9 shard_map.227
  325.6 18.9 %collective-permute-done.41.refs_2_ = bf16[512,1024]{1,0:T(8,128)(2,1)S(1)} collective-permute-done((bf16[512,1024]{1,0:T(8,128)(2,1)S(1)}, bf16[512,1024]{1,0:T(8,128)(2,1)S(1)}, u32[]{:S(2)}, u32[]{:S(2)}) %collective-permute-start.41) | collective-permute-done | bytes 1048608 | tf_op jit(solution)/shard_map/ppermute | solution.py:143
  346.8 3.7 collective-permute-start.46
  351.2 6.1 shard_map.228
  357.4 12.3 %collective-permute-done.46.refs_4_ = bf16[512,1024]{1,0:T(8,128)(2,1)S(1)} collective-permute-done((bf16[512,1024]{1,0:T(8,128)(2,1)S(1)}, bf16[512,1024]{1,0:T(8,128)(2,1)S(1)}, u32[]{:S(2)}, u32[]{:S(2)}) %collective-permute-start.46) | collective-permute-done | bytes 1048608 | tf_op jit(solution)/shard_map/ppermute | solution.py:143
  370.7 3.7 collective-permute-start.51
  379.2 10.6 %collective-permute-done.47.refs_1_ = bf16[128,2048]{1,0:T(8,128)(2,1)S(1)} collective-permute-done((bf16[128,2048]{1,0:T(8,128)(2,1)S(1)}, bf16[128,2048]{1,0:T(8,128)(2,1)S(1)}, u32[]{:S(2)}, u32[]{:S(2)}) %collective-permute-start.47) | collective-permute-done | bytes 524320 | tf_op jit(solution)/shard_map/ppermute | solution.py:143
  389.8 6.2 collective-permute-done.48.refs_2_
  404.7 8.2 %collective-permute-done.52.refs_1_ = bf16[128,2048]{1,0:T(8,128)(2,1)S(1)} collective-permute-done((bf16[128,2048]{1,0:T(8,128)(2,1)S(1)}, bf16[128,2048]{1,0:T(8,128)(2,1)S(1)}, u32[]{:S(2)}, u32[]{:S(2)}) %collective-permute-start.52) | collective-permute-done | bytes 524320 | tf_op jit(solution)/shard_map/ppermute | solution.py:143
  412.9 6.8 collective-permute-done.53.refs_2_
  422.6 2.7 collective-permute-start.60
  426.1 22.9 %shard_map.232 = (bf16[2,512,256]{2,1,0:T(8,128)(2,1)S(1)}, bf16[512,1024]{1,0:T(8,128)(2,1)S(1)}) custom-call(s32[1]{0:T(128)} %bitcast.5.here_ref, bf16[2,512,256]{2,1,0:T(8,128)(2,1)S(1)} %copy-done.36, bf16[512,2048]{1,0:T(8,128)(2,1)S(1)} %shard_map.231.mine_ref.refs_3_, bf16[512,2048]{1,0:T(8,128)(2,1)S(1)} %collective-permute-done.58.other_ref.refs_4_, ...), custom_call_target="tpu_custom_call" | custom-call | flops 1 | bytes 1 | tf_op jit(solution)/shard_map/pallas_call | solution.py:317
  455.0 19.0 %collective-permute-done.61 = bf16[512,1024]{1,0:T(8,128)(2,1)S(1)} collective-permute-done((bf16[512,1024]{1,0:T(8,128)(2,1)S(1)}, bf16[512,1024]{1,0:T(8,128)(2,1)S(1)}, u32[]{:S(2)}, u32[]{:S(2)}) %collective-permute-start.61) | collective-permute-done | bytes 1048608 | tf_op jit(solution)/shard_map/ppermute | solution.py:143
  477.8 3.7 collective-permute-start.67
  483.2 5.4 shard_map.233
  488.6 10.5 %collective-permute-done.65 = bf16[512,1024]{1,0:T(8,128)(2,1)S(1)} collective-permute-done((bf16[512,1024]{1,0:T(8,128)(2,1)S(1)}, bf16[512,1024]{1,0:T(8,128)(2,1)S(1)}, u32[]{:S(2)}, u32[]{:S(2)}) %collective-permute-start.65) | collective-permute-done | bytes 1048608 | tf_op jit(solution)/shard_map/ppermute | solution.py:143
  499.2 3.9 collective-permute-done.67.refs_4_
  505.4 4.4 collective-permute-start.70
  510.4 4.4 shard_map.234
  514.9 15.5 %collective-permute-done.70.came_ref = bf16[512,1024]{1,0:T(8,128)(2,1)S(1)} collective-permute-done((bf16[512,1024]{1,0:T(8,128)(2,1)S(1)}, bf16[512,1024]{1,0:T(8,128)(2,1)S(1)}, u32[]{:S(2)}, u32[]{:S(2)}) %collective-permute-start.70) | collective-permute-done | bytes 1048608 | tf_op jit(solution)/shard_map/ppermute | solution.py:143
  531.4 3.7 collective-permute-start.75
  539.9 11.4 %collective-permute-done.71.refs_1_ = bf16[128,2048]{1,0:T(8,128)(2,1)S(1)} collective-permute-done((bf16[128,2048]{1,0:T(8,128)(2,1)S(1)}, bf16[128,2048]{1,0:T(8,128)(2,1)S(1)}, u32[]{:S(2)}, u32[]{:S(2)}) %collective-permute-start.71) | collective-permute-done | bytes 524320 | tf_op jit(solution)/shard_map/ppermute | solution.py:143
  551.3 7.1 %collective-permute-done.72.refs_2_ = bf16[128,2048]{1,0:T(8,128)(2,1)S(1)} collective-permute-done((bf16[128,2048]{1,0:T(8,128)(2,1)S(1)}, bf16[128,2048]{1,0:T(8,128)(2,1)S(1)}, u32[]{:S(2)}, u32[]{:S(2)}) %collective-permute-start.72) | collective-permute-done | bytes 524320 | tf_op jit(solution)/shard_map/ppermute | solution.py:143
  559.4 3.1 collective-permute-start.77
  563.6 3.3 shard_map.238
  567.0 7.8 %shard_map.237 = (bf16[512,640]{1,0:T(8,128)(2,1)S(1)}, bf16[512,640]{1,0:T(8,128)(2,1)S(1)}, bf16[512,640]{1,0:T(8,128)(2,1)S(1)}, bf16[512,640]{1,0:T(8,128)(2,1)S(1)}) custom-call(bf16[512,2048]{1,0:T(8,128)(2,1)S(1)} %copy-done.32, bf16[512,2048]{1,0:T(8,128)(2,1)S(1)} %copy-done.34, bf16[1024,384]{1,0:T(8,128)(2,1)S(1)} %shard_map.236.refs_2_.refs_0_, ...), custom_call_target="tpu_custom_call" | custom-call | flops 1 | bytes 1 | tf_op jit(solution)/shard_map/pallas_call | solution.py:587
  574.8 6.3 collective-permute-done.77.refs_2_
  582.0 4.0 collective-permute-start.82
  588.6 8.7 %collective-permute-done.78 = bf16[512,640]{1,0:T(8,128)(2,1)S(1)} collective-permute-done((bf16[512,640]{1,0:T(8,128)(2,1)S(1)}, bf16[512,640]{1,0:T(8,128)(2,1)S(1)}, u32[]{:S(2)}, u32[]{:S(2)}) %collective-permute-start.78) | collective-permute-done | bytes 655392 | tf_op jit(solution)/shard_map/ppermute | solution.py:143
  598.2 6.6 collective-permute-done.82.refs_4_
  605.3 3.8 collective-permute-start.87
  614.0 8.0 %collective-permute-done.83.refs_1_ = bf16[128,2048]{1,0:T(8,128)(2,1)S(1)} collective-permute-done((bf16[128,2048]{1,0:T(8,128)(2,1)S(1)}, bf16[128,2048]{1,0:T(8,128)(2,1)S(1)}, u32[]{:S(2)}, u32[]{:S(2)}) %collective-permute-start.83) | collective-permute-done | bytes 524320 | tf_op jit(solution)/shard_map/ppermute | solution.py:143
  622.0 13.2 %collective-permute-done.84.refs_2_ = bf16[128,2048]{1,0:T(8,128)(2,1)S(1)} collective-permute-done((bf16[128,2048]{1,0:T(8,128)(2,1)S(1)}, bf16[128,2048]{1,0:T(8,128)(2,1)S(1)}, u32[]{:S(2)}, u32[]{:S(2)}) %collective-permute-start.84) | collective-permute-done | bytes 524320 | tf_op jit(solution)/shard_map/ppermute | solution.py:143
  641.2 4.2 shard_map.241
  648.3 4.0 collective-permute-start.97
  657.1 4.2 shard_map.244
  668.9 10.7 %collective-permute-done.100.refs_4_ = bf16[512,640]{1,0:T(8,128)(2,1)S(1)} collective-permute-done((bf16[512,640]{1,0:T(8,128)(2,1)S(1)}, bf16[512,640]{1,0:T(8,128)(2,1)S(1)}, u32[]{:S(2)}, u32[]{:S(2)}) %collective-permute-start.100) | collective-permute-done | bytes 655392 | tf_op jit(solution)/shard_map/ppermute | solution.py:143
  684.0 3.9 collective-permute-start.102
  691.6 4.1 collective-permute-done.101
  697.6 4.4 shard_map.246
  (455 shorter events, 193.4 us)
Async XLA Ops:
  28.2 26.9 %collective-permute-start.6 = (bf16[768,640]{1,0:T(8,128)(2,1)}, bf16[768,640]{1,0:T(8,128)(2,1)}, u32[]{:S(2)}, u32[]{:S(2)}) collective-permute-start(bf16[768,640]{1,0:T(8,128)(2,1)} %shard_map.213), channel_id=1, source_target_pairs={{0,2},{2,0},{4,6},{6,4},{1,3},{3,1},{5,7},{7,5},{8,10},{10,8},{12,... | collective-permute-start | bytes 2949128 | tf_op jit(solution)/shard_map/ppermute | solution.py:143
  31.4 23.8 %collective-permute-start.4 = (bf16[128,2048]{1,0:T(8,128)(2,1)}, bf16[128,2048]{1,0:T(8,128)(2,1)}, u32[]{:S(2)}, u32[]{:S(2)}) collective-permute-start(bf16[128,2048]{1,0:T(8,128)(2,1)} %get-tuple-element.311), channel_id=1, source_target_pairs={{0,16},{8,24},{16,0},{24,8},{1,17},{9,25},{17,1},{25,9},{2,18},{10... | collective-permute-start | bytes 1572872 | tf_op jit(solution)/shard_map/ppermute | solution.py:143
  32.2 23.0 %collective-permute-start.5 = (bf16[128,2048]{1,0:T(8,128)(2,1)}, bf16[128,2048]{1,0:T(8,128)(2,1)}, u32[]{:S(2)}, u32[]{:S(2)}) collective-permute-start(bf16[128,2048]{1,0:T(8,128)(2,1)} %get-tuple-element.312), channel_id=1, source_target_pairs={{0,24},{8,16},{16,8},{24,0},{1,25},{9,17},{17,9},{25,1},{2,26},{10... | collective-permute-start | bytes 1572872 | tf_op jit(solution)/shard_map/ppermute | solution.py:143
  56.9 25.7 %collective-permute-start.7 = (bf16[512,1024]{1,0:T(8,128)(2,1)S(1)}, bf16[512,1024]{1,0:T(8,128)(2,1)}, u32[]{:S(2)}, u32[]{:S(2)}) collective-permute-start(bf16[512,1024]{1,0:T(8,128)(2,1)S(1)} %copy-done.88), channel_id=1, source_target_pairs={{0,8},{8,0},{16,24},{24,16},{1,9},{9,1},{17,25},{25,17},{2,10},{10... | collective-permute-start | bytes 3145736 | tf_op jit(solution)/shard_map/ppermute | solution.py:143
  57.6 25.2 %collective-permute-start.8 = (bf16[512,1024]{1,0:T(8,128)(2,1)S(1)}, bf16[512,1024]{1,0:T(8,128)(2,1)S(1)}, u32[]{:S(2)}, u32[]{:S(2)}) collective-permute-start(bf16[512,1024]{1,0:T(8,128)(2,1)S(1)} %copy-done.87), channel_id=1, source_target_pairs={{0,16},{8,24},{16,0},{24,8},{1,17},{9,25},{17,1},{25,9},{2,18},{10... | collective-permute-start | bytes 3145736 | tf_op jit(solution)/shard_map/ppermute | solution.py:143
  82.8 25.4 %collective-permute-start.13 = (bf16[512,1024]{1,0:T(8,128)(2,1)S(1)}, bf16[512,1024]{1,0:T(8,128)(2,1)S(1)}, u32[]{:S(2)}, u32[]{:S(2)}) collective-permute-start(bf16[512,1024]{1,0:T(8,128)(2,1)S(1)} %pad_maximum_fusion.2), channel_id=1, source_target_pairs={{0,24},{8,16},{16,8},{24,0},{1,25},{9,17},{17,9},{25,1},{2,26},{10... | collective-permute-start | bytes 3145736 | tf_op jit(solution)/shard_map/ppermute | solution.py:143
  84.7 21.4 %collective-permute-start.11 = (bf16[2,512,128]{2,1,0:T(8,128)(2,1)S(1)}, bf16[2,512,128]{2,1,0:T(8,128)(2,1)S(1)}, u32[]{:S(2)}, u32[]{:S(2)}) collective-permute-start(bf16[2,512,128]{2,1,0:T(8,128)(2,1)S(1)} %get-tuple-element.333.refs_0_), channel_id=1, source_target_pairs={{0,4},{2,6},{4,0},{6,2},{1,5},{3,7},{5,1},{7,3},{8,12},{10,14},{12... | collective-permute-start | bytes 786440 | tf_op jit(solution)/shard_map/ppermute | solution.py:143
  87.3 19.5 %collective-permute-start.12 = (bf16[2,512,128]{2,1,0:T(8,128)(2,1)S(1)}, bf16[2,512,128]{2,1,0:T(8,128)(2,1)S(1)}, u32[]{:S(2)}, u32[]{:S(2)}) collective-permute-start(bf16[2,512,128]{2,1,0:T(8,128)(2,1)S(1)} %get-tuple-element.333.refs_0_), channel_id=1, source_target_pairs={{0,6},{2,4},{4,2},{6,0},{1,7},{3,5},{5,3},{7,1},{8,14},{10,12},{12... | collective-permute-start | bytes 786440 | tf_op jit(solution)/shard_map/ppermute | solution.py:143
  108.2 27.1 %collective-permute-start.17 = (bf16[512,1024]{1,0:T(8,128)(2,1)}, bf16[512,1024]{1,0:T(8,128)(2,1)}, u32[]{:S(2)}, u32[]{:S(2)}) collective-permute-start(bf16[512,1024]{1,0:T(8,128)(2,1)} %collective-permute-done.7.refs_4_.refs_5_), channel_id=1, source_target_pairs={{0,2},{2,0},{4,6},{6,4},{1,3},{3,1},{5,7},{7,5},{8,10},{10,8},{12,... | collective-permute-start | bytes 3145736 | tf_op jit(solution)/shard_map/ppermute | solution.py:143
  111.1 22.0 %collective-permute-start.14 = (bf16[128,2048]{1,0:T(8,128)(2,1)}, bf16[128,2048]{1,0:T(8,128)(2,1)}, u32[]{:S(2)}, u32[]{:S(2)}) collective-permute-start(bf16[128,2048]{1,0:T(8,128)(2,1)} %get-tuple-element.340), channel_id=1, source_target_pairs={{0,8},{8,0},{16,24},{24,16},{1,9},{9,1},{17,25},{25,17},{2,10},{10... | collective-permute-start | bytes 1572872 | tf_op jit(solution)/shard_map/ppermute | solution.py:143
  112.1 21.8 %collective-permute-start.15 = (bf16[128,2048]{1,0:T(8,128)(2,1)}, bf16[128,2048]{1,0:T(8,128)(2,1)}, u32[]{:S(2)}, u32[]{:S(2)}) collective-permute-start(bf16[128,2048]{1,0:T(8,128)(2,1)} %get-tuple-element.341), channel_id=1, source_target_pairs={{0,16},{8,24},{16,0},{24,8},{1,17},{9,25},{17,1},{25,9},{2,18},{10... | collective-permute-start | bytes 1572872 | tf_op jit(solution)/shard_map/ppermute | solution.py:143
  113.2 22.2 %collective-permute-start.16 = (bf16[128,2048]{1,0:T(8,128)(2,1)}, bf16[128,2048]{1,0:T(8,128)(2,1)}, u32[]{:S(2)}, u32[]{:S(2)}) collective-permute-start(bf16[128,2048]{1,0:T(8,128)(2,1)} %get-tuple-element.342), channel_id=1, source_target_pairs={{0,24},{8,16},{16,8},{24,0},{1,25},{9,17},{17,9},{25,1},{2,26},{10... | collective-permute-start | bytes 1572872 | tf_op jit(solution)/shard_map/ppermute | solution.py:143
  139.5 26.5 %collective-permute-start.19 = (bf16[512,1024]{1,0:T(8,128)(2,1)S(1)}, bf16[512,1024]{1,0:T(8,128)(2,1)S(1)}, u32[]{:S(2)}, u32[]{:S(2)}) collective-permute-start(bf16[512,1024]{1,0:T(8,128)(2,1)S(1)} %copy-done.22), channel_id=1, source_target_pairs={{0,2},{2,0},{4,6},{6,4},{1,3},{3,1},{5,7},{7,5},{8,10},{10,8},{12,... | collective-permute-start | bytes 3145736 | tf_op jit(solution)/shard_map/ppermute | solution.py:143
  141.4 24.6 %collective-permute-start.21 = (bf16[128,2048]{1,0:T(8,128)(2,1)S(1)}, bf16[128,2048]{1,0:T(8,128)(2,1)S(1)}, u32[]{:S(2)}, u32[]{:S(2)}) collective-permute-start(bf16[128,2048]{1,0:T(8,128)(2,1)S(1)} %get-tuple-element.361), channel_id=1, source_target_pairs={{0,16},{8,24},{16,0},{24,8},{1,17},{9,25},{17,1},{25,9},{2,18},{10... | collective-permute-start | bytes 1572872 | tf_op jit(solution)/shard_map/ppermute | solution.py:143
  142.8 23.3 %collective-permute-start.22 = (bf16[128,2048]{1,0:T(8,128)(2,1)S(1)}, bf16[128,2048]{1,0:T(8,128)(2,1)S(1)}, u32[]{:S(2)}, u32[]{:S(2)}) collective-permute-start(bf16[128,2048]{1,0:T(8,128)(2,1)S(1)} %get-tuple-element.362), channel_id=1, source_target_pairs={{0,24},{8,16},{16,8},{24,0},{1,25},{9,17},{17,9},{25,1},{2,26},{10... | collective-permute-start | bytes 1572872 | tf_op jit(solution)/shard_map/ppermute | solution.py:143
  166.1 29.7 %collective-permute-start.24 = (bf16[512,2048]{1,0:T(8,128)(2,1)S(1)}, bf16[512,2048]{1,0:T(8,128)(2,1)S(1)}, u32[]{:S(2)}, u32[]{:S(2)}) collective-permute-start(bf16[512,2048]{1,0:T(8,128)(2,1)S(1)} %shard_map.220.refs_1_.refs_0_), channel_id=1, source_target_pairs={{0,1},{1,0},{2,3},{3,2},{4,5},{5,4},{6,7},{7,6},{8,9},{9,8},{10,11... | collective-permute-start | bytes 6291464 | tf_op jit(solution)/shard_map/ppermute | solution.py:143
  166.1 29.6 %collective-permute-start.23 = (bf16[512,1024]{1,0:T(8,128)(2,1)S(1)}, bf16[512,1024]{1,0:T(8,128)(2,1)S(1)}, u32[]{:S(2)}, u32[]{:S(2)}) collective-permute-start(bf16[512,1024]{1,0:T(8,128)(2,1)S(1)} %copy-done.24), channel_id=1, source_target_pairs={{0,2},{2,0},{4,6},{6,4},{1,3},{3,1},{5,7},{7,5},{8,10},{10,8},{12,... | collective-permute-start | bytes 3145736 | tf_op jit(solution)/shard_map/ppermute | solution.py:143
  170.7 23.5 %collective-permute-start.26 = (bf16[128,2048]{1,0:T(8,128)(2,1)S(1)}, bf16[128,2048]{1,0:T(8,128)(2,1)S(1)}, u32[]{:S(2)}, u32[]{:S(2)}) collective-permute-start(bf16[128,2048]{1,0:T(8,128)(2,1)S(1)} %get-tuple-element.376), channel_id=1, source_target_pairs={{0,16},{8,24},{16,0},{24,8},{1,17},{9,25},{17,1},{25,9},{2,18},{10... | collective-permute-start | bytes 1572872 | tf_op jit(solution)/shard_map/ppermute | solution.py:143
  171.7 24.0 %collective-permute-start.27 = (bf16[128,2048]{1,0:T(8,128)(2,1)S(1)}, bf16[128,2048]{1,0:T(8,128)(2,1)S(1)}, u32[]{:S(2)}, u32[]{:S(2)}) collective-permute-start(bf16[128,2048]{1,0:T(8,128)(2,1)S(1)} %get-tuple-element.377), channel_id=1, source_target_pairs={{0,24},{8,16},{16,8},{24,0},{1,25},{9,17},{17,9},{25,1},{2,26},{10... | collective-permute-start | bytes 1572872 | tf_op jit(solution)/shard_map/ppermute | solution.py:143
  195.9 27.0 %collective-permute-start.28 = (bf16[512,1024]{1,0:T(8,128)(2,1)S(1)}, bf16[512,1024]{1,0:T(8,128)(2,1)S(1)}, u32[]{:S(2)}, u32[]{:S(2)}) collective-permute-start(bf16[512,1024]{1,0:T(8,128)(2,1)S(1)} %pad_maximum_fusion.3), channel_id=1, source_target_pairs={{0,8},{8,0},{16,24},{24,16},{1,9},{9,1},{17,25},{25,17},{2,10},{10... | collective-permute-start | bytes 3145736 | tf_op jit(solution)/shard_map/ppermute | solution.py:143
  197.0 26.0 %collective-permute-start.29 = (bf16[512,1024]{1,0:T(8,128)(2,1)S(1)}, bf16[512,1024]{1,0:T(8,128)(2,1)S(1)}, u32[]{:S(2)}, u32[]{:S(2)}) collective-permute-start(bf16[512,1024]{1,0:T(8,128)(2,1)S(1)} %pad_maximum_fusion.4), channel_id=1, source_target_pairs={{0,16},{8,24},{16,0},{24,8},{1,17},{9,25},{17,1},{25,9},{2,18},{10... | collective-permute-start | bytes 3145736 | tf_op jit(solution)/shard_map/ppermute | solution.py:143
  223.0 25.4 %collective-permute-start.32 = (bf16[512,1024]{1,0:T(8,128)(2,1)S(1)}, bf16[512,1024]{1,0:T(8,128)(2,1)}, u32[]{:S(2)}, u32[]{:S(2)}) collective-permute-start(bf16[512,1024]{1,0:T(8,128)(2,1)S(1)} %get-tuple-element.397), channel_id=1, source_target_pairs={{0,8},{8,0},{16,24},{24,16},{1,9},{9,1},{17,25},{25,17},{2,10},{10... | collective-permute-start | bytes 3145736 | tf_op jit(solution)/shard_map/ppermute | solution.py:143
  224.0 24.9 %collective-permute-start.33 = (bf16[512,1024]{1,0:T(8,128)(2,1)S(1)}, bf16[512,1024]{1,0:T(8,128)(2,1)S(1)}, u32[]{:S(2)}, u32[]{:S(2)}) collective-permute-start(bf16[512,1024]{1,0:T(8,128)(2,1)S(1)} %get-tuple-element.398), channel_id=1, source_target_pairs={{0,16},{8,24},{16,0},{24,8},{1,17},{9,25},{17,1},{25,9},{2,18},{10... | collective-permute-start | bytes 3145736 | tf_op jit(solution)/shard_map/ppermute | solution.py:143
  225.4 24.4 %collective-permute-start.31 = (bf16[512,1024]{1,0:T(8,128)(2,1)S(1)}, bf16[512,1024]{1,0:T(8,128)(2,1)S(1)}, u32[]{:S(2)}, u32[]{:S(2)}) collective-permute-start(bf16[512,1024]{1,0:T(8,128)(2,1)S(1)} %get-tuple-element.396), channel_id=1, source_target_pairs={{0,2},{6,4},{1,3},{7,5},{8,10},{14,12},{9,11},{15,13},{16,18},{22,... | collective-permute-start | bytes 3145736 | tf_op jit(solution)/shard_map/ppermute | solution.py:143
  252.8 28.4 %collective-permute-start.35 = (bf16[512,1024]{1,0:T(8,128)(2,1)}, bf16[512,1024]{1,0:T(8,128)(2,1)}, u32[]{:S(2)}, u32[]{:S(2)}) collective-permute-start(bf16[512,1024]{1,0:T(8,128)(2,1)} %collective-permute-done.32), channel_id=1, source_target_pairs={{0,2},{6,4},{1,3},{7,5},{8,10},{14,12},{9,11},{15,13},{16,18},{22,... | collective-permute-start | bytes 3145736 | tf_op jit(solution)/shard_map/ppermute | solution.py:143
  261.0 24.4 %collective-permute-start.36 = (bf16[512,1024]{1,0:T(8,128)(2,1)}, bf16[512,1024]{1,0:T(8,128)(2,1)}, u32[]{:S(2)}, u32[]{:S(2)}) collective-permute-start(bf16[512,1024]{1,0:T(8,128)(2,1)} %pad_maximum_fusion.8), channel_id=1, source_target_pairs={{0,24},{8,16},{16,8},{24,0},{1,25},{9,17},{17,9},{25,1},{2,26},{10... | collective-permute-start | bytes 3145736 | tf_op jit(solution)/shard_map/ppermute | solution.py:143
  285.4 34.0 %collective-permute-start.39 = (bf16[512,1024]{1,0:T(8,128)(2,1)}, bf16[512,1024]{1,0:T(8,128)(2,1)}, u32[]{:S(2)}, u32[]{:S(2)}) collective-permute-start(bf16[512,1024]{1,0:T(8,128)(2,1)} %copy-done.65), channel_id=1, source_target_pairs={{0,24},{8,16},{16,8},{24,0},{1,25},{9,17},{17,9},{25,1},{2,26},{10... | collective-permute-start | bytes 3145736 | tf_op jit(solution)/shard_map/ppermute | solution.py:143
  286.6 32.8 %collective-permute-start.37 = (bf16[512,1024]{1,0:T(8,128)(2,1)}, bf16[512,1024]{1,0:T(8,128)(2,1)}, u32[]{:S(2)}, u32[]{:S(2)}) collective-permute-start(bf16[512,1024]{1,0:T(8,128)(2,1)} %add_convert_fusion.24), channel_id=1, source_target_pairs={{2,4},{4,2},{3,5},{5,3},{10,12},{12,10},{11,13},{13,11},{18,20},{2... | collective-permute-start | bytes 3145736 | tf_op jit(solution)/shard_map/ppermute | solution.py:143
  290.8 28.6 %collective-permute-start.38 = (bf16[512,1024]{1,0:T(8,128)(2,1)S(1)}, bf16[512,1024]{1,0:T(8,128)(2,1)S(1)}, u32[]{:S(2)}, u32[]{:S(2)}) collective-permute-start(bf16[512,1024]{1,0:T(8,128)(2,1)S(1)} %fusion.refs_1_), channel_id=1, source_target_pairs={{0,2},{6,4},{2,0},{4,6},{1,3},{7,5},{3,1},{5,7},{8,10},{14,12},{10... | collective-permute-start | bytes 3145736 | tf_op jit(solution)/shard_map/ppermute | solution.py:143
  322.4 22.2 %collective-permute-start.41 = (bf16[512,1024]{1,0:T(8,128)(2,1)S(1)}, bf16[512,1024]{1,0:T(8,128)(2,1)S(1)}, u32[]{:S(2)}, u32[]{:S(2)}) collective-permute-start(bf16[512,1024]{1,0:T(8,128)(2,1)S(1)} %fusion.1.refs_3_), channel_id=1, source_target_pairs={{0,2},{6,4},{2,0},{4,6},{1,3},{7,5},{3,1},{5,7},{8,10},{14,12},{10... | collective-permute-start | bytes 3145736 | tf_op jit(solution)/shard_map/ppermute | solution.py:143
  322.5 22.0 %collective-permute-start.40 = (bf16[512,1024]{1,0:T(8,128)(2,1)S(1)}, bf16[512,1024]{1,0:T(8,128)(2,1)S(1)}, u32[]{:S(2)}, u32[]{:S(2)}) collective-permute-start(bf16[512,1024]{1,0:T(8,128)(2,1)S(1)} %add_convert_fusion.22), channel_id=1, source_target_pairs={{2,4},{4,2},{3,5},{5,3},{10,12},{12,10},{11,13},{13,11},{18,20},{2... | collective-permute-start | bytes 3145736 | tf_op jit(solution)/shard_map/ppermute | solution.py:143
  323.3 34.1 %collective-permute-start.42 = (bf16[512,2048]{1,0:T(8,128)(2,1)S(1)}, bf16[512,2048]{1,0:T(8,128)(2,1)S(1)}, u32[]{:S(2)}, u32[]{:S(2)}) collective-permute-start(bf16[512,2048]{1,0:T(8,128)(2,1)S(1)} %get-tuple-element.429), channel_id=1, source_target_pairs={{0,1},{1,0},{2,3},{3,2},{4,5},{5,4},{6,7},{7,6},{8,9},{9,8},{10,11... | collective-permute-start | bytes 6291464 | tf_op jit(solution)/shard_map/ppermute | solution.py:143
  323.3 34.0 %collective-permute-start.43 = (bf16[512,1024]{1,0:T(8,128)(2,1)S(1)}, bf16[512,1024]{1,0:T(8,128)(2,1)S(1)}, u32[]{:S(2)}, u32[]{:S(2)}) collective-permute-start(bf16[512,1024]{1,0:T(8,128)(2,1)S(1)} %get-tuple-element.430), channel_id=1, source_target_pairs={{0,8},{8,0},{16,24},{24,16},{1,9},{9,1},{17,25},{25,17},{2,10},{10... | collective-permute-start | bytes 3145736 | tf_op jit(solution)/shard_map/ppermute | solution.py:143
  324.3 33.1 %collective-permute-start.44 = (bf16[512,1024]{1,0:T(8,128)(2,1)S(1)}, bf16[512,1024]{1,0:T(8,128)(2,1)S(1)}, u32[]{:S(2)}, u32[]{:S(2)}) collective-permute-start(bf16[512,1024]{1,0:T(8,128)(2,1)S(1)} %get-tuple-element.431), channel_id=1, source_target_pairs={{0,16},{8,24},{16,0},{24,8},{1,17},{9,25},{17,1},{25,9},{2,18},{10... | collective-permute-start | bytes 3145736 | tf_op jit(solution)/shard_map/ppermute | solution.py:143
  346.8 22.9 %collective-permute-start.46 = (bf16[512,1024]{1,0:T(8,128)(2,1)S(1)}, bf16[512,1024]{1,0:T(8,128)(2,1)S(1)}, u32[]{:S(2)}, u32[]{:S(2)}) collective-permute-start(bf16[512,1024]{1,0:T(8,128)(2,1)S(1)} %fusion.2.refs_5_), channel_id=1, source_target_pairs={{0,2},{6,4},{2,0},{4,6},{1,3},{7,5},{3,1},{5,7},{8,10},{14,12},{10... | collective-permute-start | bytes 3145736 | tf_op jit(solution)/shard_map/ppermute | solution.py:143
  350.5 19.2 %collective-permute-start.45 = (bf16[512,1024]{1,0:T(8,128)(2,1)S(1)}, bf16[512,1024]{1,0:T(8,128)(2,1)S(1)}, u32[]{:S(2)}, u32[]{:S(2)}) collective-permute-start(bf16[512,1024]{1,0:T(8,128)(2,1)S(1)} %add_convert_fusion.20), channel_id=1, source_target_pairs={{2,4},{4,2},{3,5},{5,3},{10,12},{12,10},{11,13},{13,11},{18,20},{2... | collective-permute-start | bytes 3145736 | tf_op jit(solution)/shard_map/ppermute | solution.py:143
  370.7 25.3 %collective-permute-start.51 = (bf16[512,1024]{1,0:T(8,128)(2,1)S(1)}, bf16[512,1024]{1,0:T(8,128)(2,1)S(1)}, u32[]{:S(2)}, u32[]{:S(2)}) collective-permute-start(bf16[512,1024]{1,0:T(8,128)(2,1)S(1)} %fusion.3.refs_7_), channel_id=1, source_target_pairs={{0,2},{6,4},{2,0},{4,6},{1,3},{7,5},{3,1},{5,7},{8,10},{14,12},{10... | collective-permute-start | bytes 3145736 | tf_op jit(solution)/shard_map/ppermute | solution.py:143
  374.4 21.6 %collective-permute-start.50 = (bf16[512,1024]{1,0:T(8,128)(2,1)S(1)}, bf16[512,1024]{1,0:T(8,128)(2,1)S(1)}, u32[]{:S(2)}, u32[]{:S(2)}) collective-permute-start(bf16[512,1024]{1,0:T(8,128)(2,1)S(1)} %add_convert_fusion.18), channel_id=1, source_target_pairs={{2,4},{4,2},{3,5},{5,3},{10,12},{12,10},{11,13},{13,11},{18,20},{2... | collective-permute-start | bytes 3145736 | tf_op jit(solution)/shard_map/ppermute | solution.py:143
  376.6 19.4 %collective-permute-start.48 = (bf16[128,2048]{1,0:T(8,128)(2,1)S(1)}, bf16[128,2048]{1,0:T(8,128)(2,1)S(1)}, u32[]{:S(2)}, u32[]{:S(2)}) collective-permute-start(bf16[128,2048]{1,0:T(8,128)(2,1)S(1)} %get-tuple-element.441), channel_id=1, source_target_pairs={{0,16},{8,24},{16,0},{24,8},{1,17},{9,25},{17,1},{25,9},{2,18},{10... | collective-permute-start | bytes 1572872 | tf_op jit(solution)/shard_map/ppermute | solution.py:143
  397.1 24.3 %collective-permute-start.56 = (bf16[512,1024]{1,0:T(8,128)(2,1)S(1)}, bf16[512,1024]{1,0:T(8,128)(2,1)S(1)}, u32[]{:S(2)}, u32[]{:S(2)}) collective-permute-start(bf16[512,1024]{1,0:T(8,128)(2,1)S(1)} %fusion.4.refs_1_), channel_id=1, source_target_pairs={{0,2},{6,4},{2,0},{4,6},{1,3},{7,5},{3,1},{5,7},{8,10},{14,12},{10... | collective-permute-start | bytes 3145736 | tf_op jit(solution)/shard_map/ppermute | solution.py:143
  399.3 22.2 %collective-permute-start.55 = (bf16[512,1024]{1,0:T(8,128)(2,1)S(1)}, bf16[512,1024]{1,0:T(8,128)(2,1)S(1)}, u32[]{:S(2)}, u32[]{:S(2)}) collective-permute-start(bf16[512,1024]{1,0:T(8,128)(2,1)S(1)} %add_convert_fusion.16), channel_id=1, source_target_pairs={{2,4},{4,2},{3,5},{5,3},{10,12},{12,10},{11,13},{13,11},{18,20},{2... | collective-permute-start | bytes 3145736 | tf_op jit(solution)/shard_map/ppermute | solution.py:143
  419.9 29.0 %collective-permute-start.57 = (bf16[512,1024]{1,0:T(8,128)(2,1)S(1)}, bf16[512,1024]{1,0:T(8,128)(2,1)S(1)}, u32[]{:S(2)}, u32[]{:S(2)}) collective-permute-start(bf16[512,1024]{1,0:T(8,128)(2,1)S(1)} %get-tuple-element.462), channel_id=1, source_target_pairs={{0,24},{8,16},{16,8},{24,0},{1,25},{9,17},{17,9},{25,1},{2,26},{10... | collective-permute-start | bytes 3145736 | tf_op jit(solution)/shard_map/ppermute | solution.py:143
  422.6 28.5 %collective-permute-start.60 = (bf16[512,1024]{1,0:T(8,128)(2,1)S(1)}, bf16[512,1024]{1,0:T(8,128)(2,1)S(1)}, u32[]{:S(2)}, u32[]{:S(2)}) collective-permute-start(bf16[512,1024]{1,0:T(8,128)(2,1)S(1)} %fusion.5.refs_1_), channel_id=1, source_target_pairs={{0,2},{6,4},{2,0},{4,6},{1,3},{7,5},{3,1},{5,7},{8,10},{14,12},{10... | collective-permute-start | bytes 3145736 | tf_op jit(solution)/shard_map/ppermute | solution.py:143
  425.2 25.8 %collective-permute-start.59 = (bf16[512,1024]{1,0:T(8,128)(2,1)S(1)}, bf16[512,1024]{1,0:T(8,128)(2,1)S(1)}, u32[]{:S(2)}, u32[]{:S(2)}) collective-permute-start(bf16[512,1024]{1,0:T(8,128)(2,1)S(1)} %add_convert_fusion.14), channel_id=1, source_target_pairs={{2,4},{4,2},{3,5},{5,3},{10,12},{12,10},{11,13},{13,11},{18,20},{2... | collective-permute-start | bytes 3145736 | tf_op jit(solution)/shard_map/ppermute | solution.py:143
  448.9 25.0 %collective-permute-start.61 = (bf16[512,1024]{1,0:T(8,128)(2,1)S(1)}, bf16[512,1024]{1,0:T(8,128)(2,1)S(1)}, u32[]{:S(2)}, u32[]{:S(2)}) collective-permute-start(bf16[512,1024]{1,0:T(8,128)(2,1)S(1)} %get-tuple-element.477), channel_id=1, source_target_pairs={{0,8},{8,0},{16,24},{24,16},{1,9},{9,1},{17,25},{25,17},{2,10},{10... | collective-permute-start | bytes 3145736 | tf_op jit(solution)/shard_map/ppermute | solution.py:143
  449.9 24.7 %collective-permute-start.62 = (bf16[512,1024]{1,0:T(8,128)(2,1)S(1)}, bf16[512,1024]{1,0:T(8,128)(2,1)S(1)}, u32[]{:S(2)}, u32[]{:S(2)}) collective-permute-start(bf16[512,1024]{1,0:T(8,128)(2,1)S(1)} %get-tuple-element.478), channel_id=1, source_target_pairs={{0,16},{8,24},{16,0},{24,8},{1,17},{9,25},{17,1},{25,9},{2,18},{10... | collective-permute-start | bytes 3145736 | tf_op jit(solution)/shard_map/ppermute | solution.py:143
  452.1 24.7 %collective-permute-start.64 = (bf16[512,1024]{1,0:T(8,128)(2,1)S(1)}, bf16[512,1024]{1,0:T(8,128)(2,1)S(1)}, u32[]{:S(2)}, u32[]{:S(2)}) collective-permute-start(bf16[512,1024]{1,0:T(8,128)(2,1)S(1)} %fusion.6.refs_3_), channel_id=1, source_target_pairs={{0,2},{6,4},{2,0},{4,6},{1,3},{7,5},{3,1},{5,7},{8,10},{14,12},{10... | collective-permute-start | bytes 3145736 | tf_op jit(solution)/shard_map/ppermute | solution.py:143
  454.3 22.5 %collective-permute-start.63 = (bf16[512,1024]{1,0:T(8,128)(2,1)S(1)}, bf16[512,1024]{1,0:T(8,128)(2,1)S(1)}, u32[]{:S(2)}, u32[]{:S(2)}) collective-permute-start(bf16[512,1024]{1,0:T(8,128)(2,1)S(1)} %add_convert_fusion.12), channel_id=1, source_target_pairs={{2,4},{4,2},{3,5},{5,3},{10,12},{12,10},{11,13},{13,11},{18,20},{2... | collective-permute-start | bytes 3145736 | tf_op jit(solution)/shard_map/ppermute | solution.py:143
  474.5 24.7 %collective-permute-start.65 = (bf16[512,1024]{1,0:T(8,128)(2,1)S(1)}, bf16[512,1024]{1,0:T(8,128)(2,1)S(1)}, u32[]{:S(2)}, u32[]{:S(2)}) collective-permute-start(bf16[512,1024]{1,0:T(8,128)(2,1)S(1)} %get-tuple-element.485), channel_id=1, source_target_pairs={{0,24},{8,16},{16,8},{24,0},{1,25},{9,17},{17,9},{25,1},{2,26},{10... | collective-permute-start | bytes 3145736 | tf_op jit(solution)/shard_map/ppermute | solution.py:143
  477.8 25.2 %collective-permute-start.67 = (bf16[512,1024]{1,0:T(8,128)(2,1)S(1)}, bf16[512,1024]{1,0:T(8,128)(2,1)S(1)}, u32[]{:S(2)}, u32[]{:S(2)}) collective-permute-start(bf16[512,1024]{1,0:T(8,128)(2,1)S(1)} %fusion.7.refs_5_), channel_id=1, source_target_pairs={{0,2},{6,4},{2,0},{4,6},{1,3},{7,5},{3,1},{5,7},{8,10},{14,12},{10... | collective-permute-start | bytes 3145736 | tf_op jit(solution)/shard_map/ppermute | solution.py:143
  481.5 21.5 %collective-permute-start.66 = (bf16[512,1024]{1,0:T(8,128)(2,1)S(1)}, bf16[512,1024]{1,0:T(8,128)(2,1)}, u32[]{:S(2)}, u32[]{:S(2)}) collective-permute-start(bf16[512,1024]{1,0:T(8,128)(2,1)S(1)} %add_convert_fusion.10), channel_id=1, source_target_pairs={{2,4},{4,2},{3,5},{5,3},{10,12},{12,10},{11,13},{13,11},{18,20},{2... | collective-permute-start | bytes 3145736 | tf_op jit(solution)/shard_map/ppermute | solution.py:143
  505.4 25.0 %collective-permute-start.70 = (bf16[512,1024]{1,0:T(8,128)(2,1)S(1)}, bf16[512,1024]{1,0:T(8,128)(2,1)S(1)}, u32[]{:S(2)}, u32[]{:S(2)}) collective-permute-start(bf16[512,1024]{1,0:T(8,128)(2,1)S(1)} %fusion.8.sent_ref), channel_id=1, source_target_pairs={{0,2},{6,4},{2,0},{4,6},{1,3},{7,5},{3,1},{5,7},{8,10},{14,12},{10... | collective-permute-start | bytes 3145736 | tf_op jit(solution)/shard_map/ppermute | solution.py:143
  509.7 20.7 %collective-permute-start.69 = (bf16[512,1024]{1,0:T(8,128)(2,1)S(1)}, bf16[512,1024]{1,0:T(8,128)(2,1)S(1)}, u32[]{:S(2)}, u32[]{:S(2)}) collective-permute-start(bf16[512,1024]{1,0:T(8,128)(2,1)S(1)} %add_convert_fusion.8), channel_id=1, source_target_pairs={{2,4},{4,2},{3,5},{5,3},{10,12},{12,10},{11,13},{13,11},{18,20},{2... | collective-permute-start | bytes 3145736 | tf_op jit(solution)/shard_map/ppermute | solution.py:143
  531.4 26.9 %collective-permute-start.75 = (bf16[512,1024]{1,0:T(8,128)(2,1)S(1)}, bf16[512,1024]{1,0:T(8,128)(2,1)S(1)}, u32[]{:S(2)}, u32[]{:S(2)}) collective-permute-start(bf16[512,1024]{1,0:T(8,128)(2,1)S(1)} %fusion.9.refs_7_), channel_id=1, source_target_pairs={{0,2},{6,4},{2,0},{4,6},{1,3},{7,5},{3,1},{5,7},{8,10},{14,12},{10... | collective-permute-start | bytes 3145736 | tf_op jit(solution)/shard_map/ppermute | solution.py:143
  535.1 23.2 %collective-permute-start.74 = (bf16[512,1024]{1,0:T(8,128)(2,1)S(1)}, bf16[512,1024]{1,0:T(8,128)(2,1)S(1)}, u32[]{:S(2)}, u32[]{:S(2)}) collective-permute-start(bf16[512,1024]{1,0:T(8,128)(2,1)S(1)} %add_convert_fusion.6), channel_id=1, source_target_pairs={{2,4},{4,2},{3,5},{5,3},{10,12},{12,10},{11,13},{13,11},{18,20},{2... | collective-permute-start | bytes 3145736 | tf_op jit(solution)/shard_map/ppermute | solution.py:143
  537.3 21.0 %collective-permute-start.72 = (bf16[128,2048]{1,0:T(8,128)(2,1)S(1)}, bf16[128,2048]{1,0:T(8,128)(2,1)S(1)}, u32[]{:S(2)}, u32[]{:S(2)}) collective-permute-start(bf16[128,2048]{1,0:T(8,128)(2,1)S(1)} %get-tuple-element.502), channel_id=1, source_target_pairs={{0,16},{8,24},{16,0},{24,8},{1,17},{9,25},{17,1},{25,9},{2,18},{10... | collective-permute-start | bytes 1572872 | tf_op jit(solution)/shard_map/ppermute | solution.py:143
  538.4 19.9 %collective-permute-start.73 = (bf16[128,2048]{1,0:T(8,128)(2,1)S(1)}, bf16[128,2048]{1,0:T(8,128)(2,1)S(1)}, u32[]{:S(2)}, u32[]{:S(2)}) collective-permute-start(bf16[128,2048]{1,0:T(8,128)(2,1)S(1)} %get-tuple-element.503), channel_id=1, source_target_pairs={{0,24},{8,16},{16,8},{24,0},{1,25},{9,17},{17,9},{25,1},{2,26},{10... | collective-permute-start | bytes 1572872 | tf_op jit(solution)/shard_map/ppermute | solution.py:143
  559.4 21.7 %collective-permute-start.77 = (bf16[512,1024]{1,0:T(8,128)(2,1)S(1)}, bf16[512,1024]{1,0:T(8,128)(2,1)S(1)}, u32[]{:S(2)}, u32[]{:S(2)}) collective-permute-start(bf16[512,1024]{1,0:T(8,128)(2,1)S(1)} %fusion.10.refs_3_), channel_id=1, source_target_pairs={{0,2},{6,4},{2,0},{4,6},{1,3},{7,5},{3,1},{5,7},{8,10},{14,12},{10... | collective-permute-start | bytes 3145736 | tf_op jit(solution)/shard_map/ppermute | solution.py:143
  574.8 23.4 %collective-permute-start.80 = (bf16[512,2048]{1,0:T(8,128)(2,1)S(1)}, bf16[512,2048]{1,0:T(8,128)(2,1)S(1)}, u32[]{:S(2)}, u32[]{:S(2)}) collective-permute-start(bf16[512,2048]{1,0:T(8,128)(2,1)S(1)} %get-tuple-element.525), channel_id=1, source_target_pairs={{0,1},{1,0},{2,3},{3,2},{4,5},{5,4},{6,7},{7,6},{8,9},{9,8},{10,11... | collective-permute-start | bytes 6291464 | tf_op jit(solution)/shard_map/ppermute | solution.py:143
  582.0 22.8 %collective-permute-start.82 = (bf16[512,1024]{1,0:T(8,128)(2,1)S(1)}, bf16[512,1024]{1,0:T(8,128)(2,1)S(1)}, u32[]{:S(2)}, u32[]{:S(2)}) collective-permute-start(bf16[512,1024]{1,0:T(8,128)(2,1)S(1)} %fusion.11.refs_5_), channel_id=1, source_target_pairs={{0,2},{6,4},{2,0},{4,6},{1,3},{7,5},{3,1},{5,7},{8,10},{14,12},{10... | collective-permute-start | bytes 3145736 | tf_op jit(solution)/shard_map/ppermute | solution.py:143
  605.3 31.4 %collective-permute-start.87 = (bf16[512,1024]{1,0:T(8,128)(2,1)S(1)}, bf16[512,1024]{1,0:T(8,128)(2,1)S(1)}, u32[]{:S(2)}, u32[]{:S(2)}) collective-permute-start(bf16[512,1024]{1,0:T(8,128)(2,1)S(1)} %fusion.12.refs_7_), channel_id=1, source_target_pairs={{0,2},{6,4},{2,0},{4,6},{1,3},{7,5},{3,1},{5,7},{8,10},{14,12},{10... | collective-permute-start | bytes 3145736 | tf_op jit(solution)/shard_map/ppermute | solution.py:143
  609.3 27.5 %collective-permute-start.86 = (bf16[512,640]{1,0:T(8,128)(2,1)S(1)}, bf16[512,640]{1,0:T(8,128)(2,1)S(1)}, u32[]{:S(2)}, u32[]{:S(2)}) collective-permute-start(bf16[512,640]{1,0:T(8,128)(2,1)S(1)} %add_convert_fusion.33), channel_id=1, source_target_pairs={{2,4},{4,2},{3,5},{5,3},{10,12},{12,10},{11,13},{13,11},{18,20},{2... | collective-permute-start | bytes 1966088 | tf_op jit(solution)/shard_map/ppermute | solution.py:143
  611.4 23.8 %collective-permute-start.84 = (bf16[128,2048]{1,0:T(8,128)(2,1)S(1)}, bf16[128,2048]{1,0:T(8,128)(2,1)S(1)}, u32[]{:S(2)}, u32[]{:S(2)}) collective-permute-start(bf16[128,2048]{1,0:T(8,128)(2,1)S(1)} %get-tuple-element.534), channel_id=1, source_target_pairs={{0,16},{8,24},{16,0},{24,8},{1,17},{9,25},{17,1},{25,9},{2,18},{10... | collective-permute-start | bytes 1572872 | tf_op jit(solution)/shard_map/ppermute | solution.py:143
  612.4 22.8 %collective-permute-start.85 = (bf16[128,2048]{1,0:T(8,128)(2,1)S(1)}, bf16[128,2048]{1,0:T(8,128)(2,1)S(1)}, u32[]{:S(2)}, u32[]{:S(2)}) collective-permute-start(bf16[128,2048]{1,0:T(8,128)(2,1)S(1)} %get-tuple-element.535), channel_id=1, source_target_pairs={{0,24},{8,16},{16,8},{24,0},{1,25},{9,17},{17,9},{25,1},{2,26},{10... | collective-permute-start | bytes 1572872 | tf_op jit(solution)/shard_map/ppermute | solution.py:143
  (132 other events, 1412.5 us)

commit v7 on v6

--- a/solution.py
+++ b/solution.py
@@ -71,7 +71,8 @@
     )
 
 
-VMEM_LIMIT = 30 * 1024 * 1024
+VMEM_LIMIT = 28 * 1024 * 1024
+LARGE_LIMIT = 28 * 1024 * 1024
 MIDDLE_LIMIT = 20 * 1024 * 1024
 SMALL_LIMIT = 12 * 1024 * 1024
 SMALL = pl.CostEstimate(flops=1, bytes_accessed=1, transcendentals=0)
@@ -313,12 +314,18 @@
     grad_ref[...] = (d_middle_ref[...] + d_x).astype(jnp.bfloat16)
 
 
+def spec_of(array, block, index):
+    if block == array.shape:
+        return pl.BlockSpec(block, index, pipeline_mode=pl.Buffered(1))
+    return pl.BlockSpec(block, index)
+
+
 def gridded(kernel, steps, ins, outs, scalars=(), limit=None):
     return pl.pallas_call(
         kernel,
         grid=(steps,),
         in_specs=[pl.BlockSpec(memory_space=pltpu.SMEM)] * len(scalars)
-        + [pl.BlockSpec(block, index) for _, block, index in ins],
+        + [spec_of(array, block, index) for array, block, index in ins],
         out_specs=[pl.BlockSpec(block, index) for _, block, index in outs],
         out_shape=[shape for shape, _, _ in outs],
         compiler_params=pltpu.CompilerParams(vmem_limit_bytes=limit or MIDDLE_LIMIT),
@@ -452,57 +459,74 @@
     return jnp.concatenate([dot(mine_ref[...], weight), dot(other_ref[...], weight)], axis=0)
 
 
-def gate_up_kernel(count, here_steps, *refs):
-    x_refs, refs = refs[:2], refs[2:]
-    own, fetched, passed = refs[:2], refs[2 : 2 * count], refs[2 * count : 4 * count - 2]
-    gate_ref, up_ref, hidden_ref, wg_ref, wu_ref = refs[4 * count - 2 :]
+def chosen(here_steps, count, own, fetched, passed):
     here = pl.program_id(0) < here_steps
-    lins = []
-    for which, out_ref in ((0, wg_ref), (1, wu_ref)):
+    weights = []
+    for which in (0, 1):
         pieces = [own[which][...]]
         for k in range(count - 1):
             pieces.append(
                 jnp.where(here, fetched[2 * k + which][...], passed[2 * k + which][...])
             )
-        weight = jnp.concatenate(pieces, axis=0)
-        out_ref[...] = weight
-        lins.append(both(*x_refs, weight))
-    gate, up = lins
-    gate_ref[...] = gate
-    up_ref[...] = up
+        weights.append(jnp.concatenate(pieces, axis=0))
+    return weights
+
+
+def gate_up_kernel(count, here_steps, *refs):
+    x_refs, refs = refs[:2], refs[2:]
+    own, fetched, passed = refs[:2], refs[2 : 2 * count], refs[2 * count : 4 * count - 2]
+    gate_ref, up_ref, hidden_ref = refs[4 * count - 2 :]
+    weights = chosen(here_steps, count, own, fetched, passed)
+    lin = both(*x_refs, jnp.concatenate(weights, axis=1))
+    gate, up = lin[:, : lin.shape[1] // 2], lin[:, lin.shape[1] // 2 :]
+    gate_ref[...] = gate.astype(jnp.bfloat16)
+    up_ref[...] = up.astype(jnp.bfloat16)
     hidden_ref[...] = (gate * jax.nn.sigmoid(gate) * up).astype(jnp.bfloat16)
 
 
-def gate_up(x, own_gate, own_up, fetched, passed):
-    tokens, depth = 2 * x[0].shape[0], own_gate.shape[0]
-    width, units = x[0].shape[1], own_gate.shape[1]
-    count = len(fetched) + 1
+def columns_kernel(count, here_steps, *refs):
+    own, fetched, passed = refs[:2], refs[2 : 2 * count], refs[2 * count : 4 * count - 2]
+    wg_ref, wu_ref = refs[4 * count - 2 :]
+    wg_ref[...], wu_ref[...] = chosen(here_steps, count, own, fetched, passed)
+
+
+def column_blocks(own_gate, own_up, fetched, passed):
+    depth, units = own_gate.shape
     block = math.gcd(units // 2, 256)
     steps, half = units // block, units // block // 2
-    ins = [still(x[0]), still(x[1])]
-    ins += [(w, (depth, block), lambda i: (0, i)) for w in (own_gate, own_up)]
-    for arrays in (fetched, passed):
+    ins = [(w, (depth, block), lambda i: (0, i)) for w in (own_gate, own_up)]
+    for arrays, step in (
+        (fetched, lambda i: jnp.minimum(i, half - 1)),
+        (passed, lambda i: jnp.maximum(i - half, 0)),
+    ):
         for array in arrays:
-            ins.append((array, (depth, block), lambda i: (0, lax.rem(i, half))))
-            ins.append((array, (depth, block), lambda i: (0, half + lax.rem(i, half))))
-    outs = [
-        (full(tokens, units), (tokens, block), lambda i: (0, i)),
-        (full(tokens, units), (tokens, block), lambda i: (0, i)),
-        (low(tokens, units), (tokens, block), lambda i: (0, i)),
-        (low(width, units), (width, block), lambda i: (0, i)),
-        (low(width, units), (width, block), lambda i: (0, i)),
-    ]
-    kernel = functools.partial(gate_up_kernel, count, half)
-    return gridded(kernel, steps, ins, outs, limit=VMEM_LIMIT)
+            ins.append((array, (depth, block), lambda i, step=step: (0, step(i))))
+            ins.append((array, (depth, block), lambda i, step=step: (0, half + step(i))))
+    return ins, block, steps, half
+
+
+def gate_up(x, *weights):
+    tokens, units = 2 * x[0].shape[0], weights[0].shape[1]
+    ins, block, steps, half = column_blocks(*weights)
+    outs = [(low(tokens, units), (tokens, block), lambda i: (0, i))] * 3
+    kernel = functools.partial(gate_up_kernel, len(weights[2]) + 1, half)
+    return gridded(kernel, steps, [still(x[0]), still(x[1])] + ins, outs, limit=VMEM_LIMIT)
+
+
+def whole_columns(*weights):
+    depth, units = weights[0].shape
+    ins, block, steps, half = column_blocks(*weights)
+    count = len(weights[2]) + 1
+    outs = [(low(count * depth, units), (count * depth, block), lambda i: (0, i))] * 2
+    return gridded(functools.partial(columns_kernel, count, half), steps, ins, outs)
 
 
 def units_back_kernel(count, *refs):
     d_refs, refs = refs[:2], refs[2:]
-    pieces, (gate_ref, up_ref, d_gate_ref, d_up_ref, wd_ref) = refs[:count], refs[count:]
+    pieces, (gate_ref, up_ref, d_gate_ref, d_up_ref) = refs[:count], refs[count:]
     weight = jnp.concatenate([ref[...] for ref in pieces], axis=0)
-    wd_ref[...] = weight
     d_hidden = both(*d_refs, weight)
-    gate, up = gate_ref[...], up_ref[...]
+    gate, up = gate_ref[...].astype(jnp.float32), up_ref[...].astype(jnp.float32)
     chance = jax.nn.sigmoid(gate)
     d_up_ref[...] = (d_hidden * (gate * chance)).astype(jnp.bfloat16)
     slope = chance + gate * chance * (1.0 - chance)
@@ -511,17 +535,17 @@
 
 def units_back(d_out, pieces, gate, up):
     tokens, units = gate.shape
-    depth, width = pieces[0].shape[0], d_out[0].shape[1]
-    block = math.gcd(units, 256)
+    depth = pieces[0].shape[0]
+    block = math.gcd(units, 512)
 
     def by_columns(array, rows):
         return (array, (rows, block), lambda i: (0, i))
 
     ins = [still(d_out[0]), still(d_out[1])] + [by_columns(piece, depth) for piece in pieces]
     ins += [by_columns(gate, tokens), by_columns(up, tokens)]
-    outs = [by_columns(low(tokens, units), tokens)] * 2 + [by_columns(low(width, units), width)]
+    outs = [by_columns(low(tokens, units), tokens)] * 2
     kernel = functools.partial(units_back_kernel, len(pieces))
-    return gridded(kernel, units // block, ins, outs, limit=VMEM_LIMIT)
+    return gridded(kernel, units // block, ins, outs, limit=LARGE_LIMIT)
 
 
 def rows_sum_kernel(terms, *refs):
@@ -675,17 +699,16 @@
 
 
 def shares(q, k, visible):
-    scores = contract_last(q, k) * (1.0 / math.sqrt(HEAD_SIZE))
-    scores = jnp.where(visible, scores, -1e30)
+    scores = jnp.where(visible, contract_last(q, k), -1e30)
     weights = jnp.exp(scores - jnp.max(scores, axis=-1, keepdims=True))
-    weights = jnp.where(visible, weights, 0.0)
-    return weights, jnp.sum(weights, axis=-1, keepdims=True)
+    return weights, 1.0 / jnp.sum(weights, axis=-1, keepdims=True)
 
 
 def load_attention(q_ref, place_ref, start_ref, key_place_ref, kv_refs):
     q = q_ref[...]
     q = q.reshape(q.shape[0] * q.shape[1], q.shape[2])
     kv = jnp.concatenate([ref[...].reshape(q.shape[0], 2 * HEAD_SIZE) for ref in kv_refs], axis=0)
+    q = q * jnp.bfloat16(1.0 / math.sqrt(HEAD_SIZE))
     key_place = key_place_ref[0]
     visible = (key_place <= place_ref[0]) & (key_place >= start_ref[0])
     return q, kv[:, :HEAD_SIZE], kv[:, HEAD_SIZE:], visible
@@ -696,8 +719,8 @@
     q, k, v, visible = load_attention(q_ref, place_ref, start_ref, key_place_ref, kv_refs)
     mixed = []
     for g in range(groups):
-        weights, totals = shares(q[:, g * HEAD_SIZE : (g + 1) * HEAD_SIZE], k, visible)
-        mixed.append(dot(weights.astype(jnp.bfloat16), v) / totals)
+        weights, parts = shares(q[:, g * HEAD_SIZE : (g + 1) * HEAD_SIZE], k, visible)
+        mixed.append(dot(weights.astype(jnp.bfloat16), v) * parts)
     out = jnp.concatenate(mixed, axis=1).astype(jnp.bfloat16)
     out_ref[...] = out.reshape(out_ref.shape)
     branch = contract_last(out, wo_ref[...]).astype(jnp.bfloat16)
@@ -728,13 +751,13 @@
     for g in range(groups):
         q_head = q[:, g * HEAD_SIZE : (g + 1) * HEAD_SIZE]
         d_head = d_out[:, g * HEAD_SIZE : (g + 1) * HEAD_SIZE]
-        weights, totals = shares(q_head, k, visible)
-        probs = weights / totals
+        weights, parts = shares(q_head, k, visible)
+        probs = weights * parts
         d_probs = contract_last(d_head, v)
         row_delta = jnp.sum(probs * d_probs, axis=-1, keepdims=True)
         d_scores = (probs * (d_probs - row_delta)).astype(jnp.bfloat16)
         d_q.append(dot(d_scores, k) * scale)
-        d_k = d_k + contract_first(d_scores, q_head) * scale
+        d_k = d_k + contract_first(d_scores, q_head)
         d_v = d_v + contract_first(probs.astype(jnp.bfloat16), d_head)
     d_q = jnp.concatenate(d_q, axis=1)
     cosine = cos_ref[...].reshape(q.shape[0], -1)
@@ -1017,9 +1040,8 @@
     neighbours = [steps.take(("neighbour", k)) for k in far]
     normed_two = (kept["two"], unwaited("two"))
 
-    gate_val, up_val, hidden, wg, wu = gate_up(
-        normed_two, own_gate, own_up, [fetched[k] for k in far], neighbours
-    )
+    unit_weights = (own_gate, own_up, [fetched[k] for k in far], neighbours)
+    gate_val, up_val, hidden = gate_up(normed_two, *unit_weights)
     d_wd = weight_grad([(*all_cot, hidden)], packs, side_arg)
 
     def back(name, grad, ks):
@@ -1029,9 +1051,11 @@
         return ((name, k), grad[0] if k == 0 else None)
 
     steps.step(back("wd", d_wd, [1, 2]), summed=entry("wd", 0, d_wd))
-    steps.step(wd_moves([3]), summed=entry("wd", 1))
+    wg, wu = whole_columns(*unit_weights)
+    wg, wu = steps.step(wd_moves([3]), summed=entry("wd", 1), carry=(wg, wu))
     steps.step(back("wd", d_wd, [3]), summed=entry("wd", 2))
-    d_gate, d_up, wd = units_back(all_cot, [own_down] + arrived("down"), gate_val, up_val)
+    wd_pieces = [own_down] + arrived("down")
+    d_gate, d_up = units_back(all_cot, wd_pieces, gate_val, up_val)
     first, second = rows_sum([d_gate, d_up], [wg, wu])
     d_wg = weight_grad([(*normed_two, d_gate)], packs, side_arg)
     steps.step(to_core("d_two", second) + back("wg", d_wg, [1, 2]), summed=entry("wd", 3))
@@ -1053,7 +1077,7 @@
         return send_all("d_branch", sends)
 
     steps.step(summed=entry("wu", 0, d_wu), late=branch_back)
-    ff_first, ff_second = rows_sum([hidden], [wd])
+    ff_first, ff_second = rows_sum([hidden], [join(wd_pieces[0], wd_pieces[1:])])
     steps.step(
         back("wg", d_wg, [3]),
         summed=entry("wg", 1),

time: 709 us -> 699 us (0.986)
  waiting for transfers between devices: 335 us -> 320 us
  local copies, waits for them, and re-layouts: 36.4 us -> 47.4 us
    ppermute x104, waiting for transfers between devices: 332 us -> 318 us  [start(): lax.ppermute(value, axis, pairs)]
    unnamed x182 -> x228, local copies, waits for them, and re-layouts: 22.6 us -> 31.1 us
    pallas_call x12 -> x13, Pallas kernels: 101 us -> 97.9 us  [gridded(): pl.pallas_call(kernel, grid=(steps,), in_specs=[pl.BlockSpec(memory_space...]
    pallas_call x19 -> x20, Pallas kernels: 18.6 us -> 19.2 us  [in_vmem(): pl.pallas_call(kernel, out_shape=out_shape, in_specs=specs, out_specs=[pl...]
where the time goes in v7:
time: 699 us; the launch traced here: 692 us
  waiting for transfers between devices  320 us (46%)
  starting transfers between devices  148 us (21%)
  Pallas kernels  143 us (20%)
  local copies, waits for them, and re-layouts  47.4 us (7%)
  other arithmetic  30.7 us (4%)
    ppermute x104, waiting for transfers between devices, start(): lax.ppermute(value, axis, pairs)  318 us
    ppermute x104, starting transfers between devices, start(): lax.ppermute(value, axis, pairs)  148 us
    pallas_call x13, Pallas kernels, gridded(): pl.pallas_call(kernel, grid=(steps,), in_specs=[pl.BlockSpec(memory_space...  97.9 us
    unnamed x228, local copies, waits for them, and re-layouts  31.1 us
    pallas_call x4, Pallas kernels, weight_grad(): pl.pallas_call(functools.partial(weight_grad_kernel, count, len(terms), s...  26 us
    pallas_call x20, Pallas kernels, in_vmem(): pl.pallas_call(kernel, out_shape=out_shape, in_specs=specs, out_specs=[pl...  19.2 us
  transfers between devices with their start and end apart: 105, of which 49 were waited for; matrix products, arithmetic and copies ran while one was open for 4% of the time, Pallas kernels for 20%

profile of v7, /device:TPU:0, one launch (start us, length us, event | category | flops | bytes accessed | tf_op | source)
XLA Modules:
  0.0 692.2 jit_solution(4314265440140298851)
XLA Ops:
  6.6 2.9 collective-permute-start
  13.9 3.1 constant_dynamic-slice_fusion.11
  17.7 4.3 constant_dynamic-slice_fusion.5
  36.5 8.9 %collective-permute-done.3.refs_1_ = bf16[128,2048]{1,0:T(8,128)(2,1)} collective-permute-done((bf16[128,2048]{1,0:T(8,128)(2,1)}, bf16[128,2048]{1,0:T(8,128)(2,1)}, u32[]{:S(2)}, u32[]{:S(2)}) %collective-permute-start.3) | collective-permute-done | bytes 524320 | tf_op jit(solution)/shard_map/ppermute | solution.py:144
  45.3 9.8 %collective-permute-done.4.refs_2_ = bf16[128,2048]{1,0:T(8,128)(2,1)} collective-permute-done((bf16[128,2048]{1,0:T(8,128)(2,1)}, bf16[128,2048]{1,0:T(8,128)(2,1)}, u32[]{:S(2)}, u32[]{:S(2)}) %collective-permute-start.4) | collective-permute-done | bytes 524320 | tf_op jit(solution)/shard_map/ppermute | solution.py:144
  61.3 5.1 shard_map.216
  71.1 11.7 %collective-permute-done.7.refs_4_.refs_5_.refs_2_.refs_3_ = bf16[512,1024]{1,0:T(8,128)(2,1)S(1)} collective-permute-done((bf16[512,1024]{1,0:T(8,128)(2,1)S(1)}, bf16[512,1024]{1,0:T(8,128)(2,1)S(1)}, u32[]{:S(2)}, u32[]{:S(2)}) %collective-permute-start.7) | collective-permute-done | bytes 1048608 | tf_op jit(solution)/shard_map/ppermute | solution.py:144
  85.3 2.6 collective-permute-start.11
  92.6 4.5 collective-permute-done.10.refs_1_
  97.1 9.6 %collective-permute-done.11.refs_2_ = bf16[2,512,128]{2,1,0:T(8,128)(2,1)S(1)} collective-permute-done((bf16[2,512,128]{2,1,0:T(8,128)(2,1)S(1)}, bf16[2,512,128]{2,1,0:T(8,128)(2,1)S(1)}, u32[]{:S(2)}, u32[]{:S(2)}) %collective-permute-start.11) | collective-permute-done | bytes 262176 | tf_op jit(solution)/shard_map/ppermute | solution.py:144
  108.4 3.2 collective-permute-start.17
  124.4 12.4 %shard_map.218 = (bf16[2,512,256]{2,1,0:T(8,128)(2,1)S(1)}, bf16[512,2048]{1,0:T(8,128)(2,1)S(1)}, bf16[512,2048]{1,0:T(8,128)(2,1)S(1)}) custom-call(bf16[2,512,256]{2,1,0:T(8,128)(2,1)S(1)} %copy-done.46, s32[4,256,1]{2,1,0:T(8,128)S(1)} %copy-done.17, s32[4,256,1]{2,1,0:T(8,128)S(1)} %copy-done.19, s32[4,1,1024]{2,1,0:T(1,128)S(1)} %broadcast_add_fusion.key_place_ref, ...), custom_call_target="tpu_custom_call" | custom-call | flops 1 | bytes 1 | tf_op jit(solution)/shard_map/pallas_call | solution.py:324
  137.0 4.1 collective-permute-done.18.came_ref
  146.9 9.7 %collective-permute-done.20.refs_1_ = bf16[128,2048]{1,0:T(8,128)(2,1)S(1)} collective-permute-done((bf16[128,2048]{1,0:T(8,128)(2,1)S(1)}, bf16[128,2048]{1,0:T(8,128)(2,1)S(1)}, u32[]{:S(2)}, u32[]{:S(2)}) %collective-permute-start.20) | collective-permute-done | bytes 524320 | tf_op jit(solution)/shard_map/ppermute | solution.py:144
  157.1 10.4 %collective-permute-done.22.refs_3_ = bf16[128,2048]{1,0:T(8,128)(2,1)S(1)} collective-permute-done((bf16[128,2048]{1,0:T(8,128)(2,1)S(1)}, bf16[128,2048]{1,0:T(8,128)(2,1)S(1)}, u32[]{:S(2)}, u32[]{:S(2)}) %collective-permute-start.22) | collective-permute-done | bytes 524320 | tf_op jit(solution)/shard_map/ppermute | solution.py:144
  177.1 8.7 %collective-permute-done.25.refs_1_ = bf16[128,2048]{1,0:T(8,128)(2,1)S(1)} collective-permute-done((bf16[128,2048]{1,0:T(8,128)(2,1)S(1)}, bf16[128,2048]{1,0:T(8,128)(2,1)S(1)}, u32[]{:S(2)}, u32[]{:S(2)}) %collective-permute-start.25) | collective-permute-done | bytes 524320 | tf_op jit(solution)/shard_map/ppermute | solution.py:144
  185.9 11.4 %collective-permute-done.26.refs_2_ = bf16[128,2048]{1,0:T(8,128)(2,1)S(1)} collective-permute-done((bf16[128,2048]{1,0:T(8,128)(2,1)S(1)}, bf16[128,2048]{1,0:T(8,128)(2,1)S(1)}, u32[]{:S(2)}, u32[]{:S(2)}) %collective-permute-start.26) | collective-permute-done | bytes 524320 | tf_op jit(solution)/shard_map/ppermute | solution.py:144
  201.7 12.5 %shard_map.223 = (bf16[1024,1024]{1,0:T(8,128)(2,1)S(1)}, bf16[1024,1024]{1,0:T(8,128)(2,1)S(1)}, bf16[1024,1024]{1,0:T(8,128)(2,1)S(1)}) custom-call(bf16[512,2048]{1,0:T(8,128)(2,1)S(1)} %shard_map.222.refs_0_.refs_1_, bf16[512,2048]{1,0:T(8,128)(2,1)S(1)} %collective-permute-done.30.refs_1_.refs_2_, ...), custom_call_target="tpu_custom_call" | custom-call | flops 1 | bytes 1 | tf_op jit(solution)/shard_map/pallas_call | solution.py:324
  214.3 6.3 shard_map.224
  229.4 4.2 shard_map.225
  237.6 10.5 %collective-permute-done.32 = bf16[512,1024]{1,0:T(8,128)(2,1)} collective-permute-done((bf16[512,1024]{1,0:T(8,128)(2,1)S(1)}, bf16[512,1024]{1,0:T(8,128)(2,1)}, u32[]{:S(2)}, u32[]{:S(2)}) %collective-permute-start.32) | collective-permute-done | bytes 1048608 | tf_op jit(solution)/shard_map/ppermute | solution.py:144
  252.7 8.1 %collective-permute-start.35 = (bf16[512,1024]{1,0:T(8,128)(2,1)}, bf16[512,1024]{1,0:T(8,128)(2,1)}, u32[]{:S(2)}, u32[]{:S(2)}) collective-permute-start(bf16[512,1024]{1,0:T(8,128)(2,1)} %collective-permute-done.32), channel_id=1, source_target_pairs={{0,2},{6,4},{1,3},{7,5},{8,10},{14,12},{9,11},{15,13},{16,18},{22,... | collective-permute-start | bytes 3145736 | tf_op jit(solution)/shard_map/ppermute | solution.py:144
  261.9 18.3 %collective-permute-done.35 = bf16[512,1024]{1,0:T(8,128)(2,1)} collective-permute-done((bf16[512,1024]{1,0:T(8,128)(2,1)}, bf16[512,1024]{1,0:T(8,128)(2,1)}, u32[]{:S(2)}, u32[]{:S(2)}) %collective-permute-start.35) | collective-permute-done | bytes 1048608 | tf_op jit(solution)/shard_map/ppermute | solution.py:144
  296.0 6.6 shard_map.226
  302.6 9.8 %shard_map.227 = (bf16[512,2048]{1,0:T(8,128)(2,1)S(1)}, bf16[512,2048]{1,0:T(8,128)(2,1)S(1)}) custom-call(bf16[1024,1024]{1,0:T(8,128)(2,1)S(1)} %get-tuple-element.419.refs_0_.refs_3_, bf16[1024,1024]{1,0:T(8,128)(2,1)S(1)} %get-tuple-element.420.refs_1_.refs_3_, bf16[2048,1024]{1,0:T(8,128)(2,1)S(1)} %copy-done.25, bf16[2048,1024]{1,0:T(8,128)(2,1)S(1)} %copy-done.27), custom_call_target="tpu_custom_call" | custom-call | flops 1 | bytes 1 | tf_op jit(solution)/shard_map/pallas_call | solution.py:324
  312.4 5.9 shard_map.228
  323.0 17.6 %collective-permute-done.41.refs_2_ = bf16[512,1024]{1,0:T(8,128)(2,1)S(1)} collective-permute-done((bf16[512,1024]{1,0:T(8,128)(2,1)S(1)}, bf16[512,1024]{1,0:T(8,128)(2,1)S(1)}, u32[]{:S(2)}, u32[]{:S(2)}) %collective-permute-start.41) | collective-permute-done | bytes 1048608 | tf_op jit(solution)/shard_map/ppermute | solution.py:144
  341.7 3.7 collective-permute-start.46
  346.1 5.9 shard_map.229
  352.1 11.9 %collective-permute-done.46.refs_4_ = bf16[512,1024]{1,0:T(8,128)(2,1)S(1)} collective-permute-done((bf16[512,1024]{1,0:T(8,128)(2,1)S(1)}, bf16[512,1024]{1,0:T(8,128)(2,1)S(1)}, u32[]{:S(2)}, u32[]{:S(2)}) %collective-permute-start.46) | collective-permute-done | bytes 1048608 | tf_op jit(solution)/shard_map/ppermute | solution.py:144
  365.0 3.7 collective-permute-start.51
  373.5 9.3 %collective-permute-done.47.refs_1_ = bf16[128,2048]{1,0:T(8,128)(2,1)S(1)} collective-permute-done((bf16[128,2048]{1,0:T(8,128)(2,1)S(1)}, bf16[128,2048]{1,0:T(8,128)(2,1)S(1)}, u32[]{:S(2)}, u32[]{:S(2)}) %collective-permute-start.47) | collective-permute-done | bytes 524320 | tf_op jit(solution)/shard_map/ppermute | solution.py:144
  382.8 6.5 collective-permute-done.48.refs_2_
  397.9 7.5 %collective-permute-done.52.refs_1_ = bf16[128,2048]{1,0:T(8,128)(2,1)S(1)} collective-permute-done((bf16[128,2048]{1,0:T(8,128)(2,1)S(1)}, bf16[128,2048]{1,0:T(8,128)(2,1)S(1)}, u32[]{:S(2)}, u32[]{:S(2)}) %collective-permute-start.52) | collective-permute-done | bytes 524320 | tf_op jit(solution)/shard_map/ppermute | solution.py:144
  405.4 6.4 collective-permute-done.53.refs_2_
  418.3 21.6 %shard_map.233 = (bf16[2,512,256]{2,1,0:T(8,128)(2,1)S(1)}, bf16[512,1024]{1,0:T(8,128)(2,1)S(1)}) custom-call(s32[1]{0:T(128)} %bitcast.5.here_ref, bf16[2,512,256]{2,1,0:T(8,128)(2,1)S(1)} %copy-done.47, bf16[512,2048]{1,0:T(8,128)(2,1)S(1)} %shard_map.232.mine_ref.refs_3_, bf16[512,2048]{1,0:T(8,128)(2,1)S(1)} %collective-permute-done.58.other_ref.refs_4_, ...), custom_call_target="tpu_custom_call" | custom-call | flops 1 | bytes 1 | tf_op jit(solution)/shard_map/pallas_call | solution.py:324
  443.0 2.6 collective-permute-start.64
  446.4 18.6 %collective-permute-done.61 = bf16[512,1024]{1,0:T(8,128)(2,1)S(1)} collective-permute-done((bf16[512,1024]{1,0:T(8,128)(2,1)S(1)}, bf16[512,1024]{1,0:T(8,128)(2,1)S(1)}, u32[]{:S(2)}, u32[]{:S(2)}) %collective-permute-start.61) | collective-permute-done | bytes 1048608 | tf_op jit(solution)/shard_map/ppermute | solution.py:144
  469.4 3.7 collective-permute-start.67
  475.1 5.5 shard_map.235
  480.6 10.4 %collective-permute-done.65 = bf16[512,1024]{1,0:T(8,128)(2,1)S(1)} collective-permute-done((bf16[512,1024]{1,0:T(8,128)(2,1)S(1)}, bf16[512,1024]{1,0:T(8,128)(2,1)S(1)}, u32[]{:S(2)}, u32[]{:S(2)}) %collective-permute-start.65) | collective-permute-done | bytes 1048608 | tf_op jit(solution)/shard_map/ppermute | solution.py:144
  490.9 3.9 collective-permute-done.67.refs_4_
  497.1 3.9 collective-permute-start.70
  502.1 4.2 shard_map.236
  506.3 15.6 %collective-permute-done.70.came_ref = bf16[512,1024]{1,0:T(8,128)(2,1)S(1)} collective-permute-done((bf16[512,1024]{1,0:T(8,128)(2,1)S(1)}, bf16[512,1024]{1,0:T(8,128)(2,1)S(1)}, u32[]{:S(2)}, u32[]{:S(2)}) %collective-permute-start.70) | collective-permute-done | bytes 1048608 | tf_op jit(solution)/shard_map/ppermute | solution.py:144
  522.9 3.7 collective-permute-start.75
  531.4 11.4 %collective-permute-done.71.refs_1_ = bf16[128,2048]{1,0:T(8,128)(2,1)S(1)} collective-permute-done((bf16[128,2048]{1,0:T(8,128)(2,1)S(1)}, bf16[128,2048]{1,0:T(8,128)(2,1)S(1)}, u32[]{:S(2)}, u32[]{:S(2)}) %collective-permute-start.71) | collective-permute-done | bytes 524320 | tf_op jit(solution)/shard_map/ppermute | solution.py:144
  542.8 7.1 %collective-permute-done.72.refs_2_ = bf16[128,2048]{1,0:T(8,128)(2,1)S(1)} collective-permute-done((bf16[128,2048]{1,0:T(8,128)(2,1)S(1)}, bf16[128,2048]{1,0:T(8,128)(2,1)S(1)}, u32[]{:S(2)}, u32[]{:S(2)}) %collective-permute-start.72) | collective-permute-done | bytes 524320 | tf_op jit(solution)/shard_map/ppermute | solution.py:144
  554.3 3.3 shard_map.240
  557.6 7.8 %shard_map.239 = (bf16[512,640]{1,0:T(8,128)(2,1)S(1)}, bf16[512,640]{1,0:T(8,128)(2,1)S(1)}, bf16[512,640]{1,0:T(8,128)(2,1)S(1)}, bf16[512,640]{1,0:T(8,128)(2,1)S(1)}) custom-call(bf16[512,2048]{1,0:T(8,128)(2,1)S(1)} %copy-done.42, bf16[512,2048]{1,0:T(8,128)(2,1)S(1)} %copy-done.44, bf16[1024,384]{1,0:T(8,128)(2,1)S(1)} %shard_map.238.refs_2_.refs_0_, ...), custom_call_target="tpu_custom_call" | custom-call | flops 1 | bytes 1 | tf_op jit(solution)/shard_map/pallas_call | solution.py:611
  565.5 6.3 collective-permute-done.77.refs_2_
  572.6 4.0 collective-permute-start.82
  579.5 8.5 %collective-permute-done.78 = bf16[512,640]{1,0:T(8,128)(2,1)S(1)} collective-permute-done((bf16[512,640]{1,0:T(8,128)(2,1)S(1)}, bf16[512,640]{1,0:T(8,128)(2,1)S(1)}, u32[]{:S(2)}, u32[]{:S(2)}) %collective-permute-start.78) | collective-permute-done | bytes 655392 | tf_op jit(solution)/shard_map/ppermute | solution.py:144
  589.0 6.5 collective-permute-done.82.refs_4_
  596.0 3.8 collective-permute-start.87
  604.7 8.0 %collective-permute-done.83.refs_1_ = bf16[128,2048]{1,0:T(8,128)(2,1)S(1)} collective-permute-done((bf16[128,2048]{1,0:T(8,128)(2,1)S(1)}, bf16[128,2048]{1,0:T(8,128)(2,1)S(1)}, u32[]{:S(2)}, u32[]{:S(2)}) %collective-permute-start.83) | collective-permute-done | bytes 524320 | tf_op jit(solution)/shard_map/ppermute | solution.py:144
  612.7 13.1 %collective-permute-done.84.refs_2_ = bf16[128,2048]{1,0:T(8,128)(2,1)S(1)} collective-permute-done((bf16[128,2048]{1,0:T(8,128)(2,1)S(1)}, bf16[128,2048]{1,0:T(8,128)(2,1)S(1)}, u32[]{:S(2)}, u32[]{:S(2)}) %collective-permute-start.84) | collective-permute-done | bytes 524320 | tf_op jit(solution)/shard_map/ppermute | solution.py:144
  632.7 4.2 shard_map.243
  639.3 4.0 collective-permute-start.97
  648.2 4.2 shard_map.246
  659.5 10.3 %collective-permute-done.100.refs_4_ = bf16[512,640]{1,0:T(8,128)(2,1)S(1)} collective-permute-done((bf16[512,640]{1,0:T(8,128)(2,1)S(1)}, bf16[512,640]{1,0:T(8,128)(2,1)S(1)}, u32[]{:S(2)}, u32[]{:S(2)}) %collective-permute-start.100) | collective-permute-done | bytes 655392 | tf_op jit(solution)/shard_map/ppermute | solution.py:144
  672.9 2.7 collective-permute-start.103
  682.1 3.5 collective-permute-done.101
  687.3 4.4 shard_map.248
  (503 shorter events, 205.2 us)
Async XLA Ops:
  6.6 18.8 %collective-permute-start = (bf16[272,640]{1,0:T(8,128)(2,1)}, bf16[272,640]{1,0:T(8,128)(2,1)S(1)}, u32[]{:S(2)}, u32[]{:S(2)}) collective-permute-start(bf16[272,640]{1,0:T(8,128)(2,1)} %get-tuple-element.304), channel_id=1, source_target_pairs={{0,8},{8,0},{16,24},{24,16},{1,9},{9,1},{17,25},{25,17},{2,10},{10... | collective-permute-start | bytes 1044488 | tf_op jit(solution)/shard_map/ppermute | solution.py:144
  28.3 26.8 %collective-permute-start.6 = (bf16[768,640]{1,0:T(8,128)(2,1)}, bf16[768,640]{1,0:T(8,128)(2,1)S(1)}, u32[]{:S(2)}, u32[]{:S(2)}) collective-permute-start(bf16[768,640]{1,0:T(8,128)(2,1)} %shard_map.213), channel_id=1, source_target_pairs={{0,2},{2,0},{4,6},{6,4},{1,3},{3,1},{5,7},{7,5},{8,10},{10,8},{12,... | collective-permute-start | bytes 2949128 | tf_op jit(solution)/shard_map/ppermute | solution.py:144
  31.3 23.8 %collective-permute-start.4 = (bf16[128,2048]{1,0:T(8,128)(2,1)}, bf16[128,2048]{1,0:T(8,128)(2,1)}, u32[]{:S(2)}, u32[]{:S(2)}) collective-permute-start(bf16[128,2048]{1,0:T(8,128)(2,1)} %get-tuple-element.312), channel_id=1, source_target_pairs={{0,16},{8,24},{16,0},{24,8},{1,17},{9,25},{17,1},{25,9},{2,18},{10... | collective-permute-start | bytes 1572872 | tf_op jit(solution)/shard_map/ppermute | solution.py:144
  32.3 22.8 %collective-permute-start.5 = (bf16[128,2048]{1,0:T(8,128)(2,1)}, bf16[128,2048]{1,0:T(8,128)(2,1)}, u32[]{:S(2)}, u32[]{:S(2)}) collective-permute-start(bf16[128,2048]{1,0:T(8,128)(2,1)} %get-tuple-element.313), channel_id=1, source_target_pairs={{0,24},{8,16},{16,8},{24,0},{1,25},{9,17},{17,9},{25,1},{2,26},{10... | collective-permute-start | bytes 1572872 | tf_op jit(solution)/shard_map/ppermute | solution.py:144
  57.2 25.6 %collective-permute-start.7 = (bf16[512,1024]{1,0:T(8,128)(2,1)S(1)}, bf16[512,1024]{1,0:T(8,128)(2,1)S(1)}, u32[]{:S(2)}, u32[]{:S(2)}) collective-permute-start(bf16[512,1024]{1,0:T(8,128)(2,1)S(1)} %copy-done.109), channel_id=1, source_target_pairs={{0,8},{8,0},{16,24},{24,16},{1,9},{9,1},{17,25},{25,17},{2,10},{10... | collective-permute-start | bytes 3145736 | tf_op jit(solution)/shard_map/ppermute | solution.py:144
  57.9 25.2 %collective-permute-start.8 = (bf16[512,1024]{1,0:T(8,128)(2,1)S(1)}, bf16[512,1024]{1,0:T(8,128)(2,1)S(1)}, u32[]{:S(2)}, u32[]{:S(2)}) collective-permute-start(bf16[512,1024]{1,0:T(8,128)(2,1)S(1)} %copy-done.108), channel_id=1, source_target_pairs={{0,16},{8,24},{16,0},{24,8},{1,17},{9,25},{17,1},{25,9},{2,18},{10... | collective-permute-start | bytes 3145736 | tf_op jit(solution)/shard_map/ppermute | solution.py:144
  83.1 25.3 %collective-permute-start.13 = (bf16[512,1024]{1,0:T(8,128)(2,1)S(1)}, bf16[512,1024]{1,0:T(8,128)(2,1)S(1)}, u32[]{:S(2)}, u32[]{:S(2)}) collective-permute-start(bf16[512,1024]{1,0:T(8,128)(2,1)S(1)} %pad_maximum_fusion.2), channel_id=1, source_target_pairs={{0,24},{8,16},{16,8},{24,0},{1,25},{9,17},{17,9},{25,1},{2,26},{10... | collective-permute-start | bytes 3145736 | tf_op jit(solution)/shard_map/ppermute | solution.py:144
  85.3 21.4 %collective-permute-start.11 = (bf16[2,512,128]{2,1,0:T(8,128)(2,1)S(1)}, bf16[2,512,128]{2,1,0:T(8,128)(2,1)S(1)}, u32[]{:S(2)}, u32[]{:S(2)}) collective-permute-start(bf16[2,512,128]{2,1,0:T(8,128)(2,1)S(1)} %get-tuple-element.334.refs_0_), channel_id=1, source_target_pairs={{0,4},{2,6},{4,0},{6,2},{1,5},{3,7},{5,1},{7,3},{8,12},{10,14},{12... | collective-permute-start | bytes 786440 | tf_op jit(solution)/shard_map/ppermute | solution.py:144
  87.9 19.5 %collective-permute-start.12 = (bf16[2,512,128]{2,1,0:T(8,128)(2,1)S(1)}, bf16[2,512,128]{2,1,0:T(8,128)(2,1)S(1)}, u32[]{:S(2)}, u32[]{:S(2)}) collective-permute-start(bf16[2,512,128]{2,1,0:T(8,128)(2,1)S(1)} %get-tuple-element.334.refs_0_), channel_id=1, source_target_pairs={{0,6},{2,4},{4,2},{6,0},{1,7},{3,5},{5,3},{7,1},{8,14},{10,12},{12... | collective-permute-start | bytes 786440 | tf_op jit(solution)/shard_map/ppermute | solution.py:144
  108.4 28.5 %collective-permute-start.17 = (bf16[512,1024]{1,0:T(8,128)(2,1)S(1)}, bf16[512,1024]{1,0:T(8,128)(2,1)}, u32[]{:S(2)}, u32[]{:S(2)}) collective-permute-start(bf16[512,1024]{1,0:T(8,128)(2,1)S(1)} %collective-permute-done.7.refs_4_.refs_5_.refs_2_.refs_3_), channel_id=1, source_target_pairs={{0,2},{2,0},{4,6},{6,4},{1,3},{3,1},{5,7},{7,5},{8,10},{10,8},{12,... | collective-permute-start | bytes 3145736 | tf_op jit(solution)/shard_map/ppermute | solution.py:144
  111.7 25.2 %collective-permute-start.14 = (bf16[128,2048]{1,0:T(8,128)(2,1)}, bf16[128,2048]{1,0:T(8,128)(2,1)}, u32[]{:S(2)}, u32[]{:S(2)}) collective-permute-start(bf16[128,2048]{1,0:T(8,128)(2,1)} %get-tuple-element.341), channel_id=1, source_target_pairs={{0,8},{8,0},{16,24},{24,16},{1,9},{9,1},{17,25},{25,17},{2,10},{10... | collective-permute-start | bytes 1572872 | tf_op jit(solution)/shard_map/ppermute | solution.py:144
  112.4 24.5 %collective-permute-start.15 = (bf16[128,2048]{1,0:T(8,128)(2,1)}, bf16[128,2048]{1,0:T(8,128)(2,1)}, u32[]{:S(2)}, u32[]{:S(2)}) collective-permute-start(bf16[128,2048]{1,0:T(8,128)(2,1)} %get-tuple-element.342), channel_id=1, source_target_pairs={{0,16},{8,24},{16,0},{24,8},{1,17},{9,25},{17,1},{25,9},{2,18},{10... | collective-permute-start | bytes 1572872 | tf_op jit(solution)/shard_map/ppermute | solution.py:144
  113.4 23.5 %collective-permute-start.16 = (bf16[128,2048]{1,0:T(8,128)(2,1)}, bf16[128,2048]{1,0:T(8,128)(2,1)}, u32[]{:S(2)}, u32[]{:S(2)}) collective-permute-start(bf16[128,2048]{1,0:T(8,128)(2,1)} %get-tuple-element.343), channel_id=1, source_target_pairs={{0,24},{8,16},{16,8},{24,0},{1,25},{9,17},{17,9},{25,1},{2,26},{10... | collective-permute-start | bytes 1572872 | tf_op jit(solution)/shard_map/ppermute | solution.py:144
  141.2 26.3 %collective-permute-start.19 = (bf16[512,1024]{1,0:T(8,128)(2,1)S(1)}, bf16[512,1024]{1,0:T(8,128)(2,1)S(1)}, u32[]{:S(2)}, u32[]{:S(2)}) collective-permute-start(bf16[512,1024]{1,0:T(8,128)(2,1)S(1)} %collective-permute-done.8.refs_6_.refs_7_.refs_4_.refs_5_), channel_id=1, source_target_pairs={{0,2},{2,0},{4,6},{6,4},{1,3},{3,1},{5,7},{7,5},{8,10},{10,8},{12,... | collective-permute-start | bytes 3145736 | tf_op jit(solution)/shard_map/ppermute | solution.py:144
  143.5 23.9 %collective-permute-start.22 = (bf16[128,2048]{1,0:T(8,128)(2,1)S(1)}, bf16[128,2048]{1,0:T(8,128)(2,1)S(1)}, u32[]{:S(2)}, u32[]{:S(2)}) collective-permute-start(bf16[128,2048]{1,0:T(8,128)(2,1)S(1)} %get-tuple-element.363), channel_id=1, source_target_pairs={{0,24},{8,16},{16,8},{24,0},{1,25},{9,17},{17,9},{25,1},{2,26},{10... | collective-permute-start | bytes 1572872 | tf_op jit(solution)/shard_map/ppermute | solution.py:144
  167.4 29.9 %collective-permute-start.24 = (bf16[512,2048]{1,0:T(8,128)(2,1)S(1)}, bf16[512,2048]{1,0:T(8,128)(2,1)S(1)}, u32[]{:S(2)}, u32[]{:S(2)}) collective-permute-start(bf16[512,2048]{1,0:T(8,128)(2,1)S(1)} %shard_map.220.refs_1_.refs_0_), channel_id=1, source_target_pairs={{0,1},{1,0},{2,3},{3,2},{4,5},{5,4},{6,7},{7,6},{8,9},{9,8},{10,11... | collective-permute-start | bytes 6291464 | tf_op jit(solution)/shard_map/ppermute | solution.py:144
  167.4 29.9 %collective-permute-start.23 = (bf16[512,1024]{1,0:T(8,128)(2,1)S(1)}, bf16[512,1024]{1,0:T(8,128)(2,1)S(1)}, u32[]{:S(2)}, u32[]{:S(2)}) collective-permute-start(bf16[512,1024]{1,0:T(8,128)(2,1)S(1)} %collective-permute-done.13.refs_8_.refs_9_.refs_6_.refs_7_), channel_id=1, source_target_pairs={{0,2},{2,0},{4,6},{6,4},{1,3},{3,1},{5,7},{7,5},{8,10},{10,8},{12,... | collective-permute-start | bytes 3145736 | tf_op jit(solution)/shard_map/ppermute | solution.py:144
  172.4 24.9 %collective-permute-start.26 = (bf16[128,2048]{1,0:T(8,128)(2,1)S(1)}, bf16[128,2048]{1,0:T(8,128)(2,1)S(1)}, u32[]{:S(2)}, u32[]{:S(2)}) collective-permute-start(bf16[128,2048]{1,0:T(8,128)(2,1)S(1)} %get-tuple-element.377), channel_id=1, source_target_pairs={{0,16},{8,24},{16,0},{24,8},{1,17},{9,25},{17,1},{25,9},{2,18},{10... | collective-permute-start | bytes 1572872 | tf_op jit(solution)/shard_map/ppermute | solution.py:144
  173.4 23.9 %collective-permute-start.27 = (bf16[128,2048]{1,0:T(8,128)(2,1)S(1)}, bf16[128,2048]{1,0:T(8,128)(2,1)S(1)}, u32[]{:S(2)}, u32[]{:S(2)}) collective-permute-start(bf16[128,2048]{1,0:T(8,128)(2,1)S(1)} %get-tuple-element.378), channel_id=1, source_target_pairs={{0,24},{8,16},{16,8},{24,0},{1,25},{9,17},{17,9},{25,1},{2,26},{10... | collective-permute-start | bytes 1572872 | tf_op jit(solution)/shard_map/ppermute | solution.py:144
  197.6 25.6 %collective-permute-start.28 = (bf16[512,1024]{1,0:T(8,128)(2,1)S(1)}, bf16[512,1024]{1,0:T(8,128)(2,1)S(1)}, u32[]{:S(2)}, u32[]{:S(2)}) collective-permute-start(bf16[512,1024]{1,0:T(8,128)(2,1)S(1)} %pad_maximum_fusion.3), channel_id=1, source_target_pairs={{0,8},{8,0},{16,24},{24,16},{1,9},{9,1},{17,25},{25,17},{2,10},{10... | collective-permute-start | bytes 3145736 | tf_op jit(solution)/shard_map/ppermute | solution.py:144
  198.4 25.2 %collective-permute-start.29 = (bf16[512,1024]{1,0:T(8,128)(2,1)S(1)}, bf16[512,1024]{1,0:T(8,128)(2,1)S(1)}, u32[]{:S(2)}, u32[]{:S(2)}) collective-permute-start(bf16[512,1024]{1,0:T(8,128)(2,1)S(1)} %pad_maximum_fusion.4), channel_id=1, source_target_pairs={{0,16},{8,24},{16,0},{24,8},{1,17},{9,25},{17,1},{25,9},{2,18},{10... | collective-permute-start | bytes 3145736 | tf_op jit(solution)/shard_map/ppermute | solution.py:144
  223.7 24.5 %collective-permute-start.32 = (bf16[512,1024]{1,0:T(8,128)(2,1)S(1)}, bf16[512,1024]{1,0:T(8,128)(2,1)}, u32[]{:S(2)}, u32[]{:S(2)}) collective-permute-start(bf16[512,1024]{1,0:T(8,128)(2,1)S(1)} %get-tuple-element.398), channel_id=1, source_target_pairs={{0,8},{8,0},{16,24},{24,16},{1,9},{9,1},{17,25},{25,17},{2,10},{10... | collective-permute-start | bytes 3145736 | tf_op jit(solution)/shard_map/ppermute | solution.py:144
  224.9 24.1 %collective-permute-start.33 = (bf16[512,1024]{1,0:T(8,128)(2,1)S(1)}, bf16[512,1024]{1,0:T(8,128)(2,1)S(1)}, u32[]{:S(2)}, u32[]{:S(2)}) collective-permute-start(bf16[512,1024]{1,0:T(8,128)(2,1)S(1)} %get-tuple-element.399), channel_id=1, source_target_pairs={{0,16},{8,24},{16,0},{24,8},{1,17},{9,25},{17,1},{25,9},{2,18},{10... | collective-permute-start | bytes 3145736 | tf_op jit(solution)/shard_map/ppermute | solution.py:144
  226.0 23.5 %collective-permute-start.31 = (bf16[512,1024]{1,0:T(8,128)(2,1)S(1)}, bf16[512,1024]{1,0:T(8,128)(2,1)S(1)}, u32[]{:S(2)}, u32[]{:S(2)}) collective-permute-start(bf16[512,1024]{1,0:T(8,128)(2,1)S(1)} %get-tuple-element.397), channel_id=1, source_target_pairs={{0,2},{6,4},{1,3},{7,5},{8,10},{14,12},{9,11},{15,13},{16,18},{22,... | collective-permute-start | bytes 3145736 | tf_op jit(solution)/shard_map/ppermute | solution.py:144
  252.7 27.5 %collective-permute-start.35 = (bf16[512,1024]{1,0:T(8,128)(2,1)}, bf16[512,1024]{1,0:T(8,128)(2,1)}, u32[]{:S(2)}, u32[]{:S(2)}) collective-permute-start(bf16[512,1024]{1,0:T(8,128)(2,1)} %collective-permute-done.32), channel_id=1, source_target_pairs={{0,2},{6,4},{1,3},{7,5},{8,10},{14,12},{9,11},{15,13},{16,18},{22,... | collective-permute-start | bytes 3145736 | tf_op jit(solution)/shard_map/ppermute | solution.py:144
  260.7 23.5 %collective-permute-start.36 = (bf16[512,1024]{1,0:T(8,128)(2,1)}, bf16[512,1024]{1,0:T(8,128)(2,1)S(1)}, u32[]{:S(2)}, u32[]{:S(2)}) collective-permute-start(bf16[512,1024]{1,0:T(8,128)(2,1)} %pad_maximum_fusion.8), channel_id=1, source_target_pairs={{0,24},{8,16},{16,8},{24,0},{1,25},{9,17},{17,9},{25,1},{2,26},{10... | collective-permute-start | bytes 3145736 | tf_op jit(solution)/shard_map/ppermute | solution.py:144
  285.2 33.2 %collective-permute-start.39 = (bf16[512,1024]{1,0:T(8,128)(2,1)}, bf16[512,1024]{1,0:T(8,128)(2,1)S(1)}, u32[]{:S(2)}, u32[]{:S(2)}) collective-permute-start(bf16[512,1024]{1,0:T(8,128)(2,1)} %copy-done.84), channel_id=1, source_target_pairs={{0,24},{8,16},{16,8},{24,0},{1,25},{9,17},{17,9},{25,1},{2,26},{10... | collective-permute-start | bytes 3145736 | tf_op jit(solution)/shard_map/ppermute | solution.py:144
  286.3 32.1 %collective-permute-start.37 = (bf16[512,1024]{1,0:T(8,128)(2,1)S(1)}, bf16[512,1024]{1,0:T(8,128)(2,1)S(1)}, u32[]{:S(2)}, u32[]{:S(2)}) collective-permute-start(bf16[512,1024]{1,0:T(8,128)(2,1)S(1)} %add_convert_fusion.24), channel_id=1, source_target_pairs={{2,4},{4,2},{3,5},{5,3},{10,12},{12,10},{11,13},{13,11},{18,20},{2... | collective-permute-start | bytes 3145736 | tf_op jit(solution)/shard_map/ppermute | solution.py:144
  289.7 28.7 %collective-permute-start.38 = (bf16[512,1024]{1,0:T(8,128)(2,1)S(1)}, bf16[512,1024]{1,0:T(8,128)(2,1)S(1)}, u32[]{:S(2)}, u32[]{:S(2)}) collective-permute-start(bf16[512,1024]{1,0:T(8,128)(2,1)S(1)} %fusion.refs_1_), channel_id=1, source_target_pairs={{0,2},{6,4},{2,0},{4,6},{1,3},{7,5},{3,1},{5,7},{8,10},{14,12},{10... | collective-permute-start | bytes 3145736 | tf_op jit(solution)/shard_map/ppermute | solution.py:144
  319.5 21.2 %collective-permute-start.41 = (bf16[512,1024]{1,0:T(8,128)(2,1)S(1)}, bf16[512,1024]{1,0:T(8,128)(2,1)S(1)}, u32[]{:S(2)}, u32[]{:S(2)}) collective-permute-start(bf16[512,1024]{1,0:T(8,128)(2,1)S(1)} %fusion.1.refs_3_), channel_id=1, source_target_pairs={{0,2},{6,4},{2,0},{4,6},{1,3},{7,5},{3,1},{5,7},{8,10},{14,12},{10... | collective-permute-start | bytes 3145736 | tf_op jit(solution)/shard_map/ppermute | solution.py:144
  319.8 20.9 %collective-permute-start.40 = (bf16[512,1024]{1,0:T(8,128)(2,1)S(1)}, bf16[512,1024]{1,0:T(8,128)(2,1)S(1)}, u32[]{:S(2)}, u32[]{:S(2)}) collective-permute-start(bf16[512,1024]{1,0:T(8,128)(2,1)S(1)} %add_convert_fusion.22), channel_id=1, source_target_pairs={{2,4},{4,2},{3,5},{5,3},{10,12},{12,10},{11,13},{13,11},{18,20},{2... | collective-permute-start | bytes 3145736 | tf_op jit(solution)/shard_map/ppermute | solution.py:144
  320.7 31.4 %collective-permute-start.42 = (bf16[512,2048]{1,0:T(8,128)(2,1)S(1)}, bf16[512,2048]{1,0:T(8,128)(2,1)S(1)}, u32[]{:S(2)}, u32[]{:S(2)}) collective-permute-start(bf16[512,2048]{1,0:T(8,128)(2,1)S(1)} %get-tuple-element.432), channel_id=1, source_target_pairs={{0,1},{1,0},{2,3},{3,2},{4,5},{5,4},{6,7},{7,6},{8,9},{9,8},{10,11... | collective-permute-start | bytes 6291464 | tf_op jit(solution)/shard_map/ppermute | solution.py:144
  320.8 31.3 %collective-permute-start.43 = (bf16[512,1024]{1,0:T(8,128)(2,1)S(1)}, bf16[512,1024]{1,0:T(8,128)(2,1)S(1)}, u32[]{:S(2)}, u32[]{:S(2)}) collective-permute-start(bf16[512,1024]{1,0:T(8,128)(2,1)S(1)} %get-tuple-element.433), channel_id=1, source_target_pairs={{0,8},{8,0},{16,24},{24,16},{1,9},{9,1},{17,25},{25,17},{2,10},{10... | collective-permute-start | bytes 3145736 | tf_op jit(solution)/shard_map/ppermute | solution.py:144
  322.0 30.1 %collective-permute-start.44 = (bf16[512,1024]{1,0:T(8,128)(2,1)S(1)}, bf16[512,1024]{1,0:T(8,128)(2,1)S(1)}, u32[]{:S(2)}, u32[]{:S(2)}) collective-permute-start(bf16[512,1024]{1,0:T(8,128)(2,1)S(1)} %get-tuple-element.434), channel_id=1, source_target_pairs={{0,16},{8,24},{16,0},{24,8},{1,17},{9,25},{17,1},{25,9},{2,18},{10... | collective-permute-start | bytes 3145736 | tf_op jit(solution)/shard_map/ppermute | solution.py:144
  341.7 22.3 %collective-permute-start.46 = (bf16[512,1024]{1,0:T(8,128)(2,1)S(1)}, bf16[512,1024]{1,0:T(8,128)(2,1)S(1)}, u32[]{:S(2)}, u32[]{:S(2)}) collective-permute-start(bf16[512,1024]{1,0:T(8,128)(2,1)S(1)} %fusion.2.refs_5_), channel_id=1, source_target_pairs={{0,2},{6,4},{2,0},{4,6},{1,3},{7,5},{3,1},{5,7},{8,10},{14,12},{10... | collective-permute-start | bytes 3145736 | tf_op jit(solution)/shard_map/ppermute | solution.py:144
  365.0 24.3 %collective-permute-start.51 = (bf16[512,1024]{1,0:T(8,128)(2,1)S(1)}, bf16[512,1024]{1,0:T(8,128)(2,1)S(1)}, u32[]{:S(2)}, u32[]{:S(2)}) collective-permute-start(bf16[512,1024]{1,0:T(8,128)(2,1)S(1)} %fusion.3.refs_7_), channel_id=1, source_target_pairs={{0,2},{6,4},{2,0},{4,6},{1,3},{7,5},{3,1},{5,7},{8,10},{14,12},{10... | collective-permute-start | bytes 3145736 | tf_op jit(solution)/shard_map/ppermute | solution.py:144
  368.7 20.6 %collective-permute-start.50 = (bf16[512,1024]{1,0:T(8,128)(2,1)S(1)}, bf16[512,1024]{1,0:T(8,128)(2,1)S(1)}, u32[]{:S(2)}, u32[]{:S(2)}) collective-permute-start(bf16[512,1024]{1,0:T(8,128)(2,1)S(1)} %add_convert_fusion.18), channel_id=1, source_target_pairs={{2,4},{4,2},{3,5},{5,3},{10,12},{12,10},{11,13},{13,11},{18,20},{2... | collective-permute-start | bytes 3145736 | tf_op jit(solution)/shard_map/ppermute | solution.py:144
  390.4 23.2 %collective-permute-start.56 = (bf16[512,1024]{1,0:T(8,128)(2,1)S(1)}, bf16[512,1024]{1,0:T(8,128)(2,1)S(1)}, u32[]{:S(2)}, u32[]{:S(2)}) collective-permute-start(bf16[512,1024]{1,0:T(8,128)(2,1)S(1)} %fusion.4.refs_1_), channel_id=1, source_target_pairs={{0,2},{6,4},{2,0},{4,6},{1,3},{7,5},{3,1},{5,7},{8,10},{14,12},{10... | collective-permute-start | bytes 3145736 | tf_op jit(solution)/shard_map/ppermute | solution.py:144
  392.5 21.1 %collective-permute-start.55 = (bf16[512,1024]{1,0:T(8,128)(2,1)S(1)}, bf16[512,1024]{1,0:T(8,128)(2,1)S(1)}, u32[]{:S(2)}, u32[]{:S(2)}) collective-permute-start(bf16[512,1024]{1,0:T(8,128)(2,1)S(1)} %add_convert_fusion.16), channel_id=1, source_target_pairs={{2,4},{4,2},{3,5},{5,3},{10,12},{12,10},{11,13},{13,11},{18,20},{2... | collective-permute-start | bytes 3145736 | tf_op jit(solution)/shard_map/ppermute | solution.py:144
  412.0 28.0 %collective-permute-start.57 = (bf16[512,1024]{1,0:T(8,128)(2,1)S(1)}, bf16[512,1024]{1,0:T(8,128)(2,1)S(1)}, u32[]{:S(2)}, u32[]{:S(2)}) collective-permute-start(bf16[512,1024]{1,0:T(8,128)(2,1)S(1)} %get-tuple-element.465), channel_id=1, source_target_pairs={{0,24},{8,16},{16,8},{24,0},{1,25},{9,17},{17,9},{25,1},{2,26},{10... | collective-permute-start | bytes 3145736 | tf_op jit(solution)/shard_map/ppermute | solution.py:144
  414.8 27.2 %collective-permute-start.60 = (bf16[512,1024]{1,0:T(8,128)(2,1)S(1)}, bf16[512,1024]{1,0:T(8,128)(2,1)S(1)}, u32[]{:S(2)}, u32[]{:S(2)}) collective-permute-start(bf16[512,1024]{1,0:T(8,128)(2,1)S(1)} %fusion.5.refs_1_), channel_id=1, source_target_pairs={{0,2},{6,4},{2,0},{4,6},{1,3},{7,5},{3,1},{5,7},{8,10},{14,12},{10... | collective-permute-start | bytes 3145736 | tf_op jit(solution)/shard_map/ppermute | solution.py:144
  417.3 24.7 %collective-permute-start.59 = (bf16[512,1024]{1,0:T(8,128)(2,1)S(1)}, bf16[512,1024]{1,0:T(8,128)(2,1)S(1)}, u32[]{:S(2)}, u32[]{:S(2)}) collective-permute-start(bf16[512,1024]{1,0:T(8,128)(2,1)S(1)} %add_convert_fusion.14), channel_id=1, source_target_pairs={{2,4},{4,2},{3,5},{5,3},{10,12},{12,10},{11,13},{13,11},{18,20},{2... | collective-permute-start | bytes 3145736 | tf_op jit(solution)/shard_map/ppermute | solution.py:144
  440.0 25.0 %collective-permute-start.61 = (bf16[512,1024]{1,0:T(8,128)(2,1)S(1)}, bf16[512,1024]{1,0:T(8,128)(2,1)S(1)}, u32[]{:S(2)}, u32[]{:S(2)}) collective-permute-start(bf16[512,1024]{1,0:T(8,128)(2,1)S(1)} %get-tuple-element.480), channel_id=1, source_target_pairs={{0,8},{8,0},{16,24},{24,16},{1,9},{9,1},{17,25},{25,17},{2,10},{10... | collective-permute-start | bytes 3145736 | tf_op jit(solution)/shard_map/ppermute | solution.py:144
  440.9 24.7 %collective-permute-start.62 = (bf16[512,1024]{1,0:T(8,128)(2,1)S(1)}, bf16[512,1024]{1,0:T(8,128)(2,1)S(1)}, u32[]{:S(2)}, u32[]{:S(2)}) collective-permute-start(bf16[512,1024]{1,0:T(8,128)(2,1)S(1)} %get-tuple-element.481), channel_id=1, source_target_pairs={{0,16},{8,24},{16,0},{24,8},{1,17},{9,25},{17,1},{25,9},{2,18},{10... | collective-permute-start | bytes 3145736 | tf_op jit(solution)/shard_map/ppermute | solution.py:144
  443.0 25.3 %collective-permute-start.64 = (bf16[512,1024]{1,0:T(8,128)(2,1)S(1)}, bf16[512,1024]{1,0:T(8,128)(2,1)S(1)}, u32[]{:S(2)}, u32[]{:S(2)}) collective-permute-start(bf16[512,1024]{1,0:T(8,128)(2,1)S(1)} %fusion.6.refs_3_), channel_id=1, source_target_pairs={{0,2},{6,4},{2,0},{4,6},{1,3},{7,5},{3,1},{5,7},{8,10},{14,12},{10... | collective-permute-start | bytes 3145736 | tf_op jit(solution)/shard_map/ppermute | solution.py:144
  445.6 22.7 %collective-permute-start.63 = (bf16[512,1024]{1,0:T(8,128)(2,1)S(1)}, bf16[512,1024]{1,0:T(8,128)(2,1)S(1)}, u32[]{:S(2)}, u32[]{:S(2)}) collective-permute-start(bf16[512,1024]{1,0:T(8,128)(2,1)S(1)} %add_convert_fusion.12), channel_id=1, source_target_pairs={{2,4},{4,2},{3,5},{5,3},{10,12},{12,10},{11,13},{13,11},{18,20},{2... | collective-permute-start | bytes 3145736 | tf_op jit(solution)/shard_map/ppermute | solution.py:144
  466.0 25.0 %collective-permute-start.65 = (bf16[512,1024]{1,0:T(8,128)(2,1)S(1)}, bf16[512,1024]{1,0:T(8,128)(2,1)S(1)}, u32[]{:S(2)}, u32[]{:S(2)}) collective-permute-start(bf16[512,1024]{1,0:T(8,128)(2,1)S(1)} %get-tuple-element.488), channel_id=1, source_target_pairs={{0,24},{8,16},{16,8},{24,0},{1,25},{9,17},{17,9},{25,1},{2,26},{10... | collective-permute-start | bytes 3145736 | tf_op jit(solution)/shard_map/ppermute | solution.py:144
  469.4 25.4 %collective-permute-start.67 = (bf16[512,1024]{1,0:T(8,128)(2,1)S(1)}, bf16[512,1024]{1,0:T(8,128)(2,1)S(1)}, u32[]{:S(2)}, u32[]{:S(2)}) collective-permute-start(bf16[512,1024]{1,0:T(8,128)(2,1)S(1)} %fusion.7.refs_5_), channel_id=1, source_target_pairs={{0,2},{6,4},{2,0},{4,6},{1,3},{7,5},{3,1},{5,7},{8,10},{14,12},{10... | collective-permute-start | bytes 3145736 | tf_op jit(solution)/shard_map/ppermute | solution.py:144
  473.1 21.7 %collective-permute-start.66 = (bf16[512,1024]{1,0:T(8,128)(2,1)S(1)}, bf16[512,1024]{1,0:T(8,128)(2,1)}, u32[]{:S(2)}, u32[]{:S(2)}) collective-permute-start(bf16[512,1024]{1,0:T(8,128)(2,1)S(1)} %add_convert_fusion.10), channel_id=1, source_target_pairs={{2,4},{4,2},{3,5},{5,3},{10,12},{12,10},{11,13},{13,11},{18,20},{2... | collective-permute-start | bytes 3145736 | tf_op jit(solution)/shard_map/ppermute | solution.py:144
  497.1 24.8 %collective-permute-start.70 = (bf16[512,1024]{1,0:T(8,128)(2,1)S(1)}, bf16[512,1024]{1,0:T(8,128)(2,1)S(1)}, u32[]{:S(2)}, u32[]{:S(2)}) collective-permute-start(bf16[512,1024]{1,0:T(8,128)(2,1)S(1)} %fusion.8.sent_ref), channel_id=1, source_target_pairs={{0,2},{6,4},{2,0},{4,6},{1,3},{7,5},{3,1},{5,7},{8,10},{14,12},{10... | collective-permute-start | bytes 3145736 | tf_op jit(solution)/shard_map/ppermute | solution.py:144
  501.1 20.8 %collective-permute-start.69 = (bf16[512,1024]{1,0:T(8,128)(2,1)S(1)}, bf16[512,1024]{1,0:T(8,128)(2,1)S(1)}, u32[]{:S(2)}, u32[]{:S(2)}) collective-permute-start(bf16[512,1024]{1,0:T(8,128)(2,1)S(1)} %add_convert_fusion.8), channel_id=1, source_target_pairs={{2,4},{4,2},{3,5},{5,3},{10,12},{12,10},{11,13},{13,11},{18,20},{2... | collective-permute-start | bytes 3145736 | tf_op jit(solution)/shard_map/ppermute | solution.py:144
  522.9 27.0 %collective-permute-start.75 = (bf16[512,1024]{1,0:T(8,128)(2,1)S(1)}, bf16[512,1024]{1,0:T(8,128)(2,1)S(1)}, u32[]{:S(2)}, u32[]{:S(2)}) collective-permute-start(bf16[512,1024]{1,0:T(8,128)(2,1)S(1)} %fusion.9.refs_7_), channel_id=1, source_target_pairs={{0,2},{6,4},{2,0},{4,6},{1,3},{7,5},{3,1},{5,7},{8,10},{14,12},{10... | collective-permute-start | bytes 3145736 | tf_op jit(solution)/shard_map/ppermute | solution.py:144
  526.7 23.3 %collective-permute-start.74 = (bf16[512,1024]{1,0:T(8,128)(2,1)S(1)}, bf16[512,1024]{1,0:T(8,128)(2,1)S(1)}, u32[]{:S(2)}, u32[]{:S(2)}) collective-permute-start(bf16[512,1024]{1,0:T(8,128)(2,1)S(1)} %add_convert_fusion.6), channel_id=1, source_target_pairs={{2,4},{4,2},{3,5},{5,3},{10,12},{12,10},{11,13},{13,11},{18,20},{2... | collective-permute-start | bytes 3145736 | tf_op jit(solution)/shard_map/ppermute | solution.py:144
  528.8 21.1 %collective-permute-start.72 = (bf16[128,2048]{1,0:T(8,128)(2,1)S(1)}, bf16[128,2048]{1,0:T(8,128)(2,1)S(1)}, u32[]{:S(2)}, u32[]{:S(2)}) collective-permute-start(bf16[128,2048]{1,0:T(8,128)(2,1)S(1)} %get-tuple-element.504), channel_id=1, source_target_pairs={{0,16},{8,24},{16,0},{24,8},{1,17},{9,25},{17,1},{25,9},{2,18},{10... | collective-permute-start | bytes 1572872 | tf_op jit(solution)/shard_map/ppermute | solution.py:144
  529.9 20.0 %collective-permute-start.73 = (bf16[128,2048]{1,0:T(8,128)(2,1)S(1)}, bf16[128,2048]{1,0:T(8,128)(2,1)S(1)}, u32[]{:S(2)}, u32[]{:S(2)}) collective-permute-start(bf16[128,2048]{1,0:T(8,128)(2,1)S(1)} %get-tuple-element.505), channel_id=1, source_target_pairs={{0,24},{8,16},{16,8},{24,0},{1,25},{9,17},{17,9},{25,1},{2,26},{10... | collective-permute-start | bytes 1572872 | tf_op jit(solution)/shard_map/ppermute | solution.py:144
  551.0 20.8 %collective-permute-start.77 = (bf16[512,1024]{1,0:T(8,128)(2,1)S(1)}, bf16[512,1024]{1,0:T(8,128)(2,1)S(1)}, u32[]{:S(2)}, u32[]{:S(2)}) collective-permute-start(bf16[512,1024]{1,0:T(8,128)(2,1)S(1)} %fusion.10.refs_3_), channel_id=1, source_target_pairs={{0,2},{6,4},{2,0},{4,6},{1,3},{7,5},{3,1},{5,7},{8,10},{14,12},{10... | collective-permute-start | bytes 3145736 | tf_op jit(solution)/shard_map/ppermute | solution.py:144
  553.2 18.6 %collective-permute-start.76 = (bf16[512,1024]{1,0:T(8,128)(2,1)S(1)}, bf16[512,1024]{1,0:T(8,128)(2,1)S(1)}, u32[]{:S(2)}, u32[]{:S(2)}) collective-permute-start(bf16[512,1024]{1,0:T(8,128)(2,1)S(1)} %add_convert_fusion.4), channel_id=1, source_target_pairs={{2,4},{4,2},{3,5},{5,3},{10,12},{12,10},{11,13},{13,11},{18,20},{2... | collective-permute-start | bytes 3145736 | tf_op jit(solution)/shard_map/ppermute | solution.py:144
  565.4 23.6 %collective-permute-start.80 = (bf16[512,2048]{1,0:T(8,128)(2,1)S(1)}, bf16[512,2048]{1,0:T(8,128)(2,1)S(1)}, u32[]{:S(2)}, u32[]{:S(2)}) collective-permute-start(bf16[512,2048]{1,0:T(8,128)(2,1)S(1)} %get-tuple-element.527), channel_id=1, source_target_pairs={{0,1},{1,0},{2,3},{3,2},{4,5},{5,4},{6,7},{7,6},{8,9},{9,8},{10,11... | collective-permute-start | bytes 6291464 | tf_op jit(solution)/shard_map/ppermute | solution.py:144
  572.6 22.8 %collective-permute-start.82 = (bf16[512,1024]{1,0:T(8,128)(2,1)S(1)}, bf16[512,1024]{1,0:T(8,128)(2,1)S(1)}, u32[]{:S(2)}, u32[]{:S(2)}) collective-permute-start(bf16[512,1024]{1,0:T(8,128)(2,1)S(1)} %fusion.11.refs_5_), channel_id=1, source_target_pairs={{0,2},{6,4},{2,0},{4,6},{1,3},{7,5},{3,1},{5,7},{8,10},{14,12},{10... | collective-permute-start | bytes 3145736 | tf_op jit(solution)/shard_map/ppermute | solution.py:144
  576.6 18.9 %collective-permute-start.81 = (bf16[512,1024]{1,0:T(8,128)(2,1)S(1)}, bf16[512,1024]{1,0:T(8,128)(2,1)S(1)}, u32[]{:S(2)}, u32[]{:S(2)}) collective-permute-start(bf16[512,1024]{1,0:T(8,128)(2,1)S(1)} %add_convert_fusion.2), channel_id=1, source_target_pairs={{2,4},{4,2},{3,5},{5,3},{10,12},{12,10},{11,13},{13,11},{18,20},{2... | collective-permute-start | bytes 3145736 | tf_op jit(solution)/shard_map/ppermute | solution.py:144
  596.0 31.4 %collective-permute-start.87 = (bf16[512,1024]{1,0:T(8,128)(2,1)S(1)}, bf16[512,1024]{1,0:T(8,128)(2,1)S(1)}, u32[]{:S(2)}, u32[]{:S(2)}) collective-permute-start(bf16[512,1024]{1,0:T(8,128)(2,1)S(1)} %fusion.12.refs_7_), channel_id=1, source_target_pairs={{0,2},{6,4},{2,0},{4,6},{1,3},{7,5},{3,1},{5,7},{8,10},{14,12},{10... | collective-permute-start | bytes 3145736 | tf_op jit(solution)/shard_map/ppermute | solution.py:144
  599.9 27.4 %collective-permute-start.86 = (bf16[512,640]{1,0:T(8,128)(2,1)S(1)}, bf16[512,640]{1,0:T(8,128)(2,1)S(1)}, u32[]{:S(2)}, u32[]{:S(2)}) collective-permute-start(bf16[512,640]{1,0:T(8,128)(2,1)S(1)} %add_convert_fusion.33), channel_id=1, source_target_pairs={{2,4},{4,2},{3,5},{5,3},{10,12},{12,10},{11,13},{13,11},{18,20},{2... | collective-permute-start | bytes 1966088 | tf_op jit(solution)/shard_map/ppermute | solution.py:144
  602.2 23.6 %collective-permute-start.84 = (bf16[128,2048]{1,0:T(8,128)(2,1)S(1)}, bf16[128,2048]{1,0:T(8,128)(2,1)S(1)}, u32[]{:S(2)}, u32[]{:S(2)}) collective-permute-start(bf16[128,2048]{1,0:T(8,128)(2,1)S(1)} %get-tuple-element.536), channel_id=1, source_target_pairs={{0,16},{8,24},{16,0},{24,8},{1,17},{9,25},{17,1},{25,9},{2,18},{10... | collective-permute-start | bytes 1572872 | tf_op jit(solution)/shard_map/ppermute | solution.py:144
  603.3 22.6 %collective-permute-start.85 = (bf16[128,2048]{1,0:T(8,128)(2,1)S(1)}, bf16[128,2048]{1,0:T(8,128)(2,1)S(1)}, u32[]{:S(2)}, u32[]{:S(2)}) collective-permute-start(bf16[128,2048]{1,0:T(8,128)(2,1)S(1)} %get-tuple-element.537), channel_id=1, source_target_pairs={{0,24},{8,16},{16,8},{24,0},{1,25},{9,17},{17,9},{25,1},{2,26},{10... | collective-permute-start | bytes 1572872 | tf_op jit(solution)/shard_map/ppermute | solution.py:144
  (155 other events, 1429.7 us)

commit v8 on v7

--- a/solution.py
+++ b/solution.py
@@ -76,6 +76,7 @@
 MIDDLE_LIMIT = 20 * 1024 * 1024
 SMALL_LIMIT = 12 * 1024 * 1024
 SMALL = pl.CostEstimate(flops=1, bytes_accessed=1, transcendentals=0)
+LARGE = pl.CostEstimate(flops=12_000_000_000, bytes_accessed=1, transcendentals=0)
 
 
 def pairs_by(distance, size):
@@ -116,6 +117,9 @@
                 pairs = inwards + outwards
             leaving = (name, sent)
             moves.append(("ends", sent, self.axis, pairs))
+        elif entering is not None and halfway is not None:
+            sent = jnp.where(self.at_end[0] == 1, entering[1], halfway[1])
+            moves.append(("ends", sent, self.axis, inwards + outwards))
         elif entering is not None:
             moves.append(("ends", entering[1], self.axis, inwards))
         self.entered, self.halfway, self.leaving = entering, halfway, leaving
@@ -143,31 +147,27 @@
     def start(self, moves):
         return [(name, lax.ppermute(value, axis, pairs)) for name, value, axis, pairs in moves]
 
-    def step(self, moves=(), summed=None, late=None, carry=(), hold=False):
-        moves, carry = list(moves), list(carry)
+    def step(self, moves=(), summed=None, late=None, carry=(), first=()):
+        moves, carry, first = list(moves), list(carry), list(first)
         arrays = [move[1] for move in moves] + carry
         fresh = [summed[1]] if summed is not None and summed[1] is not None else []
         together = summed is not None and not fresh and summed[0] not in self.got
-        if together or not self.on_line:
-            held = self.wait(self.on_line + self.others, fresh + arrays)
-            held_fresh, held = held[: len(fresh)], held[len(fresh) :]
-        else:
-            held_fresh = self.wait(self.on_line, fresh)
+        together = together or not self.on_line
+        flying = self.on_line + (self.others if together else [])
+        held = self.wait(flying, fresh + first + (arrays if together else []))
+        held_fresh, held = held[: len(fresh)], held[len(fresh) :]
+        held_first, held = held[: len(first)], held[len(first) :]
         entering = summed
         if summed is not None:
             entering = (summed[0], held_fresh[0] if fresh else self.take(summed[0]))
-        along = self.line.advance(self.got, entering)
-        if not together and self.on_line:
-            self.on_line = self.start(along)
-            held = self.wait([] if hold else self.others, arrays)
-        else:
-            self.on_line = self.start(along)
+        self.on_line = self.start(self.line.advance(self.got, entering))
+        if not together:
+            held = self.wait(self.others, arrays)
         moves = [
             (name, value, axis, pairs) for (name, _, axis, pairs), value in zip(moves, held)
         ]
-        before = self.others if hold else []
-        self.others = before + self.start(moves + (late() if late is not None else []))
-        return held[len(moves) :]
+        self.others = self.start(moves + (late() if late is not None else []))
+        return held[len(moves) :] + held_first
 
     def take(self, name):
         return self.got.pop(name)
@@ -320,7 +320,7 @@
     return pl.BlockSpec(block, index)
 
 
-def gridded(kernel, steps, ins, outs, scalars=(), limit=None):
+def gridded(kernel, steps, ins, outs, scalars=(), limit=None, cost=SMALL):
     return pl.pallas_call(
         kernel,
         grid=(steps,),
@@ -329,7 +329,7 @@
         out_specs=[pl.BlockSpec(block, index) for _, block, index in outs],
         out_shape=[shape for shape, _, _ in outs],
         compiler_params=pltpu.CompilerParams(vmem_limit_bytes=limit or MIDDLE_LIMIT),
-        cost_estimate=SMALL,
+        cost_estimate=cost,
     )(*scalars, *[array for array, _, _ in ins])
 
 
@@ -366,7 +366,7 @@
         )
 
 
-def settle(at_end, index, pairs, width):
+def settle(at_end, index, pairs, width, cost=SMALL):
     count = len(pairs)
     arrays = [array for pair in pairs for array in pair]
     depth = arrays[0].shape[0]
@@ -374,7 +374,7 @@
     ins = [(array, (rows, width), lambda i: (i, 0)) for array in arrays]
     outs = [row_blocks(full(depth, width * count), rows)]
     kernel = functools.partial(settle_kernel, count)
-    return gridded(kernel, depth // rows, ins, outs, scalars=(at_end, index))[0]
+    return gridded(kernel, depth // rows, ins, outs, scalars=(at_end, index), cost=cost)[0]
 
 
 def settle_attention_kernel(count, q_width, kv_width, at_end_ref, index_ref, *refs):
@@ -559,13 +559,31 @@
     second_ref[...] = total[half:]
 
 
-def rows_sum(lefts, rights):
+def rows_sum(lefts, rights, cost=SMALL):
     tokens, width = lefts[0].shape[0], rights[0].shape[0]
     block = math.gcd(width, 512)
     ins = [still(left) for left in lefts]
     ins += [(right, (block, right.shape[1]), lambda i: (i, 0)) for right in rights]
     outs = [(low(tokens // 2, width), (tokens // 2, block), lambda i: (0, i))] * 2
-    return gridded(functools.partial(rows_sum_kernel, len(lefts)), width // block, ins, outs)
+    kernel = functools.partial(rows_sum_kernel, len(lefts))
+    return gridded(kernel, width // block, ins, outs, cost=cost)
+
+
+def half_rows_kernel(terms, *refs):
+    total = 0.0
+    for left_ref, right_ref in zip(refs[:terms], refs[terms : 2 * terms]):
+        total = total + contract_last(left_ref[...], right_ref[...])
+    refs[-1][...] = total.astype(jnp.bfloat16)
+
+
+def half_rows(lefts, rights, which):
+    half, width = lefts[0].shape[0] // 2, rights[0].shape[0]
+    block = math.gcd(width, 512)
+    ins = [(left, (half, left.shape[1]), lambda i: (which, 0)) for left in lefts]
+    ins += [(right, (block, right.shape[1]), lambda i: (i, 0)) for right in rights]
+    outs = [(low(half, width), (half, block), lambda i: (0, i))]
+    kernel = functools.partial(half_rows_kernel, len(lefts))
+    return gridded(kernel, width // block, ins, outs)[0]
 
 
 def weight_grad_kernel(count, terms, turn, *refs):
@@ -595,25 +613,28 @@
         first += columns
 
 
-def weight_grad(terms, count, side=None):
+def weight_grad(terms, count, side=None, packs=None):
     columns = sum(right.shape[1] for _, _, right in terms)
     depth = terms[0][0].shape[1] // count
+    packs = range(count) if packs is None else packs
+    first, apart = packs[0], packs[1] - packs[0]
     ins = []
     if side is not None:
         ins.append((side, None, None))
     for mine, other, right in terms:
-        ins += [(left, (left.shape[0], depth), lambda i: (0, i)) for left in (mine, other)]
+        for left in (mine, other):
+            ins.append((left, (left.shape[0], depth), lambda i: (0, first + apart * i)))
         ins.append(still(right))
     specs = [
         pl.BlockSpec(memory_space=pltpu.SMEM) if block is None else pl.BlockSpec(block, index)
         for _, block, index in ins
     ]
     return pl.pallas_call(
-        functools.partial(weight_grad_kernel, count, len(terms), side is not None),
-        grid=(count,),
+        functools.partial(weight_grad_kernel, len(packs), len(terms), side is not None),
+        grid=(len(packs),),
         in_specs=specs,
-        out_specs=[pl.BlockSpec((depth, columns), lambda i: (0, 0))] * count,
-        out_shape=[low(depth, columns)] * count,
+        out_specs=[pl.BlockSpec((depth, columns), lambda i: (0, 0))] * len(packs),
+        out_shape=[low(depth, columns)] * len(packs),
         compiler_params=pltpu.CompilerParams(vmem_limit_bytes=MIDDLE_LIMIT),
         cost_estimate=SMALL,
     )(*[array for array, _, _ in ins])
@@ -1056,9 +1077,11 @@
     steps.step(back("wd", d_wd, [3]), summed=entry("wd", 2))
     wd_pieces = [own_down] + arrived("down")
     d_gate, d_up = units_back(all_cot, wd_pieces, gate_val, up_val)
-    first, second = rows_sum([d_gate, d_up], [wg, wu])
-    d_wg = weight_grad([(*normed_two, d_gate)], packs, side_arg)
+    second = half_rows([d_gate, d_up], [wg, wu], 1)
+    d_wg = dict(zip((1, 2), weight_grad([(*normed_two, d_gate)], packs, side_arg, (1, 2))))
     steps.step(to_core("d_two", second) + back("wg", d_wg, [1, 2]), summed=entry("wd", 3))
+    first = half_rows([d_gate, d_up], [wg, wu], 0)
+    d_wg.update(zip((0, 3), weight_grad([(*normed_two, d_gate)], packs, side_arg, (0, 3))))
     d_wu = weight_grad([(*normed_two, d_up)], packs, side_arg)
     steps.step(
         summed=entry("wg", 0, d_wg), late=functools.partial(to_rows, "d_two", first)
@@ -1077,28 +1100,29 @@
         return send_all("d_branch", sends)
 
     steps.step(summed=entry("wu", 0, d_wu), late=branch_back)
-    ff_first, ff_second = rows_sum([hidden], [join(wd_pieces[0], wd_pieces[1:])])
-    steps.step(
+    ff_first, ff_second = rows_sum([hidden], [join(wd_pieces[0], wd_pieces[1:])], LARGE)
+    ff_first, ff_second = steps.step(
         back("wg", d_wg, [3]),
         summed=entry("wg", 1),
         late=lambda: joined("all_branch", kept["d_branch"], arrived("d_branch")),
+        first=(ff_first, ff_second),
     )
     sums = steps.line.sums
 
-    def settle_all(name):
-        return settle(at_end, index, [sums[name, k] for k in range(packs)], ff_width)
+    def settle_all(name, cost=SMALL):
+        return settle(at_end, index, [sums[name, k] for k in range(packs)], ff_width, cost)
 
     d_branch = (kept["all_branch"], unwaited("all_branch"))
     d_q, d_kv = attend_back(
         here_arg, q_rot, d_branch, cosine, sine, place_args, wo, kvs, packs, groups
     )
-    d_q, d_kv = steps.step(back("wu", d_wu, [1, 2]), summed=entry("wg", 2), carry=(d_q, d_kv))
-    steps.step(back("wu", d_wu, [3]), summed=("d_kv", d_kv))
-    down_grad = settle_all("wd")
-    steps.step(to_core("ff", ff_second), summed=entry("wg", 3))
-    (down_grad,) = steps.step(
-        summed=entry("wu", 1), late=functools.partial(to_rows, "ff", ff_first), carry=(down_grad,)
-    )
+    down_grad = settle_all("wd", LARGE)
+    d_q, d_kv, down_grad = steps.step(
+        back("wu", d_wu, [1, 2]), summed=entry("wg", 2), carry=(d_q, d_kv), first=(down_grad,)
+    )
+    steps.step(back("wu", d_wu, [3]) + to_core("ff", ff_second), summed=("d_kv", d_kv))
+    steps.step(summed=entry("wg", 3), late=functools.partial(to_rows, "ff", ff_first))
+    steps.step(summed=entry("wu", 1))
     steps.step(summed=entry("wu", 2))
     result = in_vmem(
         result_kernel, [low(half, width)], kept["middle"], kept["ff"], *arrived("ff")
@@ -1133,7 +1157,7 @@
             scalars=1,
         )[0]
 
-    gate_grad = settle_all("wg")
+    gate_grad = settle_all("wg", LARGE)
     def gains_to_core():
         kept["in_grad"], d_gain_one = in_vmem(
             functools.partial(in_grad_kernel, packs),
@@ -1159,7 +1183,7 @@
 
     steps.step(back("wqkvo", d_wqkvo, [3]), summed=entry("wqkvo", 1), late=gains_to_core)
     (gate_grad,) = steps.step(
-        summed=entry("wqkvo", 2), late=gains_to_packs, carry=(gate_grad,)
+        summed=entry("wqkvo", 2), late=gains_to_packs, first=(gate_grad,)
     )
     up_grad = settle_all("wu")
     in_grad = both_rows(kept["in_grad"], steps.take("in_grad"))

time: 699 us -> 684 us (0.979)
  waiting for transfers between devices: 320 us -> 292 us
  other arithmetic: 30.7 us -> 39.7 us
    ppermute x104, waiting for transfers between devices: 318 us -> 290 us  [start(): lax.ppermute(value, axis, pairs)]
    pallas_call x4 -> x5, Pallas kernels: 26 us -> 29.3 us  [weight_grad(): pl.pallas_call(functools.partial(weight_grad_kernel, len(packs), len(term...]
    pallas_call x13 -> x14, Pallas kernels: 97.9 us -> 99 us  [gridded(): pl.pallas_call(kernel, grid=(steps,), in_specs=[pl.BlockSpec(memory_space...]
    unnamed x228 -> x230, local copies, waits for them, and re-layouts: 31.1 us -> 31.9 us
  transfers between devices with their start and end apart: 105 -> 105, of which waited for: 49 -> 50; matrix products, arithmetic and copies ran while one was open for 4% -> 6% of each run, Pallas kernels for 20% -> 21%
where the time goes in v8:
time: 684 us; the launch traced here: 678 us
  waiting for transfers between devices  292 us (43%)
  starting transfers between devices  148 us (22%)
  Pallas kernels  148 us (22%)
  local copies, waits for them, and re-layouts  48.2 us (7%)
  other arithmetic  39.7 us (6%)
    ppermute x104, waiting for transfers between devices, start(): lax.ppermute(value, axis, pairs)  290 us
    ppermute x104, starting transfers between devices, start(): lax.ppermute(value, axis, pairs)  148 us
    pallas_call x14, Pallas kernels, gridded(): pl.pallas_call(kernel, grid=(steps,), in_specs=[pl.BlockSpec(memory_space...  99 us
    unnamed x230, local copies, waits for them, and re-layouts  31.9 us
    pallas_call x5, Pallas kernels, weight_grad(): pl.pallas_call(functools.partial(weight_grad_kernel, len(packs), len(term...  29.3 us
    pallas_call x20, Pallas kernels, in_vmem(): pl.pallas_call(kernel, out_shape=out_shape, in_specs=specs, out_specs=[pl...  19.2 us
    select_n x15, other arithmetic, either_way(): return jnp.where(at_end[0] == 1, fresh, total)  14.1 us
  transfers between devices with their start and end apart: 105, of which 50 were waited for; matrix products, arithmetic and copies ran while one was open for 6% of the time, Pallas kernels for 21%

profile of v8, /device:TPU:0, one launch (start us, length us, event | category | flops | bytes accessed | tf_op | source)
XLA Modules:
  0.0 677.9 jit_solution(3612302952975270732)
XLA Ops:
  6.6 2.9 collective-permute-start
  13.9 3.1 constant_dynamic-slice_fusion.11
  17.7 4.3 constant_dynamic-slice_fusion.5
  36.5 8.9 %collective-permute-done.3.refs_1_ = bf16[128,2048]{1,0:T(8,128)(2,1)} collective-permute-done((bf16[128,2048]{1,0:T(8,128)(2,1)}, bf16[128,2048]{1,0:T(8,128)(2,1)}, u32[]{:S(2)}, u32[]{:S(2)}) %collective-permute-start.3) | collective-permute-done | bytes 524320 | tf_op jit(solution)/shard_map/ppermute | solution.py:148
  45.4 9.7 %collective-permute-done.4.refs_2_ = bf16[128,2048]{1,0:T(8,128)(2,1)} collective-permute-done((bf16[128,2048]{1,0:T(8,128)(2,1)}, bf16[128,2048]{1,0:T(8,128)(2,1)}, u32[]{:S(2)}, u32[]{:S(2)}) %collective-permute-start.4) | collective-permute-done | bytes 524320 | tf_op jit(solution)/shard_map/ppermute | solution.py:148
  61.3 5.2 shard_map.216
  71.2 11.6 %collective-permute-done.7.refs_4_.refs_5_.refs_2_.refs_3_ = bf16[512,1024]{1,0:T(8,128)(2,1)S(1)} collective-permute-done((bf16[512,1024]{1,0:T(8,128)(2,1)S(1)}, bf16[512,1024]{1,0:T(8,128)(2,1)S(1)}, u32[]{:S(2)}, u32[]{:S(2)}) %collective-permute-start.7) | collective-permute-done | bytes 1048608 | tf_op jit(solution)/shard_map/ppermute | solution.py:148
  92.6 4.6 collective-permute-done.10.refs_1_
  97.2 9.6 %collective-permute-done.11.refs_2_ = bf16[2,512,128]{2,1,0:T(8,128)(2,1)S(1)} collective-permute-done((bf16[2,512,128]{2,1,0:T(8,128)(2,1)S(1)}, bf16[2,512,128]{2,1,0:T(8,128)(2,1)S(1)}, u32[]{:S(2)}, u32[]{:S(2)}) %collective-permute-start.11) | collective-permute-done | bytes 262176 | tf_op jit(solution)/shard_map/ppermute | solution.py:148
  108.5 3.2 collective-permute-start.17
  124.5 12.5 %shard_map.218 = (bf16[2,512,256]{2,1,0:T(8,128)(2,1)S(1)}, bf16[512,2048]{1,0:T(8,128)(2,1)S(1)}, bf16[512,2048]{1,0:T(8,128)(2,1)S(1)}) custom-call(bf16[2,512,256]{2,1,0:T(8,128)(2,1)S(1)} %copy-done.48, s32[4,256,1]{2,1,0:T(8,128)S(1)} %copy-done.25, s32[4,256,1]{2,1,0:T(8,128)S(1)} %copy-done.27, s32[4,1,1024]{2,1,0:T(1,128)S(1)} %broadcast_add_fusion.key_place_ref, ...), custom_call_target="tpu_custom_call" | custom-call | flops 1 | bytes 1 | tf_op jit(solution)/shard_map/pallas_call | solution.py:324
  137.1 4.1 collective-permute-done.18.came_ref
  147.0 9.7 %collective-permute-done.20.refs_1_ = bf16[128,2048]{1,0:T(8,128)(2,1)S(1)} collective-permute-done((bf16[128,2048]{1,0:T(8,128)(2,1)S(1)}, bf16[128,2048]{1,0:T(8,128)(2,1)S(1)}, u32[]{:S(2)}, u32[]{:S(2)}) %collective-permute-start.20) | collective-permute-done | bytes 524320 | tf_op jit(solution)/shard_map/ppermute | solution.py:148
  157.0 10.4 %collective-permute-done.22.refs_3_ = bf16[128,2048]{1,0:T(8,128)(2,1)S(1)} collective-permute-done((bf16[128,2048]{1,0:T(8,128)(2,1)S(1)}, bf16[128,2048]{1,0:T(8,128)(2,1)S(1)}, u32[]{:S(2)}, u32[]{:S(2)}) %collective-permute-start.22) | collective-permute-done | bytes 524320 | tf_op jit(solution)/shard_map/ppermute | solution.py:148
  177.2 8.7 %collective-permute-done.25.refs_1_ = bf16[128,2048]{1,0:T(8,128)(2,1)S(1)} collective-permute-done((bf16[128,2048]{1,0:T(8,128)(2,1)S(1)}, bf16[128,2048]{1,0:T(8,128)(2,1)S(1)}, u32[]{:S(2)}, u32[]{:S(2)}) %collective-permute-start.25) | collective-permute-done | bytes 524320 | tf_op jit(solution)/shard_map/ppermute | solution.py:148
  185.9 11.6 %collective-permute-done.26.refs_2_ = bf16[128,2048]{1,0:T(8,128)(2,1)S(1)} collective-permute-done((bf16[128,2048]{1,0:T(8,128)(2,1)S(1)}, bf16[128,2048]{1,0:T(8,128)(2,1)S(1)}, u32[]{:S(2)}, u32[]{:S(2)}) %collective-permute-start.26) | collective-permute-done | bytes 524320 | tf_op jit(solution)/shard_map/ppermute | solution.py:148
  201.9 12.5 %shard_map.223 = (bf16[1024,1024]{1,0:T(8,128)(2,1)S(1)}, bf16[1024,1024]{1,0:T(8,128)(2,1)S(1)}, bf16[1024,1024]{1,0:T(8,128)(2,1)S(1)}) custom-call(bf16[512,2048]{1,0:T(8,128)(2,1)S(1)} %shard_map.222.refs_0_.refs_1_, bf16[512,2048]{1,0:T(8,128)(2,1)S(1)} %collective-permute-done.30.refs_1_.refs_2_, ...), custom_call_target="tpu_custom_call" | custom-call | flops 1 | bytes 1 | tf_op jit(solution)/shard_map/pallas_call | solution.py:324
  214.5 8.2 %shard_map.224 = (bf16[512,1024]{1,0:T(8,128)(2,1)}, bf16[512,1024]{1,0:T(8,128)(2,1)}, bf16[512,1024]{1,0:T(8,128)(2,1)}, bf16[512,1024]{1,0:T(8,128)(2,1)S(1)}) custom-call(s32[1]{0:T(128)S(6)} %and.22.side_ref.refs_0_, bf16[512,2048]{1,0:T(8,128)(2,1)S(1)} %shard_map.220.refs_1_.refs_0_, bf16[512,2048]{1,0:T(8,128)(2,1)S(1)} %collective-permute-done.24.refs_2_.refs_1_, ...), custom_call_target="tpu_custom_call" | custom-call | flops 1 | bytes 1 | tf_op jit(solution)/shard_map/pallas_call | solution.py:632
  227.4 3.2 collective-permute-start.31
  237.3 4.2 shard_map.225
  241.5 9.7 %collective-permute-done.32 = bf16[512,1024]{1,0:T(8,128)(2,1)} collective-permute-done((bf16[512,1024]{1,0:T(8,128)(2,1)}, bf16[512,1024]{1,0:T(8,128)(2,1)}, u32[]{:S(2)}, u32[]{:S(2)}) %collective-permute-start.32) | collective-permute-done | bytes 1048608 | tf_op jit(solution)/shard_map/ppermute | solution.py:148
  259.6 19.4 %collective-permute-done.35 = bf16[512,1024]{1,0:T(8,128)(2,1)S(1)} collective-permute-done((bf16[512,1024]{1,0:T(8,128)(2,1)S(1)}, bf16[512,1024]{1,0:T(8,128)(2,1)S(1)}, u32[]{:S(2)}, u32[]{:S(2)}) %collective-permute-start.35) | collective-permute-done | bytes 1048608 | tf_op jit(solution)/shard_map/ppermute | solution.py:148
  283.9 6.0 collective-permute-start.38
  291.7 6.7 shard_map.226
  298.4 5.3 shard_map.227
  303.7 4.3 shard_map.228
  316.6 3.1 shard_map.229
  322.1 14.6 %collective-permute-done.41.refs_2_ = bf16[512,1024]{1,0:T(8,128)(2,1)S(1)} collective-permute-done((bf16[512,1024]{1,0:T(8,128)(2,1)S(1)}, bf16[512,1024]{1,0:T(8,128)(2,1)S(1)}, u32[]{:S(2)}, u32[]{:S(2)}) %collective-permute-start.41) | collective-permute-done | bytes 1048608 | tf_op jit(solution)/shard_map/ppermute | solution.py:148
  339.1 3.3 collective-permute-start.46
  344.3 5.3 shard_map.231.first_ref
  349.6 5.9 shard_map.230
  363.7 4.0 collective-permute-start.51
  368.4 5.5 shard_map.234
  383.2 3.3 collective-permute-done.51.refs_6_
  393.1 6.4 collective-permute-done.53.refs_2_
  401.7 4.4 shard_map.236
  414.9 21.6 %shard_map.238 = (bf16[2,512,256]{2,1,0:T(8,128)(2,1)S(1)}, bf16[512,1024]{1,0:T(8,128)(2,1)S(1)}) custom-call(s32[1]{0:T(128)} %bitcast.5.here_ref, bf16[2,512,256]{2,1,0:T(8,128)(2,1)S(1)} %copy-done.49, bf16[512,2048]{1,0:T(8,128)(2,1)S(1)} %shard_map.237.mine_ref.refs_3_, bf16[512,2048]{1,0:T(8,128)(2,1)S(1)} %collective-permute-done.58.other_ref.refs_4_, ...), custom_call_target="tpu_custom_call" | custom-call | flops 1 | bytes 1 | tf_op jit(solution)/shard_map/pallas_call | solution.py:324
  444.6 12.7 %collective-permute-done.61 = bf16[512,1024]{1,0:T(8,128)(2,1)S(1)} collective-permute-done((bf16[512,1024]{1,0:T(8,128)(2,1)S(1)}, bf16[512,1024]{1,0:T(8,128)(2,1)S(1)}, u32[]{:S(2)}, u32[]{:S(2)}) %collective-permute-start.61) | collective-permute-done | bytes 1048608 | tf_op jit(solution)/shard_map/ppermute | solution.py:148
  459.6 3.6 collective-permute-done.64.refs_2_
  464.3 3.7 collective-permute-start.68
  468.7 16.0 %collective-permute-done.65 = bf16[512,1024]{1,0:T(8,128)(2,1)S(1)} collective-permute-done((bf16[512,1024]{1,0:T(8,128)(2,1)S(1)}, bf16[512,1024]{1,0:T(8,128)(2,1)S(1)}, u32[]{:S(2)}, u32[]{:S(2)}) %collective-permute-start.65) | collective-permute-done | bytes 1048608 | tf_op jit(solution)/shard_map/ppermute | solution.py:148
  484.8 3.2 collective-permute-done.68.refs_4_
  489.0 3.7 collective-permute-start.73
  497.9 11.4 %collective-permute-done.69.refs_1_ = bf16[128,2048]{1,0:T(8,128)(2,1)S(1)} collective-permute-done((bf16[128,2048]{1,0:T(8,128)(2,1)S(1)}, bf16[128,2048]{1,0:T(8,128)(2,1)S(1)}, u32[]{:S(2)}, u32[]{:S(2)}) %collective-permute-start.69) | collective-permute-done | bytes 524320 | tf_op jit(solution)/shard_map/ppermute | solution.py:148
  509.7 6.5 collective-permute-done.71.refs_3_
  520.2 17.9 %collective-permute-done.75.refs_6_ = bf16[512,1024]{1,0:T(8,128)(2,1)S(1)} collective-permute-done((bf16[512,1024]{1,0:T(8,128)(2,1)S(1)}, bf16[512,1024]{1,0:T(8,128)(2,1)S(1)}, u32[]{:S(2)}, u32[]{:S(2)}) %collective-permute-start.75) | collective-permute-done | bytes 1048608 | tf_op jit(solution)/shard_map/ppermute | solution.py:148
  539.2 3.7 collective-permute-start.77
  544.0 3.3 shard_map.242
  547.4 7.8 %shard_map.241 = (bf16[512,640]{1,0:T(8,128)(2,1)S(1)}, bf16[512,640]{1,0:T(8,128)(2,1)S(1)}, bf16[512,640]{1,0:T(8,128)(2,1)S(1)}, bf16[512,640]{1,0:T(8,128)(2,1)S(1)}) custom-call(bf16[512,2048]{1,0:T(8,128)(2,1)S(1)} %copy-done.42, bf16[512,2048]{1,0:T(8,128)(2,1)S(1)} %copy-done.44, bf16[1024,384]{1,0:T(8,128)(2,1)S(1)} %shard_map.240.refs_2_.refs_0_, ...), custom_call_target="tpu_custom_call" | custom-call | flops 1 | bytes 1 | tf_op jit(solution)/shard_map/pallas_call | solution.py:632
  555.2 6.0 collective-permute-done.77.refs_2_
  562.1 4.0 collective-permute-start.82
  567.8 9.6 %collective-permute-done.78 = bf16[512,640]{1,0:T(8,128)(2,1)S(1)} collective-permute-done((bf16[512,640]{1,0:T(8,128)(2,1)S(1)}, bf16[512,640]{1,0:T(8,128)(2,1)S(1)}, u32[]{:S(2)}, u32[]{:S(2)}) %collective-permute-start.78) | collective-permute-done | bytes 655392 | tf_op jit(solution)/shard_map/ppermute | solution.py:148
  577.5 5.6 collective-permute-done.82.refs_4_
  588.5 6.2 collective-permute-start.87
  594.7 4.2 shard_map.244
  598.9 11.2 %collective-permute-done.84.refs_2_ = bf16[128,2048]{1,0:T(8,128)(2,1)S(1)} collective-permute-done((bf16[128,2048]{1,0:T(8,128)(2,1)S(1)}, bf16[128,2048]{1,0:T(8,128)(2,1)S(1)}, u32[]{:S(2)}, u32[]{:S(2)}) %collective-permute-start.84) | collective-permute-done | bytes 524320 | tf_op jit(solution)/shard_map/ppermute | solution.py:148
  611.8 3.8 collective-permute-done.87.refs_6_
  621.8 6.0 collective-permute-done.92.refs_0_
  628.2 4.3 collective-permute-start.97
  637.3 4.2 shard_map.248
  648.2 8.1 %collective-permute-done.100.refs_4_ = bf16[512,640]{1,0:T(8,128)(2,1)S(1)} collective-permute-done((bf16[512,640]{1,0:T(8,128)(2,1)S(1)}, bf16[512,640]{1,0:T(8,128)(2,1)S(1)}, u32[]{:S(2)}, u32[]{:S(2)}) %collective-permute-start.100) | collective-permute-done | bytes 655392 | tf_op jit(solution)/shard_map/ppermute | solution.py:148
  660.6 4.3 collective-permute-start.102
  668.6 2.9 collective-permute-done.101
  673.4 4.4 shard_map.250
  (507 shorter events, 220.1 us)
Async XLA Ops:
  6.6 18.9 %collective-permute-start = (bf16[272,640]{1,0:T(8,128)(2,1)}, bf16[272,640]{1,0:T(8,128)(2,1)S(1)}, u32[]{:S(2)}, u32[]{:S(2)}) collective-permute-start(bf16[272,640]{1,0:T(8,128)(2,1)} %get-tuple-element.303), channel_id=1, source_target_pairs={{0,8},{8,0},{16,24},{24,16},{1,9},{9,1},{17,25},{25,17},{2,10},{10... | collective-permute-start | bytes 1044488 | tf_op jit(solution)/shard_map/ppermute | solution.py:148
  28.3 26.8 %collective-permute-start.6 = (bf16[768,640]{1,0:T(8,128)(2,1)}, bf16[768,640]{1,0:T(8,128)(2,1)S(1)}, u32[]{:S(2)}, u32[]{:S(2)}) collective-permute-start(bf16[768,640]{1,0:T(8,128)(2,1)} %shard_map.213), channel_id=1, source_target_pairs={{0,2},{2,0},{4,6},{6,4},{1,3},{3,1},{5,7},{7,5},{8,10},{10,8},{12,... | collective-permute-start | bytes 2949128 | tf_op jit(solution)/shard_map/ppermute | solution.py:148
  31.3 23.8 %collective-permute-start.4 = (bf16[128,2048]{1,0:T(8,128)(2,1)}, bf16[128,2048]{1,0:T(8,128)(2,1)}, u32[]{:S(2)}, u32[]{:S(2)}) collective-permute-start(bf16[128,2048]{1,0:T(8,128)(2,1)} %get-tuple-element.311), channel_id=1, source_target_pairs={{0,16},{8,24},{16,0},{24,8},{1,17},{9,25},{17,1},{25,9},{2,18},{10... | collective-permute-start | bytes 1572872 | tf_op jit(solution)/shard_map/ppermute | solution.py:148
  32.3 22.8 %collective-permute-start.5 = (bf16[128,2048]{1,0:T(8,128)(2,1)}, bf16[128,2048]{1,0:T(8,128)(2,1)}, u32[]{:S(2)}, u32[]{:S(2)}) collective-permute-start(bf16[128,2048]{1,0:T(8,128)(2,1)} %get-tuple-element.312), channel_id=1, source_target_pairs={{0,24},{8,16},{16,8},{24,0},{1,25},{9,17},{17,9},{25,1},{2,26},{10... | collective-permute-start | bytes 1572872 | tf_op jit(solution)/shard_map/ppermute | solution.py:148
  57.2 25.6 %collective-permute-start.7 = (bf16[512,1024]{1,0:T(8,128)(2,1)S(1)}, bf16[512,1024]{1,0:T(8,128)(2,1)S(1)}, u32[]{:S(2)}, u32[]{:S(2)}) collective-permute-start(bf16[512,1024]{1,0:T(8,128)(2,1)S(1)} %copy-done.110), channel_id=1, source_target_pairs={{0,8},{8,0},{16,24},{24,16},{1,9},{9,1},{17,25},{25,17},{2,10},{10... | collective-permute-start | bytes 3145736 | tf_op jit(solution)/shard_map/ppermute | solution.py:148
  58.0 25.2 %collective-permute-start.8 = (bf16[512,1024]{1,0:T(8,128)(2,1)S(1)}, bf16[512,1024]{1,0:T(8,128)(2,1)S(1)}, u32[]{:S(2)}, u32[]{:S(2)}) collective-permute-start(bf16[512,1024]{1,0:T(8,128)(2,1)S(1)} %copy-done.109), channel_id=1, source_target_pairs={{0,16},{8,24},{16,0},{24,8},{1,17},{9,25},{17,1},{25,9},{2,18},{10... | collective-permute-start | bytes 3145736 | tf_op jit(solution)/shard_map/ppermute | solution.py:148
  83.2 25.3 %collective-permute-start.13 = (bf16[512,1024]{1,0:T(8,128)(2,1)S(1)}, bf16[512,1024]{1,0:T(8,128)(2,1)S(1)}, u32[]{:S(2)}, u32[]{:S(2)}) collective-permute-start(bf16[512,1024]{1,0:T(8,128)(2,1)S(1)} %pad_maximum_fusion.2), channel_id=1, source_target_pairs={{0,24},{8,16},{16,8},{24,0},{1,25},{9,17},{17,9},{25,1},{2,26},{10... | collective-permute-start | bytes 3145736 | tf_op jit(solution)/shard_map/ppermute | solution.py:148
  85.4 21.4 %collective-permute-start.11 = (bf16[2,512,128]{2,1,0:T(8,128)(2,1)S(1)}, bf16[2,512,128]{2,1,0:T(8,128)(2,1)S(1)}, u32[]{:S(2)}, u32[]{:S(2)}) collective-permute-start(bf16[2,512,128]{2,1,0:T(8,128)(2,1)S(1)} %get-tuple-element.333.refs_0_), channel_id=1, source_target_pairs={{0,4},{2,6},{4,0},{6,2},{1,5},{3,7},{5,1},{7,3},{8,12},{10,14},{12... | collective-permute-start | bytes 786440 | tf_op jit(solution)/shard_map/ppermute | solution.py:148
  88.0 19.5 %collective-permute-start.12 = (bf16[2,512,128]{2,1,0:T(8,128)(2,1)S(1)}, bf16[2,512,128]{2,1,0:T(8,128)(2,1)S(1)}, u32[]{:S(2)}, u32[]{:S(2)}) collective-permute-start(bf16[2,512,128]{2,1,0:T(8,128)(2,1)S(1)} %get-tuple-element.333.refs_0_), channel_id=1, source_target_pairs={{0,6},{2,4},{4,2},{6,0},{1,7},{3,5},{5,3},{7,1},{8,14},{10,12},{12... | collective-permute-start | bytes 786440 | tf_op jit(solution)/shard_map/ppermute | solution.py:148
  108.5 28.5 %collective-permute-start.17 = (bf16[512,1024]{1,0:T(8,128)(2,1)S(1)}, bf16[512,1024]{1,0:T(8,128)(2,1)}, u32[]{:S(2)}, u32[]{:S(2)}) collective-permute-start(bf16[512,1024]{1,0:T(8,128)(2,1)S(1)} %collective-permute-done.7.refs_4_.refs_5_.refs_2_.refs_3_), channel_id=1, source_target_pairs={{0,2},{2,0},{4,6},{6,4},{1,3},{3,1},{5,7},{7,5},{8,10},{10,8},{12,... | collective-permute-start | bytes 3145736 | tf_op jit(solution)/shard_map/ppermute | solution.py:148
  111.7 25.2 %collective-permute-start.14 = (bf16[128,2048]{1,0:T(8,128)(2,1)}, bf16[128,2048]{1,0:T(8,128)(2,1)}, u32[]{:S(2)}, u32[]{:S(2)}) collective-permute-start(bf16[128,2048]{1,0:T(8,128)(2,1)} %get-tuple-element.340), channel_id=1, source_target_pairs={{0,8},{8,0},{16,24},{24,16},{1,9},{9,1},{17,25},{25,17},{2,10},{10... | collective-permute-start | bytes 1572872 | tf_op jit(solution)/shard_map/ppermute | solution.py:148
  112.4 24.5 %collective-permute-start.15 = (bf16[128,2048]{1,0:T(8,128)(2,1)}, bf16[128,2048]{1,0:T(8,128)(2,1)}, u32[]{:S(2)}, u32[]{:S(2)}) collective-permute-start(bf16[128,2048]{1,0:T(8,128)(2,1)} %get-tuple-element.341), channel_id=1, source_target_pairs={{0,16},{8,24},{16,0},{24,8},{1,17},{9,25},{17,1},{25,9},{2,18},{10... | collective-permute-start | bytes 1572872 | tf_op jit(solution)/shard_map/ppermute | solution.py:148
  113.5 23.5 %collective-permute-start.16 = (bf16[128,2048]{1,0:T(8,128)(2,1)}, bf16[128,2048]{1,0:T(8,128)(2,1)}, u32[]{:S(2)}, u32[]{:S(2)}) collective-permute-start(bf16[128,2048]{1,0:T(8,128)(2,1)} %get-tuple-element.342), channel_id=1, source_target_pairs={{0,24},{8,16},{16,8},{24,0},{1,25},{9,17},{17,9},{25,1},{2,26},{10... | collective-permute-start | bytes 1572872 | tf_op jit(solution)/shard_map/ppermute | solution.py:148
  141.2 26.2 %collective-permute-start.19 = (bf16[512,1024]{1,0:T(8,128)(2,1)S(1)}, bf16[512,1024]{1,0:T(8,128)(2,1)S(1)}, u32[]{:S(2)}, u32[]{:S(2)}) collective-permute-start(bf16[512,1024]{1,0:T(8,128)(2,1)S(1)} %collective-permute-done.8.refs_6_.refs_7_.refs_4_.refs_5_), channel_id=1, source_target_pairs={{0,2},{2,0},{4,6},{6,4},{1,3},{3,1},{5,7},{7,5},{8,10},{10,8},{12,... | collective-permute-start | bytes 3145736 | tf_op jit(solution)/shard_map/ppermute | solution.py:148
  143.6 23.8 %collective-permute-start.22 = (bf16[128,2048]{1,0:T(8,128)(2,1)S(1)}, bf16[128,2048]{1,0:T(8,128)(2,1)S(1)}, u32[]{:S(2)}, u32[]{:S(2)}) collective-permute-start(bf16[128,2048]{1,0:T(8,128)(2,1)S(1)} %get-tuple-element.362), channel_id=1, source_target_pairs={{0,24},{8,16},{16,8},{24,0},{1,25},{9,17},{17,9},{25,1},{2,26},{10... | collective-permute-start | bytes 1572872 | tf_op jit(solution)/shard_map/ppermute | solution.py:148
  167.4 30.0 %collective-permute-start.24 = (bf16[512,2048]{1,0:T(8,128)(2,1)S(1)}, bf16[512,2048]{1,0:T(8,128)(2,1)S(1)}, u32[]{:S(2)}, u32[]{:S(2)}) collective-permute-start(bf16[512,2048]{1,0:T(8,128)(2,1)S(1)} %shard_map.220.refs_1_.refs_0_), channel_id=1, source_target_pairs={{0,1},{1,0},{2,3},{3,2},{4,5},{5,4},{6,7},{7,6},{8,9},{9,8},{10,11... | collective-permute-start | bytes 6291464 | tf_op jit(solution)/shard_map/ppermute | solution.py:148
  167.4 30.0 %collective-permute-start.23 = (bf16[512,1024]{1,0:T(8,128)(2,1)S(1)}, bf16[512,1024]{1,0:T(8,128)(2,1)S(1)}, u32[]{:S(2)}, u32[]{:S(2)}) collective-permute-start(bf16[512,1024]{1,0:T(8,128)(2,1)S(1)} %collective-permute-done.13.refs_8_.refs_9_.refs_6_.refs_7_), channel_id=1, source_target_pairs={{0,2},{2,0},{4,6},{6,4},{1,3},{3,1},{5,7},{7,5},{8,10},{10,8},{12,... | collective-permute-start | bytes 3145736 | tf_op jit(solution)/shard_map/ppermute | solution.py:148
  172.5 24.9 %collective-permute-start.26 = (bf16[128,2048]{1,0:T(8,128)(2,1)S(1)}, bf16[128,2048]{1,0:T(8,128)(2,1)S(1)}, u32[]{:S(2)}, u32[]{:S(2)}) collective-permute-start(bf16[128,2048]{1,0:T(8,128)(2,1)S(1)} %get-tuple-element.376), channel_id=1, source_target_pairs={{0,16},{8,24},{16,0},{24,8},{1,17},{9,25},{17,1},{25,9},{2,18},{10... | collective-permute-start | bytes 1572872 | tf_op jit(solution)/shard_map/ppermute | solution.py:148
  173.5 23.9 %collective-permute-start.27 = (bf16[128,2048]{1,0:T(8,128)(2,1)S(1)}, bf16[128,2048]{1,0:T(8,128)(2,1)S(1)}, u32[]{:S(2)}, u32[]{:S(2)}) collective-permute-start(bf16[128,2048]{1,0:T(8,128)(2,1)S(1)} %get-tuple-element.377), channel_id=1, source_target_pairs={{0,24},{8,16},{16,8},{24,0},{1,25},{9,17},{17,9},{25,1},{2,26},{10... | collective-permute-start | bytes 1572872 | tf_op jit(solution)/shard_map/ppermute | solution.py:148
  197.7 26.0 %collective-permute-start.28 = (bf16[512,1024]{1,0:T(8,128)(2,1)S(1)}, bf16[512,1024]{1,0:T(8,128)(2,1)S(1)}, u32[]{:S(2)}, u32[]{:S(2)}) collective-permute-start(bf16[512,1024]{1,0:T(8,128)(2,1)S(1)} %pad_maximum_fusion.3), channel_id=1, source_target_pairs={{0,8},{8,0},{16,24},{24,16},{1,9},{9,1},{17,25},{25,17},{2,10},{10... | collective-permute-start | bytes 3145736 | tf_op jit(solution)/shard_map/ppermute | solution.py:148
  198.5 26.2 %collective-permute-start.29 = (bf16[512,1024]{1,0:T(8,128)(2,1)S(1)}, bf16[512,1024]{1,0:T(8,128)(2,1)S(1)}, u32[]{:S(2)}, u32[]{:S(2)}) collective-permute-start(bf16[512,1024]{1,0:T(8,128)(2,1)S(1)} %pad_maximum_fusion.4), channel_id=1, source_target_pairs={{0,16},{8,24},{16,0},{24,8},{1,17},{9,25},{17,1},{25,9},{2,18},{10... | collective-permute-start | bytes 3145736 | tf_op jit(solution)/shard_map/ppermute | solution.py:148
  225.6 25.5 %collective-permute-start.32 = (bf16[512,1024]{1,0:T(8,128)(2,1)}, bf16[512,1024]{1,0:T(8,128)(2,1)}, u32[]{:S(2)}, u32[]{:S(2)}) collective-permute-start(bf16[512,1024]{1,0:T(8,128)(2,1)} %get-tuple-element.397), channel_id=1, source_target_pairs={{0,8},{8,0},{16,24},{24,16},{1,9},{9,1},{17,25},{25,17},{2,10},{10... | collective-permute-start | bytes 3145736 | tf_op jit(solution)/shard_map/ppermute | solution.py:148
  226.4 25.2 %collective-permute-start.33 = (bf16[512,1024]{1,0:T(8,128)(2,1)}, bf16[512,1024]{1,0:T(8,128)(2,1)}, u32[]{:S(2)}, u32[]{:S(2)}) collective-permute-start(bf16[512,1024]{1,0:T(8,128)(2,1)} %get-tuple-element.398), channel_id=1, source_target_pairs={{0,16},{8,24},{16,0},{24,8},{1,17},{9,25},{17,1},{25,9},{2,18},{10... | collective-permute-start | bytes 3145736 | tf_op jit(solution)/shard_map/ppermute | solution.py:148
  227.4 24.6 %collective-permute-start.31 = (bf16[512,1024]{1,0:T(8,128)(2,1)}, bf16[512,1024]{1,0:T(8,128)(2,1)}, u32[]{:S(2)}, u32[]{:S(2)}) collective-permute-start(bf16[512,1024]{1,0:T(8,128)(2,1)} %get-tuple-element.396), channel_id=1, source_target_pairs={{0,2},{6,4},{1,3},{7,5},{8,10},{14,12},{9,11},{15,13},{16,18},{22,... | collective-permute-start | bytes 3145736 | tf_op jit(solution)/shard_map/ppermute | solution.py:148
  254.8 24.2 %collective-permute-start.35 = (bf16[512,1024]{1,0:T(8,128)(2,1)S(1)}, bf16[512,1024]{1,0:T(8,128)(2,1)S(1)}, u32[]{:S(2)}, u32[]{:S(2)}) collective-permute-start(bf16[512,1024]{1,0:T(8,128)(2,1)S(1)} %get-tuple-element.597), channel_id=1, source_target_pairs={{0,2},{6,4},{2,0},{4,6},{1,3},{7,5},{3,1},{5,7},{8,10},{14,12},{10... | collective-permute-start | bytes 3145736 | tf_op jit(solution)/shard_map/ppermute | solution.py:148
  257.0 22.0 %collective-permute-start.34 = (bf16[512,1024]{1,0:T(8,128)(2,1)S(1)}, bf16[512,1024]{1,0:T(8,128)(2,1)S(1)}, u32[]{:S(2)}, u32[]{:S(2)}) collective-permute-start(bf16[512,1024]{1,0:T(8,128)(2,1)S(1)} %get-tuple-element.598), channel_id=1, source_target_pairs={{2,4},{4,2},{3,5},{5,3},{10,12},{12,10},{11,13},{13,11},{18,20},{2... | collective-permute-start | bytes 3145736 | tf_op jit(solution)/shard_map/ppermute | solution.py:148
  257.8 32.1 %collective-permute-start.36 = (bf16[512,1024]{1,0:T(8,128)(2,1)S(1)}, bf16[512,1024]{1,0:T(8,128)(2,1)S(1)}, u32[]{:S(2)}, u32[]{:S(2)}) collective-permute-start(bf16[512,1024]{1,0:T(8,128)(2,1)S(1)} %pad_maximum_fusion.8), channel_id=1, source_target_pairs={{0,24},{8,16},{16,8},{24,0},{1,25},{9,17},{17,9},{25,1},{2,26},{10... | collective-permute-start | bytes 3145736 | tf_op jit(solution)/shard_map/ppermute | solution.py:148
  280.8 27.1 %collective-permute-start.37 = (bf16[512,1024]{1,0:T(8,128)(2,1)S(1)}, bf16[512,1024]{1,0:T(8,128)(2,1)S(1)}, u32[]{:S(2)}, u32[]{:S(2)}) collective-permute-start(bf16[512,1024]{1,0:T(8,128)(2,1)S(1)} %add_convert_fusion.24), channel_id=1, source_target_pairs={{2,4},{4,2},{3,5},{5,3},{10,12},{12,10},{11,13},{13,11},{18,20},{2... | collective-permute-start | bytes 3145736 | tf_op jit(solution)/shard_map/ppermute | solution.py:148
  283.9 26.8 %collective-permute-start.38 = (bf16[512,1024]{1,0:T(8,128)(2,1)S(1)}, bf16[512,1024]{1,0:T(8,128)(2,1)S(1)}, u32[]{:S(2)}, u32[]{:S(2)}) collective-permute-start(bf16[512,1024]{1,0:T(8,128)(2,1)S(1)} %fusion.refs_1_), channel_id=1, source_target_pairs={{0,2},{6,4},{2,0},{4,6},{1,3},{7,5},{3,1},{5,7},{8,10},{14,12},{10... | collective-permute-start | bytes 3145736 | tf_op jit(solution)/shard_map/ppermute | solution.py:148
  289.9 23.2 %collective-permute-start.39 = (bf16[512,1024]{1,0:T(8,128)(2,1)S(1)}, bf16[512,1024]{1,0:T(8,128)(2,1)S(1)}, u32[]{:S(2)}, u32[]{:S(2)}) collective-permute-start(bf16[512,1024]{1,0:T(8,128)(2,1)S(1)} %copy-done.95), channel_id=1, source_target_pairs={{0,24},{8,16},{16,8},{24,0},{1,25},{9,17},{17,9},{25,1},{2,26},{10... | collective-permute-start | bytes 3145736 | tf_op jit(solution)/shard_map/ppermute | solution.py:148
  315.3 21.4 %collective-permute-start.41 = (bf16[512,1024]{1,0:T(8,128)(2,1)S(1)}, bf16[512,1024]{1,0:T(8,128)(2,1)S(1)}, u32[]{:S(2)}, u32[]{:S(2)}) collective-permute-start(bf16[512,1024]{1,0:T(8,128)(2,1)S(1)} %fusion.1.refs_3_), channel_id=1, source_target_pairs={{0,2},{6,4},{2,0},{4,6},{1,3},{7,5},{3,1},{5,7},{8,10},{14,12},{10... | collective-permute-start | bytes 3145736 | tf_op jit(solution)/shard_map/ppermute | solution.py:148
  315.8 21.0 %collective-permute-start.40 = (bf16[512,1024]{1,0:T(8,128)(2,1)S(1)}, bf16[512,1024]{1,0:T(8,128)(2,1)S(1)}, u32[]{:S(2)}, u32[]{:S(2)}) collective-permute-start(bf16[512,1024]{1,0:T(8,128)(2,1)S(1)} %add_convert_fusion.22), channel_id=1, source_target_pairs={{2,4},{4,2},{3,5},{5,3},{10,12},{12,10},{11,13},{13,11},{18,20},{2... | collective-permute-start | bytes 3145736 | tf_op jit(solution)/shard_map/ppermute | solution.py:148
  316.5 39.1 %collective-permute-start.42 = (bf16[512,2048]{1,0:T(8,128)(2,1)S(1)}, bf16[512,2048]{1,0:T(8,128)(2,1)S(1)}, u32[]{:S(2)}, u32[]{:S(2)}) collective-permute-start(bf16[512,2048]{1,0:T(8,128)(2,1)S(1)} %shard_map.227), channel_id=1, source_target_pairs={{0,1},{1,0},{2,3},{3,2},{4,5},{5,4},{6,7},{7,6},{8,9},{9,8},{10,11... | collective-permute-start | bytes 6291464 | tf_op jit(solution)/shard_map/ppermute | solution.py:148
  319.7 35.8 %collective-permute-start.43 = (bf16[512,1024]{1,0:T(8,128)(2,1)}, bf16[512,1024]{1,0:T(8,128)(2,1)}, u32[]{:S(2)}, u32[]{:S(2)}) collective-permute-start(bf16[512,1024]{1,0:T(8,128)(2,1)} %get-tuple-element.431), channel_id=1, source_target_pairs={{0,8},{8,0},{16,24},{24,16},{1,9},{9,1},{17,25},{25,17},{2,10},{10... | collective-permute-start | bytes 3145736 | tf_op jit(solution)/shard_map/ppermute | solution.py:148
  321.0 34.5 %collective-permute-start.44 = (bf16[512,1024]{1,0:T(8,128)(2,1)}, bf16[512,1024]{1,0:T(8,128)(2,1)}, u32[]{:S(2)}, u32[]{:S(2)}) collective-permute-start(bf16[512,1024]{1,0:T(8,128)(2,1)} %get-tuple-element.432), channel_id=1, source_target_pairs={{0,16},{8,24},{16,0},{24,8},{1,17},{9,25},{17,1},{25,9},{2,18},{10... | collective-permute-start | bytes 3145736 | tf_op jit(solution)/shard_map/ppermute | solution.py:148
  339.1 21.8 %collective-permute-start.46 = (bf16[512,1024]{1,0:T(8,128)(2,1)S(1)}, bf16[512,1024]{1,0:T(8,128)(2,1)S(1)}, u32[]{:S(2)}, u32[]{:S(2)}) collective-permute-start(bf16[512,1024]{1,0:T(8,128)(2,1)S(1)} %fusion.2.refs_5_), channel_id=1, source_target_pairs={{0,2},{6,4},{2,0},{4,6},{1,3},{7,5},{3,1},{5,7},{8,10},{14,12},{10... | collective-permute-start | bytes 3145736 | tf_op jit(solution)/shard_map/ppermute | solution.py:148
  357.4 18.6 %collective-permute-start.48 = (bf16[128,2048]{1,0:T(8,128)(2,1)S(1)}, bf16[128,2048]{1,0:T(8,128)(2,1)S(1)}, u32[]{:S(2)}, u32[]{:S(2)}) collective-permute-start(bf16[128,2048]{1,0:T(8,128)(2,1)S(1)} %get-tuple-element.441), channel_id=1, source_target_pairs={{0,16},{8,24},{16,0},{24,8},{1,17},{9,25},{17,1},{25,9},{2,18},{10... | collective-permute-start | bytes 1572872 | tf_op jit(solution)/shard_map/ppermute | solution.py:148
  358.5 20.0 %collective-permute-start.49 = (bf16[128,2048]{1,0:T(8,128)(2,1)S(1)}, bf16[128,2048]{1,0:T(8,128)(2,1)S(1)}, u32[]{:S(2)}, u32[]{:S(2)}) collective-permute-start(bf16[128,2048]{1,0:T(8,128)(2,1)S(1)} %get-tuple-element.442), channel_id=1, source_target_pairs={{0,24},{8,16},{16,8},{24,0},{1,25},{9,17},{17,9},{25,1},{2,26},{10... | collective-permute-start | bytes 1572872 | tf_op jit(solution)/shard_map/ppermute | solution.py:148
  363.7 22.8 %collective-permute-start.51 = (bf16[512,1024]{1,0:T(8,128)(2,1)S(1)}, bf16[512,1024]{1,0:T(8,128)(2,1)S(1)}, u32[]{:S(2)}, u32[]{:S(2)}) collective-permute-start(bf16[512,1024]{1,0:T(8,128)(2,1)S(1)} %fusion.3.refs_7_), channel_id=1, source_target_pairs={{0,2},{6,4},{2,0},{4,6},{1,3},{7,5},{3,1},{5,7},{8,10},{14,12},{10... | collective-permute-start | bytes 3145736 | tf_op jit(solution)/shard_map/ppermute | solution.py:148
  367.7 18.8 %collective-permute-start.50 = (bf16[512,1024]{1,0:T(8,128)(2,1)S(1)}, bf16[512,1024]{1,0:T(8,128)(2,1)S(1)}, u32[]{:S(2)}, u32[]{:S(2)}) collective-permute-start(bf16[512,1024]{1,0:T(8,128)(2,1)S(1)} %add_convert_fusion.18), channel_id=1, source_target_pairs={{2,4},{4,2},{3,5},{5,3},{10,12},{12,10},{11,13},{13,11},{18,20},{2... | collective-permute-start | bytes 3145736 | tf_op jit(solution)/shard_map/ppermute | solution.py:148
  388.4 19.3 %collective-permute-start.56 = (bf16[512,1024]{1,0:T(8,128)(2,1)S(1)}, bf16[512,1024]{1,0:T(8,128)(2,1)S(1)}, u32[]{:S(2)}, u32[]{:S(2)}) collective-permute-start(bf16[512,1024]{1,0:T(8,128)(2,1)S(1)} %fusion.4.refs_1_), channel_id=1, source_target_pairs={{0,2},{6,4},{2,0},{4,6},{1,3},{7,5},{3,1},{5,7},{8,10},{14,12},{10... | collective-permute-start | bytes 3145736 | tf_op jit(solution)/shard_map/ppermute | solution.py:148
  406.1 30.4 %collective-permute-start.57 = (bf16[512,1024]{1,0:T(8,128)(2,1)S(1)}, bf16[512,1024]{1,0:T(8,128)(2,1)S(1)}, u32[]{:S(2)}, u32[]{:S(2)}) collective-permute-start(bf16[512,1024]{1,0:T(8,128)(2,1)S(1)} %copy-done.93), channel_id=1, source_target_pairs={{0,24},{8,16},{16,8},{24,0},{1,25},{9,17},{17,9},{25,1},{2,26},{10... | collective-permute-start | bytes 3145736 | tf_op jit(solution)/shard_map/ppermute | solution.py:148
  411.5 27.4 %collective-permute-start.60 = (bf16[512,1024]{1,0:T(8,128)(2,1)S(1)}, bf16[512,1024]{1,0:T(8,128)(2,1)S(1)}, u32[]{:S(2)}, u32[]{:S(2)}) collective-permute-start(bf16[512,1024]{1,0:T(8,128)(2,1)S(1)} %fusion.5.refs_1_), channel_id=1, source_target_pairs={{0,2},{6,4},{2,0},{4,6},{1,3},{7,5},{3,1},{5,7},{8,10},{14,12},{10... | collective-permute-start | bytes 3145736 | tf_op jit(solution)/shard_map/ppermute | solution.py:148
  414.1 24.9 %collective-permute-start.59 = (bf16[512,1024]{1,0:T(8,128)(2,1)S(1)}, bf16[512,1024]{1,0:T(8,128)(2,1)S(1)}, u32[]{:S(2)}, u32[]{:S(2)}) collective-permute-start(bf16[512,1024]{1,0:T(8,128)(2,1)S(1)} %add_convert_fusion.14), channel_id=1, source_target_pairs={{2,4},{4,2},{3,5},{5,3},{10,12},{12,10},{11,13},{13,11},{18,20},{2... | collective-permute-start | bytes 3145736 | tf_op jit(solution)/shard_map/ppermute | solution.py:148
  436.5 20.7 %collective-permute-start.61 = (bf16[512,1024]{1,0:T(8,128)(2,1)S(1)}, bf16[512,1024]{1,0:T(8,128)(2,1)S(1)}, u32[]{:S(2)}, u32[]{:S(2)}) collective-permute-start(bf16[512,1024]{1,0:T(8,128)(2,1)S(1)} %get-tuple-element.479), channel_id=1, source_target_pairs={{0,8},{8,0},{16,24},{24,16},{1,9},{9,1},{17,25},{25,17},{2,10},{10... | collective-permute-start | bytes 3145736 | tf_op jit(solution)/shard_map/ppermute | solution.py:148
  437.8 20.5 %collective-permute-start.62 = (bf16[512,1024]{1,0:T(8,128)(2,1)S(1)}, bf16[512,1024]{1,0:T(8,128)(2,1)S(1)}, u32[]{:S(2)}, u32[]{:S(2)}) collective-permute-start(bf16[512,1024]{1,0:T(8,128)(2,1)S(1)} %get-tuple-element.480), channel_id=1, source_target_pairs={{0,16},{8,24},{16,0},{24,8},{1,17},{9,25},{17,1},{25,9},{2,18},{10... | collective-permute-start | bytes 3145736 | tf_op jit(solution)/shard_map/ppermute | solution.py:148
  441.2 22.0 %collective-permute-start.64 = (bf16[512,1024]{1,0:T(8,128)(2,1)S(1)}, bf16[512,1024]{1,0:T(8,128)(2,1)S(1)}, u32[]{:S(2)}, u32[]{:S(2)}) collective-permute-start(bf16[512,1024]{1,0:T(8,128)(2,1)S(1)} %fusion.6.refs_3_), channel_id=1, source_target_pairs={{0,2},{6,4},{2,0},{4,6},{1,3},{7,5},{3,1},{5,7},{8,10},{14,12},{10... | collective-permute-start | bytes 3145736 | tf_op jit(solution)/shard_map/ppermute | solution.py:148
  443.9 19.4 %collective-permute-start.63 = (bf16[512,1024]{1,0:T(8,128)(2,1)S(1)}, bf16[512,1024]{1,0:T(8,128)(2,1)S(1)}, u32[]{:S(2)}, u32[]{:S(2)}) collective-permute-start(bf16[512,1024]{1,0:T(8,128)(2,1)S(1)} %add_convert_fusion.12), channel_id=1, source_target_pairs={{2,4},{4,2},{3,5},{5,3},{10,12},{12,10},{11,13},{13,11},{18,20},{2... | collective-permute-start | bytes 3145736 | tf_op jit(solution)/shard_map/ppermute | solution.py:148
  458.3 26.5 %collective-permute-start.66 = (bf16[512,2048]{1,0:T(8,128)(2,1)S(1)}, bf16[512,2048]{1,0:T(8,128)(2,1)S(1)}, u32[]{:S(2)}, u32[]{:S(2)}) collective-permute-start(bf16[512,2048]{1,0:T(8,128)(2,1)S(1)} %get-tuple-element.489), channel_id=1, source_target_pairs={{0,1},{1,0},{2,3},{3,2},{4,5},{5,4},{6,7},{7,6},{8,9},{9,8},{10,11... | collective-permute-start | bytes 6291464 | tf_op jit(solution)/shard_map/ppermute | solution.py:148
  458.3 26.5 %collective-permute-start.65 = (bf16[512,1024]{1,0:T(8,128)(2,1)S(1)}, bf16[512,1024]{1,0:T(8,128)(2,1)S(1)}, u32[]{:S(2)}, u32[]{:S(2)}) collective-permute-start(bf16[512,1024]{1,0:T(8,128)(2,1)S(1)} %get-tuple-element.488), channel_id=1, source_target_pairs={{0,24},{8,16},{16,8},{24,0},{1,25},{9,17},{17,9},{25,1},{2,26},{10... | collective-permute-start | bytes 3145736 | tf_op jit(solution)/shard_map/ppermute | solution.py:148
  464.3 23.7 %collective-permute-start.68 = (bf16[512,1024]{1,0:T(8,128)(2,1)S(1)}, bf16[512,1024]{1,0:T(8,128)(2,1)S(1)}, u32[]{:S(2)}, u32[]{:S(2)}) collective-permute-start(bf16[512,1024]{1,0:T(8,128)(2,1)S(1)} %fusion.7.refs_5_), channel_id=1, source_target_pairs={{0,2},{6,4},{2,0},{4,6},{1,3},{7,5},{3,1},{5,7},{8,10},{14,12},{10... | collective-permute-start | bytes 3145736 | tf_op jit(solution)/shard_map/ppermute | solution.py:148
  468.0 20.0 %collective-permute-start.67 = (bf16[512,1024]{1,0:T(8,128)(2,1)S(1)}, bf16[512,1024]{1,0:T(8,128)(2,1)S(1)}, u32[]{:S(2)}, u32[]{:S(2)}) collective-permute-start(bf16[512,1024]{1,0:T(8,128)(2,1)S(1)} %add_convert_fusion.10), channel_id=1, source_target_pairs={{2,4},{4,2},{3,5},{5,3},{10,12},{12,10},{11,13},{13,11},{18,20},{2... | collective-permute-start | bytes 3145736 | tf_op jit(solution)/shard_map/ppermute | solution.py:148
  489.0 27.2 %collective-permute-start.73 = (bf16[512,1024]{1,0:T(8,128)(2,1)S(1)}, bf16[512,1024]{1,0:T(8,128)(2,1)S(1)}, u32[]{:S(2)}, u32[]{:S(2)}) collective-permute-start(bf16[512,1024]{1,0:T(8,128)(2,1)S(1)} %fusion.8.sent_ref), channel_id=1, source_target_pairs={{0,2},{6,4},{2,0},{4,6},{1,3},{7,5},{3,1},{5,7},{8,10},{14,12},{10... | collective-permute-start | bytes 3145736 | tf_op jit(solution)/shard_map/ppermute | solution.py:148
  492.7 23.5 %collective-permute-start.72 = (bf16[512,1024]{1,0:T(8,128)(2,1)S(1)}, bf16[512,1024]{1,0:T(8,128)(2,1)S(1)}, u32[]{:S(2)}, u32[]{:S(2)}) collective-permute-start(bf16[512,1024]{1,0:T(8,128)(2,1)S(1)} %add_convert_fusion.8), channel_id=1, source_target_pairs={{2,4},{4,2},{3,5},{5,3},{10,12},{12,10},{11,13},{13,11},{18,20},{2... | collective-permute-start | bytes 3145736 | tf_op jit(solution)/shard_map/ppermute | solution.py:148
  496.6 19.6 %collective-permute-start.71 = (bf16[128,2048]{1,0:T(8,128)(2,1)S(1)}, bf16[128,2048]{1,0:T(8,128)(2,1)S(1)}, u32[]{:S(2)}, u32[]{:S(2)}) collective-permute-start(bf16[128,2048]{1,0:T(8,128)(2,1)S(1)} %get-tuple-element.499), channel_id=1, source_target_pairs={{0,24},{8,16},{16,8},{24,0},{1,25},{9,17},{17,9},{25,1},{2,26},{10... | collective-permute-start | bytes 1572872 | tf_op jit(solution)/shard_map/ppermute | solution.py:148
  517.3 20.8 %collective-permute-start.75 = (bf16[512,1024]{1,0:T(8,128)(2,1)S(1)}, bf16[512,1024]{1,0:T(8,128)(2,1)S(1)}, u32[]{:S(2)}, u32[]{:S(2)}) collective-permute-start(bf16[512,1024]{1,0:T(8,128)(2,1)S(1)} %fusion.9.refs_7_), channel_id=1, source_target_pairs={{0,2},{6,4},{2,0},{4,6},{1,3},{7,5},{3,1},{5,7},{8,10},{14,12},{10... | collective-permute-start | bytes 3145736 | tf_op jit(solution)/shard_map/ppermute | solution.py:148
  519.5 18.7 %collective-permute-start.74 = (bf16[512,1024]{1,0:T(8,128)(2,1)S(1)}, bf16[512,1024]{1,0:T(8,128)(2,1)S(1)}, u32[]{:S(2)}, u32[]{:S(2)}) collective-permute-start(bf16[512,1024]{1,0:T(8,128)(2,1)S(1)} %add_convert_fusion.6), channel_id=1, source_target_pairs={{2,4},{4,2},{3,5},{5,3},{10,12},{12,10},{11,13},{13,11},{18,20},{2... | collective-permute-start | bytes 3145736 | tf_op jit(solution)/shard_map/ppermute | solution.py:148
  539.2 22.0 %collective-permute-start.77 = (bf16[512,1024]{1,0:T(8,128)(2,1)S(1)}, bf16[512,1024]{1,0:T(8,128)(2,1)S(1)}, u32[]{:S(2)}, u32[]{:S(2)}) collective-permute-start(bf16[512,1024]{1,0:T(8,128)(2,1)S(1)} %fusion.10.refs_3_), channel_id=1, source_target_pairs={{0,2},{6,4},{2,0},{4,6},{1,3},{7,5},{3,1},{5,7},{8,10},{14,12},{10... | collective-permute-start | bytes 3145736 | tf_op jit(solution)/shard_map/ppermute | solution.py:148
  555.2 22.3 %collective-permute-start.80 = (bf16[512,2048]{1,0:T(8,128)(2,1)S(1)}, bf16[512,2048]{1,0:T(8,128)(2,1)S(1)}, u32[]{:S(2)}, u32[]{:S(2)}) collective-permute-start(bf16[512,2048]{1,0:T(8,128)(2,1)S(1)} %get-tuple-element.525), channel_id=1, source_target_pairs={{0,1},{1,0},{2,3},{3,2},{4,5},{5,4},{6,7},{7,6},{8,9},{9,8},{10,11... | collective-permute-start | bytes 6291464 | tf_op jit(solution)/shard_map/ppermute | solution.py:148
  562.1 21.0 %collective-permute-start.82 = (bf16[512,1024]{1,0:T(8,128)(2,1)S(1)}, bf16[512,1024]{1,0:T(8,128)(2,1)S(1)}, u32[]{:S(2)}, u32[]{:S(2)}) collective-permute-start(bf16[512,1024]{1,0:T(8,128)(2,1)S(1)} %fusion.11.refs_5_), channel_id=1, source_target_pairs={{0,2},{6,4},{2,0},{4,6},{1,3},{7,5},{3,1},{5,7},{8,10},{14,12},{10... | collective-permute-start | bytes 3145736 | tf_op jit(solution)/shard_map/ppermute | solution.py:148
  584.5 25.6 %collective-permute-start.84 = (bf16[128,2048]{1,0:T(8,128)(2,1)S(1)}, bf16[128,2048]{1,0:T(8,128)(2,1)S(1)}, u32[]{:S(2)}, u32[]{:S(2)}) collective-permute-start(bf16[128,2048]{1,0:T(8,128)(2,1)S(1)} %get-tuple-element.534), channel_id=1, source_target_pairs={{0,16},{8,24},{16,0},{24,8},{1,17},{9,25},{17,1},{25,9},{2,18},{10... | collective-permute-start | bytes 1572872 | tf_op jit(solution)/shard_map/ppermute | solution.py:148
  585.3 24.8 %collective-permute-start.85 = (bf16[128,2048]{1,0:T(8,128)(2,1)S(1)}, bf16[128,2048]{1,0:T(8,128)(2,1)S(1)}, u32[]{:S(2)}, u32[]{:S(2)}) collective-permute-start(bf16[128,2048]{1,0:T(8,128)(2,1)S(1)} %get-tuple-element.535), channel_id=1, source_target_pairs={{0,24},{8,16},{16,8},{24,0},{1,25},{9,17},{17,9},{25,1},{2,26},{10... | collective-permute-start | bytes 1572872 | tf_op jit(solution)/shard_map/ppermute | solution.py:148
  587.3 24.4 %collective-permute-start.86 = (bf16[512,640]{1,0:T(8,128)(2,1)S(1)}, bf16[512,640]{1,0:T(8,128)(2,1)S(1)}, u32[]{:S(2)}, u32[]{:S(2)}) collective-permute-start(bf16[512,640]{1,0:T(8,128)(2,1)S(1)} %add_convert_fusion.33), channel_id=1, source_target_pairs={{2,4},{4,2},{3,5},{5,3},{10,12},{12,10},{11,13},{13,11},{18,20},{2... | collective-permute-start | bytes 1966088 | tf_op jit(solution)/shard_map/ppermute | solution.py:148
  588.5 27.0 %collective-permute-start.87 = (bf16[512,1024]{1,0:T(8,128)(2,1)S(1)}, bf16[512,1024]{1,0:T(8,128)(2,1)S(1)}, u32[]{:S(2)}, u32[]{:S(2)}) collective-permute-start(bf16[512,1024]{1,0:T(8,128)(2,1)S(1)} %fusion.12.refs_7_), channel_id=1, source_target_pairs={{0,2},{6,4},{2,0},{4,6},{1,3},{7,5},{3,1},{5,7},{8,10},{14,12},{10... | collective-permute-start | bytes 3145736 | tf_op jit(solution)/shard_map/ppermute | solution.py:148
  (156 other events, 1569.0 us)

commit v9 on v8

--- a/solution.py
+++ b/solution.py
@@ -576,14 +576,14 @@
     refs[-1][...] = total.astype(jnp.bfloat16)
 
 
-def half_rows(lefts, rights, which):
+def half_rows(lefts, rights, which, cost=SMALL):
     half, width = lefts[0].shape[0] // 2, rights[0].shape[0]
     block = math.gcd(width, 512)
     ins = [(left, (half, left.shape[1]), lambda i: (which, 0)) for left in lefts]
     ins += [(right, (block, right.shape[1]), lambda i: (i, 0)) for right in rights]
     outs = [(low(half, width), (half, block), lambda i: (0, i))]
     kernel = functools.partial(half_rows_kernel, len(lefts))
-    return gridded(kernel, width // block, ins, outs)[0]
+    return gridded(kernel, width // block, ins, outs, cost=cost)[0]
 
 
 def weight_grad_kernel(count, terms, turn, *refs):
@@ -617,7 +617,8 @@
     columns = sum(right.shape[1] for _, _, right in terms)
     depth = terms[0][0].shape[1] // count
     packs = range(count) if packs is None else packs
-    first, apart = packs[0], packs[1] - packs[0]
+    first, apart = packs[0], packs[-1] - packs[0]
+    apart = apart // max(len(packs) - 1, 1)
     ins = []
     if side is not None:
         ins.append((side, None, None))
@@ -778,14 +779,14 @@
         row_delta = jnp.sum(probs * d_probs, axis=-1, keepdims=True)
         d_scores = (probs * (d_probs - row_delta)).astype(jnp.bfloat16)
         d_q.append(dot(d_scores, k) * scale)
-        d_k = d_k + contract_first(d_scores, q_head)
-        d_v = d_v + contract_first(probs.astype(jnp.bfloat16), d_head)
+        d_k = d_k + contract_first(q_head, d_scores)
+        d_v = d_v + contract_first(d_head, probs.astype(jnp.bfloat16))
     d_q = jnp.concatenate(d_q, axis=1)
     cosine = cos_ref[...].reshape(q.shape[0], -1)
     sine = sin_ref[...].reshape(q.shape[0], -1)
     d_q = turned(d_q, side_by_side(cosine, q.shape[1]), -side_by_side(sine, q.shape[1]))
     dq_ref[...] = d_q.astype(jnp.bfloat16).reshape(dq_ref.shape)
-    d_kv = jnp.concatenate([d_k, d_v], axis=1).astype(jnp.bfloat16)
+    d_kv = jnp.concatenate([d_k, d_v], axis=0).T.astype(jnp.bfloat16)
     half, lanes, cycle = dkv_ref.shape[0], 2 * HEAD_SIZE, len(kv_refs)
     for j in range(cycle):
         for core_side in range(2):
@@ -1078,14 +1079,12 @@
     wd_pieces = [own_down] + arrived("down")
     d_gate, d_up = units_back(all_cot, wd_pieces, gate_val, up_val)
     second = half_rows([d_gate, d_up], [wg, wu], 1)
-    d_wg = dict(zip((1, 2), weight_grad([(*normed_two, d_gate)], packs, side_arg, (1, 2))))
-    steps.step(to_core("d_two", second) + back("wg", d_wg, [1, 2]), summed=entry("wd", 3))
+    d_wg = dict(zip((0, 1, 2), weight_grad([(*normed_two, d_gate)], packs, side_arg, (0, 1, 2))))
+    steps.step(to_core("d_two", second) + back("wg", d_wg, [1, 2]), summed=entry("wg", 0, d_wg))
     first = half_rows([d_gate, d_up], [wg, wu], 0)
-    d_wg.update(zip((0, 3), weight_grad([(*normed_two, d_gate)], packs, side_arg, (0, 3))))
+    (d_wg[3],) = weight_grad([(*normed_two, d_gate)], packs, side_arg, (3,))
     d_wu = weight_grad([(*normed_two, d_up)], packs, side_arg)
-    steps.step(
-        summed=entry("wg", 0, d_wg), late=functools.partial(to_rows, "d_two", first)
-    )
+    steps.step(summed=entry("wd", 3), late=functools.partial(to_rows, "d_two", first))
 
     def branch_back():
         kept["d_middle"], kept["d_gain_two"], kept["d_branch"], *sends = in_vmem(
@@ -1100,12 +1099,13 @@
         return send_all("d_branch", sends)
 
     steps.step(summed=entry("wu", 0, d_wu), late=branch_back)
-    ff_first, ff_second = rows_sum([hidden], [join(wd_pieces[0], wd_pieces[1:])], LARGE)
-    ff_first, ff_second = steps.step(
+    wd = join(wd_pieces[0], wd_pieces[1:])
+    ff_second = half_rows([hidden], [wd], 1, LARGE)
+    (ff_second,) = steps.step(
         back("wg", d_wg, [3]),
         summed=entry("wg", 1),
         late=lambda: joined("all_branch", kept["d_branch"], arrived("d_branch")),
-        first=(ff_first, ff_second),
+        first=(ff_second,),
     )
     sums = steps.line.sums
 
@@ -1116,14 +1116,15 @@
     d_q, d_kv = attend_back(
         here_arg, q_rot, d_branch, cosine, sine, place_args, wo, kvs, packs, groups
     )
-    down_grad = settle_all("wd", LARGE)
-    d_q, d_kv, down_grad = steps.step(
-        back("wu", d_wu, [1, 2]), summed=entry("wg", 2), carry=(d_q, d_kv), first=(down_grad,)
+    ff_first = half_rows([hidden], [wd], 0, LARGE)
+    d_q, d_kv, ff_first = steps.step(
+        back("wu", d_wu, [1, 2]), summed=entry("wg", 2), carry=(d_q, d_kv), first=(ff_first,)
     )
     steps.step(back("wu", d_wu, [3]) + to_core("ff", ff_second), summed=("d_kv", d_kv))
     steps.step(summed=entry("wg", 3), late=functools.partial(to_rows, "ff", ff_first))
     steps.step(summed=entry("wu", 1))
-    steps.step(summed=entry("wu", 2))
+    down_grad = settle_all("wd", LARGE)
+    (down_grad,) = steps.step(summed=entry("wu", 2), first=(down_grad,))
     result = in_vmem(
         result_kernel, [low(half, width)], kept["middle"], kept["ff"], *arrived("ff")
     )[0]

time: 684 us -> 679 us (level)
  starting transfers between devices: 148 us -> 155 us
    ppermute x104, starting transfers between devices: 148 us -> 155 us  [start(): lax.ppermute(value, axis, pairs)]
    unnamed x230 -> x238, local copies, waits for them, and re-layouts: 31.9 us -> 29.1 us
    pallas_call x14 -> x15, Pallas kernels: 99 us -> 98 us  [gridded(): pl.pallas_call(kernel, grid=(steps,), in_specs=[pl.BlockSpec(memory_space...]
  transfers between devices with their start and end apart: 105 -> 105, of which waited for: 50 -> 50; matrix products, arithmetic and copies ran while one was open for 6% -> 6% of each run, Pallas kernels for 21% -> 20%
where the time goes in v9:
time: 679 us; the launch traced here: 672 us
  waiting for transfers between devices  287 us (42%)
  starting transfers between devices  155 us (23%)
  Pallas kernels  145 us (21%)
  local copies, waits for them, and re-layouts  45.5 us (7%)
  other arithmetic  36.9 us (5%)
    ppermute x104, waiting for transfers between devices, start(): lax.ppermute(value, axis, pairs)  285 us
    ppermute x104, starting transfers between devices, start(): lax.ppermute(value, axis, pairs)  155 us
    pallas_call x15, Pallas kernels, gridded(): pl.pallas_call(kernel, grid=(steps,), in_specs=[pl.BlockSpec(memory_space...  98 us
    unnamed x238, local copies, waits for them, and re-layouts  29.1 us
    pallas_call x5, Pallas kernels, weight_grad(): pl.pallas_call(functools.partial(weight_grad_kernel, len(packs), len(term...  27.6 us
    pallas_call x20, Pallas kernels, in_vmem(): pl.pallas_call(kernel, out_shape=out_shape, in_specs=specs, out_specs=[pl...  19.2 us
  transfers between devices with their start and end apart: 105, of which 50 were waited for; matrix products, arithmetic and copies ran while one was open for 6% of the time, Pallas kernels for 20%

profile of v9, /device:TPU:0, one launch (start us, length us, event | category | flops | bytes accessed | tf_op | source)
XLA Modules:
  0.0 672.3 jit_solution(4660275517939693203)
XLA Ops:
  13.9 3.1 constant_dynamic-slice_fusion.11
  17.7 4.3 constant_dynamic-slice_fusion.5
  36.5 8.9 %collective-permute-done.3.refs_1_ = bf16[128,2048]{1,0:T(8,128)(2,1)} collective-permute-done((bf16[128,2048]{1,0:T(8,128)(2,1)}, bf16[128,2048]{1,0:T(8,128)(2,1)}, u32[]{:S(2)}, u32[]{:S(2)}) %collective-permute-start.3) | collective-permute-done | bytes 524320 | tf_op jit(solution)/shard_map/ppermute | solution.py:148
  45.4 9.7 %collective-permute-done.4.refs_2_ = bf16[128,2048]{1,0:T(8,128)(2,1)} collective-permute-done((bf16[128,2048]{1,0:T(8,128)(2,1)}, bf16[128,2048]{1,0:T(8,128)(2,1)}, u32[]{:S(2)}, u32[]{:S(2)}) %collective-permute-start.4) | collective-permute-done | bytes 524320 | tf_op jit(solution)/shard_map/ppermute | solution.py:148
  61.3 5.4 shard_map.216
  71.3 11.4 %collective-permute-done.7.refs_4_.refs_5_.refs_2_.refs_3_ = bf16[512,1024]{1,0:T(8,128)(2,1)S(1)} collective-permute-done((bf16[512,1024]{1,0:T(8,128)(2,1)S(1)}, bf16[512,1024]{1,0:T(8,128)(2,1)S(1)}, u32[]{:S(2)}, u32[]{:S(2)}) %collective-permute-start.7) | collective-permute-done | bytes 1048608 | tf_op jit(solution)/shard_map/ppermute | solution.py:148
  92.6 4.6 collective-permute-done.10.refs_1_
  97.2 9.6 %collective-permute-done.11.refs_2_ = bf16[2,512,128]{2,1,0:T(8,128)(2,1)S(1)} collective-permute-done((bf16[2,512,128]{2,1,0:T(8,128)(2,1)S(1)}, bf16[2,512,128]{2,1,0:T(8,128)(2,1)S(1)}, u32[]{:S(2)}, u32[]{:S(2)}) %collective-permute-start.11) | collective-permute-done | bytes 262176 | tf_op jit(solution)/shard_map/ppermute | solution.py:148
  108.4 3.3 collective-permute-start.17
  124.5 12.5 %shard_map.218 = (bf16[2,512,256]{2,1,0:T(8,128)(2,1)S(1)}, bf16[512,2048]{1,0:T(8,128)(2,1)S(1)}, bf16[512,2048]{1,0:T(8,128)(2,1)S(1)}) custom-call(bf16[2,512,256]{2,1,0:T(8,128)(2,1)S(1)} %copy-done.48, s32[4,256,1]{2,1,0:T(8,128)S(1)} %copy-done.25, s32[4,256,1]{2,1,0:T(8,128)S(1)} %copy-done.27, s32[4,1,1024]{2,1,0:T(1,128)S(1)} %broadcast_add_fusion.key_place_ref, ...), custom_call_target="tpu_custom_call" | custom-call | flops 1 | bytes 1 | tf_op jit(solution)/shard_map/pallas_call | solution.py:324
  137.0 4.1 collective-permute-done.18.came_ref
  146.9 9.7 %collective-permute-done.20.refs_1_ = bf16[128,2048]{1,0:T(8,128)(2,1)S(1)} collective-permute-done((bf16[128,2048]{1,0:T(8,128)(2,1)S(1)}, bf16[128,2048]{1,0:T(8,128)(2,1)S(1)}, u32[]{:S(2)}, u32[]{:S(2)}) %collective-permute-start.20) | collective-permute-done | bytes 524320 | tf_op jit(solution)/shard_map/ppermute | solution.py:148
  157.1 10.4 %collective-permute-done.22.refs_3_ = bf16[128,2048]{1,0:T(8,128)(2,1)S(1)} collective-permute-done((bf16[128,2048]{1,0:T(8,128)(2,1)S(1)}, bf16[128,2048]{1,0:T(8,128)(2,1)S(1)}, u32[]{:S(2)}, u32[]{:S(2)}) %collective-permute-start.22) | collective-permute-done | bytes 524320 | tf_op jit(solution)/shard_map/ppermute | solution.py:148
  177.2 8.7 %collective-permute-done.25.refs_1_ = bf16[128,2048]{1,0:T(8,128)(2,1)S(1)} collective-permute-done((bf16[128,2048]{1,0:T(8,128)(2,1)S(1)}, bf16[128,2048]{1,0:T(8,128)(2,1)S(1)}, u32[]{:S(2)}, u32[]{:S(2)}) %collective-permute-start.25) | collective-permute-done | bytes 524320 | tf_op jit(solution)/shard_map/ppermute | solution.py:148
  185.9 11.5 %collective-permute-done.26.refs_2_ = bf16[128,2048]{1,0:T(8,128)(2,1)S(1)} collective-permute-done((bf16[128,2048]{1,0:T(8,128)(2,1)S(1)}, bf16[128,2048]{1,0:T(8,128)(2,1)S(1)}, u32[]{:S(2)}, u32[]{:S(2)}) %collective-permute-start.26) | collective-permute-done | bytes 524320 | tf_op jit(solution)/shard_map/ppermute | solution.py:148
  201.9 12.5 %shard_map.223 = (bf16[1024,1024]{1,0:T(8,128)(2,1)S(1)}, bf16[1024,1024]{1,0:T(8,128)(2,1)S(1)}, bf16[1024,1024]{1,0:T(8,128)(2,1)S(1)}) custom-call(bf16[512,2048]{1,0:T(8,128)(2,1)S(1)} %shard_map.222.refs_0_.refs_1_, bf16[512,2048]{1,0:T(8,128)(2,1)S(1)} %collective-permute-done.30.refs_1_.refs_2_, ...), custom_call_target="tpu_custom_call" | custom-call | flops 1 | bytes 1 | tf_op jit(solution)/shard_map/pallas_call | solution.py:324
  214.5 8.2 %shard_map.224 = (bf16[512,1024]{1,0:T(8,128)(2,1)}, bf16[512,1024]{1,0:T(8,128)(2,1)}, bf16[512,1024]{1,0:T(8,128)(2,1)}, bf16[512,1024]{1,0:T(8,128)(2,1)}) custom-call(s32[1]{0:T(128)S(6)} %and.22.side_ref.refs_0_, bf16[512,2048]{1,0:T(8,128)(2,1)S(1)} %shard_map.220.refs_1_.refs_0_, bf16[512,2048]{1,0:T(8,128)(2,1)S(1)} %collective-permute-done.24.refs_2_.refs_1_, ...), custom_call_target="tpu_custom_call" | custom-call | flops 1 | bytes 1 | tf_op jit(solution)/shard_map/pallas_call | solution.py:633
  227.1 3.2 collective-permute-start.31
  237.0 4.2 shard_map.225
  241.2 9.1 %collective-permute-done.32 = bf16[512,1024]{1,0:T(8,128)(2,1)} collective-permute-done((bf16[512,1024]{1,0:T(8,128)(2,1)}, bf16[512,1024]{1,0:T(8,128)(2,1)}, u32[]{:S(2)}, u32[]{:S(2)}) %collective-permute-start.32) | collective-permute-done | bytes 1048608 | tf_op jit(solution)/shard_map/ppermute | solution.py:148
  258.7 18.9 %collective-permute-done.35 = bf16[512,1024]{1,0:T(8,128)(2,1)S(1)} collective-permute-done((bf16[512,1024]{1,0:T(8,128)(2,1)S(1)}, bf16[512,1024]{1,0:T(8,128)(2,1)S(1)}, u32[]{:S(2)}, u32[]{:S(2)}) %collective-permute-start.35) | collective-permute-done | bytes 1048608 | tf_op jit(solution)/shard_map/ppermute | solution.py:148
  282.5 6.0 collective-permute-start.38
  290.4 6.7 shard_map.226
  297.0 4.4 shard_map.227
  301.5 7.2 %collective-permute-done.38.refs_0_ = bf16[512,1024]{1,0:T(8,128)(2,1)S(1)} collective-permute-done((bf16[512,1024]{1,0:T(8,128)(2,1)S(1)}, bf16[512,1024]{1,0:T(8,128)(2,1)S(1)}, u32[]{:S(2)}, u32[]{:S(2)}) %collective-permute-start.38) | collective-permute-done | bytes 1048608 | tf_op jit(solution)/shard_map/ppermute | solution.py:148
  313.9 5.5 shard_map.228
  322.0 10.9 %collective-permute-done.41.refs_2_ = bf16[512,1024]{1,0:T(8,128)(2,1)S(1)} collective-permute-done((bf16[512,1024]{1,0:T(8,128)(2,1)S(1)}, bf16[512,1024]{1,0:T(8,128)(2,1)S(1)}, u32[]{:S(2)}, u32[]{:S(2)}) %collective-permute-start.41) | collective-permute-done | bytes 1048608 | tf_op jit(solution)/shard_map/ppermute | solution.py:148
  339.6 5.3 shard_map.230.first_ref
  344.9 5.9 shard_map.229
  360.2 3.4 collective-permute-start.51
  364.4 3.1 shard_map.233
  371.5 3.5 collective-permute-done.49.refs_3_
  383.3 3.3 collective-permute-start.56
  388.8 7.0 %collective-permute-done.53.refs_2_ = bf16[128,2048]{1,0:T(8,128)(2,1)S(1)} collective-permute-done((bf16[128,2048]{1,0:T(8,128)(2,1)S(1)}, bf16[128,2048]{1,0:T(8,128)(2,1)S(1)}, u32[]{:S(2)}, u32[]{:S(2)}) %collective-permute-start.53) | collective-permute-done | bytes 524320 | tf_op jit(solution)/shard_map/ppermute | solution.py:148
  396.0 3.6 shard_map.236.first_ref
  404.9 3.7 collective-permute-start.60
  409.4 19.0 %shard_map.238 = (bf16[2,512,256]{2,1,0:T(8,128)(2,1)S(1)}, bf16[512,1024]{1,0:T(8,128)(2,1)S(1)}) custom-call(s32[1]{0:T(128)} %bitcast.5.here_ref, bf16[2,512,256]{2,1,0:T(8,128)(2,1)S(1)} %copy-done.49, bf16[512,2048]{1,0:T(8,128)(2,1)S(1)} %shard_map.237.mine_ref.refs_3_, bf16[512,2048]{1,0:T(8,128)(2,1)S(1)} %collective-permute-done.58.other_ref.refs_4_, ...), custom_call_target="tpu_custom_call" | custom-call | flops 1 | bytes 1 | tf_op jit(solution)/shard_map/pallas_call | solution.py:324
  435.7 15.2 %collective-permute-done.61 = bf16[512,1024]{1,0:T(8,128)(2,1)S(1)} collective-permute-done((bf16[512,1024]{1,0:T(8,128)(2,1)S(1)}, bf16[512,1024]{1,0:T(8,128)(2,1)S(1)}, u32[]{:S(2)}, u32[]{:S(2)}) %collective-permute-start.61) | collective-permute-done | bytes 1048608 | tf_op jit(solution)/shard_map/ppermute | solution.py:148
  454.2 3.7 collective-permute-start.68
  458.7 19.2 %collective-permute-done.65 = bf16[512,1024]{1,0:T(8,128)(2,1)S(1)} collective-permute-done((bf16[512,1024]{1,0:T(8,128)(2,1)S(1)}, bf16[512,1024]{1,0:T(8,128)(2,1)S(1)}, u32[]{:S(2)}, u32[]{:S(2)}) %collective-permute-start.65) | collective-permute-done | bytes 1048608 | tf_op jit(solution)/shard_map/ppermute | solution.py:148
  484.5 3.7 collective-permute-start.73
  489.0 4.4 shard_map.240
  495.2 9.4 %collective-permute-done.70.refs_2_ = bf16[128,2048]{1,0:T(8,128)(2,1)S(1)} collective-permute-done((bf16[128,2048]{1,0:T(8,128)(2,1)S(1)}, bf16[128,2048]{1,0:T(8,128)(2,1)S(1)}, u32[]{:S(2)}, u32[]{:S(2)}) %collective-permute-start.70) | collective-permute-done | bytes 524320 | tf_op jit(solution)/shard_map/ppermute | solution.py:148
  504.6 3.2 collective-permute-done.73.came_ref
  508.9 3.7 collective-permute-start.75
  513.3 18.0 %collective-permute-done.75.refs_6_ = bf16[512,1024]{1,0:T(8,128)(2,1)S(1)} collective-permute-done((bf16[512,1024]{1,0:T(8,128)(2,1)S(1)}, bf16[512,1024]{1,0:T(8,128)(2,1)S(1)}, u32[]{:S(2)}, u32[]{:S(2)}) %collective-permute-start.75) | collective-permute-done | bytes 1048608 | tf_op jit(solution)/shard_map/ppermute | solution.py:148
  532.3 3.7 collective-permute-start.77
  537.2 3.3 shard_map.243
  540.5 7.8 %shard_map.242 = (bf16[512,640]{1,0:T(8,128)(2,1)S(1)}, bf16[512,640]{1,0:T(8,128)(2,1)S(1)}, bf16[512,640]{1,0:T(8,128)(2,1)S(1)}, bf16[512,640]{1,0:T(8,128)(2,1)S(1)}) custom-call(bf16[512,2048]{1,0:T(8,128)(2,1)S(1)} %copy-done.42, bf16[512,2048]{1,0:T(8,128)(2,1)S(1)} %copy-done.44, bf16[1024,384]{1,0:T(8,128)(2,1)S(1)} %shard_map.241.refs_2_.refs_0_, ...), custom_call_target="tpu_custom_call" | custom-call | flops 1 | bytes 1 | tf_op jit(solution)/shard_map/pallas_call | solution.py:633
  548.4 5.6 collective-permute-done.77.refs_2_
  554.9 4.0 collective-permute-start.82
  561.6 8.6 %collective-permute-done.78 = bf16[512,640]{1,0:T(8,128)(2,1)S(1)} collective-permute-done((bf16[512,640]{1,0:T(8,128)(2,1)S(1)}, bf16[512,640]{1,0:T(8,128)(2,1)S(1)}, u32[]{:S(2)}, u32[]{:S(2)}) %collective-permute-start.78) | collective-permute-done | bytes 655392 | tf_op jit(solution)/shard_map/ppermute | solution.py:148
  570.8 5.5 collective-permute-done.82.refs_4_
  581.7 6.7 collective-permute-start.87
  588.4 4.2 shard_map.245
  592.5 8.0 %collective-permute-done.85.refs_3_ = bf16[128,2048]{1,0:T(8,128)(2,1)S(1)} collective-permute-done((bf16[128,2048]{1,0:T(8,128)(2,1)S(1)}, bf16[128,2048]{1,0:T(8,128)(2,1)S(1)}, u32[]{:S(2)}, u32[]{:S(2)}) %collective-permute-start.85) | collective-permute-done | bytes 524320 | tf_op jit(solution)/shard_map/ppermute | solution.py:148
  600.5 4.0 collective-permute-start.88
  604.6 4.6 collective-permute-done.87.refs_6_
  615.4 6.4 collective-permute-done.92.refs_0_
  622.2 4.3 collective-permute-start.97
  631.1 4.2 shard_map.249
  642.0 8.6 %collective-permute-done.100.refs_4_ = bf16[512,640]{1,0:T(8,128)(2,1)S(1)} collective-permute-done((bf16[512,640]{1,0:T(8,128)(2,1)S(1)}, bf16[512,640]{1,0:T(8,128)(2,1)S(1)}, u32[]{:S(2)}, u32[]{:S(2)}) %collective-permute-start.100) | collective-permute-done | bytes 655392 | tf_op jit(solution)/shard_map/ppermute | solution.py:148
  654.5 4.8 collective-permute-start.102
  667.7 4.4 shard_map.251
  (516 shorter events, 218.7 us)
Async XLA Ops:
  6.6 18.8 %collective-permute-start = (bf16[272,640]{1,0:T(8,128)(2,1)}, bf16[272,640]{1,0:T(8,128)(2,1)S(1)}, u32[]{:S(2)}, u32[]{:S(2)}) collective-permute-start(bf16[272,640]{1,0:T(8,128)(2,1)} %get-tuple-element.301), channel_id=1, source_target_pairs={{0,8},{8,0},{16,24},{24,16},{1,9},{9,1},{17,25},{25,17},{2,10},{10... | collective-permute-start | bytes 1044488 | tf_op jit(solution)/shard_map/ppermute | solution.py:148
  28.3 26.8 %collective-permute-start.6 = (bf16[768,640]{1,0:T(8,128)(2,1)}, bf16[768,640]{1,0:T(8,128)(2,1)S(1)}, u32[]{:S(2)}, u32[]{:S(2)}) collective-permute-start(bf16[768,640]{1,0:T(8,128)(2,1)} %shard_map.213), channel_id=1, source_target_pairs={{0,2},{2,0},{4,6},{6,4},{1,3},{3,1},{5,7},{7,5},{8,10},{10,8},{12,... | collective-permute-start | bytes 2949128 | tf_op jit(solution)/shard_map/ppermute | solution.py:148
  31.3 23.8 %collective-permute-start.4 = (bf16[128,2048]{1,0:T(8,128)(2,1)}, bf16[128,2048]{1,0:T(8,128)(2,1)}, u32[]{:S(2)}, u32[]{:S(2)}) collective-permute-start(bf16[128,2048]{1,0:T(8,128)(2,1)} %get-tuple-element.309), channel_id=1, source_target_pairs={{0,16},{8,24},{16,0},{24,8},{1,17},{9,25},{17,1},{25,9},{2,18},{10... | collective-permute-start | bytes 1572872 | tf_op jit(solution)/shard_map/ppermute | solution.py:148
  32.3 22.8 %collective-permute-start.5 = (bf16[128,2048]{1,0:T(8,128)(2,1)}, bf16[128,2048]{1,0:T(8,128)(2,1)}, u32[]{:S(2)}, u32[]{:S(2)}) collective-permute-start(bf16[128,2048]{1,0:T(8,128)(2,1)} %get-tuple-element.310), channel_id=1, source_target_pairs={{0,24},{8,16},{16,8},{24,0},{1,25},{9,17},{17,9},{25,1},{2,26},{10... | collective-permute-start | bytes 1572872 | tf_op jit(solution)/shard_map/ppermute | solution.py:148
  57.2 25.6 %collective-permute-start.7 = (bf16[512,1024]{1,0:T(8,128)(2,1)S(1)}, bf16[512,1024]{1,0:T(8,128)(2,1)S(1)}, u32[]{:S(2)}, u32[]{:S(2)}) collective-permute-start(bf16[512,1024]{1,0:T(8,128)(2,1)S(1)} %copy-done.114), channel_id=1, source_target_pairs={{0,8},{8,0},{16,24},{24,16},{1,9},{9,1},{17,25},{25,17},{2,10},{10... | collective-permute-start | bytes 3145736 | tf_op jit(solution)/shard_map/ppermute | solution.py:148
  57.9 25.2 %collective-permute-start.8 = (bf16[512,1024]{1,0:T(8,128)(2,1)S(1)}, bf16[512,1024]{1,0:T(8,128)(2,1)S(1)}, u32[]{:S(2)}, u32[]{:S(2)}) collective-permute-start(bf16[512,1024]{1,0:T(8,128)(2,1)S(1)} %copy-done.113), channel_id=1, source_target_pairs={{0,16},{8,24},{16,0},{24,8},{1,17},{9,25},{17,1},{25,9},{2,18},{10... | collective-permute-start | bytes 3145736 | tf_op jit(solution)/shard_map/ppermute | solution.py:148
  83.1 25.3 %collective-permute-start.13 = (bf16[512,1024]{1,0:T(8,128)(2,1)S(1)}, bf16[512,1024]{1,0:T(8,128)(2,1)S(1)}, u32[]{:S(2)}, u32[]{:S(2)}) collective-permute-start(bf16[512,1024]{1,0:T(8,128)(2,1)S(1)} %pad_maximum_fusion.2), channel_id=1, source_target_pairs={{0,24},{8,16},{16,8},{24,0},{1,25},{9,17},{17,9},{25,1},{2,26},{10... | collective-permute-start | bytes 3145736 | tf_op jit(solution)/shard_map/ppermute | solution.py:148
  85.4 21.4 %collective-permute-start.11 = (bf16[2,512,128]{2,1,0:T(8,128)(2,1)S(1)}, bf16[2,512,128]{2,1,0:T(8,128)(2,1)S(1)}, u32[]{:S(2)}, u32[]{:S(2)}) collective-permute-start(bf16[2,512,128]{2,1,0:T(8,128)(2,1)S(1)} %get-tuple-element.331.refs_0_), channel_id=1, source_target_pairs={{0,4},{2,6},{4,0},{6,2},{1,5},{3,7},{5,1},{7,3},{8,12},{10,14},{12... | collective-permute-start | bytes 786440 | tf_op jit(solution)/shard_map/ppermute | solution.py:148
  87.9 19.5 %collective-permute-start.12 = (bf16[2,512,128]{2,1,0:T(8,128)(2,1)S(1)}, bf16[2,512,128]{2,1,0:T(8,128)(2,1)S(1)}, u32[]{:S(2)}, u32[]{:S(2)}) collective-permute-start(bf16[2,512,128]{2,1,0:T(8,128)(2,1)S(1)} %get-tuple-element.331.refs_0_), channel_id=1, source_target_pairs={{0,6},{2,4},{4,2},{6,0},{1,7},{3,5},{5,3},{7,1},{8,14},{10,12},{12... | collective-permute-start | bytes 786440 | tf_op jit(solution)/shard_map/ppermute | solution.py:148
  108.4 28.5 %collective-permute-start.17 = (bf16[512,1024]{1,0:T(8,128)(2,1)S(1)}, bf16[512,1024]{1,0:T(8,128)(2,1)}, u32[]{:S(2)}, u32[]{:S(2)}) collective-permute-start(bf16[512,1024]{1,0:T(8,128)(2,1)S(1)} %collective-permute-done.7.refs_4_.refs_5_.refs_2_.refs_3_), channel_id=1, source_target_pairs={{0,2},{2,0},{4,6},{6,4},{1,3},{3,1},{5,7},{7,5},{8,10},{10,8},{12,... | collective-permute-start | bytes 3145736 | tf_op jit(solution)/shard_map/ppermute | solution.py:148
  111.7 25.2 %collective-permute-start.14 = (bf16[128,2048]{1,0:T(8,128)(2,1)}, bf16[128,2048]{1,0:T(8,128)(2,1)}, u32[]{:S(2)}, u32[]{:S(2)}) collective-permute-start(bf16[128,2048]{1,0:T(8,128)(2,1)} %get-tuple-element.338), channel_id=1, source_target_pairs={{0,8},{8,0},{16,24},{24,16},{1,9},{9,1},{17,25},{25,17},{2,10},{10... | collective-permute-start | bytes 1572872 | tf_op jit(solution)/shard_map/ppermute | solution.py:148
  112.4 24.5 %collective-permute-start.15 = (bf16[128,2048]{1,0:T(8,128)(2,1)}, bf16[128,2048]{1,0:T(8,128)(2,1)}, u32[]{:S(2)}, u32[]{:S(2)}) collective-permute-start(bf16[128,2048]{1,0:T(8,128)(2,1)} %get-tuple-element.339), channel_id=1, source_target_pairs={{0,16},{8,24},{16,0},{24,8},{1,17},{9,25},{17,1},{25,9},{2,18},{10... | collective-permute-start | bytes 1572872 | tf_op jit(solution)/shard_map/ppermute | solution.py:148
  113.4 23.5 %collective-permute-start.16 = (bf16[128,2048]{1,0:T(8,128)(2,1)}, bf16[128,2048]{1,0:T(8,128)(2,1)}, u32[]{:S(2)}, u32[]{:S(2)}) collective-permute-start(bf16[128,2048]{1,0:T(8,128)(2,1)} %get-tuple-element.340), channel_id=1, source_target_pairs={{0,24},{8,16},{16,8},{24,0},{1,25},{9,17},{17,9},{25,1},{2,26},{10... | collective-permute-start | bytes 1572872 | tf_op jit(solution)/shard_map/ppermute | solution.py:148
  141.2 26.3 %collective-permute-start.19 = (bf16[512,1024]{1,0:T(8,128)(2,1)S(1)}, bf16[512,1024]{1,0:T(8,128)(2,1)S(1)}, u32[]{:S(2)}, u32[]{:S(2)}) collective-permute-start(bf16[512,1024]{1,0:T(8,128)(2,1)S(1)} %collective-permute-done.8.refs_6_.refs_7_.refs_4_.refs_5_), channel_id=1, source_target_pairs={{0,2},{2,0},{4,6},{6,4},{1,3},{3,1},{5,7},{7,5},{8,10},{10,8},{12,... | collective-permute-start | bytes 3145736 | tf_op jit(solution)/shard_map/ppermute | solution.py:148
  143.6 23.9 %collective-permute-start.22 = (bf16[128,2048]{1,0:T(8,128)(2,1)S(1)}, bf16[128,2048]{1,0:T(8,128)(2,1)S(1)}, u32[]{:S(2)}, u32[]{:S(2)}) collective-permute-start(bf16[128,2048]{1,0:T(8,128)(2,1)S(1)} %get-tuple-element.360), channel_id=1, source_target_pairs={{0,24},{8,16},{16,8},{24,0},{1,25},{9,17},{17,9},{25,1},{2,26},{10... | collective-permute-start | bytes 1572872 | tf_op jit(solution)/shard_map/ppermute | solution.py:148
  167.5 30.0 %collective-permute-start.24 = (bf16[512,2048]{1,0:T(8,128)(2,1)S(1)}, bf16[512,2048]{1,0:T(8,128)(2,1)S(1)}, u32[]{:S(2)}, u32[]{:S(2)}) collective-permute-start(bf16[512,2048]{1,0:T(8,128)(2,1)S(1)} %shard_map.220.refs_1_.refs_0_), channel_id=1, source_target_pairs={{0,1},{1,0},{2,3},{3,2},{4,5},{5,4},{6,7},{7,6},{8,9},{9,8},{10,11... | collective-permute-start | bytes 6291464 | tf_op jit(solution)/shard_map/ppermute | solution.py:148
  167.5 30.0 %collective-permute-start.23 = (bf16[512,1024]{1,0:T(8,128)(2,1)S(1)}, bf16[512,1024]{1,0:T(8,128)(2,1)S(1)}, u32[]{:S(2)}, u32[]{:S(2)}) collective-permute-start(bf16[512,1024]{1,0:T(8,128)(2,1)S(1)} %collective-permute-done.13.refs_8_.refs_9_.refs_6_.refs_7_), channel_id=1, source_target_pairs={{0,2},{2,0},{4,6},{6,4},{1,3},{3,1},{5,7},{7,5},{8,10},{10,8},{12,... | collective-permute-start | bytes 3145736 | tf_op jit(solution)/shard_map/ppermute | solution.py:148
  172.5 24.9 %collective-permute-start.26 = (bf16[128,2048]{1,0:T(8,128)(2,1)S(1)}, bf16[128,2048]{1,0:T(8,128)(2,1)S(1)}, u32[]{:S(2)}, u32[]{:S(2)}) collective-permute-start(bf16[128,2048]{1,0:T(8,128)(2,1)S(1)} %get-tuple-element.374), channel_id=1, source_target_pairs={{0,16},{8,24},{16,0},{24,8},{1,17},{9,25},{17,1},{25,9},{2,18},{10... | collective-permute-start | bytes 1572872 | tf_op jit(solution)/shard_map/ppermute | solution.py:148
  173.5 23.9 %collective-permute-start.27 = (bf16[128,2048]{1,0:T(8,128)(2,1)S(1)}, bf16[128,2048]{1,0:T(8,128)(2,1)S(1)}, u32[]{:S(2)}, u32[]{:S(2)}) collective-permute-start(bf16[128,2048]{1,0:T(8,128)(2,1)S(1)} %get-tuple-element.375), channel_id=1, source_target_pairs={{0,24},{8,16},{16,8},{24,0},{1,25},{9,17},{17,9},{25,1},{2,26},{10... | collective-permute-start | bytes 1572872 | tf_op jit(solution)/shard_map/ppermute | solution.py:148
  197.7 25.6 %collective-permute-start.28 = (bf16[512,1024]{1,0:T(8,128)(2,1)S(1)}, bf16[512,1024]{1,0:T(8,128)(2,1)S(1)}, u32[]{:S(2)}, u32[]{:S(2)}) collective-permute-start(bf16[512,1024]{1,0:T(8,128)(2,1)S(1)} %pad_maximum_fusion.3), channel_id=1, source_target_pairs={{0,8},{8,0},{16,24},{24,16},{1,9},{9,1},{17,25},{25,17},{2,10},{10... | collective-permute-start | bytes 3145736 | tf_op jit(solution)/shard_map/ppermute | solution.py:148
  198.5 25.7 %collective-permute-start.29 = (bf16[512,1024]{1,0:T(8,128)(2,1)S(1)}, bf16[512,1024]{1,0:T(8,128)(2,1)S(1)}, u32[]{:S(2)}, u32[]{:S(2)}) collective-permute-start(bf16[512,1024]{1,0:T(8,128)(2,1)S(1)} %pad_maximum_fusion.4), channel_id=1, source_target_pairs={{0,16},{8,24},{16,0},{24,8},{1,17},{9,25},{17,1},{25,9},{2,18},{10... | collective-permute-start | bytes 3145736 | tf_op jit(solution)/shard_map/ppermute | solution.py:148
  225.3 25.0 %collective-permute-start.32 = (bf16[512,1024]{1,0:T(8,128)(2,1)}, bf16[512,1024]{1,0:T(8,128)(2,1)}, u32[]{:S(2)}, u32[]{:S(2)}) collective-permute-start(bf16[512,1024]{1,0:T(8,128)(2,1)} %get-tuple-element.395), channel_id=1, source_target_pairs={{0,8},{8,0},{16,24},{24,16},{1,9},{9,1},{17,25},{25,17},{2,10},{10... | collective-permute-start | bytes 3145736 | tf_op jit(solution)/shard_map/ppermute | solution.py:148
  226.0 24.8 %collective-permute-start.33 = (bf16[512,1024]{1,0:T(8,128)(2,1)}, bf16[512,1024]{1,0:T(8,128)(2,1)}, u32[]{:S(2)}, u32[]{:S(2)}) collective-permute-start(bf16[512,1024]{1,0:T(8,128)(2,1)} %get-tuple-element.396), channel_id=1, source_target_pairs={{0,16},{8,24},{16,0},{24,8},{1,17},{9,25},{17,1},{25,9},{2,18},{10... | collective-permute-start | bytes 3145736 | tf_op jit(solution)/shard_map/ppermute | solution.py:148
  227.1 24.1 %collective-permute-start.31 = (bf16[512,1024]{1,0:T(8,128)(2,1)}, bf16[512,1024]{1,0:T(8,128)(2,1)}, u32[]{:S(2)}, u32[]{:S(2)}) collective-permute-start(bf16[512,1024]{1,0:T(8,128)(2,1)} %get-tuple-element.394), channel_id=1, source_target_pairs={{0,2},{6,4},{1,3},{7,5},{8,10},{14,12},{9,11},{15,13},{16,18},{22,... | collective-permute-start | bytes 3145736 | tf_op jit(solution)/shard_map/ppermute | solution.py:148
  254.0 23.7 %collective-permute-start.35 = (bf16[512,1024]{1,0:T(8,128)(2,1)S(1)}, bf16[512,1024]{1,0:T(8,128)(2,1)S(1)}, u32[]{:S(2)}, u32[]{:S(2)}) collective-permute-start(bf16[512,1024]{1,0:T(8,128)(2,1)S(1)} %get-tuple-element.593), channel_id=1, source_target_pairs={{0,2},{6,4},{2,0},{4,6},{1,3},{7,5},{3,1},{5,7},{8,10},{14,12},{10... | collective-permute-start | bytes 3145736 | tf_op jit(solution)/shard_map/ppermute | solution.py:148
  256.2 21.4 %collective-permute-start.34 = (bf16[512,1024]{1,0:T(8,128)(2,1)S(1)}, bf16[512,1024]{1,0:T(8,128)(2,1)S(1)}, u32[]{:S(2)}, u32[]{:S(2)}) collective-permute-start(bf16[512,1024]{1,0:T(8,128)(2,1)S(1)} %get-tuple-element.594), channel_id=1, source_target_pairs={{2,4},{4,2},{3,5},{5,3},{10,12},{12,10},{11,13},{13,11},{18,20},{2... | collective-permute-start | bytes 3145736 | tf_op jit(solution)/shard_map/ppermute | solution.py:148
  256.9 31.6 %collective-permute-start.36 = (bf16[512,1024]{1,0:T(8,128)(2,1)S(1)}, bf16[512,1024]{1,0:T(8,128)(2,1)S(1)}, u32[]{:S(2)}, u32[]{:S(2)}) collective-permute-start(bf16[512,1024]{1,0:T(8,128)(2,1)S(1)} %pad_maximum_fusion.8), channel_id=1, source_target_pairs={{0,24},{8,16},{16,8},{24,0},{1,25},{9,17},{17,9},{25,1},{2,26},{10... | collective-permute-start | bytes 3145736 | tf_op jit(solution)/shard_map/ppermute | solution.py:148
  279.4 22.1 %collective-permute-start.37 = (bf16[512,1024]{1,0:T(8,128)(2,1)S(1)}, bf16[512,1024]{1,0:T(8,128)(2,1)S(1)}, u32[]{:S(2)}, u32[]{:S(2)}) collective-permute-start(bf16[512,1024]{1,0:T(8,128)(2,1)S(1)} %add_convert_fusion.24), channel_id=1, source_target_pairs={{2,4},{4,2},{3,5},{5,3},{10,12},{12,10},{11,13},{13,11},{18,20},{2... | collective-permute-start | bytes 3145736 | tf_op jit(solution)/shard_map/ppermute | solution.py:148
  282.5 26.2 %collective-permute-start.38 = (bf16[512,1024]{1,0:T(8,128)(2,1)S(1)}, bf16[512,1024]{1,0:T(8,128)(2,1)S(1)}, u32[]{:S(2)}, u32[]{:S(2)}) collective-permute-start(bf16[512,1024]{1,0:T(8,128)(2,1)S(1)} %fusion.refs_1_), channel_id=1, source_target_pairs={{0,2},{6,4},{2,0},{4,6},{1,3},{7,5},{3,1},{5,7},{8,10},{14,12},{10... | collective-permute-start | bytes 3145736 | tf_op jit(solution)/shard_map/ppermute | solution.py:148
  288.5 31.0 %collective-permute-start.39 = (bf16[512,1024]{1,0:T(8,128)(2,1)}, bf16[512,1024]{1,0:T(8,128)(2,1)}, u32[]{:S(2)}, u32[]{:S(2)}) collective-permute-start(bf16[512,1024]{1,0:T(8,128)(2,1)} %get-tuple-element.418), channel_id=1, source_target_pairs={{0,24},{8,16},{16,8},{24,0},{1,25},{9,17},{17,9},{25,1},{2,26},{10... | collective-permute-start | bytes 3145736 | tf_op jit(solution)/shard_map/ppermute | solution.py:148
  311.4 21.5 %collective-permute-start.41 = (bf16[512,1024]{1,0:T(8,128)(2,1)S(1)}, bf16[512,1024]{1,0:T(8,128)(2,1)S(1)}, u32[]{:S(2)}, u32[]{:S(2)}) collective-permute-start(bf16[512,1024]{1,0:T(8,128)(2,1)S(1)} %fusion.1.refs_3_), channel_id=1, source_target_pairs={{0,2},{6,4},{2,0},{4,6},{1,3},{7,5},{3,1},{5,7},{8,10},{14,12},{10... | collective-permute-start | bytes 3145736 | tf_op jit(solution)/shard_map/ppermute | solution.py:148
  313.2 19.7 %collective-permute-start.40 = (bf16[512,1024]{1,0:T(8,128)(2,1)S(1)}, bf16[512,1024]{1,0:T(8,128)(2,1)S(1)}, u32[]{:S(2)}, u32[]{:S(2)}) collective-permute-start(bf16[512,1024]{1,0:T(8,128)(2,1)S(1)} %add_convert_fusion.22), channel_id=1, source_target_pairs={{2,4},{4,2},{3,5},{5,3},{10,12},{12,10},{11,13},{13,11},{18,20},{2... | collective-permute-start | bytes 3145736 | tf_op jit(solution)/shard_map/ppermute | solution.py:148
  319.4 31.4 %collective-permute-start.42 = (bf16[512,2048]{1,0:T(8,128)(2,1)S(1)}, bf16[512,2048]{1,0:T(8,128)(2,1)S(1)}, u32[]{:S(2)}, u32[]{:S(2)}) collective-permute-start(bf16[512,2048]{1,0:T(8,128)(2,1)S(1)} %shard_map.228), channel_id=1, source_target_pairs={{0,1},{1,0},{2,3},{3,2},{4,5},{5,4},{6,7},{7,6},{8,9},{9,8},{10,11... | collective-permute-start | bytes 6291464 | tf_op jit(solution)/shard_map/ppermute | solution.py:148
  319.5 31.3 %collective-permute-start.43 = (bf16[512,1024]{1,0:T(8,128)(2,1)S(1)}, bf16[512,1024]{1,0:T(8,128)(2,1)S(1)}, u32[]{:S(2)}, u32[]{:S(2)}) collective-permute-start(bf16[512,1024]{1,0:T(8,128)(2,1)S(1)} %get-tuple-element.430), channel_id=1, source_target_pairs={{0,8},{8,0},{16,24},{24,16},{1,9},{9,1},{17,25},{25,17},{2,10},{10... | collective-permute-start | bytes 3145736 | tf_op jit(solution)/shard_map/ppermute | solution.py:148
  321.1 29.8 %collective-permute-start.44 = (bf16[512,1024]{1,0:T(8,128)(2,1)S(1)}, bf16[512,1024]{1,0:T(8,128)(2,1)S(1)}, u32[]{:S(2)}, u32[]{:S(2)}) collective-permute-start(bf16[512,1024]{1,0:T(8,128)(2,1)S(1)} %get-tuple-element.431), channel_id=1, source_target_pairs={{0,16},{8,24},{16,0},{24,8},{1,17},{9,25},{17,1},{25,9},{2,18},{10... | collective-permute-start | bytes 3145736 | tf_op jit(solution)/shard_map/ppermute | solution.py:148
  335.6 20.6 %collective-permute-start.46 = (bf16[512,1024]{1,0:T(8,128)(2,1)S(1)}, bf16[512,1024]{1,0:T(8,128)(2,1)S(1)}, u32[]{:S(2)}, u32[]{:S(2)}) collective-permute-start(bf16[512,1024]{1,0:T(8,128)(2,1)S(1)} %fusion.2.refs_5_), channel_id=1, source_target_pairs={{0,2},{6,4},{2,0},{4,6},{1,3},{7,5},{3,1},{5,7},{8,10},{14,12},{10... | collective-permute-start | bytes 3145736 | tf_op jit(solution)/shard_map/ppermute | solution.py:148
  337.7 18.5 %collective-permute-start.45 = (bf16[512,1024]{1,0:T(8,128)(2,1)S(1)}, bf16[512,1024]{1,0:T(8,128)(2,1)}, u32[]{:S(2)}, u32[]{:S(2)}) collective-permute-start(bf16[512,1024]{1,0:T(8,128)(2,1)S(1)} %add_convert_fusion.20), channel_id=1, source_target_pairs={{2,4},{4,2},{3,5},{5,3},{10,12},{12,10},{11,13},{13,11},{18,20},{2... | collective-permute-start | bytes 3145736 | tf_op jit(solution)/shard_map/ppermute | solution.py:148
  354.4 20.6 %collective-permute-start.49 = (bf16[128,2048]{1,0:T(8,128)(2,1)S(1)}, bf16[128,2048]{1,0:T(8,128)(2,1)S(1)}, u32[]{:S(2)}, u32[]{:S(2)}) collective-permute-start(bf16[128,2048]{1,0:T(8,128)(2,1)S(1)} %get-tuple-element.441), channel_id=1, source_target_pairs={{0,24},{8,16},{16,8},{24,0},{1,25},{9,17},{17,9},{25,1},{2,26},{10... | collective-permute-start | bytes 1572872 | tf_op jit(solution)/shard_map/ppermute | solution.py:148
  360.2 22.4 %collective-permute-start.51 = (bf16[512,1024]{1,0:T(8,128)(2,1)S(1)}, bf16[512,1024]{1,0:T(8,128)(2,1)S(1)}, u32[]{:S(2)}, u32[]{:S(2)}) collective-permute-start(bf16[512,1024]{1,0:T(8,128)(2,1)S(1)} %fusion.3.refs_1_), channel_id=1, source_target_pairs={{0,2},{6,4},{2,0},{4,6},{1,3},{7,5},{3,1},{5,7},{8,10},{14,12},{10... | collective-permute-start | bytes 3145736 | tf_op jit(solution)/shard_map/ppermute | solution.py:148
  363.7 19.0 %collective-permute-start.50 = (bf16[512,1024]{1,0:T(8,128)(2,1)S(1)}, bf16[512,1024]{1,0:T(8,128)(2,1)S(1)}, u32[]{:S(2)}, u32[]{:S(2)}) collective-permute-start(bf16[512,1024]{1,0:T(8,128)(2,1)S(1)} %add_convert_fusion.18), channel_id=1, source_target_pairs={{2,4},{4,2},{3,5},{5,3},{10,12},{12,10},{11,13},{13,11},{18,20},{2... | collective-permute-start | bytes 3145736 | tf_op jit(solution)/shard_map/ppermute | solution.py:148
  377.0 18.8 %collective-permute-start.53 = (bf16[128,2048]{1,0:T(8,128)(2,1)S(1)}, bf16[128,2048]{1,0:T(8,128)(2,1)S(1)}, u32[]{:S(2)}, u32[]{:S(2)}) collective-permute-start(bf16[128,2048]{1,0:T(8,128)(2,1)S(1)} %get-tuple-element.453), channel_id=1, source_target_pairs={{0,16},{8,24},{16,0},{24,8},{1,17},{9,25},{17,1},{25,9},{2,18},{10... | collective-permute-start | bytes 1572872 | tf_op jit(solution)/shard_map/ppermute | solution.py:148
  383.3 20.4 %collective-permute-start.56 = (bf16[512,1024]{1,0:T(8,128)(2,1)S(1)}, bf16[512,1024]{1,0:T(8,128)(2,1)S(1)}, u32[]{:S(2)}, u32[]{:S(2)}) collective-permute-start(bf16[512,1024]{1,0:T(8,128)(2,1)S(1)} %fusion.4.refs_7_), channel_id=1, source_target_pairs={{0,2},{6,4},{2,0},{4,6},{1,3},{7,5},{3,1},{5,7},{8,10},{14,12},{10... | collective-permute-start | bytes 3145736 | tf_op jit(solution)/shard_map/ppermute | solution.py:148
  399.6 28.7 %collective-permute-start.57 = (bf16[512,1024]{1,0:T(8,128)(2,1)S(1)}, bf16[512,1024]{1,0:T(8,128)(2,1)S(1)}, u32[]{:S(2)}, u32[]{:S(2)}) collective-permute-start(bf16[512,1024]{1,0:T(8,128)(2,1)S(1)} %shard_map.235), channel_id=1, source_target_pairs={{0,24},{8,16},{16,8},{24,0},{1,25},{9,17},{17,9},{25,1},{2,26},{10... | collective-permute-start | bytes 3145736 | tf_op jit(solution)/shard_map/ppermute | solution.py:148
  404.9 26.2 %collective-permute-start.60 = (bf16[512,1024]{1,0:T(8,128)(2,1)S(1)}, bf16[512,1024]{1,0:T(8,128)(2,1)S(1)}, u32[]{:S(2)}, u32[]{:S(2)}) collective-permute-start(bf16[512,1024]{1,0:T(8,128)(2,1)S(1)} %fusion.5.refs_1_), channel_id=1, source_target_pairs={{0,2},{6,4},{2,0},{4,6},{1,3},{7,5},{3,1},{5,7},{8,10},{14,12},{10... | collective-permute-start | bytes 3145736 | tf_op jit(solution)/shard_map/ppermute | solution.py:148
  408.6 22.5 %collective-permute-start.59 = (bf16[512,1024]{1,0:T(8,128)(2,1)S(1)}, bf16[512,1024]{1,0:T(8,128)(2,1)S(1)}, u32[]{:S(2)}, u32[]{:S(2)}) collective-permute-start(bf16[512,1024]{1,0:T(8,128)(2,1)S(1)} %add_convert_fusion.14), channel_id=1, source_target_pairs={{2,4},{4,2},{3,5},{5,3},{10,12},{12,10},{11,13},{13,11},{18,20},{2... | collective-permute-start | bytes 3145736 | tf_op jit(solution)/shard_map/ppermute | solution.py:148
  428.4 22.5 %collective-permute-start.61 = (bf16[512,1024]{1,0:T(8,128)(2,1)S(1)}, bf16[512,1024]{1,0:T(8,128)(2,1)S(1)}, u32[]{:S(2)}, u32[]{:S(2)}) collective-permute-start(bf16[512,1024]{1,0:T(8,128)(2,1)S(1)} %get-tuple-element.475), channel_id=1, source_target_pairs={{0,8},{8,0},{16,24},{24,16},{1,9},{9,1},{17,25},{25,17},{2,10},{10... | collective-permute-start | bytes 3145736 | tf_op jit(solution)/shard_map/ppermute | solution.py:148
  430.1 21.4 %collective-permute-start.62 = (bf16[512,1024]{1,0:T(8,128)(2,1)S(1)}, bf16[512,1024]{1,0:T(8,128)(2,1)S(1)}, u32[]{:S(2)}, u32[]{:S(2)}) collective-permute-start(bf16[512,1024]{1,0:T(8,128)(2,1)S(1)} %get-tuple-element.476), channel_id=1, source_target_pairs={{0,16},{8,24},{16,0},{24,8},{1,17},{9,25},{17,1},{25,9},{2,18},{10... | collective-permute-start | bytes 3145736 | tf_op jit(solution)/shard_map/ppermute | solution.py:148
  432.1 21.1 %collective-permute-start.64 = (bf16[512,1024]{1,0:T(8,128)(2,1)S(1)}, bf16[512,1024]{1,0:T(8,128)(2,1)S(1)}, u32[]{:S(2)}, u32[]{:S(2)}) collective-permute-start(bf16[512,1024]{1,0:T(8,128)(2,1)S(1)} %fusion.6.refs_3_), channel_id=1, source_target_pairs={{0,2},{6,4},{2,0},{4,6},{1,3},{7,5},{3,1},{5,7},{8,10},{14,12},{10... | collective-permute-start | bytes 3145736 | tf_op jit(solution)/shard_map/ppermute | solution.py:148
  451.4 26.5 %collective-permute-start.66 = (bf16[512,2048]{1,0:T(8,128)(2,1)S(1)}, bf16[512,2048]{1,0:T(8,128)(2,1)S(1)}, u32[]{:S(2)}, u32[]{:S(2)}) collective-permute-start(bf16[512,2048]{1,0:T(8,128)(2,1)S(1)} %shard_map.233), channel_id=1, source_target_pairs={{0,1},{1,0},{2,3},{3,2},{4,5},{5,4},{6,7},{7,6},{8,9},{9,8},{10,11... | collective-permute-start | bytes 6291464 | tf_op jit(solution)/shard_map/ppermute | solution.py:148
  451.4 26.5 %collective-permute-start.65 = (bf16[512,1024]{1,0:T(8,128)(2,1)S(1)}, bf16[512,1024]{1,0:T(8,128)(2,1)S(1)}, u32[]{:S(2)}, u32[]{:S(2)}) collective-permute-start(bf16[512,1024]{1,0:T(8,128)(2,1)S(1)} %get-tuple-element.484), channel_id=1, source_target_pairs={{0,24},{8,16},{16,8},{24,0},{1,25},{9,17},{17,9},{25,1},{2,26},{10... | collective-permute-start | bytes 3145736 | tf_op jit(solution)/shard_map/ppermute | solution.py:148
  454.2 25.1 %collective-permute-start.68 = (bf16[512,1024]{1,0:T(8,128)(2,1)S(1)}, bf16[512,1024]{1,0:T(8,128)(2,1)S(1)}, u32[]{:S(2)}, u32[]{:S(2)}) collective-permute-start(bf16[512,1024]{1,0:T(8,128)(2,1)S(1)} %fusion.7.refs_5_), channel_id=1, source_target_pairs={{0,2},{6,4},{2,0},{4,6},{1,3},{7,5},{3,1},{5,7},{8,10},{14,12},{10... | collective-permute-start | bytes 3145736 | tf_op jit(solution)/shard_map/ppermute | solution.py:148
  457.9 21.4 %collective-permute-start.67 = (bf16[512,1024]{1,0:T(8,128)(2,1)S(1)}, bf16[512,1024]{1,0:T(8,128)(2,1)S(1)}, u32[]{:S(2)}, u32[]{:S(2)}) collective-permute-start(bf16[512,1024]{1,0:T(8,128)(2,1)S(1)} %add_convert_fusion.10), channel_id=1, source_target_pairs={{2,4},{4,2},{3,5},{5,3},{10,12},{12,10},{11,13},{13,11},{18,20},{2... | collective-permute-start | bytes 3145736 | tf_op jit(solution)/shard_map/ppermute | solution.py:148
  481.2 23.4 %collective-permute-start.70 = (bf16[128,2048]{1,0:T(8,128)(2,1)S(1)}, bf16[128,2048]{1,0:T(8,128)(2,1)S(1)}, u32[]{:S(2)}, u32[]{:S(2)}) collective-permute-start(bf16[128,2048]{1,0:T(8,128)(2,1)S(1)} %get-tuple-element.494), channel_id=1, source_target_pairs={{0,16},{8,24},{16,0},{24,8},{1,17},{9,25},{17,1},{25,9},{2,18},{10... | collective-permute-start | bytes 1572872 | tf_op jit(solution)/shard_map/ppermute | solution.py:148
  482.3 22.3 %collective-permute-start.71 = (bf16[128,2048]{1,0:T(8,128)(2,1)S(1)}, bf16[128,2048]{1,0:T(8,128)(2,1)S(1)}, u32[]{:S(2)}, u32[]{:S(2)}) collective-permute-start(bf16[128,2048]{1,0:T(8,128)(2,1)S(1)} %get-tuple-element.495), channel_id=1, source_target_pairs={{0,24},{8,16},{16,8},{24,0},{1,25},{9,17},{17,9},{25,1},{2,26},{10... | collective-permute-start | bytes 1572872 | tf_op jit(solution)/shard_map/ppermute | solution.py:148
  484.5 23.3 %collective-permute-start.73 = (bf16[512,1024]{1,0:T(8,128)(2,1)S(1)}, bf16[512,1024]{1,0:T(8,128)(2,1)S(1)}, u32[]{:S(2)}, u32[]{:S(2)}) collective-permute-start(bf16[512,1024]{1,0:T(8,128)(2,1)S(1)} %fusion.8.sent_ref), channel_id=1, source_target_pairs={{0,2},{6,4},{2,0},{4,6},{1,3},{7,5},{3,1},{5,7},{8,10},{14,12},{10... | collective-permute-start | bytes 3145736 | tf_op jit(solution)/shard_map/ppermute | solution.py:148
  488.2 19.6 %collective-permute-start.72 = (bf16[512,1024]{1,0:T(8,128)(2,1)S(1)}, bf16[512,1024]{1,0:T(8,128)(2,1)S(1)}, u32[]{:S(2)}, u32[]{:S(2)}) collective-permute-start(bf16[512,1024]{1,0:T(8,128)(2,1)S(1)} %add_convert_fusion.8), channel_id=1, source_target_pairs={{2,4},{4,2},{3,5},{5,3},{10,12},{12,10},{11,13},{13,11},{18,20},{2... | collective-permute-start | bytes 3145736 | tf_op jit(solution)/shard_map/ppermute | solution.py:148
  508.9 22.4 %collective-permute-start.75 = (bf16[512,1024]{1,0:T(8,128)(2,1)S(1)}, bf16[512,1024]{1,0:T(8,128)(2,1)S(1)}, u32[]{:S(2)}, u32[]{:S(2)}) collective-permute-start(bf16[512,1024]{1,0:T(8,128)(2,1)S(1)} %fusion.9.refs_7_), channel_id=1, source_target_pairs={{0,2},{6,4},{2,0},{4,6},{1,3},{7,5},{3,1},{5,7},{8,10},{14,12},{10... | collective-permute-start | bytes 3145736 | tf_op jit(solution)/shard_map/ppermute | solution.py:148
  512.6 18.7 %collective-permute-start.74 = (bf16[512,1024]{1,0:T(8,128)(2,1)S(1)}, bf16[512,1024]{1,0:T(8,128)(2,1)S(1)}, u32[]{:S(2)}, u32[]{:S(2)}) collective-permute-start(bf16[512,1024]{1,0:T(8,128)(2,1)S(1)} %add_convert_fusion.6), channel_id=1, source_target_pairs={{2,4},{4,2},{3,5},{5,3},{10,12},{12,10},{11,13},{13,11},{18,20},{2... | collective-permute-start | bytes 3145736 | tf_op jit(solution)/shard_map/ppermute | solution.py:148
  532.3 21.7 %collective-permute-start.77 = (bf16[512,1024]{1,0:T(8,128)(2,1)S(1)}, bf16[512,1024]{1,0:T(8,128)(2,1)S(1)}, u32[]{:S(2)}, u32[]{:S(2)}) collective-permute-start(bf16[512,1024]{1,0:T(8,128)(2,1)S(1)} %fusion.10.refs_3_), channel_id=1, source_target_pairs={{0,2},{6,4},{2,0},{4,6},{1,3},{7,5},{3,1},{5,7},{8,10},{14,12},{10... | collective-permute-start | bytes 3145736 | tf_op jit(solution)/shard_map/ppermute | solution.py:148
  548.3 22.5 %collective-permute-start.80 = (bf16[512,2048]{1,0:T(8,128)(2,1)S(1)}, bf16[512,2048]{1,0:T(8,128)(2,1)S(1)}, u32[]{:S(2)}, u32[]{:S(2)}) collective-permute-start(bf16[512,2048]{1,0:T(8,128)(2,1)S(1)} %get-tuple-element.521), channel_id=1, source_target_pairs={{0,1},{1,0},{2,3},{3,2},{4,5},{5,4},{6,7},{7,6},{8,9},{9,8},{10,11... | collective-permute-start | bytes 6291464 | tf_op jit(solution)/shard_map/ppermute | solution.py:148
  554.9 21.4 %collective-permute-start.82 = (bf16[512,1024]{1,0:T(8,128)(2,1)S(1)}, bf16[512,1024]{1,0:T(8,128)(2,1)S(1)}, u32[]{:S(2)}, u32[]{:S(2)}) collective-permute-start(bf16[512,1024]{1,0:T(8,128)(2,1)S(1)} %fusion.11.refs_5_), channel_id=1, source_target_pairs={{0,2},{6,4},{2,0},{4,6},{1,3},{7,5},{3,1},{5,7},{8,10},{14,12},{10... | collective-permute-start | bytes 3145736 | tf_op jit(solution)/shard_map/ppermute | solution.py:148
  578.4 22.1 %collective-permute-start.85 = (bf16[128,2048]{1,0:T(8,128)(2,1)S(1)}, bf16[128,2048]{1,0:T(8,128)(2,1)S(1)}, u32[]{:S(2)}, u32[]{:S(2)}) collective-permute-start(bf16[128,2048]{1,0:T(8,128)(2,1)S(1)} %get-tuple-element.531), channel_id=1, source_target_pairs={{0,24},{8,16},{16,8},{24,0},{1,25},{9,17},{17,9},{25,1},{2,26},{10... | collective-permute-start | bytes 1572872 | tf_op jit(solution)/shard_map/ppermute | solution.py:148
  580.5 24.0 %collective-permute-start.86 = (bf16[512,640]{1,0:T(8,128)(2,1)S(1)}, bf16[512,640]{1,0:T(8,128)(2,1)S(1)}, u32[]{:S(2)}, u32[]{:S(2)}) collective-permute-start(bf16[512,640]{1,0:T(8,128)(2,1)S(1)} %add_convert_fusion.33), channel_id=1, source_target_pairs={{2,4},{4,2},{3,5},{5,3},{10,12},{12,10},{11,13},{13,11},{18,20},{2... | collective-permute-start | bytes 1966088 | tf_op jit(solution)/shard_map/ppermute | solution.py:148
  581.7 27.5 %collective-permute-start.87 = (bf16[512,1024]{1,0:T(8,128)(2,1)S(1)}, bf16[512,1024]{1,0:T(8,128)(2,1)S(1)}, u32[]{:S(2)}, u32[]{:S(2)}) collective-permute-start(bf16[512,1024]{1,0:T(8,128)(2,1)S(1)} %fusion.12.refs_7_), channel_id=1, source_target_pairs={{0,2},{6,4},{2,0},{4,6},{1,3},{7,5},{3,1},{5,7},{8,10},{14,12},{10... | collective-permute-start | bytes 3145736 | tf_op jit(solution)/shard_map/ppermute | solution.py:148
  (160 other events, 1584.2 us)

commit v10 on v9

--- a/solution.py
+++ b/solution.py
@@ -71,9 +71,9 @@
     )
 
 
-VMEM_LIMIT = 28 * 1024 * 1024
-LARGE_LIMIT = 28 * 1024 * 1024
-MIDDLE_LIMIT = 20 * 1024 * 1024
+VMEM_LIMIT = 22 * 1024 * 1024
+LARGE_LIMIT = 22 * 1024 * 1024
+MIDDLE_LIMIT = 16 * 1024 * 1024
 SMALL_LIMIT = 12 * 1024 * 1024
 SMALL = pl.CostEstimate(flops=1, bytes_accessed=1, transcendentals=0)
 LARGE = pl.CostEstimate(flops=12_000_000_000, bytes_accessed=1, transcendentals=0)
@@ -102,7 +102,15 @@
             self.sums[name] = (got["ends"], sent)
         moves = []
         halfway = None
-        if self.entered is not None:
+        together = None
+        if self.leaving is None and self.halfway is not None:
+            name, value = self.entered
+            together, summed = both_ways(
+                self.at_end, entering[1], self.halfway[1], got["middle"], value, got["ends"]
+            )
+            halfway = (name, summed)
+            moves.append(("middle", summed, self.axis, [(1, 2), (2, 1)]))
+        elif self.entered is not None:
             name, value = self.entered
             halfway = (name, add_low(value, got["ends"]))
             moves.append(("middle", halfway[1], self.axis, [(1, 2), (2, 1)]))
@@ -113,8 +121,9 @@
             if entering is None:
                 sent, pairs = add_low(value, got["middle"]), outwards
             else:
-                sent = either_way(self.at_end, entering[1], value, got["middle"])
-                pairs = inwards + outwards
+                sent, pairs = together, inwards + outwards
+                if together is None:
+                    sent = either_way(self.at_end, entering[1], value, got["middle"])
             leaving = (name, sent)
             moves.append(("ends", sent, self.axis, pairs))
         elif entering is not None and halfway is not None:
@@ -352,6 +361,22 @@
     return jnp.where(at_end[0] == 1, fresh, total)
 
 
+def both_ways_kernel(at_end_ref, fresh_ref, half_ref, across_ref, value_ref, came_ref, sent_ref, sum_ref):
+    def add(left_ref, right_ref):
+        total = left_ref[...].astype(jnp.float32) + right_ref[...].astype(jnp.float32)
+        return total.astype(jnp.bfloat16)
+
+    sum_ref[...] = add(value_ref, came_ref)
+    sent_ref[...] = jnp.where(at_end_ref[0] == 1, fresh_ref[...], add(half_ref, across_ref))
+
+
+def both_ways(at_end, *arrays):
+    rows = math.gcd(arrays[0].shape[0], 256)
+    ins = [row_blocks(array, rows) for array in arrays]
+    outs = [row_blocks(low(*arrays[0].shape), rows)] * 2
+    return gridded(both_ways_kernel, arrays[0].shape[0] // rows, ins, outs, scalars=(at_end,))
+
+
 def settled(at_end, came_ref, sent_ref, columns):
     return jnp.where(at_end == 1, came_ref[:, columns], sent_ref[:, columns]).astype(jnp.float32)
 
@@ -409,7 +434,7 @@
     depth = arrays[0].shape[0]
     width = min(array.shape[1] for array in arrays)
     o_width = width - q_width - kv_width
-    rows = math.gcd(depth, 128)
+    rows = math.gcd(depth, 256)
     ins = [(array, (rows, width), lambda i: (i, 0)) for array in arrays]
     widths = (q_width, kv_width // 2, kv_width // 2, o_width)
     outs = [row_blocks(full(depth, each * count), rows) for each in widths]

time: 679 us -> 677 us (level)
  other arithmetic: 36.9 us -> 27.9 us
    pallas_call x15 -> x16, Pallas kernels: 98 us -> 98.4 us  [gridded(): pl.pallas_call(kernel, grid=(steps,), in_specs=[pl.BlockSpec(memory_space...]
    unnamed x238 -> x230, local copies, waits for them, and re-layouts: 29.1 us -> 29.5 us
  transfers between devices with their start and end apart: 105 -> 105, of which waited for: 50 -> 49; matrix products, arithmetic and copies ran while one was open for 6% -> 4% of each run, Pallas kernels for 20% -> 20%
where the time goes in v10:
time: 677 us; the launch traced here: 671 us
  waiting for transfers between devices  292 us (43%)
  starting transfers between devices  156 us (23%)
  Pallas kernels  145 us (21%)
  local copies, waits for them, and re-layouts  45.9 us (7%)
  other arithmetic  27.9 us (4%)
    ppermute x104, waiting for transfers between devices, start(): lax.ppermute(value, axis, pairs)  290 us
    ppermute x104, starting transfers between devices, start(): lax.ppermute(value, axis, pairs)  156 us
    pallas_call x16, Pallas kernels, gridded(): pl.pallas_call(kernel, grid=(steps,), in_specs=[pl.BlockSpec(memory_space...  98.4 us
    unnamed x230, local copies, waits for them, and re-layouts  29.5 us
    pallas_call x5, Pallas kernels, weight_grad(): pl.pallas_call(functools.partial(weight_grad_kernel, len(packs), len(term...  27.5 us
    pallas_call x20, Pallas kernels, in_vmem(): pl.pallas_call(kernel, out_shape=out_shape, in_specs=specs, out_specs=[pl...  19.2 us
  transfers between devices with their start and end apart: 105, of which 49 were waited for; matrix products, arithmetic and copies ran while one was open for 4% of the time, Pallas kernels for 20%

profile of v10, /device:TPU:0, one launch (start us, length us, event | category | flops | bytes accessed | tf_op | source)
XLA Modules:
  0.0 670.7 jit_solution(5264742556963334095)
XLA Ops:
  13.9 3.1 constant_dynamic-slice_fusion.11
  17.7 4.3 constant_dynamic-slice_fusion.5
  36.5 8.9 %collective-permute-done.3.refs_1_ = bf16[128,2048]{1,0:T(8,128)(2,1)} collective-permute-done((bf16[128,2048]{1,0:T(8,128)(2,1)}, bf16[128,2048]{1,0:T(8,128)(2,1)}, u32[]{:S(2)}, u32[]{:S(2)}) %collective-permute-start.3) | collective-permute-done | bytes 524320 | tf_op jit(solution)/shard_map/ppermute | solution.py:157
  45.4 9.7 %collective-permute-done.4.refs_2_ = bf16[128,2048]{1,0:T(8,128)(2,1)} collective-permute-done((bf16[128,2048]{1,0:T(8,128)(2,1)}, bf16[128,2048]{1,0:T(8,128)(2,1)}, u32[]{:S(2)}, u32[]{:S(2)}) %collective-permute-start.4) | collective-permute-done | bytes 524320 | tf_op jit(solution)/shard_map/ppermute | solution.py:157
  61.3 5.2 shard_map.216
  71.1 11.6 %collective-permute-done.7.refs_4_.refs_5_.refs_2_.refs_3_ = bf16[512,1024]{1,0:T(8,128)(2,1)S(1)} collective-permute-done((bf16[512,1024]{1,0:T(8,128)(2,1)S(1)}, bf16[512,1024]{1,0:T(8,128)(2,1)S(1)}, u32[]{:S(2)}, u32[]{:S(2)}) %collective-permute-start.7) | collective-permute-done | bytes 1048608 | tf_op jit(solution)/shard_map/ppermute | solution.py:157
  92.6 4.6 collective-permute-done.10.refs_1_
  97.2 9.6 %collective-permute-done.11.refs_2_ = bf16[2,512,128]{2,1,0:T(8,128)(2,1)S(1)} collective-permute-done((bf16[2,512,128]{2,1,0:T(8,128)(2,1)S(1)}, bf16[2,512,128]{2,1,0:T(8,128)(2,1)S(1)}, u32[]{:S(2)}, u32[]{:S(2)}) %collective-permute-start.11) | collective-permute-done | bytes 262176 | tf_op jit(solution)/shard_map/ppermute | solution.py:157
  108.5 3.2 collective-permute-start.17
  124.5 12.5 %shard_map.218 = (bf16[2,512,256]{2,1,0:T(8,128)(2,1)S(1)}, bf16[512,2048]{1,0:T(8,128)(2,1)S(1)}, bf16[512,2048]{1,0:T(8,128)(2,1)S(1)}) custom-call(bf16[2,512,256]{2,1,0:T(8,128)(2,1)S(1)} %copy-done.48, s32[4,256,1]{2,1,0:T(8,128)S(1)} %copy-done.25, s32[4,256,1]{2,1,0:T(8,128)S(1)} %copy-done.27, s32[4,1,1024]{2,1,0:T(1,128)S(1)} %broadcast_add_fusion.key_place_ref, ...), custom_call_target="tpu_custom_call" | custom-call | flops 1 | bytes 1 | tf_op jit(solution)/shard_map/pallas_call | solution.py:333
  137.1 4.1 collective-permute-done.18.came_ref
  147.0 9.7 %collective-permute-done.20.refs_1_ = bf16[128,2048]{1,0:T(8,128)(2,1)S(1)} collective-permute-done((bf16[128,2048]{1,0:T(8,128)(2,1)S(1)}, bf16[128,2048]{1,0:T(8,128)(2,1)S(1)}, u32[]{:S(2)}, u32[]{:S(2)}) %collective-permute-start.20) | collective-permute-done | bytes 524320 | tf_op jit(solution)/shard_map/ppermute | solution.py:157
  157.1 10.3 %collective-permute-done.22.refs_3_ = bf16[128,2048]{1,0:T(8,128)(2,1)S(1)} collective-permute-done((bf16[128,2048]{1,0:T(8,128)(2,1)S(1)}, bf16[128,2048]{1,0:T(8,128)(2,1)S(1)}, u32[]{:S(2)}, u32[]{:S(2)}) %collective-permute-start.22) | collective-permute-done | bytes 524320 | tf_op jit(solution)/shard_map/ppermute | solution.py:157
  177.1 8.8 %collective-permute-done.25.refs_1_ = bf16[128,2048]{1,0:T(8,128)(2,1)S(1)} collective-permute-done((bf16[128,2048]{1,0:T(8,128)(2,1)S(1)}, bf16[128,2048]{1,0:T(8,128)(2,1)S(1)}, u32[]{:S(2)}, u32[]{:S(2)}) %collective-permute-start.25) | collective-permute-done | bytes 524320 | tf_op jit(solution)/shard_map/ppermute | solution.py:157
  185.9 11.6 %collective-permute-done.26.refs_2_ = bf16[128,2048]{1,0:T(8,128)(2,1)S(1)} collective-permute-done((bf16[128,2048]{1,0:T(8,128)(2,1)S(1)}, bf16[128,2048]{1,0:T(8,128)(2,1)S(1)}, u32[]{:S(2)}, u32[]{:S(2)}) %collective-permute-start.26) | collective-permute-done | bytes 524320 | tf_op jit(solution)/shard_map/ppermute | solution.py:157
  201.9 12.5 %shard_map.223 = (bf16[1024,1024]{1,0:T(8,128)(2,1)S(1)}, bf16[1024,1024]{1,0:T(8,128)(2,1)S(1)}, bf16[1024,1024]{1,0:T(8,128)(2,1)S(1)}) custom-call(bf16[512,2048]{1,0:T(8,128)(2,1)S(1)} %shard_map.222.refs_0_.refs_1_, bf16[512,2048]{1,0:T(8,128)(2,1)S(1)} %collective-permute-done.30.refs_1_.refs_2_, ...), custom_call_target="tpu_custom_call" | custom-call | flops 1 | bytes 1 | tf_op jit(solution)/shard_map/pallas_call | solution.py:333
  214.5 8.1 %shard_map.224 = (bf16[512,1024]{1,0:T(8,128)(2,1)}, bf16[512,1024]{1,0:T(8,128)(2,1)}, bf16[512,1024]{1,0:T(8,128)(2,1)}, bf16[512,1024]{1,0:T(8,128)(2,1)S(1)}) custom-call(s32[1]{0:T(128)S(6)} %and.22.side_ref.refs_0_, bf16[512,2048]{1,0:T(8,128)(2,1)S(1)} %shard_map.220.refs_1_.refs_0_, bf16[512,2048]{1,0:T(8,128)(2,1)S(1)} %collective-permute-done.24.refs_2_.refs_1_, ...), custom_call_target="tpu_custom_call" | custom-call | flops 1 | bytes 1 | tf_op jit(solution)/shard_map/pallas_call | solution.py:658
  227.2 3.2 collective-permute-start.31
  237.2 4.3 shard_map.225
  241.5 9.5 %collective-permute-done.32.value_ref = bf16[512,1024]{1,0:T(8,128)(2,1)} collective-permute-done((bf16[512,1024]{1,0:T(8,128)(2,1)}, bf16[512,1024]{1,0:T(8,128)(2,1)}, u32[]{:S(2)}, u32[]{:S(2)}) %collective-permute-start.32) | collective-permute-done | bytes 1048608 | tf_op jit(solution)/shard_map/ppermute | solution.py:157
  259.4 19.4 %collective-permute-done.35.came_ref = bf16[512,1024]{1,0:T(8,128)(2,1)S(1)} collective-permute-done((bf16[512,1024]{1,0:T(8,128)(2,1)S(1)}, bf16[512,1024]{1,0:T(8,128)(2,1)S(1)}, u32[]{:S(2)}, u32[]{:S(2)}) %collective-permute-start.35) | collective-permute-done | bytes 1048608 | tf_op jit(solution)/shard_map/ppermute | solution.py:157
  281.8 7.3 %collective-permute-start.38 = (bf16[512,1024]{1,0:T(8,128)(2,1)S(1)}, bf16[512,1024]{1,0:T(8,128)(2,1)S(1)}, u32[]{:S(2)}, u32[]{:S(2)}) collective-permute-start(bf16[512,1024]{1,0:T(8,128)(2,1)S(1)} %get-tuple-element.412.refs_1_), channel_id=1, source_target_pairs={{0,2},{6,4},{2,0},{4,6},{1,3},{7,5},{3,1},{5,7},{8,10},{14,12},{10... | collective-permute-start | bytes 3145736 | tf_op jit(solution)/shard_map/ppermute | solution.py:157
  291.0 6.7 shard_map.227
  297.7 4.4 shard_map.228
  302.1 7.8 %collective-permute-done.38.refs_0_ = bf16[512,1024]{1,0:T(8,128)(2,1)S(1)} collective-permute-done((bf16[512,1024]{1,0:T(8,128)(2,1)S(1)}, bf16[512,1024]{1,0:T(8,128)(2,1)S(1)}, u32[]{:S(2)}, u32[]{:S(2)}) %collective-permute-start.38) | collective-permute-done | bytes 1048608 | tf_op jit(solution)/shard_map/ppermute | solution.py:157
  314.7 5.3 shard_map.229
  322.5 11.7 %collective-permute-done.41.refs_2_ = bf16[512,1024]{1,0:T(8,128)(2,1)S(1)} collective-permute-done((bf16[512,1024]{1,0:T(8,128)(2,1)S(1)}, bf16[512,1024]{1,0:T(8,128)(2,1)S(1)}, u32[]{:S(2)}, u32[]{:S(2)}) %collective-permute-start.41) | collective-permute-done | bytes 1048608 | tf_op jit(solution)/shard_map/ppermute | solution.py:157
  335.2 3.7 collective-permute-start.46
  340.1 5.3 shard_map.231.first_ref
  345.4 5.9 shard_map.230
  358.9 3.7 collective-permute-start.51
  363.3 3.1 shard_map.234
  367.8 5.0 collective-permute-done.48.refs_2_
  382.2 3.3 collective-permute-start.56
  389.2 6.6 collective-permute-done.53.refs_2_
  404.3 3.7 collective-permute-start.60
  409.0 19.0 %shard_map.239 = (bf16[2,512,256]{2,1,0:T(8,128)(2,1)S(1)}, bf16[512,1024]{1,0:T(8,128)(2,1)S(1)}) custom-call(s32[1]{0:T(128)} %bitcast.5.here_ref, bf16[2,512,256]{2,1,0:T(8,128)(2,1)S(1)} %copy-done.49, bf16[512,2048]{1,0:T(8,128)(2,1)S(1)} %shard_map.238.mine_ref.refs_3_, bf16[512,2048]{1,0:T(8,128)(2,1)S(1)} %collective-permute-done.58.other_ref.refs_4_, ...), custom_call_target="tpu_custom_call" | custom-call | flops 1 | bytes 1 | tf_op jit(solution)/shard_map/pallas_call | solution.py:333
  435.0 15.4 %collective-permute-done.61 = bf16[512,1024]{1,0:T(8,128)(2,1)S(1)} collective-permute-done((bf16[512,1024]{1,0:T(8,128)(2,1)S(1)}, bf16[512,1024]{1,0:T(8,128)(2,1)S(1)}, u32[]{:S(2)}, u32[]{:S(2)}) %collective-permute-start.61) | collective-permute-done | bytes 1048608 | tf_op jit(solution)/shard_map/ppermute | solution.py:157
  454.5 3.7 collective-permute-start.68
  459.0 18.5 %collective-permute-done.65 = bf16[512,1024]{1,0:T(8,128)(2,1)S(1)} collective-permute-done((bf16[512,1024]{1,0:T(8,128)(2,1)S(1)}, bf16[512,1024]{1,0:T(8,128)(2,1)S(1)}, u32[]{:S(2)}, u32[]{:S(2)}) %collective-permute-start.65) | collective-permute-done | bytes 1048608 | tf_op jit(solution)/shard_map/ppermute | solution.py:157
  484.7 3.7 collective-permute-start.73
  489.2 4.2 shard_map.241
  495.5 8.7 %collective-permute-done.70.refs_2_ = bf16[128,2048]{1,0:T(8,128)(2,1)S(1)} collective-permute-done((bf16[128,2048]{1,0:T(8,128)(2,1)S(1)}, bf16[128,2048]{1,0:T(8,128)(2,1)S(1)}, u32[]{:S(2)}, u32[]{:S(2)}) %collective-permute-start.70) | collective-permute-done | bytes 524320 | tf_op jit(solution)/shard_map/ppermute | solution.py:157
  504.1 3.9 collective-permute-done.73.came_ref
  509.1 3.7 collective-permute-start.75
  513.8 17.7 %collective-permute-done.75.refs_6_ = bf16[512,1024]{1,0:T(8,128)(2,1)S(1)} collective-permute-done((bf16[512,1024]{1,0:T(8,128)(2,1)S(1)}, bf16[512,1024]{1,0:T(8,128)(2,1)S(1)}, u32[]{:S(2)}, u32[]{:S(2)}) %collective-permute-start.75) | collective-permute-done | bytes 1048608 | tf_op jit(solution)/shard_map/ppermute | solution.py:157
  532.5 3.7 collective-permute-start.77
  537.4 3.3 shard_map.244
  540.7 7.8 %shard_map.243 = (bf16[512,640]{1,0:T(8,128)(2,1)S(1)}, bf16[512,640]{1,0:T(8,128)(2,1)S(1)}, bf16[512,640]{1,0:T(8,128)(2,1)S(1)}, bf16[512,640]{1,0:T(8,128)(2,1)S(1)}) custom-call(bf16[512,2048]{1,0:T(8,128)(2,1)S(1)} %copy-done.42, bf16[512,2048]{1,0:T(8,128)(2,1)S(1)} %copy-done.44, bf16[1024,384]{1,0:T(8,128)(2,1)S(1)} %shard_map.242.refs_2_.refs_0_, ...), custom_call_target="tpu_custom_call" | custom-call | flops 1 | bytes 1 | tf_op jit(solution)/shard_map/pallas_call | solution.py:658
  548.6 6.1 collective-permute-done.77.refs_2_
  555.6 4.0 collective-permute-start.82
  561.7 9.3 %collective-permute-done.78 = bf16[512,640]{1,0:T(8,128)(2,1)S(1)} collective-permute-done((bf16[512,640]{1,0:T(8,128)(2,1)S(1)}, bf16[512,640]{1,0:T(8,128)(2,1)S(1)}, u32[]{:S(2)}, u32[]{:S(2)}) %collective-permute-start.78) | collective-permute-done | bytes 655392 | tf_op jit(solution)/shard_map/ppermute | solution.py:157
  571.2 5.3 collective-permute-done.82.refs_4_
  581.9 6.1 collective-permute-start.87
  588.0 4.2 shard_map.246
  592.2 8.3 %collective-permute-done.85.refs_3_ = bf16[128,2048]{1,0:T(8,128)(2,1)S(1)} collective-permute-done((bf16[128,2048]{1,0:T(8,128)(2,1)S(1)}, bf16[128,2048]{1,0:T(8,128)(2,1)S(1)}, u32[]{:S(2)}, u32[]{:S(2)}) %collective-permute-start.85) | collective-permute-done | bytes 524320 | tf_op jit(solution)/shard_map/ppermute | solution.py:157
  600.5 4.0 collective-permute-start.88
  604.5 4.3 collective-permute-done.87.refs_6_
  615.1 5.9 collective-permute-done.92.refs_0_
  621.5 4.3 collective-permute-start.97
  630.3 4.2 shard_map.250
  641.3 8.1 %collective-permute-done.100.refs_4_ = bf16[512,640]{1,0:T(8,128)(2,1)S(1)} collective-permute-done((bf16[512,640]{1,0:T(8,128)(2,1)S(1)}, bf16[512,640]{1,0:T(8,128)(2,1)S(1)}, u32[]{:S(2)}, u32[]{:S(2)}) %collective-permute-start.100) | collective-permute-done | bytes 655392 | tf_op jit(solution)/shard_map/ppermute | solution.py:157
  654.1 4.0 collective-permute-start.102
  666.6 3.6 shard_map.252
  (507 shorter events, 215.1 us)
Async XLA Ops:
  28.3 26.8 %collective-permute-start.6 = (bf16[768,640]{1,0:T(8,128)(2,1)}, bf16[768,640]{1,0:T(8,128)(2,1)S(1)}, u32[]{:S(2)}, u32[]{:S(2)}) collective-permute-start(bf16[768,640]{1,0:T(8,128)(2,1)} %shard_map.213), channel_id=1, source_target_pairs={{0,2},{2,0},{4,6},{6,4},{1,3},{3,1},{5,7},{7,5},{8,10},{10,8},{12,... | collective-permute-start | bytes 2949128 | tf_op jit(solution)/shard_map/ppermute | solution.py:157
  31.3 23.8 %collective-permute-start.4 = (bf16[128,2048]{1,0:T(8,128)(2,1)}, bf16[128,2048]{1,0:T(8,128)(2,1)}, u32[]{:S(2)}, u32[]{:S(2)}) collective-permute-start(bf16[128,2048]{1,0:T(8,128)(2,1)} %get-tuple-element.311), channel_id=1, source_target_pairs={{0,16},{8,24},{16,0},{24,8},{1,17},{9,25},{17,1},{25,9},{2,18},{10... | collective-permute-start | bytes 1572872 | tf_op jit(solution)/shard_map/ppermute | solution.py:157
  32.3 22.8 %collective-permute-start.5 = (bf16[128,2048]{1,0:T(8,128)(2,1)}, bf16[128,2048]{1,0:T(8,128)(2,1)}, u32[]{:S(2)}, u32[]{:S(2)}) collective-permute-start(bf16[128,2048]{1,0:T(8,128)(2,1)} %get-tuple-element.312), channel_id=1, source_target_pairs={{0,24},{8,16},{16,8},{24,0},{1,25},{9,17},{17,9},{25,1},{2,26},{10... | collective-permute-start | bytes 1572872 | tf_op jit(solution)/shard_map/ppermute | solution.py:157
  57.2 25.6 %collective-permute-start.7 = (bf16[512,1024]{1,0:T(8,128)(2,1)S(1)}, bf16[512,1024]{1,0:T(8,128)(2,1)S(1)}, u32[]{:S(2)}, u32[]{:S(2)}) collective-permute-start(bf16[512,1024]{1,0:T(8,128)(2,1)S(1)} %copy-done.110), channel_id=1, source_target_pairs={{0,8},{8,0},{16,24},{24,16},{1,9},{9,1},{17,25},{25,17},{2,10},{10... | collective-permute-start | bytes 3145736 | tf_op jit(solution)/shard_map/ppermute | solution.py:157
  57.9 25.2 %collective-permute-start.8 = (bf16[512,1024]{1,0:T(8,128)(2,1)S(1)}, bf16[512,1024]{1,0:T(8,128)(2,1)S(1)}, u32[]{:S(2)}, u32[]{:S(2)}) collective-permute-start(bf16[512,1024]{1,0:T(8,128)(2,1)S(1)} %copy-done.109), channel_id=1, source_target_pairs={{0,16},{8,24},{16,0},{24,8},{1,17},{9,25},{17,1},{25,9},{2,18},{10... | collective-permute-start | bytes 3145736 | tf_op jit(solution)/shard_map/ppermute | solution.py:157
  83.2 25.3 %collective-permute-start.13 = (bf16[512,1024]{1,0:T(8,128)(2,1)S(1)}, bf16[512,1024]{1,0:T(8,128)(2,1)S(1)}, u32[]{:S(2)}, u32[]{:S(2)}) collective-permute-start(bf16[512,1024]{1,0:T(8,128)(2,1)S(1)} %pad_maximum_fusion.2), channel_id=1, source_target_pairs={{0,24},{8,16},{16,8},{24,0},{1,25},{9,17},{17,9},{25,1},{2,26},{10... | collective-permute-start | bytes 3145736 | tf_op jit(solution)/shard_map/ppermute | solution.py:157
  85.4 21.4 %collective-permute-start.11 = (bf16[2,512,128]{2,1,0:T(8,128)(2,1)S(1)}, bf16[2,512,128]{2,1,0:T(8,128)(2,1)S(1)}, u32[]{:S(2)}, u32[]{:S(2)}) collective-permute-start(bf16[2,512,128]{2,1,0:T(8,128)(2,1)S(1)} %get-tuple-element.333.refs_0_), channel_id=1, source_target_pairs={{0,4},{2,6},{4,0},{6,2},{1,5},{3,7},{5,1},{7,3},{8,12},{10,14},{12... | collective-permute-start | bytes 786440 | tf_op jit(solution)/shard_map/ppermute | solution.py:157
  88.0 19.5 %collective-permute-start.12 = (bf16[2,512,128]{2,1,0:T(8,128)(2,1)S(1)}, bf16[2,512,128]{2,1,0:T(8,128)(2,1)S(1)}, u32[]{:S(2)}, u32[]{:S(2)}) collective-permute-start(bf16[2,512,128]{2,1,0:T(8,128)(2,1)S(1)} %get-tuple-element.333.refs_0_), channel_id=1, source_target_pairs={{0,6},{2,4},{4,2},{6,0},{1,7},{3,5},{5,3},{7,1},{8,14},{10,12},{12... | collective-permute-start | bytes 786440 | tf_op jit(solution)/shard_map/ppermute | solution.py:157
  108.5 28.5 %collective-permute-start.17 = (bf16[512,1024]{1,0:T(8,128)(2,1)S(1)}, bf16[512,1024]{1,0:T(8,128)(2,1)}, u32[]{:S(2)}, u32[]{:S(2)}) collective-permute-start(bf16[512,1024]{1,0:T(8,128)(2,1)S(1)} %collective-permute-done.7.refs_4_.refs_5_.refs_2_.refs_3_), channel_id=1, source_target_pairs={{0,2},{2,0},{4,6},{6,4},{1,3},{3,1},{5,7},{7,5},{8,10},{10,8},{12,... | collective-permute-start | bytes 3145736 | tf_op jit(solution)/shard_map/ppermute | solution.py:157
  111.7 25.3 %collective-permute-start.14 = (bf16[128,2048]{1,0:T(8,128)(2,1)}, bf16[128,2048]{1,0:T(8,128)(2,1)}, u32[]{:S(2)}, u32[]{:S(2)}) collective-permute-start(bf16[128,2048]{1,0:T(8,128)(2,1)} %get-tuple-element.340), channel_id=1, source_target_pairs={{0,8},{8,0},{16,24},{24,16},{1,9},{9,1},{17,25},{25,17},{2,10},{10... | collective-permute-start | bytes 1572872 | tf_op jit(solution)/shard_map/ppermute | solution.py:157
  112.4 24.5 %collective-permute-start.15 = (bf16[128,2048]{1,0:T(8,128)(2,1)}, bf16[128,2048]{1,0:T(8,128)(2,1)}, u32[]{:S(2)}, u32[]{:S(2)}) collective-permute-start(bf16[128,2048]{1,0:T(8,128)(2,1)} %get-tuple-element.341), channel_id=1, source_target_pairs={{0,16},{8,24},{16,0},{24,8},{1,17},{9,25},{17,1},{25,9},{2,18},{10... | collective-permute-start | bytes 1572872 | tf_op jit(solution)/shard_map/ppermute | solution.py:157
  113.4 23.6 %collective-permute-start.16 = (bf16[128,2048]{1,0:T(8,128)(2,1)}, bf16[128,2048]{1,0:T(8,128)(2,1)}, u32[]{:S(2)}, u32[]{:S(2)}) collective-permute-start(bf16[128,2048]{1,0:T(8,128)(2,1)} %get-tuple-element.342), channel_id=1, source_target_pairs={{0,24},{8,16},{16,8},{24,0},{1,25},{9,17},{17,9},{25,1},{2,26},{10... | collective-permute-start | bytes 1572872 | tf_op jit(solution)/shard_map/ppermute | solution.py:157
  141.2 26.2 %collective-permute-start.19 = (bf16[512,1024]{1,0:T(8,128)(2,1)S(1)}, bf16[512,1024]{1,0:T(8,128)(2,1)S(1)}, u32[]{:S(2)}, u32[]{:S(2)}) collective-permute-start(bf16[512,1024]{1,0:T(8,128)(2,1)S(1)} %collective-permute-done.8.refs_6_.refs_7_.refs_4_.refs_5_), channel_id=1, source_target_pairs={{0,2},{2,0},{4,6},{6,4},{1,3},{3,1},{5,7},{7,5},{8,10},{10,8},{12,... | collective-permute-start | bytes 3145736 | tf_op jit(solution)/shard_map/ppermute | solution.py:157
  143.6 23.8 %collective-permute-start.22 = (bf16[128,2048]{1,0:T(8,128)(2,1)S(1)}, bf16[128,2048]{1,0:T(8,128)(2,1)S(1)}, u32[]{:S(2)}, u32[]{:S(2)}) collective-permute-start(bf16[128,2048]{1,0:T(8,128)(2,1)S(1)} %get-tuple-element.362), channel_id=1, source_target_pairs={{0,24},{8,16},{16,8},{24,0},{1,25},{9,17},{17,9},{25,1},{2,26},{10... | collective-permute-start | bytes 1572872 | tf_op jit(solution)/shard_map/ppermute | solution.py:157
  167.4 30.0 %collective-permute-start.24 = (bf16[512,2048]{1,0:T(8,128)(2,1)S(1)}, bf16[512,2048]{1,0:T(8,128)(2,1)S(1)}, u32[]{:S(2)}, u32[]{:S(2)}) collective-permute-start(bf16[512,2048]{1,0:T(8,128)(2,1)S(1)} %shard_map.220.refs_1_.refs_0_), channel_id=1, source_target_pairs={{0,1},{1,0},{2,3},{3,2},{4,5},{5,4},{6,7},{7,6},{8,9},{9,8},{10,11... | collective-permute-start | bytes 6291464 | tf_op jit(solution)/shard_map/ppermute | solution.py:157
  167.4 30.0 %collective-permute-start.23 = (bf16[512,1024]{1,0:T(8,128)(2,1)S(1)}, bf16[512,1024]{1,0:T(8,128)(2,1)S(1)}, u32[]{:S(2)}, u32[]{:S(2)}) collective-permute-start(bf16[512,1024]{1,0:T(8,128)(2,1)S(1)} %collective-permute-done.13.refs_8_.refs_9_.refs_6_.refs_7_), channel_id=1, source_target_pairs={{0,2},{2,0},{4,6},{6,4},{1,3},{3,1},{5,7},{7,5},{8,10},{10,8},{12,... | collective-permute-start | bytes 3145736 | tf_op jit(solution)/shard_map/ppermute | solution.py:157
  172.5 24.9 %collective-permute-start.26 = (bf16[128,2048]{1,0:T(8,128)(2,1)S(1)}, bf16[128,2048]{1,0:T(8,128)(2,1)S(1)}, u32[]{:S(2)}, u32[]{:S(2)}) collective-permute-start(bf16[128,2048]{1,0:T(8,128)(2,1)S(1)} %get-tuple-element.376), channel_id=1, source_target_pairs={{0,16},{8,24},{16,0},{24,8},{1,17},{9,25},{17,1},{25,9},{2,18},{10... | collective-permute-start | bytes 1572872 | tf_op jit(solution)/shard_map/ppermute | solution.py:157
  173.5 23.9 %collective-permute-start.27 = (bf16[128,2048]{1,0:T(8,128)(2,1)S(1)}, bf16[128,2048]{1,0:T(8,128)(2,1)S(1)}, u32[]{:S(2)}, u32[]{:S(2)}) collective-permute-start(bf16[128,2048]{1,0:T(8,128)(2,1)S(1)} %get-tuple-element.377), channel_id=1, source_target_pairs={{0,24},{8,16},{16,8},{24,0},{1,25},{9,17},{17,9},{25,1},{2,26},{10... | collective-permute-start | bytes 1572872 | tf_op jit(solution)/shard_map/ppermute | solution.py:157
  197.7 25.8 %collective-permute-start.28 = (bf16[512,1024]{1,0:T(8,128)(2,1)S(1)}, bf16[512,1024]{1,0:T(8,128)(2,1)S(1)}, u32[]{:S(2)}, u32[]{:S(2)}) collective-permute-start(bf16[512,1024]{1,0:T(8,128)(2,1)S(1)} %pad_maximum_fusion.3), channel_id=1, source_target_pairs={{0,8},{8,0},{16,24},{24,16},{1,9},{9,1},{17,25},{25,17},{2,10},{10... | collective-permute-start | bytes 3145736 | tf_op jit(solution)/shard_map/ppermute | solution.py:157
  198.5 26.0 %collective-permute-start.29 = (bf16[512,1024]{1,0:T(8,128)(2,1)S(1)}, bf16[512,1024]{1,0:T(8,128)(2,1)S(1)}, u32[]{:S(2)}, u32[]{:S(2)}) collective-permute-start(bf16[512,1024]{1,0:T(8,128)(2,1)S(1)} %pad_maximum_fusion.4), channel_id=1, source_target_pairs={{0,16},{8,24},{16,0},{24,8},{1,17},{9,25},{17,1},{25,9},{2,18},{10... | collective-permute-start | bytes 3145736 | tf_op jit(solution)/shard_map/ppermute | solution.py:157
  225.5 25.5 %collective-permute-start.32 = (bf16[512,1024]{1,0:T(8,128)(2,1)}, bf16[512,1024]{1,0:T(8,128)(2,1)}, u32[]{:S(2)}, u32[]{:S(2)}) collective-permute-start(bf16[512,1024]{1,0:T(8,128)(2,1)} %get-tuple-element.397), channel_id=1, source_target_pairs={{0,8},{8,0},{16,24},{24,16},{1,9},{9,1},{17,25},{25,17},{2,10},{10... | collective-permute-start | bytes 3145736 | tf_op jit(solution)/shard_map/ppermute | solution.py:157
  226.2 25.2 %collective-permute-start.33 = (bf16[512,1024]{1,0:T(8,128)(2,1)}, bf16[512,1024]{1,0:T(8,128)(2,1)}, u32[]{:S(2)}, u32[]{:S(2)}) collective-permute-start(bf16[512,1024]{1,0:T(8,128)(2,1)} %get-tuple-element.398), channel_id=1, source_target_pairs={{0,16},{8,24},{16,0},{24,8},{1,17},{9,25},{17,1},{25,9},{2,18},{10... | collective-permute-start | bytes 3145736 | tf_op jit(solution)/shard_map/ppermute | solution.py:157
  227.2 24.7 %collective-permute-start.31 = (bf16[512,1024]{1,0:T(8,128)(2,1)}, bf16[512,1024]{1,0:T(8,128)(2,1)}, u32[]{:S(2)}, u32[]{:S(2)}) collective-permute-start(bf16[512,1024]{1,0:T(8,128)(2,1)} %get-tuple-element.396), channel_id=1, source_target_pairs={{0,2},{6,4},{1,3},{7,5},{8,10},{14,12},{9,11},{15,13},{16,18},{22,... | collective-permute-start | bytes 3145736 | tf_op jit(solution)/shard_map/ppermute | solution.py:157
  254.6 24.2 %collective-permute-start.35 = (bf16[512,1024]{1,0:T(8,128)(2,1)S(1)}, bf16[512,1024]{1,0:T(8,128)(2,1)S(1)}, u32[]{:S(2)}, u32[]{:S(2)}) collective-permute-start(bf16[512,1024]{1,0:T(8,128)(2,1)S(1)} %get-tuple-element.597), channel_id=1, source_target_pairs={{0,2},{6,4},{2,0},{4,6},{1,3},{7,5},{3,1},{5,7},{8,10},{14,12},{10... | collective-permute-start | bytes 3145736 | tf_op jit(solution)/shard_map/ppermute | solution.py:157
  256.9 22.0 %collective-permute-start.34 = (bf16[512,1024]{1,0:T(8,128)(2,1)S(1)}, bf16[512,1024]{1,0:T(8,128)(2,1)S(1)}, u32[]{:S(2)}, u32[]{:S(2)}) collective-permute-start(bf16[512,1024]{1,0:T(8,128)(2,1)S(1)} %get-tuple-element.598.half_ref), channel_id=1, source_target_pairs={{2,4},{4,2},{3,5},{5,3},{10,12},{12,10},{11,13},{13,11},{18,20},{2... | collective-permute-start | bytes 3145736 | tf_op jit(solution)/shard_map/ppermute | solution.py:157
  257.6 31.6 %collective-permute-start.36 = (bf16[512,1024]{1,0:T(8,128)(2,1)S(1)}, bf16[512,1024]{1,0:T(8,128)(2,1)S(1)}, u32[]{:S(2)}, u32[]{:S(2)}) collective-permute-start(bf16[512,1024]{1,0:T(8,128)(2,1)S(1)} %pad_maximum_fusion.8), channel_id=1, source_target_pairs={{0,24},{8,16},{16,8},{24,0},{1,25},{9,17},{17,9},{25,1},{2,26},{10... | collective-permute-start | bytes 3145736 | tf_op jit(solution)/shard_map/ppermute | solution.py:157
  280.9 21.2 %collective-permute-start.37 = (bf16[512,1024]{1,0:T(8,128)(2,1)S(1)}, bf16[512,1024]{1,0:T(8,128)(2,1)S(1)}, u32[]{:S(2)}, u32[]{:S(2)}) collective-permute-start(bf16[512,1024]{1,0:T(8,128)(2,1)S(1)} %get-tuple-element.411), channel_id=1, source_target_pairs={{2,4},{4,2},{3,5},{5,3},{10,12},{12,10},{11,13},{13,11},{18,20},{2... | collective-permute-start | bytes 3145736 | tf_op jit(solution)/shard_map/ppermute | solution.py:157
  281.8 28.1 %collective-permute-start.38 = (bf16[512,1024]{1,0:T(8,128)(2,1)S(1)}, bf16[512,1024]{1,0:T(8,128)(2,1)S(1)}, u32[]{:S(2)}, u32[]{:S(2)}) collective-permute-start(bf16[512,1024]{1,0:T(8,128)(2,1)S(1)} %get-tuple-element.412.refs_1_), channel_id=1, source_target_pairs={{0,2},{6,4},{2,0},{4,6},{1,3},{7,5},{3,1},{5,7},{8,10},{14,12},{10... | collective-permute-start | bytes 3145736 | tf_op jit(solution)/shard_map/ppermute | solution.py:157
  289.2 30.9 %collective-permute-start.39 = (bf16[512,1024]{1,0:T(8,128)(2,1)S(1)}, bf16[512,1024]{1,0:T(8,128)(2,1)S(1)}, u32[]{:S(2)}, u32[]{:S(2)}) collective-permute-start(bf16[512,1024]{1,0:T(8,128)(2,1)S(1)} %copy-done.91), channel_id=1, source_target_pairs={{0,24},{8,16},{16,8},{24,0},{1,25},{9,17},{17,9},{25,1},{2,26},{10... | collective-permute-start | bytes 3145736 | tf_op jit(solution)/shard_map/ppermute | solution.py:157
  312.2 21.9 %collective-permute-start.41 = (bf16[512,1024]{1,0:T(8,128)(2,1)S(1)}, bf16[512,1024]{1,0:T(8,128)(2,1)S(1)}, u32[]{:S(2)}, u32[]{:S(2)}) collective-permute-start(bf16[512,1024]{1,0:T(8,128)(2,1)S(1)} %fusion.refs_3_), channel_id=1, source_target_pairs={{0,2},{6,4},{2,0},{4,6},{1,3},{7,5},{3,1},{5,7},{8,10},{14,12},{10... | collective-permute-start | bytes 3145736 | tf_op jit(solution)/shard_map/ppermute | solution.py:157
  314.0 20.1 %collective-permute-start.40 = (bf16[512,1024]{1,0:T(8,128)(2,1)S(1)}, bf16[512,1024]{1,0:T(8,128)(2,1)S(1)}, u32[]{:S(2)}, u32[]{:S(2)}) collective-permute-start(bf16[512,1024]{1,0:T(8,128)(2,1)S(1)} %add_convert_fusion.22), channel_id=1, source_target_pairs={{2,4},{4,2},{3,5},{5,3},{10,12},{12,10},{11,13},{13,11},{18,20},{2... | collective-permute-start | bytes 3145736 | tf_op jit(solution)/shard_map/ppermute | solution.py:157
  320.0 31.3 %collective-permute-start.42 = (bf16[512,2048]{1,0:T(8,128)(2,1)S(1)}, bf16[512,2048]{1,0:T(8,128)(2,1)S(1)}, u32[]{:S(2)}, u32[]{:S(2)}) collective-permute-start(bf16[512,2048]{1,0:T(8,128)(2,1)S(1)} %shard_map.229), channel_id=1, source_target_pairs={{0,1},{1,0},{2,3},{3,2},{4,5},{5,4},{6,7},{7,6},{8,9},{9,8},{10,11... | collective-permute-start | bytes 6291464 | tf_op jit(solution)/shard_map/ppermute | solution.py:157
  320.1 31.2 %collective-permute-start.43 = (bf16[512,1024]{1,0:T(8,128)(2,1)S(1)}, bf16[512,1024]{1,0:T(8,128)(2,1)S(1)}, u32[]{:S(2)}, u32[]{:S(2)}) collective-permute-start(bf16[512,1024]{1,0:T(8,128)(2,1)S(1)} %get-tuple-element.434), channel_id=1, source_target_pairs={{0,8},{8,0},{16,24},{24,16},{1,9},{9,1},{17,25},{25,17},{2,10},{10... | collective-permute-start | bytes 3145736 | tf_op jit(solution)/shard_map/ppermute | solution.py:157
  321.5 29.9 %collective-permute-start.44 = (bf16[512,1024]{1,0:T(8,128)(2,1)S(1)}, bf16[512,1024]{1,0:T(8,128)(2,1)S(1)}, u32[]{:S(2)}, u32[]{:S(2)}) collective-permute-start(bf16[512,1024]{1,0:T(8,128)(2,1)S(1)} %get-tuple-element.435), channel_id=1, source_target_pairs={{0,16},{8,24},{16,0},{24,8},{1,17},{9,25},{17,1},{25,9},{2,18},{10... | collective-permute-start | bytes 3145736 | tf_op jit(solution)/shard_map/ppermute | solution.py:157
  335.2 22.6 %collective-permute-start.46 = (bf16[512,1024]{1,0:T(8,128)(2,1)S(1)}, bf16[512,1024]{1,0:T(8,128)(2,1)S(1)}, u32[]{:S(2)}, u32[]{:S(2)}) collective-permute-start(bf16[512,1024]{1,0:T(8,128)(2,1)S(1)} %fusion.1.refs_5_), channel_id=1, source_target_pairs={{0,2},{6,4},{2,0},{4,6},{1,3},{7,5},{3,1},{5,7},{8,10},{14,12},{10... | collective-permute-start | bytes 3145736 | tf_op jit(solution)/shard_map/ppermute | solution.py:157
  338.9 18.9 %collective-permute-start.45 = (bf16[512,1024]{1,0:T(8,128)(2,1)S(1)}, bf16[512,1024]{1,0:T(8,128)(2,1)S(1)}, u32[]{:S(2)}, u32[]{:S(2)}) collective-permute-start(bf16[512,1024]{1,0:T(8,128)(2,1)S(1)} %add_convert_fusion.20), channel_id=1, source_target_pairs={{2,4},{4,2},{3,5},{5,3},{10,12},{12,10},{11,13},{13,11},{18,20},{2... | collective-permute-start | bytes 3145736 | tf_op jit(solution)/shard_map/ppermute | solution.py:157
  353.2 19.6 %collective-permute-start.48 = (bf16[128,2048]{1,0:T(8,128)(2,1)S(1)}, bf16[128,2048]{1,0:T(8,128)(2,1)S(1)}, u32[]{:S(2)}, u32[]{:S(2)}) collective-permute-start(bf16[128,2048]{1,0:T(8,128)(2,1)S(1)} %get-tuple-element.444), channel_id=1, source_target_pairs={{0,16},{8,24},{16,0},{24,8},{1,17},{9,25},{17,1},{25,9},{2,18},{10... | collective-permute-start | bytes 1572872 | tf_op jit(solution)/shard_map/ppermute | solution.py:157
  354.2 20.1 %collective-permute-start.49 = (bf16[128,2048]{1,0:T(8,128)(2,1)S(1)}, bf16[128,2048]{1,0:T(8,128)(2,1)S(1)}, u32[]{:S(2)}, u32[]{:S(2)}) collective-permute-start(bf16[128,2048]{1,0:T(8,128)(2,1)S(1)} %get-tuple-element.445), channel_id=1, source_target_pairs={{0,24},{8,16},{16,8},{24,0},{1,25},{9,17},{17,9},{25,1},{2,26},{10... | collective-permute-start | bytes 1572872 | tf_op jit(solution)/shard_map/ppermute | solution.py:157
  358.9 22.7 %collective-permute-start.51 = (bf16[512,1024]{1,0:T(8,128)(2,1)S(1)}, bf16[512,1024]{1,0:T(8,128)(2,1)S(1)}, u32[]{:S(2)}, u32[]{:S(2)}) collective-permute-start(bf16[512,1024]{1,0:T(8,128)(2,1)S(1)} %fusion.2.refs_1_), channel_id=1, source_target_pairs={{0,2},{6,4},{2,0},{4,6},{1,3},{7,5},{3,1},{5,7},{8,10},{14,12},{10... | collective-permute-start | bytes 3145736 | tf_op jit(solution)/shard_map/ppermute | solution.py:157
  362.6 19.0 %collective-permute-start.50 = (bf16[512,1024]{1,0:T(8,128)(2,1)S(1)}, bf16[512,1024]{1,0:T(8,128)(2,1)S(1)}, u32[]{:S(2)}, u32[]{:S(2)}) collective-permute-start(bf16[512,1024]{1,0:T(8,128)(2,1)S(1)} %add_convert_fusion.18), channel_id=1, source_target_pairs={{2,4},{4,2},{3,5},{5,3},{10,12},{12,10},{11,13},{13,11},{18,20},{2... | collective-permute-start | bytes 3145736 | tf_op jit(solution)/shard_map/ppermute | solution.py:157
  376.9 18.9 %collective-permute-start.53 = (bf16[128,2048]{1,0:T(8,128)(2,1)S(1)}, bf16[128,2048]{1,0:T(8,128)(2,1)S(1)}, u32[]{:S(2)}, u32[]{:S(2)}) collective-permute-start(bf16[128,2048]{1,0:T(8,128)(2,1)S(1)} %get-tuple-element.457), channel_id=1, source_target_pairs={{0,16},{8,24},{16,0},{24,8},{1,17},{9,25},{17,1},{25,9},{2,18},{10... | collective-permute-start | bytes 1572872 | tf_op jit(solution)/shard_map/ppermute | solution.py:157
  382.2 20.9 %collective-permute-start.56 = (bf16[512,1024]{1,0:T(8,128)(2,1)S(1)}, bf16[512,1024]{1,0:T(8,128)(2,1)S(1)}, u32[]{:S(2)}, u32[]{:S(2)}) collective-permute-start(bf16[512,1024]{1,0:T(8,128)(2,1)S(1)} %fusion.3.refs_7_), channel_id=1, source_target_pairs={{0,2},{6,4},{2,0},{4,6},{1,3},{7,5},{3,1},{5,7},{8,10},{14,12},{10... | collective-permute-start | bytes 3145736 | tf_op jit(solution)/shard_map/ppermute | solution.py:157
  399.2 28.8 %collective-permute-start.57 = (bf16[512,1024]{1,0:T(8,128)(2,1)S(1)}, bf16[512,1024]{1,0:T(8,128)(2,1)S(1)}, u32[]{:S(2)}, u32[]{:S(2)}) collective-permute-start(bf16[512,1024]{1,0:T(8,128)(2,1)S(1)} %shard_map.236), channel_id=1, source_target_pairs={{0,24},{8,16},{16,8},{24,0},{1,25},{9,17},{17,9},{25,1},{2,26},{10... | collective-permute-start | bytes 3145736 | tf_op jit(solution)/shard_map/ppermute | solution.py:157
  404.3 26.1 %collective-permute-start.60 = (bf16[512,1024]{1,0:T(8,128)(2,1)S(1)}, bf16[512,1024]{1,0:T(8,128)(2,1)S(1)}, u32[]{:S(2)}, u32[]{:S(2)}) collective-permute-start(bf16[512,1024]{1,0:T(8,128)(2,1)S(1)} %fusion.4.refs_1_), channel_id=1, source_target_pairs={{0,2},{6,4},{2,0},{4,6},{1,3},{7,5},{3,1},{5,7},{8,10},{14,12},{10... | collective-permute-start | bytes 3145736 | tf_op jit(solution)/shard_map/ppermute | solution.py:157
  408.0 22.4 %collective-permute-start.59 = (bf16[512,1024]{1,0:T(8,128)(2,1)S(1)}, bf16[512,1024]{1,0:T(8,128)(2,1)S(1)}, u32[]{:S(2)}, u32[]{:S(2)}) collective-permute-start(bf16[512,1024]{1,0:T(8,128)(2,1)S(1)} %add_convert_fusion.14), channel_id=1, source_target_pairs={{2,4},{4,2},{3,5},{5,3},{10,12},{12,10},{11,13},{13,11},{18,20},{2... | collective-permute-start | bytes 3145736 | tf_op jit(solution)/shard_map/ppermute | solution.py:157
  428.0 22.4 %collective-permute-start.61 = (bf16[512,1024]{1,0:T(8,128)(2,1)S(1)}, bf16[512,1024]{1,0:T(8,128)(2,1)S(1)}, u32[]{:S(2)}, u32[]{:S(2)}) collective-permute-start(bf16[512,1024]{1,0:T(8,128)(2,1)S(1)} %get-tuple-element.479), channel_id=1, source_target_pairs={{0,8},{8,0},{16,24},{24,16},{1,9},{9,1},{17,25},{25,17},{2,10},{10... | collective-permute-start | bytes 3145736 | tf_op jit(solution)/shard_map/ppermute | solution.py:157
  429.4 21.6 %collective-permute-start.62 = (bf16[512,1024]{1,0:T(8,128)(2,1)S(1)}, bf16[512,1024]{1,0:T(8,128)(2,1)S(1)}, u32[]{:S(2)}, u32[]{:S(2)}) collective-permute-start(bf16[512,1024]{1,0:T(8,128)(2,1)S(1)} %get-tuple-element.480), channel_id=1, source_target_pairs={{0,16},{8,24},{16,0},{24,8},{1,17},{9,25},{17,1},{25,9},{2,18},{10... | collective-permute-start | bytes 3145736 | tf_op jit(solution)/shard_map/ppermute | solution.py:157
  431.5 22.0 %collective-permute-start.64 = (bf16[512,1024]{1,0:T(8,128)(2,1)S(1)}, bf16[512,1024]{1,0:T(8,128)(2,1)S(1)}, u32[]{:S(2)}, u32[]{:S(2)}) collective-permute-start(bf16[512,1024]{1,0:T(8,128)(2,1)S(1)} %fusion.5.refs_3_), channel_id=1, source_target_pairs={{0,2},{6,4},{2,0},{4,6},{1,3},{7,5},{3,1},{5,7},{8,10},{14,12},{10... | collective-permute-start | bytes 3145736 | tf_op jit(solution)/shard_map/ppermute | solution.py:157
  434.3 19.2 %collective-permute-start.63 = (bf16[512,1024]{1,0:T(8,128)(2,1)S(1)}, bf16[512,1024]{1,0:T(8,128)(2,1)S(1)}, u32[]{:S(2)}, u32[]{:S(2)}) collective-permute-start(bf16[512,1024]{1,0:T(8,128)(2,1)S(1)} %add_convert_fusion.12), channel_id=1, source_target_pairs={{2,4},{4,2},{3,5},{5,3},{10,12},{12,10},{11,13},{13,11},{18,20},{2... | collective-permute-start | bytes 3145736 | tf_op jit(solution)/shard_map/ppermute | solution.py:157
  451.0 26.5 %collective-permute-start.66 = (bf16[512,2048]{1,0:T(8,128)(2,1)S(1)}, bf16[512,2048]{1,0:T(8,128)(2,1)S(1)}, u32[]{:S(2)}, u32[]{:S(2)}) collective-permute-start(bf16[512,2048]{1,0:T(8,128)(2,1)S(1)} %shard_map.234), channel_id=1, source_target_pairs={{0,1},{1,0},{2,3},{3,2},{4,5},{5,4},{6,7},{7,6},{8,9},{9,8},{10,11... | collective-permute-start | bytes 6291464 | tf_op jit(solution)/shard_map/ppermute | solution.py:157
  451.0 26.5 %collective-permute-start.65 = (bf16[512,1024]{1,0:T(8,128)(2,1)S(1)}, bf16[512,1024]{1,0:T(8,128)(2,1)S(1)}, u32[]{:S(2)}, u32[]{:S(2)}) collective-permute-start(bf16[512,1024]{1,0:T(8,128)(2,1)S(1)} %get-tuple-element.488), channel_id=1, source_target_pairs={{0,24},{8,16},{16,8},{24,0},{1,25},{9,17},{17,9},{25,1},{2,26},{10... | collective-permute-start | bytes 3145736 | tf_op jit(solution)/shard_map/ppermute | solution.py:157
  454.5 25.1 %collective-permute-start.68 = (bf16[512,1024]{1,0:T(8,128)(2,1)S(1)}, bf16[512,1024]{1,0:T(8,128)(2,1)S(1)}, u32[]{:S(2)}, u32[]{:S(2)}) collective-permute-start(bf16[512,1024]{1,0:T(8,128)(2,1)S(1)} %fusion.6.refs_5_), channel_id=1, source_target_pairs={{0,2},{6,4},{2,0},{4,6},{1,3},{7,5},{3,1},{5,7},{8,10},{14,12},{10... | collective-permute-start | bytes 3145736 | tf_op jit(solution)/shard_map/ppermute | solution.py:157
  458.3 21.4 %collective-permute-start.67 = (bf16[512,1024]{1,0:T(8,128)(2,1)S(1)}, bf16[512,1024]{1,0:T(8,128)(2,1)S(1)}, u32[]{:S(2)}, u32[]{:S(2)}) collective-permute-start(bf16[512,1024]{1,0:T(8,128)(2,1)S(1)} %add_convert_fusion.10), channel_id=1, source_target_pairs={{2,4},{4,2},{3,5},{5,3},{10,12},{12,10},{11,13},{13,11},{18,20},{2... | collective-permute-start | bytes 3145736 | tf_op jit(solution)/shard_map/ppermute | solution.py:157
  481.5 22.6 %collective-permute-start.70 = (bf16[128,2048]{1,0:T(8,128)(2,1)S(1)}, bf16[128,2048]{1,0:T(8,128)(2,1)S(1)}, u32[]{:S(2)}, u32[]{:S(2)}) collective-permute-start(bf16[128,2048]{1,0:T(8,128)(2,1)S(1)} %get-tuple-element.498), channel_id=1, source_target_pairs={{0,16},{8,24},{16,0},{24,8},{1,17},{9,25},{17,1},{25,9},{2,18},{10... | collective-permute-start | bytes 1572872 | tf_op jit(solution)/shard_map/ppermute | solution.py:157
  482.5 21.7 %collective-permute-start.71 = (bf16[128,2048]{1,0:T(8,128)(2,1)S(1)}, bf16[128,2048]{1,0:T(8,128)(2,1)S(1)}, u32[]{:S(2)}, u32[]{:S(2)}) collective-permute-start(bf16[128,2048]{1,0:T(8,128)(2,1)S(1)} %get-tuple-element.499), channel_id=1, source_target_pairs={{0,24},{8,16},{16,8},{24,0},{1,25},{9,17},{17,9},{25,1},{2,26},{10... | collective-permute-start | bytes 1572872 | tf_op jit(solution)/shard_map/ppermute | solution.py:157
  484.7 23.3 %collective-permute-start.73 = (bf16[512,1024]{1,0:T(8,128)(2,1)S(1)}, bf16[512,1024]{1,0:T(8,128)(2,1)S(1)}, u32[]{:S(2)}, u32[]{:S(2)}) collective-permute-start(bf16[512,1024]{1,0:T(8,128)(2,1)S(1)} %fusion.7.sent_ref), channel_id=1, source_target_pairs={{0,2},{6,4},{2,0},{4,6},{1,3},{7,5},{3,1},{5,7},{8,10},{14,12},{10... | collective-permute-start | bytes 3145736 | tf_op jit(solution)/shard_map/ppermute | solution.py:157
  488.4 19.6 %collective-permute-start.72 = (bf16[512,1024]{1,0:T(8,128)(2,1)S(1)}, bf16[512,1024]{1,0:T(8,128)(2,1)S(1)}, u32[]{:S(2)}, u32[]{:S(2)}) collective-permute-start(bf16[512,1024]{1,0:T(8,128)(2,1)S(1)} %add_convert_fusion.8), channel_id=1, source_target_pairs={{2,4},{4,2},{3,5},{5,3},{10,12},{12,10},{11,13},{13,11},{18,20},{2... | collective-permute-start | bytes 3145736 | tf_op jit(solution)/shard_map/ppermute | solution.py:157
  509.1 22.4 %collective-permute-start.75 = (bf16[512,1024]{1,0:T(8,128)(2,1)S(1)}, bf16[512,1024]{1,0:T(8,128)(2,1)S(1)}, u32[]{:S(2)}, u32[]{:S(2)}) collective-permute-start(bf16[512,1024]{1,0:T(8,128)(2,1)S(1)} %fusion.8.refs_7_), channel_id=1, source_target_pairs={{0,2},{6,4},{2,0},{4,6},{1,3},{7,5},{3,1},{5,7},{8,10},{14,12},{10... | collective-permute-start | bytes 3145736 | tf_op jit(solution)/shard_map/ppermute | solution.py:157
  532.5 22.2 %collective-permute-start.77 = (bf16[512,1024]{1,0:T(8,128)(2,1)S(1)}, bf16[512,1024]{1,0:T(8,128)(2,1)S(1)}, u32[]{:S(2)}, u32[]{:S(2)}) collective-permute-start(bf16[512,1024]{1,0:T(8,128)(2,1)S(1)} %fusion.9.refs_3_), channel_id=1, source_target_pairs={{0,2},{6,4},{2,0},{4,6},{1,3},{7,5},{3,1},{5,7},{8,10},{14,12},{10... | collective-permute-start | bytes 3145736 | tf_op jit(solution)/shard_map/ppermute | solution.py:157
  548.5 22.7 %collective-permute-start.80 = (bf16[512,2048]{1,0:T(8,128)(2,1)S(1)}, bf16[512,2048]{1,0:T(8,128)(2,1)S(1)}, u32[]{:S(2)}, u32[]{:S(2)}) collective-permute-start(bf16[512,2048]{1,0:T(8,128)(2,1)S(1)} %get-tuple-element.525), channel_id=1, source_target_pairs={{0,1},{1,0},{2,3},{3,2},{4,5},{5,4},{6,7},{7,6},{8,9},{9,8},{10,11... | collective-permute-start | bytes 6291464 | tf_op jit(solution)/shard_map/ppermute | solution.py:157
  555.6 20.9 %collective-permute-start.82 = (bf16[512,1024]{1,0:T(8,128)(2,1)S(1)}, bf16[512,1024]{1,0:T(8,128)(2,1)S(1)}, u32[]{:S(2)}, u32[]{:S(2)}) collective-permute-start(bf16[512,1024]{1,0:T(8,128)(2,1)S(1)} %fusion.10.refs_5_), channel_id=1, source_target_pairs={{0,2},{6,4},{2,0},{4,6},{1,3},{7,5},{3,1},{5,7},{8,10},{14,12},{10... | collective-permute-start | bytes 3145736 | tf_op jit(solution)/shard_map/ppermute | solution.py:157
  578.5 22.0 %collective-permute-start.85 = (bf16[128,2048]{1,0:T(8,128)(2,1)S(1)}, bf16[128,2048]{1,0:T(8,128)(2,1)S(1)}, u32[]{:S(2)}, u32[]{:S(2)}) collective-permute-start(bf16[128,2048]{1,0:T(8,128)(2,1)S(1)} %get-tuple-element.535), channel_id=1, source_target_pairs={{0,24},{8,16},{16,8},{24,0},{1,25},{9,17},{17,9},{25,1},{2,26},{10... | collective-permute-start | bytes 1572872 | tf_op jit(solution)/shard_map/ppermute | solution.py:157
  580.7 23.8 %collective-permute-start.86 = (bf16[512,640]{1,0:T(8,128)(2,1)S(1)}, bf16[512,640]{1,0:T(8,128)(2,1)S(1)}, u32[]{:S(2)}, u32[]{:S(2)}) collective-permute-start(bf16[512,640]{1,0:T(8,128)(2,1)S(1)} %add_convert_fusion.31), channel_id=1, source_target_pairs={{2,4},{4,2},{3,5},{5,3},{10,12},{12,10},{11,13},{13,11},{18,20},{2... | collective-permute-start | bytes 1966088 | tf_op jit(solution)/shard_map/ppermute | solution.py:157
  581.9 26.9 %collective-permute-start.87 = (bf16[512,1024]{1,0:T(8,128)(2,1)S(1)}, bf16[512,1024]{1,0:T(8,128)(2,1)S(1)}, u32[]{:S(2)}, u32[]{:S(2)}) collective-permute-start(bf16[512,1024]{1,0:T(8,128)(2,1)S(1)} %fusion.11.refs_7_), channel_id=1, source_target_pairs={{0,2},{6,4},{2,0},{4,6},{1,3},{7,5},{3,1},{5,7},{8,10},{14,12},{10... | collective-permute-start | bytes 3145736 | tf_op jit(solution)/shard_map/ppermute | solution.py:157
  (156 other events, 1735.1 us)
